TPU v7x, 32 devices: a whole 2x2x4 slice. The times are simulated.
32 devices in a mesh: gx: 4 (over z), gy: 8 (over y, x, core).
Axes of the slice: x: 2, y: 2, z: 4, core: 2. Of those that a mesh axis runs over, the one named last changes fastest.
Arguments:
- fine_rhs: float32 [4, 8, 4, 32, 1024], P('gx', 'gy'), may hold values from -6 to 6
- fine_beta: float32 [4, 8, 4, 32, 1024], P('gx', 'gy'), may hold values from 0.5 to 5
- base_rhs: float32 [64, 128, 128], P('gx', 'gy'), may hold values from -6 to 6
- base_beta: float32 [64, 128, 128], P('gx', 'gy'), may hold values from 0.5 to 5
- slot_site: int32 [4, 8, 4], P('gx', 'gy'), may hold values from 0 to 7, as said below
- ghost_list: int32 [4, 8, 4, 6], P('gx', 'gy'), may hold values from -1 to 3, as said below
- box_count: int32 [4, 8], P('gx', 'gy'), may hold values from 1 to 4, as said below
Outputs:
- fine_solution: float32 [4, 8, 4, 32, 1024], P('gx', 'gy')
- base_solution: float32 [64, 128, 128], P('gx', 'gy')
Inputs may be any that keep to these rules, and one draw needn't show every extreme that they name: `slot_site`: the slots of one column name distinct sites. `box_count`: some column holds exactly 4 live boxes in every draw. `ghost_list`: for a live slot, entry d is the slot of the live box at the adjacent site across face d (same site in the column beside it for x and y faces, the site below or above in the same column for z faces), or -1 if there is none; all entries of slots that are not live are -1.
All inputs are finite; a program needn't handle non-finite values.
Results may differ from a plain program's by a relative error of at most 0.0003.
Values sent between devices are 32-bit elements; how exact they have to be, the bound alone decides.
No kernel may reach another device: no remote copies, remote signals or barrier semaphores. Data moves between devices by JAX's collectives and lax.ppermute only.
A program may use at most 128 MiB of HBM per device.

v0:
```python
import jax
import jax.numpy as jnp
from jax import lax
from jax.sharding import PartitionSpec as P

CYCLES = 2
SWEEPS = 6


damping = 2.0 / 3.0


def with_halo(block, sides, width):
    for axis, dim in sides:
        count = lax.axis_size(axis)
        forward = [(i, i + 1) for i in range(count - 1)]
        backward = [(target, source) for source, target in forward]
        low = lax.ppermute(
            lax.slice_in_dim(block, block.shape[dim] - width, None, axis=dim), axis, forward
        )
        high = lax.ppermute(lax.slice_in_dim(block, 0, width, axis=dim), axis, backward)
        block = jnp.concatenate([low, block, high], axis=dim)
    return block


def from_behind(value, axis, steps):
    count = lax.axis_size(axis)
    first, last = (max(0, -steps), min(count, count - steps))
    return lax.ppermute(value, axis, [(source, source + steps) for source in range(first, last)])


def upsample(values, axis_list):
    for which_axis in axis_list:
        values = jnp.repeat(values, 2, axis=which_axis)
    return values


def shrink(values):
    size_x, size_y, size_z = values.shape
    blocks = values.reshape(size_x // 2, 2, size_y // 2, 2, size_z // 2, 2)
    return jnp.sum(blocks, axis=(1, 3, 5)) * 0.125


def level_apply(field, padded, coeffs, factor):
    nearby = padded[2:, 1:-1, 1:-1] + padded[:-2, 1:-1, 1:-1]
    nearby = nearby + padded[1:-1, 2:, 1:-1] + padded[1:-1, :-2, 1:-1]
    nearby = nearby + padded[1:-1, 1:-1, 2:] + padded[1:-1, 1:-1, :-2]
    return coeffs * factor * (6.0 * field - nearby)


def coarse_ghosts(halo_box, box_sites, extent):
    site_total = (halo_box.shape[2] - 2) // extent

    def from_plane(face_plane):
        slabs = jnp.take(face_plane.reshape(extent, site_total, extent), box_sites, axis=1)
        slabs = upsample(jnp.transpose(slabs, (1, 0, 2)), (1, 2))
        return slabs.reshape(slabs.shape[0], -1)

    column = halo_box[1:-1, 1:-1, :]

    def from_layer(layer_index):
        slabs = jnp.take(column, layer_index, axis=2)
        slabs = upsample(jnp.transpose(slabs, (2, 0, 1)), (1, 2))
        return slabs.reshape(slabs.shape[0], -1)

    return (
        from_plane(halo_box[0, 1:-1, 1:-1]),
        from_plane(halo_box[-1, 1:-1, 1:-1]),
        from_plane(halo_box[1:-1, 0, 1:-1]),
        from_plane(halo_box[1:-1, -1, 1:-1]),
        from_layer(box_sites * extent),
        from_layer((box_sites + 1) * extent + 1),
    )


def fine_faces(field):
    slot_total, fine_edge, face_area = field.shape
    return (
        field[:, 0, :],
        field[:, -1, :],
        field[:, :, :fine_edge].reshape(slot_total, face_area),
        field[:, :, face_area - fine_edge :].reshape(slot_total, face_area),
        field[:, :, 0::fine_edge].reshape(slot_total, face_area),
        field[:, :, fine_edge - 1 :: fine_edge].reshape(slot_total, face_area),
    )


def choose(received, link_index, fallback):
    picked = jnp.take(received, jnp.maximum(link_index, 0), axis=0)
    return jnp.where((link_index >= 0)[:, None], picked, fallback)


def assemble(face_set, from_west, from_east, from_south, from_north, coarse, link_table):
    return (
        choose(from_west, link_table[:, 0], coarse[0]),
        choose(from_east, link_table[:, 1], coarse[1]),
        choose(from_south, link_table[:, 2], coarse[2]),
        choose(from_north, link_table[:, 3], coarse[3]),
        choose(face_set[5], link_table[:, 4], coarse[4]),
        choose(face_set[4], link_table[:, 5], coarse[5]),
    )


def apply_fine(field, coeffs, layers):
    slot_total, fine_edge, face_area = field.shape
    depth_pos = jnp.arange(face_area) % fine_edge
    west_side = jnp.concatenate([layers[0][:, None, :], field[:, :-1, :]], axis=1)
    east_side = jnp.concatenate([field[:, 1:, :], layers[1][:, None, :]], axis=1)
    south_side = jnp.concatenate(
        [layers[2].reshape(slot_total, fine_edge, fine_edge), field[:, :, : face_area - fine_edge]],
        axis=2,
    )
    north_side = jnp.concatenate(
        [field[:, :, fine_edge:], layers[3].reshape(slot_total, fine_edge, fine_edge)], axis=2
    )
    zero_slab = jnp.zeros((slot_total, fine_edge, 1), field.dtype)
    lower_side = jnp.where(
        depth_pos == 0,
        jnp.repeat(layers[4].reshape(slot_total, fine_edge, fine_edge), fine_edge, axis=2),
        jnp.concatenate([zero_slab, field[:, :, :-1]], axis=2),
    )
    upper_side = jnp.where(
        depth_pos == fine_edge - 1,
        jnp.repeat(layers[5].reshape(slot_total, fine_edge, fine_edge), fine_edge, axis=2),
        jnp.concatenate([field[:, :, 1:], zero_slab], axis=2),
    )
    return coeffs * (
        6.0 * field - (west_side + east_side + south_side + north_side + lower_side + upper_side)
    )


def restrict_fine(field):
    slot_total, fine_edge, face_area = field.shape
    half_edge = fine_edge // 2
    blocks = field.reshape(slot_total, half_edge, 2, half_edge, 2, half_edge, 2)
    return jnp.sum(blocks, axis=(2, 4, 6)) * 0.125


def insert_blocks(coarse, blocks, box_sites, live_slots):
    extent = coarse.shape[0]
    site_total = coarse.shape[2] // extent
    slot_ids = jnp.arange(blocks.shape[0], dtype=jnp.int32)
    matches = (box_sites[None, :] == jnp.arange(site_total, dtype=jnp.int32)[:, None]) & live_slots[
        None, :
    ]
    owner = jnp.sum(jnp.where(matches, slot_ids[None, :] + 1, 0), axis=1) - 1
    picked = jnp.transpose(jnp.take(blocks, jnp.maximum(owner, 0), axis=0), (1, 2, 0, 3))
    stacked = coarse.reshape(extent, extent, site_total, extent)
    merged = jnp.where((owner >= 0)[None, None, :, None], picked, stacked)
    return merged.reshape(coarse.shape)


def prolong_fine(coarse, box_sites):
    extent = coarse.shape[0]
    site_total = coarse.shape[2] // extent
    slabs = jnp.take(coarse.reshape(extent, extent, site_total, extent), box_sites, axis=2)
    slabs = upsample(jnp.transpose(slabs, (2, 0, 1, 3)), (1, 2, 3))
    return slabs.reshape(slabs.shape[0], 2 * extent, -1)


def pad_depth(values):
    return jnp.pad(values, ((0, 0), (0, 0), (1, 1)))


def pad_solution(field):
    return pad_depth(with_halo(field, (("gx", 0), ("gy", 1)), 1))


def pad_correction(field):
    return pad_depth(with_halo(field, (("gx", 0), ("gy", 1)), 1))


def pad_coarsest(field):
    return pad_depth(with_halo(field, (("gx", 0), ("gy", 1)), 1))


def neighbour_faces(face_set):
    from_west = from_behind(face_set[1], "gx", 1)
    from_east = from_behind(face_set[0], "gx", -1)
    from_south = from_behind(face_set[3], "gy", 1)
    from_north = from_behind(face_set[2], "gy", -1)
    return (from_west, from_east, from_south, from_north)


def local(fine_rhs, fine_beta, base_rhs, base_beta, slot_site, ghost_list, box_count):
    rhs_fine = fine_rhs[0, 0]
    coeff_fine = fine_beta[0, 0]
    box_sites = slot_site[0, 0]
    link_table = ghost_list[0, 0]
    slot_total = rhs_fine.shape[0]
    extent = base_rhs.shape[0]
    live_slots = jnp.arange(slot_total, dtype=jnp.int32) < box_count[0, 0]
    keep_mask = live_slots.astype(jnp.float32)[:, None, None]
    coeff_levels = [base_beta]
    for level_index in range(3):
        coeff_levels.append(shrink(coeff_levels[-1]))
    factor_levels = [0.25 ** (level_index + 1) for level_index in range(4)]

    def multigrid(residual, level_index):
        coeffs = coeff_levels[level_index]
        factor = factor_levels[level_index]
        diagonal = 6.0 * coeffs * factor
        if level_index == 3:
            correction = damping * residual / diagonal
            for sweep_index in range(SWEEPS - 1):
                correction = (
                    correction
                    + damping
                    * (residual - level_apply(correction, pad_coarsest(correction), coeffs, factor))
                    / diagonal
                )
            return correction
        correction = damping * residual / diagonal
        leftover_part = residual - level_apply(
            correction, pad_correction(correction), coeffs, factor
        )
        correction = correction + upsample(
            multigrid(shrink(leftover_part), level_index + 1), (0, 1, 2)
        )
        return (
            correction
            + damping
            * (residual - level_apply(correction, pad_correction(correction), coeffs, factor))
            / diagonal
        )

    def ghost_layers(field, halo_box, received):
        face_set = fine_faces(field)
        received = neighbour_faces(face_set)
        from_west, from_east, from_south, from_north = received
        coarse = coarse_ghosts(halo_box, box_sites, extent)
        return assemble(face_set, from_west, from_east, from_south, from_north, coarse, link_table)

    def smooth(field, halo_box, received):
        layers = ghost_layers(field, halo_box, received)
        return (
            field
            + damping * (rhs_fine - apply_fine(field, coeff_fine, layers)) / (6.0 * coeff_fine)
        ) * keep_mask

    def prepare(base_values):
        return (pad_solution(base_values), None)

    fine_field = jnp.zeros_like(rhs_fine)
    base_field = jnp.zeros_like(base_rhs)
    for cycle_index in range(CYCLES):
        halo_box, received = prepare(base_field)
        fine_field = smooth(fine_field, halo_box, received)
        fine_left = rhs_fine - apply_fine(
            fine_field, coeff_fine, ghost_layers(fine_field, halo_box, None)
        )
        base_left = base_rhs - level_apply(base_field, halo_box, coeff_levels[0], factor_levels[0])
        base_left = insert_blocks(base_left, restrict_fine(fine_left), box_sites, live_slots)
        correction = multigrid(base_left, 0)
        base_field = base_field + correction
        fine_field = (fine_field + prolong_fine(correction, box_sites)) * keep_mask
        next_box, next_received = prepare(base_field)
        fine_field = smooth(fine_field, next_box, next_received)
        base_field = insert_blocks(base_field, restrict_fine(fine_field), box_sites, live_slots)
    return (fine_field[None, None], base_field)


def solution(mesh):
    return jax.shard_map(
        local,
        mesh=mesh,
        in_specs=(
            P("gx", "gy", None, None, None),
            P("gx", "gy", None, None, None),
            P("gx", "gy", None),
            P("gx", "gy", None),
            P("gx", "gy", None),
            P("gx", "gy", None, None),
            P("gx", "gy"),
        ),
        out_specs=(P("gx", "gy", None, None, None), P("gx", "gy", None)),
        check_vma=False,
    )
```

profile of v0, /device:TPU:28, one launch (start us, length us, event | category | flops | bytes accessed | tf_op | source)
XLA Modules:
  0.0 881.4 jit_solution(11705792087609733756)
XLA Ops:
  1.9 4.5 collective-permute-start.3
  8.4 4.5 collective-permute-start.6
  32.9 4.5 collective-permute-start.7
  66.3 4.5 collective-permute-start.11
  70.8 4.5 collective-permute-start.9
  96.1 8.3 copy.1792
  104.4 13.7 %reduce_sum.139 = f32[4,16,16,16]{0,3,2,1:T(8,128)} reduce(f32[4,16,2,16,2,16,2]{0,6,5,4,3,2,1:T(2,128)} %bitcast.325, f32[]{:T(128)} %constant.92.clone.1), dimensions={2,4,6}, to_apply=%region_1.5 | reduce | flops 114688 | bytes 589828 | tf_op jit(solution)/shard_map/reduce_sum | solution.py:136
  124.8 4.5 collective-permute-start.12
  130.7 4.2 collective-permute-done.13
  139.7 9.7 %reshape.476 = f32[8,2,8,2,64,2]{5,4,3,2,1,0:T(8,128)} reshape(f32[16,16,128]{2,1,0:T(8,128)S(1)} %copy-done.2) | data formatting | bytes 262144 | tf_op jit(solution)/shard_map/reshape | solution.py:40
  153.8 9.7 %reshape.475 = f32[8,2,8,2,64,2]{5,4,3,2,1,0:T(8,128)} reshape(f32[16,16,128]{2,1,0:T(8,128)S(1)} %fusion.80) | data formatting | bytes 262144 | tf_op jit(solution)/shard_map/reshape | solution.py:40
  171.3 4.2 collective-permute-done.17
  190.2 4.2 collective-permute-done.21
  206.0 4.2 collective-permute-done.25
  221.3 4.2 collective-permute-done.29
  236.6 4.2 collective-permute-done.33
  251.9 4.2 collective-permute-done.37
  282.8 4.2 collective-permute-done.45
  298.4 4.2 collective-permute-done.49
  316.6 4.2 collective-permute-done.53
  348.0 4.5 collective-permute-start.59
  353.8 4.5 collective-permute-start.58
  360.5 4.5 collective-permute-start.62
  367.0 4.7 collective-permute-start.63
  416.9 8.3 copy.1832
  428.5 14.1 %reduce_sum.146 = f32[4,16,16,16]{0,3,2,1:T(8,128)} reduce(f32[4,16,2,16,2,16,2]{0,6,5,4,3,2,1:T(2,128)} %bitcast.324, f32[]{:T(128)} %constant.92.clone.1), dimensions={2,4,6}, to_apply=%region_8.14 | reduce | flops 114688 | bytes 589828 | tf_op jit(solution)/shard_map/reduce_sum | solution.py:136
  442.6 4.2 copy.1833
  455.8 4.5 collective-permute-start.67
  461.6 4.5 collective-permute-start.66
  468.4 4.5 collective-permute-start.70
  475.0 4.5 collective-permute-start.71
  561.1 9.2 %copy.1878 = f32[4,32,1024]{0,2,1:T(8,128)} copy(f32[4,32,1024]{2,0,1:T(4,128)} %fusion.27) | data formatting | bytes 1048576 | tf_op jit(solution)/shard_map/sub | solution.py:249
  570.3 13.7 %reduce_sum.147 = f32[4,16,16,16]{0,3,2,1:T(8,128)} reduce(f32[4,16,2,16,2,16,2]{0,6,5,4,3,2,1:T(2,128)} %bitcast.326, f32[]{:T(128)} %constant.92.clone.1), dimensions={2,4,6}, to_apply=%region_9.15 | reduce | flops 114688 | bytes 589828 | tf_op jit(solution)/shard_map/reduce_sum | solution.py:136
  590.8 4.5 collective-permute-start.76
  596.7 4.2 collective-permute-done.77
  609.3 9.7 %reshape.538 = f32[8,2,8,2,64,2]{5,4,3,2,1,0:T(8,128)} reshape(f32[16,16,128]{2,1,0:T(8,128)S(1)} %fusion.59) | data formatting | bytes 262144 | tf_op jit(solution)/shard_map/reshape | solution.py:40
  626.6 4.2 collective-permute-done.81
  643.5 4.2 collective-permute-done.85
  659.1 4.2 collective-permute-done.89
  735.9 4.2 collective-permute-done.109
  751.6 4.2 collective-permute-done.113
  769.7 4.2 collective-permute-done.117
  795.3 4.5 collective-permute-start.123
  801.1 4.5 collective-permute-start.122
  807.8 4.5 collective-permute-start.126
  814.4 4.8 collective-permute-start.127
  853.0 8.3 copy.1918
  861.3 12.7 %reduce_sum.151 = f32[4,16,16,16]{0,3,2,1:T(8,128)S(1)} reduce(f32[4,16,2,16,2,16,2]{0,6,5,4,3,2,1:T(2,128)} %bitcast.327, f32[]{:T(128)} %constant.92.clone.1), dimensions={2,4,6}, to_apply=%region_13.19 | reduce | flops 114688 | bytes 589828 | tf_op jit(solution)/shard_map/reduce_sum | solution.py:136
  (1172 shorter events, 595.0 us)
Async XLA Ops:
  0.6 24.7 %collective-permute-start.1 = (f32[1,16,128]{2,1,0:T(8,128)S(1)}, f32[1,16,128]{2,1,0:T(8,128)S(1)}, u32[]{:S(2)}, u32[]{:S(2)}) collective-permute-start(f32[1,16,128]{2,1,0:T(8,128)S(1)} %broadcast.305), channel_id=1, source_target_pairs={{0,8},{8,16},{16,24},{1,9},{9,17},{17,25},{2,10},{10,18},{18,26},{... | collective-permute-start | bytes 24584 | tf_op jit(solution)/shard_map/ppermute | solution.py:18
  1.9 24.7 %collective-permute-start.3 = (f32[1,16,128]{2,1,0:T(8,128)S(1)}, f32[1,16,128]{2,1,0:T(8,128)S(1)}, u32[]{:S(2)}, u32[]{:S(2)}) collective-permute-start(f32[1,16,128]{2,1,0:T(8,128)S(1)} %broadcast.305), channel_id=1, source_target_pairs={{8,0},{16,8},{24,16},{9,1},{17,9},{25,17},{10,2},{18,10},{26,18},{... | collective-permute-start | bytes 24584 | tf_op jit(solution)/shard_map/ppermute | solution.py:21
  6.5 26.3 %collective-permute-start.4 = (f32[4,1024]{1,0:T(4,128)S(1)}, f32[4,1024]{1,0:T(4,128)S(1)}, u32[]{:S(2)}, u32[]{:S(2)}) collective-permute-start(f32[4,1024]{1,0:T(4,128)S(1)} %broadcast.304), channel_id=1, source_target_pairs={{0,1},{1,2},{2,3},{3,4},{4,5},{5,6},{6,7},{8,9},{9,10},{10,11},{11... | collective-permute-start | bytes 49160 | tf_op jit(solution)/shard_map/ppermute | solution.py:29
  8.4 29.5 %collective-permute-start.6 = (f32[4,1024]{1,0:T(4,128)S(1)}, f32[4,1024]{1,0:T(4,128)S(1)}, u32[]{:S(2)}, u32[]{:S(2)}) collective-permute-start(f32[4,1024]{1,0:T(4,128)S(1)} %broadcast.304), channel_id=1, source_target_pairs={{1,0},{2,1},{3,2},{4,3},{5,4},{6,5},{7,6},{9,8},{10,9},{11,10},{12... | collective-permute-start | bytes 49160 | tf_op jit(solution)/shard_map/ppermute | solution.py:29
  13.0 25.6 %collective-permute-start.2 = (f32[4,1024]{1,0:T(4,128)S(1)}, f32[4,1024]{1,0:T(4,128)S(1)}, u32[]{:S(2)}, u32[]{:S(2)}) collective-permute-start(f32[4,1024]{1,0:T(4,128)S(1)} %broadcast.304), channel_id=1, source_target_pairs={{8,0},{16,8},{24,16},{9,1},{17,9},{25,17},{10,2},{18,10},{26,18},{... | collective-permute-start | bytes 49160 | tf_op jit(solution)/shard_map/ppermute | solution.py:29
  25.4 14.4 %collective-permute-start = (f32[4,1024]{1,0:T(4,128)S(1)}, f32[4,1024]{1,0:T(4,128)S(1)}, u32[]{:S(2)}, u32[]{:S(2)}) collective-permute-start(f32[4,1024]{1,0:T(4,128)S(1)} %broadcast.304), channel_id=1, source_target_pairs={{0,8},{8,16},{16,24},{1,9},{9,17},{17,25},{2,10},{10,18},{18,26},{... | collective-permute-start | bytes 49160 | tf_op jit(solution)/shard_map/ppermute | solution.py:29
  26.7 14.2 %collective-permute-start.5 = (f32[18,1,128]{2,1,0:T(1,128)S(1)}, f32[18,1,128]{2,1,0:T(1,128)S(1)}, u32[]{:S(2)}, u32[]{:S(2)}) collective-permute-start(f32[18,1,128]{2,1,0:T(1,128)S(1)} %get-tuple-element.109), channel_id=1, source_target_pairs={{0,1},{1,2},{2,3},{3,4},{4,5},{5,6},{6,7},{8,9},{9,10},{10,11},{11... | collective-permute-start | bytes 27656 | tf_op jit(solution)/shard_map/ppermute | solution.py:18
  32.9 8.7 collective-permute-start.7
  64.3 25.1 %collective-permute-start.10 = (f32[4,1024]{1,0:T(4,128)S(1)}, f32[4,1024]{1,0:T(4,128)S(1)}, u32[]{:S(2)}, u32[]{:S(2)}) collective-permute-start(f32[4,1024]{1,0:T(4,128)S(1)} %reshape.462), channel_id=1, source_target_pairs={{0,1},{1,2},{2,3},{3,4},{4,5},{5,6},{6,7},{8,9},{9,10},{10,11},{11... | collective-permute-start | bytes 49160 | tf_op jit(solution)/shard_map/ppermute | solution.py:29
  66.3 23.9 %collective-permute-start.11 = (f32[4,1024]{1,0:T(4,128)S(1)}, f32[4,1024]{1,0:T(4,128)S(1)}, u32[]{:S(2)}, u32[]{:S(2)}) collective-permute-start(f32[4,1024]{1,0:T(4,128)S(1)} %reshape.464), channel_id=1, source_target_pairs={{1,0},{2,1},{3,2},{4,3},{5,4},{6,5},{7,6},{9,8},{10,9},{11,10},{12... | collective-permute-start | bytes 49160 | tf_op jit(solution)/shard_map/ppermute | solution.py:29
  70.8 20.1 %collective-permute-start.9 = (f32[4,1024]{1,0:T(4,128)S(1)}, f32[4,1024]{1,0:T(4,128)S(1)}, u32[]{:S(2)}, u32[]{:S(2)}) collective-permute-start(f32[4,1024]{1,0:T(4,128)S(1)} %get-tuple-element.93), channel_id=1, source_target_pairs={{8,0},{16,8},{24,16},{9,1},{17,9},{25,17},{10,2},{18,10},{26,18},{... | collective-permute-start | bytes 49160 | tf_op jit(solution)/shard_map/ppermute | solution.py:29
  75.4 16.6 %collective-permute-start.8 = (f32[4,1024]{1,0:T(4,128)S(1)}, f32[4,1024]{1,0:T(4,128)S(1)}, u32[]{:S(2)}, u32[]{:S(2)}) collective-permute-start(f32[4,1024]{1,0:T(4,128)S(1)} %get-tuple-element.94), channel_id=1, source_target_pairs={{0,8},{8,16},{16,24},{1,9},{9,17},{17,25},{2,10},{10,18},{18,26},{... | collective-permute-start | bytes 49160 | tf_op jit(solution)/shard_map/ppermute | solution.py:29
  124.8 5.9 collective-permute-start.12
  135.0 18.5 %collective-permute-start.14 = (f32[18,1,128]{2,1,0:T(1,128)S(1)}, f32[18,1,128]{2,1,0:T(1,128)S(1)}, u32[]{:S(2)}, u32[]{:S(2)}) collective-permute-start(f32[18,1,128]{2,1,0:T(1,128)S(1)} %get-tuple-element.108), channel_id=1, source_target_pairs={{1,0},{2,1},{3,2},{4,3},{5,4},{6,5},{7,6},{9,8},{10,9},{11,10},{12... | collective-permute-start | bytes 27656 | tf_op jit(solution)/shard_map/ppermute | solution.py:21
  136.9 16.6 %collective-permute-start.15 = (f32[18,1,128]{2,1,0:T(1,128)S(1)}, f32[18,1,128]{2,1,0:T(1,128)S(1)}, u32[]{:S(2)}, u32[]{:S(2)}) collective-permute-start(f32[18,1,128]{2,1,0:T(1,128)S(1)} %get-tuple-element.107), channel_id=1, source_target_pairs={{0,1},{1,2},{2,3},{3,4},{4,5},{5,6},{6,7},{8,9},{9,10},{10,11},{11... | collective-permute-start | bytes 27656 | tf_op jit(solution)/shard_map/ppermute | solution.py:18
  304.6 5.8 collective-permute-start.51
  322.7 5.9 collective-permute-start.55
  346.7 13.9 %collective-permute-start.57 = (f32[1,16,128]{2,1,0:T(8,128)S(1)}, f32[1,16,128]{2,1,0:T(8,128)S(1)}, u32[]{:S(2)}, u32[]{:S(2)}) collective-permute-start(f32[1,16,128]{2,1,0:T(8,128)S(1)} %get-tuple-element.117), channel_id=1, source_target_pairs={{0,8},{8,16},{16,24},{1,9},{9,17},{17,25},{2,10},{10,18},{18,26},{... | collective-permute-start | bytes 24584 | tf_op jit(solution)/shard_map/ppermute | solution.py:18
  348.0 17.1 %collective-permute-start.59 = (f32[1,16,128]{2,1,0:T(8,128)S(1)}, f32[1,16,128]{2,1,0:T(8,128)S(1)}, u32[]{:S(2)}, u32[]{:S(2)}) collective-permute-start(f32[1,16,128]{2,1,0:T(8,128)S(1)} %get-tuple-element.118), channel_id=1, source_target_pairs={{8,0},{16,8},{24,16},{9,1},{17,9},{25,17},{10,2},{18,10},{26,18},{... | collective-permute-start | bytes 24584 | tf_op jit(solution)/shard_map/ppermute | solution.py:21
  352.5 14.5 %collective-permute-start.56 = (f32[4,1024]{1,0:T(4,128)S(1)}, f32[4,1024]{1,0:T(4,128)S(1)}, u32[]{:S(2)}, u32[]{:S(2)}) collective-permute-start(f32[4,1024]{1,0:T(4,128)S(1)} %get-tuple-element.75), channel_id=1, source_target_pairs={{0,8},{8,16},{16,24},{1,9},{9,17},{17,25},{2,10},{10,18},{18,26},{... | collective-permute-start | bytes 49160 | tf_op jit(solution)/shard_map/ppermute | solution.py:29
  353.8 26.3 %collective-permute-start.58 = (f32[4,1024]{1,0:T(4,128)S(1)}, f32[4,1024]{1,0:T(4,128)S(1)}, u32[]{:S(2)}, u32[]{:S(2)}) collective-permute-start(f32[4,1024]{1,0:T(4,128)S(1)} %get-tuple-element.76), channel_id=1, source_target_pairs={{8,0},{16,8},{24,16},{9,1},{17,9},{25,17},{10,2},{18,10},{26,18},{... | collective-permute-start | bytes 49160 | tf_op jit(solution)/shard_map/ppermute | solution.py:29
  358.5 22.9 %collective-permute-start.60 = (f32[4,1024]{1,0:T(4,128)S(1)}, f32[4,1024]{1,0:T(4,128)S(1)}, u32[]{:S(2)}, u32[]{:S(2)}) collective-permute-start(f32[4,1024]{1,0:T(4,128)S(1)} %reshape.493), channel_id=1, source_target_pairs={{0,1},{1,2},{2,3},{3,4},{4,5},{5,6},{6,7},{8,9},{9,10},{10,11},{11... | collective-permute-start | bytes 49160 | tf_op jit(solution)/shard_map/ppermute | solution.py:29
  360.5 22.1 %collective-permute-start.62 = (f32[4,1024]{1,0:T(4,128)S(1)}, f32[4,1024]{1,0:T(4,128)S(1)}, u32[]{:S(2)}, u32[]{:S(2)}) collective-permute-start(f32[4,1024]{1,0:T(4,128)S(1)} %reshape.496), channel_id=1, source_target_pairs={{1,0},{2,1},{3,2},{4,3},{5,4},{6,5},{7,6},{9,8},{10,9},{11,10},{12... | collective-permute-start | bytes 49160 | tf_op jit(solution)/shard_map/ppermute | solution.py:29
  365.1 18.8 %collective-permute-start.61 = (f32[18,1,128]{2,1,0:T(1,128)S(1)}, f32[18,1,128]{2,1,0:T(1,128)S(1)}, u32[]{:S(2)}, u32[]{:S(2)}) collective-permute-start(f32[18,1,128]{2,1,0:T(1,128)S(1)} %get-tuple-element.103), channel_id=1, source_target_pairs={{0,1},{1,2},{2,3},{3,4},{4,5},{5,6},{6,7},{8,9},{9,10},{10,11},{11... | collective-permute-start | bytes 27656 | tf_op jit(solution)/shard_map/ppermute | solution.py:18
  367.0 16.9 %collective-permute-start.63 = (f32[18,1,128]{2,1,0:T(1,128)S(1)}, f32[18,1,128]{2,1,0:T(1,128)S(1)}, u32[]{:S(2)}, u32[]{:S(2)}) collective-permute-start(f32[18,1,128]{2,1,0:T(1,128)S(1)} %get-tuple-element.104), channel_id=1, source_target_pairs={{1,0},{2,1},{3,2},{4,3},{5,4},{6,5},{7,6},{9,8},{10,9},{11,10},{12... | collective-permute-start | bytes 27656 | tf_op jit(solution)/shard_map/ppermute | solution.py:21
  452.2 16.1 %collective-permute-start.65 = (f32[1,16,128]{2,1,0:T(8,128)S(1)}, f32[1,16,128]{2,1,0:T(8,128)S(1)}, u32[]{:S(2)}, u32[]{:S(2)}) collective-permute-start(f32[1,16,128]{2,1,0:T(8,128)S(1)} %slice.1458), channel_id=1, source_target_pairs={{0,8},{8,16},{16,24},{1,9},{9,17},{17,25},{2,10},{10,18},{18,26},{... | collective-permute-start | bytes 24584 | tf_op jit(solution)/shard_map/ppermute | solution.py:18
  455.8 17.2 %collective-permute-start.67 = (f32[1,16,128]{2,1,0:T(8,128)S(1)}, f32[1,16,128]{2,1,0:T(8,128)S(1)}, u32[]{:S(2)}, u32[]{:S(2)}) collective-permute-start(f32[1,16,128]{2,1,0:T(8,128)S(1)} %slice.1463), channel_id=1, source_target_pairs={{8,0},{16,8},{24,16},{9,1},{17,9},{25,17},{10,2},{18,10},{26,18},{... | collective-permute-start | bytes 24584 | tf_op jit(solution)/shard_map/ppermute | solution.py:21
  460.3 14.6 %collective-permute-start.64 = (f32[4,1024]{1,0:T(4,128)S(1)}, f32[4,1024]{1,0:T(4,128)S(1)}, u32[]{:S(2)}, u32[]{:S(2)}) collective-permute-start(f32[4,1024]{1,0:T(4,128)S(1)} %get-tuple-element.65), channel_id=1, source_target_pairs={{0,8},{8,16},{16,24},{1,9},{9,17},{17,25},{2,10},{10,18},{18,26},{... | collective-permute-start | bytes 49160 | tf_op jit(solution)/shard_map/ppermute | solution.py:29
  461.6 26.2 %collective-permute-start.66 = (f32[4,1024]{1,0:T(4,128)S(1)}, f32[4,1024]{1,0:T(4,128)S(1)}, u32[]{:S(2)}, u32[]{:S(2)}) collective-permute-start(f32[4,1024]{1,0:T(4,128)S(1)} %get-tuple-element.66), channel_id=1, source_target_pairs={{8,0},{16,8},{24,16},{9,1},{17,9},{25,17},{10,2},{18,10},{26,18},{... | collective-permute-start | bytes 49160 | tf_op jit(solution)/shard_map/ppermute | solution.py:29
  466.3 22.8 %collective-permute-start.68 = (f32[4,1024]{1,0:T(4,128)S(1)}, f32[4,1024]{1,0:T(4,128)S(1)}, u32[]{:S(2)}, u32[]{:S(2)}) collective-permute-start(f32[4,1024]{1,0:T(4,128)S(1)} %reshape.510), channel_id=1, source_target_pairs={{0,1},{1,2},{2,3},{3,4},{4,5},{5,6},{6,7},{8,9},{9,10},{10,11},{11... | collective-permute-start | bytes 49160 | tf_op jit(solution)/shard_map/ppermute | solution.py:29
  468.4 22.0 %collective-permute-start.70 = (f32[4,1024]{1,0:T(4,128)S(1)}, f32[4,1024]{1,0:T(4,128)S(1)}, u32[]{:S(2)}, u32[]{:S(2)}) collective-permute-start(f32[4,1024]{1,0:T(4,128)S(1)} %reshape.514), channel_id=1, source_target_pairs={{1,0},{2,1},{3,2},{4,3},{5,4},{6,5},{7,6},{9,8},{10,9},{11,10},{12... | collective-permute-start | bytes 49160 | tf_op jit(solution)/shard_map/ppermute | solution.py:29
  473.0 18.6 %collective-permute-start.69 = (f32[18,1,128]{2,1,0:T(1,128)S(1)}, f32[18,1,128]{2,1,0:T(1,128)S(1)}, u32[]{:S(2)}, u32[]{:S(2)}) collective-permute-start(f32[18,1,128]{2,1,0:T(1,128)S(1)} %get-tuple-element.101), channel_id=1, source_target_pairs={{0,1},{1,2},{2,3},{3,4},{4,5},{5,6},{6,7},{8,9},{9,10},{10,11},{11... | collective-permute-start | bytes 27656 | tf_op jit(solution)/shard_map/ppermute | solution.py:18
  475.0 16.7 %collective-permute-start.71 = (f32[18,1,128]{2,1,0:T(1,128)S(1)}, f32[18,1,128]{2,1,0:T(1,128)S(1)}, u32[]{:S(2)}, u32[]{:S(2)}) collective-permute-start(f32[18,1,128]{2,1,0:T(1,128)S(1)} %get-tuple-element.102), channel_id=1, source_target_pairs={{1,0},{2,1},{3,2},{4,3},{5,4},{6,5},{7,6},{9,8},{10,9},{11,10},{12... | collective-permute-start | bytes 27656 | tf_op jit(solution)/shard_map/ppermute | solution.py:21
  538.0 13.1 %collective-permute-start.75 = (f32[4,1024]{1,0:T(4,128)}, f32[4,1024]{1,0:T(4,128)S(1)}, u32[]{:S(2)}, u32[]{:S(2)}) collective-permute-start(f32[4,1024]{1,0:T(4,128)} %reshape.527), channel_id=1, source_target_pairs={{1,0},{2,1},{3,2},{4,3},{5,4},{6,5},{7,6},{9,8},{10,9},{11,10},{12... | collective-permute-start | bytes 49160 | tf_op jit(solution)/shard_map/ppermute | solution.py:29
  541.5 11.2 %collective-permute-start.74 = (f32[4,1024]{1,0:T(4,128)}, f32[4,1024]{1,0:T(4,128)S(1)}, u32[]{:S(2)}, u32[]{:S(2)}) collective-permute-start(f32[4,1024]{1,0:T(4,128)} %reshape.525), channel_id=1, source_target_pairs={{0,1},{1,2},{2,3},{3,4},{4,5},{5,6},{6,7},{8,9},{9,10},{10,11},{11... | collective-permute-start | bytes 49160 | tf_op jit(solution)/shard_map/ppermute | solution.py:29
  543.9 10.2 %collective-permute-start.73 = (f32[4,1024]{1,0:T(4,128)}, f32[4,1024]{1,0:T(4,128)S(1)}, u32[]{:S(2)}, u32[]{:S(2)}) collective-permute-start(f32[4,1024]{1,0:T(4,128)} %get-tuple-element.63), channel_id=1, source_target_pairs={{8,0},{16,8},{24,16},{9,1},{17,9},{25,17},{10,2},{18,10},{26,18},{... | collective-permute-start | bytes 49160 | tf_op jit(solution)/shard_map/ppermute | solution.py:29
  545.8 9.9 %collective-permute-start.72 = (f32[4,1024]{1,0:T(4,128)}, f32[4,1024]{1,0:T(4,128)S(1)}, u32[]{:S(2)}, u32[]{:S(2)}) collective-permute-start(f32[4,1024]{1,0:T(4,128)} %get-tuple-element.64), channel_id=1, source_target_pairs={{0,8},{8,16},{16,24},{1,9},{9,17},{17,25},{2,10},{10,18},{18,26},{... | collective-permute-start | bytes 49160 | tf_op jit(solution)/shard_map/ppermute | solution.py:29
  590.8 5.9 collective-permute-start.76
  603.0 5.9 collective-permute-start.79
  775.8 5.9 collective-permute-start.119
  794.0 13.9 %collective-permute-start.121 = (f32[1,16,128]{2,1,0:T(8,128)S(1)}, f32[1,16,128]{2,1,0:T(8,128)S(1)}, u32[]{:S(2)}, u32[]{:S(2)}) collective-permute-start(f32[1,16,128]{2,1,0:T(8,128)S(1)} %get-tuple-element.111), channel_id=1, source_target_pairs={{0,8},{8,16},{16,24},{1,9},{9,17},{17,25},{2,10},{10,18},{18,26},{... | collective-permute-start | bytes 24584 | tf_op jit(solution)/shard_map/ppermute | solution.py:18
  795.3 17.1 %collective-permute-start.123 = (f32[1,16,128]{2,1,0:T(8,128)S(1)}, f32[1,16,128]{2,1,0:T(8,128)S(1)}, u32[]{:S(2)}, u32[]{:S(2)}) collective-permute-start(f32[1,16,128]{2,1,0:T(8,128)S(1)} %get-tuple-element.112), channel_id=1, source_target_pairs={{8,0},{16,8},{24,16},{9,1},{17,9},{25,17},{10,2},{18,10},{26,18},{... | collective-permute-start | bytes 24584 | tf_op jit(solution)/shard_map/ppermute | solution.py:21
  799.8 14.5 %collective-permute-start.120 = (f32[4,1024]{1,0:T(4,128)S(1)}, f32[4,1024]{1,0:T(4,128)S(1)}, u32[]{:S(2)}, u32[]{:S(2)}) collective-permute-start(f32[4,1024]{1,0:T(4,128)S(1)} %get-tuple-element.45), channel_id=1, source_target_pairs={{0,8},{8,16},{16,24},{1,9},{9,17},{17,25},{2,10},{10,18},{18,26},{... | collective-permute-start | bytes 49160 | tf_op jit(solution)/shard_map/ppermute | solution.py:29
  801.1 25.9 %collective-permute-start.122 = (f32[4,1024]{1,0:T(4,128)S(1)}, f32[4,1024]{1,0:T(4,128)S(1)}, u32[]{:S(2)}, u32[]{:S(2)}) collective-permute-start(f32[4,1024]{1,0:T(4,128)S(1)} %get-tuple-element.46), channel_id=1, source_target_pairs={{8,0},{16,8},{24,16},{9,1},{17,9},{25,17},{10,2},{18,10},{26,18},{... | collective-permute-start | bytes 49160 | tf_op jit(solution)/shard_map/ppermute | solution.py:29
  805.8 21.9 %collective-permute-start.124 = (f32[4,1024]{1,0:T(4,128)S(1)}, f32[4,1024]{1,0:T(4,128)S(1)}, u32[]{:S(2)}, u32[]{:S(2)}) collective-permute-start(f32[4,1024]{1,0:T(4,128)S(1)} %reshape.555), channel_id=1, source_target_pairs={{0,1},{1,2},{2,3},{3,4},{4,5},{5,6},{6,7},{8,9},{9,10},{10,11},{11... | collective-permute-start | bytes 49160 | tf_op jit(solution)/shard_map/ppermute | solution.py:29
  807.8 20.6 %collective-permute-start.126 = (f32[4,1024]{1,0:T(4,128)S(1)}, f32[4,1024]{1,0:T(4,128)S(1)}, u32[]{:S(2)}, u32[]{:S(2)}) collective-permute-start(f32[4,1024]{1,0:T(4,128)S(1)} %reshape.558), channel_id=1, source_target_pairs={{1,0},{2,1},{3,2},{4,3},{5,4},{6,5},{7,6},{9,8},{10,9},{11,10},{12... | collective-permute-start | bytes 49160 | tf_op jit(solution)/shard_map/ppermute | solution.py:29
  812.4 16.7 %collective-permute-start.125 = (f32[18,1,128]{2,1,0:T(1,128)S(1)}, f32[18,1,128]{2,1,0:T(1,128)S(1)}, u32[]{:S(2)}, u32[]{:S(2)}) collective-permute-start(f32[18,1,128]{2,1,0:T(1,128)S(1)} %get-tuple-element.95), channel_id=1, source_target_pairs={{0,1},{1,2},{2,3},{3,4},{4,5},{5,6},{6,7},{8,9},{9,10},{10,11},{11... | collective-permute-start | bytes 27656 | tf_op jit(solution)/shard_map/ppermute | solution.py:18
  814.4 14.8 %collective-permute-start.127 = (f32[18,1,128]{2,1,0:T(1,128)S(1)}, f32[18,1,128]{2,1,0:T(1,128)S(1)}, u32[]{:S(2)}, u32[]{:S(2)}) collective-permute-start(f32[18,1,128]{2,1,0:T(1,128)S(1)} %get-tuple-element.96), channel_id=1, source_target_pairs={{1,0},{2,1},{3,2},{4,3},{5,4},{6,5},{7,6},{9,8},{10,9},{11,10},{12... | collective-permute-start | bytes 27656 | tf_op jit(solution)/shard_map/ppermute | solution.py:21
  (221 other events, 1476.1 us)
where the time goes:
time: 895 us; the launch traced here: 881 us
  local copies, waits for them, and re-layouts  299 us (33%)
  starting transfers between devices  290 us (32%)
  waiting for transfers between devices  164 us (18%)
  other arithmetic  122 us (14%)
    ppermute x52, waiting for transfers between devices, with_halo(): lax.ppermute(lax.slice_in_dim(block, block.shape[dim] - width, None, axis...  164 us
    ppermute x52, starting transfers between devices, with_halo(): lax.ppermute(lax.slice_in_dim(block, 0, width, axis=dim), axis, backward)  129 us
    ppermute x52, starting transfers between devices, with_halo(): lax.ppermute(lax.slice_in_dim(block, block.shape[dim] - width, None, axis...  94.2 us
    ppermute x24, starting transfers between devices, from_behind(): lax.ppermute(value, axis, [(source, source + steps) for source in range(f...  67 us
    reduce_sum x4, other arithmetic, restrict_fine(): return jnp.sum(blocks, axis=(2, 4, 6)) * 0.125  54 us
    gather x36, local copies, waits for them, and re-layouts, choose(): picked = jnp.take(received, jnp.maximum(link_index, 0), axis=0)  32.9 us
    reshape x7, local copies, waits for them, and re-layouts, shrink(): blocks = values.reshape(size_x // 2, 2, size_y // 2, 2, size_z // 2, 2)  31.5 us
  transfers between devices with their start and end apart: 128, of which 43 were waited for; matrix products, arithmetic and copies ran while one was open for 11% of the time, Pallas kernels for 0%

commit v1 on v0

v1 whole, which is shorter than its diff:
```python
import functools

import jax
import jax.numpy as jnp
from jax import lax
from jax.experimental import pallas as pl
from jax.experimental.pallas import tpu as pltpu
from jax.sharding import PartitionSpec as P

CYCLES = 2
SWEEPS = 6
THIRD = 1.0 / 3.0
NINTH = 1.0 / 9.0
F32 = jnp.float32
LANES = 128
VMEM_LIMIT = 16 * 1024 * 1024
UNROLL = 4


def lanes_of(v):
    return lax.broadcasted_iota(jnp.int32, v.shape, v.ndim - 1)


def rows_of(v):
    return lax.broadcasted_iota(jnp.int32, v.shape, v.ndim - 2)


def z_low(v, n):
    return jnp.where(lanes_of(v) >= n, pltpu.roll(v, n, v.ndim - 1), 0.0)


def z_high(v, n):
    return jnp.where(lanes_of(v) < LANES - n, pltpu.roll(v, LANES - n, v.ndim - 1), 0.0)


def x_low(v, n):
    return pltpu.roll(v, n, v.ndim - 2)


def x_high(v, n):
    return pltpu.roll(v, v.shape[-2] - n, v.ndim - 2)


def pair_x(v, n):
    return v + jnp.where((rows_of(v) & n) == 0, x_high(v, n), x_low(v, n))


def pair_z(v, n):
    lane = lanes_of(v)
    return v + jnp.where(
        (lane & n) == 0, pltpu.roll(v, LANES - n, v.ndim - 1), pltpu.roll(v, n, v.ndim - 1)
    )


def lane_gather(v, idx):
    return jnp.take_along_axis(v, idx, axis=1)


def around(v, low_y, high_y, n):
    return (x_low(v, n) + x_high(v, n)) + (low_y + high_y) + (z_low(v, n) + z_high(v, n))


def relax(v, low_y, high_y, n):
    return v * THIRD + around(v, low_y, high_y, n) * NINTH


YF = 20
XF = 24


def fine_relax(ref, y, f1_rows):
    below = jnp.where(y == 0, YF - 1, y - 1)
    above = jnp.where(y == YF - 1, 0, y + 1)
    cur = [ref[o, y] for o in range(8)]
    out = []
    for o in range(8):
        ox, oy, oz = o ^ 4, o ^ 2, o ^ 1
        s = (cur[ox] + cur[oy]) + cur[oz]
        s = s + (x_low(cur[ox], 1) if o & 4 == 0 else x_high(cur[ox], 1))
        s = s + (ref[oy, below] if o & 2 == 0 else ref[oy, above])
        s = s + (z_low(cur[oz], 1) if o & 1 == 0 else z_high(cur[oz], 1))
        out.append(cur[o] * THIRD + s * NINTH + f1_rows[o])
    return cur, out


def inside(axis):
    at = lax.axis_index(axis)
    return at > 0, at < lax.axis_size(axis) - 1


def kept(here, v):
    return jnp.where(here, v, 0.0)


def mean8(rows):
    return (
        ((rows[0] + rows[1]) + (rows[2] + rows[3])) + ((rows[4] + rows[5]) + (rows[6] + rows[7]))
    ) * 0.125


def box_lanes(site_ref, count_ref, s, shape):
    lane = lax.broadcasted_iota(jnp.int32, shape, len(shape) - 1)
    site = jnp.where(s < count_ref[0, 0], site_ref[0, 0, s], -1)
    return (lane // 16) == site


def prepare_kernel(
    site_ref, count_ref, rhs_ref, beta_ref, bbeta_ref,
    f1_ref, q_ref, k0_ref, fxlo_ref, fxhi_ref, fylo_ref, fyhi_ref,
    f_ref, c_ref,
):
    for s in range(4):
        for t in range(8):
            at = slice(t * LANES, (t + 1) * LANES)
            q = beta_ref[0, 0, s, :, at] * 9.0
            c_ref[s, t] = q
            f_ref[s, t] = rhs_ref[0, 0, s, :, at] / q
    masks = [box_lanes(site_ref, count_ref, s, (16, LANES)) for s in range(4)]
    lane = lax.broadcasted_iota(jnp.int32, (16, LANES), 1)
    base_idx = 2 * (lane & 15)
    for px in range(2):
        for t in range(8):
            f_acc = [jnp.zeros((16, LANES), F32) for _ in range(8)]
            q_acc = [jnp.zeros((16, LANES), F32) for _ in range(8)]
            for s in range(4):
                f = f_ref[s, t, pl.ds(px, 16, stride=2), :]
                q = c_ref[s, t, pl.ds(px, 16, stride=2), :]
                for g in range(8):
                    idx = base_idx + ((g // 2) * 32 + g % 2)
                    f_acc[g] = jnp.where(masks[s], lane_gather(f, idx), f_acc[g])
                    q_acc[g] = jnp.where(masks[s], lane_gather(q, idx), q_acc[g])
            for g in range(8):
                yy, pz = g // 2, g % 2
                y, o = 2 * t + yy // 2, px * 4 + (yy % 2) * 2 + pz
                f1_ref[o, y] = f_acc[g]
                q_ref[o, y] = q_acc[g]
                k = (yy % 2) * 2 + pz
                fxlo_ref[px * 16 + y, 2 * k : 2 * k + 2, :] = f_acc[g][0:2]
                fxhi_ref[px * 16 + y, 2 * k : 2 * k + 2, :] = f_acc[g][14:16]
                if y < 2:
                    fylo_ref[o * 2 + y] = f_acc[g]
                if y >= 14:
                    fyhi_ref[o * 2 + y - 14] = f_acc[g]
    live = jnp.where(masks[0] | masks[1] | masks[2] | masks[3], 1.0, 0.0).astype(F32)
    fxlo_ref[32] = live[0:8]
    fxhi_ref[32] = live[0:8]
    fylo_ref[16] = live
    fyhi_ref[16] = live
    for y in range(16):
        k0_ref[y] = bbeta_ref[pl.ds(y, 16, stride=16), :] * 2.25


def side_tile(lo_ref, hi_ref, j, k):
    lo_here, hi_here = inside("gx")
    return jnp.concatenate(
        [
            kept(hi_here, hi_ref[j, 2 * k : 2 * k + 2, :]),
            jnp.zeros((4, LANES), F32),
            kept(lo_here, lo_ref[j, 2 * k : 2 * k + 2, :]),
        ],
        axis=0,
    )


def side_live(lo_ref, hi_ref, row):
    lo_here, hi_here = inside("gx")
    return jnp.where(row < 4, kept(hi_here, hi_ref[32]), kept(lo_here, lo_ref[32]))


def first_residual_kernel(
    f1_ref, q_ref, k0_ref, brhs_ref, rxlo_ref, rxhi_ref, rylo_ref, ryhi_ref,
    e0_ref, exlo_ref, exhi_ref, u_ref,
):
    ylo_here, yhi_here = inside("gy")
    for o in range(8):
        for j in range(2):
            u_ref[o, 16 + j, 0:16, :] = kept(yhi_here, ryhi_ref[o * 2 + j])
            u_ref[o, 18 + j, 0:16, :] = kept(ylo_here, rylo_ref[o * 2 + j])

    def fill(y, carry):
        for o in range(8):
            u_ref[o, y, 0:16, :] = f1_ref[o, y]
            u_ref[o, y, 16:24, :] = side_tile(rxlo_ref, rxhi_ref, (o // 4) * 16 + y, o % 4)
        return carry

    lax.fori_loop(0, 16, fill, 0, unroll=UNROLL)

    def row(y, carry):
        zero = jnp.zeros((XF, LANES), F32)
        cur, new = fine_relax(u_ref, y, [zero] * 8)
        left = []
        covered = None
        for o in range(8):
            q = q_ref[o, y]
            left.append(q * new[o][0:16])
            covered = q if covered is None else covered
        k0 = k0_ref[y]
        r0 = jnp.where(covered > 0.0, mean8(left), brhs_ref[pl.ds(y, 16, stride=16), :])
        e0 = r0 / k0
        e0_ref[y] = e0
        exlo_ref[y] = e0[0:8]
        exhi_ref[y] = e0[8:16]
        exlo_ref[16 + y] = k0[0:8]
        exhi_ref[16 + y] = k0[8:16]
        return carry

    lax.fori_loop(0, 16, row, 0, unroll=UNROLL)


def pack_y_first_kernel(e0_ref, k0_ref, exlo_ref, exhi_ref, fxlo_ref, fxhi_ref, eylo_ref, eyhi_ref):
    lo_here, hi_here = inside("gx")

    def row(y, carry):
        for j, src in ((0, e0_ref), (1, k0_ref)):
            for out, at in ((eylo_ref, y), (eyhi_ref, y + 8)):
                v = src[at]
                n = (j * 8 + y) * 4
                out[n] = v[0:8]
                out[n + 1] = v[8:16]
                out[n + 2] = kept(hi_here, exhi_ref[j * 16 + at])
                out[n + 3] = kept(lo_here, exlo_ref[j * 16 + at])
        return carry

    lax.fori_loop(0, 8, row, 0, unroll=UNROLL)
    for o in range(8):
        for j in range(2):
            eylo_ref[64 + o * 2 + j] = side_tile(fxlo_ref, fxhi_ref, (o // 4) * 16 + j, o % 4)
            eyhi_ref[64 + o * 2 + j] = side_tile(fxlo_ref, fxhi_ref, (o // 4) * 16 + 14 + j, o % 4)
    row8 = lax.broadcasted_iota(jnp.int32, (8, LANES), 0)
    eylo_ref[80] = side_live(fxlo_ref, fxhi_ref, row8)
    eyhi_ref[80] = side_live(fxlo_ref, fxhi_ref, row8)


def pack_y_kernel(e0_ref, exlo_ref, exhi_ref, eylo_ref, eyhi_ref):
    lo_here, hi_here = inside("gx")

    def row(y, carry):
        for out, at in ((eylo_ref, y), (eyhi_ref, y + 8)):
            v = e0_ref[at]
            n = y * 4
            out[n] = v[0:8]
            out[n + 1] = v[8:16]
            out[n + 2] = kept(hi_here, exhi_ref[at])
            out[n + 3] = kept(lo_here, exlo_ref[at])
        return carry

    lax.fori_loop(0, 8, row, 0, unroll=UNROLL)


def assemble_base(dst_ref, own_ref, exlo_ref, exhi_ref, eylo_ref, eyhi_ref, x_at, y_at):
    xlo_here, xhi_here = inside("gx")
    ylo_here, yhi_here = inside("gy")

    def own(y, carry):
        dst_ref[y, 0:16, :] = own_ref[y]
        dst_ref[y, 16:24, :] = kept(xhi_here, exhi_ref[x_at + y])
        dst_ref[y, 24:32, :] = kept(xlo_here, exlo_ref[x_at + y])
        return carry

    lax.fori_loop(0, 16, own, 0, unroll=UNROLL)

    def side(y, carry):
        for t in range(4):
            dst_ref[16 + y, 8 * t : 8 * t + 8, :] = kept(yhi_here, eyhi_ref[y_at + y * 4 + t])
            dst_ref[24 + y, 8 * t : 8 * t + 8, :] = kept(ylo_here, eylo_ref[y_at + y * 4 + t])
        return carry

    lax.fori_loop(0, 8, side, 0, unroll=UNROLL)


def down_level0(e_ref, k_ref, e1_ref, k1_ref, make_k1):
    def row(y1, carry):
        parts = []
        for j in range(2):
            y = 2 * y1 + j
            low = e_ref[(y + 31) % 32]
            high = e_ref[(y + 1) % 32]
            parts.append(k_ref[y] * relax(e_ref[y], low, high, 1))
        r1 = pair_z(pair_x(parts[0] + parts[1], 1), 1) * 0.125
        if make_k1:
            k1 = pair_z(pair_x(k_ref[2 * y1] + k_ref[2 * y1 + 1], 1), 1) * (0.125 * 0.25)
            k1_ref[y1] = k1
        else:
            k1 = k1_ref[y1]
        e1_ref[y1] = jnp.where(k1 > 0.0, r1 / jnp.where(k1 > 0.0, k1, 1.0), 0.0)
        return carry

    lax.fori_loop(0, 16, row, 0, unroll=UNROLL)


def pack_four(rows, pack_ref):
    lane = lanes_of(rows[0]) & 3
    v = jnp.where(
        lane < 2,
        jnp.where(lane == 0, rows[0], rows[1]),
        jnp.where(lane == 2, rows[2], rows[3]),
    )
    pack_ref[...] = v
    return pack_ref[pl.ds(0, 4, stride=4), :]


def down_level1(e1_ref, k1_ref, pack_ref):
    r2 = []
    for y2 in range(4):
        parts = []
        for j in range(2):
            y = 2 * y2 + j
            parts.append(
                k1_ref[y] * relax(e1_ref[y], e1_ref[(y + 15) % 16], e1_ref[(y + 1) % 16], 2)
            )
        r2.append((pair_z(pair_x(parts[0] + parts[1], 2), 2) * 0.125)[0:16])
    return pack_four(r2, pack_ref)


def down_first_kernel(
    e0_ref, k0_ref, exlo_ref, exhi_ref, eylo_ref, eyhi_ref,
    send_ref, e0x_ref, k0x_ref, e1_ref, k1_ref, pack_ref,
):
    assemble_base(e0x_ref, e0_ref, exlo_ref, exhi_ref, eylo_ref, eyhi_ref, 0, 0)
    assemble_base(k0x_ref, k0_ref, exlo_ref, exhi_ref, eylo_ref, eyhi_ref, 16, 32)
    down_level0(e0x_ref, k0x_ref, e1_ref, k1_ref, True)
    r2 = down_level1(e1_ref, k1_ref, pack_ref)
    k2 = []
    for y2 in range(4):
        v = pair_z(pair_x(k1_ref[2 * y2] + k1_ref[2 * y2 + 1], 2), 2) * (0.125 * 0.25)
        k2.append(v[0:16])
    k2 = pack_four(k2, pack_ref)
    both = jnp.concatenate([r2, k2], axis=0)

    def put(d, carry):
        send_ref[d] = both
        return carry

    lax.fori_loop(0, send_ref.shape[0], put, 0, unroll=UNROLL)


def down_kernel(
    e0_ref, k0x_ref, k1_ref, exlo_ref, exhi_ref, eylo_ref, eyhi_ref,
    send_ref, e0x_ref, e1_ref, pack_ref,
):
    assemble_base(e0x_ref, e0_ref, exlo_ref, exhi_ref, eylo_ref, eyhi_ref, 0, 0)
    down_level0(e0x_ref, k0x_ref, e1_ref, k1_ref, False)
    r2 = down_level1(e1_ref, k1_ref, pack_ref)

    def put(d, carry):
        send_ref[d] = r2
        return carry

    lax.fori_loop(0, send_ref.shape[0], put, 0, unroll=UNROLL)


def coarse_shift_x(v, n):
    rows = v.shape[1]
    r = rows_of(v)
    low = jnp.where(r >= n, pltpu.roll(v, n, 1), 0.0)
    high = jnp.where(r < rows - n, pltpu.roll(v, rows - n, 1), 0.0)
    return low + high


def coarse_shift_y(v, n):
    zero = jnp.zeros_like(v[0:1])
    above = jnp.concatenate([v[1:], zero], axis=0)
    below = jnp.concatenate([zero, v[:-1]], axis=0)
    lane = lanes_of(v) & 3
    high = jnp.where(lane < 4 - n, pltpu.roll(v, LANES - n, 2), pltpu.roll(above, 4 - n, 2))
    low = jnp.where(lane >= n, pltpu.roll(v, n, 2), pltpu.roll(below, LANES - 4 + n, 2))
    return low + high


def coarse_relax(v, n):
    s = coarse_shift_x(v, n) + coarse_shift_y(v, n) + (z_low(v, 4 * n) + z_high(v, 4 * n))
    return v * THIRD + s * NINTH


def coarse_solve(r2, k2):
    e2 = r2 / k2
    left = k2 * coarse_relax(e2, 1)

    def pool(v):
        v = pair_x(v, 1)
        v = pair_z(v, 1)
        return pair_z(v, 4) * 0.125

    k3 = pool(k2) * 0.25
    first = pool(left) / k3
    e3 = first
    for _ in range(SWEEPS - 1):
        e3 = coarse_relax(e3, 2) + first
    mid = e2 + e3
    return coarse_relax(mid, 1) + e2


def spread_coarse(mg2, table_ref, row_ref, m2_ref):
    gy_total, rows = mg2.shape[0], mg2.shape[1]
    gx_total = rows // 4
    zero = jnp.zeros((8, LANES), F32)
    for j in range(gx_total + 2):
        table_ref[0, j] = zero
        table_ref[gy_total + 1, j] = zero
    for j in range(gy_total):
        table_ref[j + 1, 0] = zero
        table_ref[j + 1, gx_total + 1] = zero
        for i in range(gx_total):
            table_ref[j + 1, i + 1, 0:4, :] = mg2[j, 4 * i : 4 * i + 4, :]
    gx = lax.axis_index("gx") + 1
    gy = lax.axis_index("gy") + 1
    lane = lax.broadcasted_iota(jnp.int32, (32, LANES), 1)
    group = lane & ~3
    for dy, picks in ((0, ((0, 0), (1, 1), (2, 2), (3, 3))), (1, ((4, 0), (5, 1))), (-1, ((6, 2), (7, 3)))):
        own = table_ref[gy + dy, gx, 0:4, :]
        high = table_ref[gy + dy, gx + 1, 0:2, :]
        low = table_ref[gy + dy, gx - 1, 2:4, :]
        for r in range(4):
            row_ref[pl.ds(r, 4, stride=4), :] = own
            row_ref[pl.ds(16 + r, 2, stride=4), :] = high
            row_ref[pl.ds(24 + r, 2, stride=4), :] = low
        v = row_ref[...]
        for at, y in picks:
            m2_ref[at] = lane_gather(v, group + y)


def up_levels(m2_ref, e1_ref, k1_ref, mg1_ref, e0x_ref, k0x_ref, corr_ref, e1p_ref, e0p_ref):
    def mid1(y, carry):
        e1p_ref[y] = jnp.where(k1_ref[y] > 0.0, e1_ref[y] + m2_ref[y // 2], 0.0)
        return carry

    lax.fori_loop(0, 16, mid1, 0, unroll=UNROLL)

    def post1(y, carry):
        v = relax(e1p_ref[y], e1p_ref[(y + 15) % 16], e1p_ref[(y + 1) % 16], 2) + e1_ref[y]
        mg1_ref[y] = jnp.where(k1_ref[y] > 0.0, v, 0.0)
        return carry

    lax.fori_loop(0, 16, post1, 0, unroll=UNROLL)

    def mid0(y, carry):
        e0p_ref[y] = e0x_ref[y] + mg1_ref[y // 2]
        return carry

    lax.fori_loop(0, 32, mid0, 0, unroll=UNROLL)

    def post0(i, carry):
        y = jnp.where(i >= 18, i + 12, i)
        v = relax(e0p_ref[y], e0p_ref[(y + 31) % 32], e0p_ref[(y + 1) % 32], 1) + e0x_ref[y]
        v = jnp.where(k0x_ref[y] > 0.0, v, 0.0)
        third = jnp.where(rows_of(v[16:24]) < 4, v[16:24], v[24:32])
        corr_ref[i] = jnp.concatenate([v[0:16], third], axis=0)
        return carry

    lax.fori_loop(0, YF, post0, 0, unroll=UNROLL)


def gather_coarse(recv_ref, at, w_ref):
    gy_total, rows = w_ref.shape[0], w_ref.shape[1]
    for i in range(rows // 4):
        for j in range(gy_total):
            w_ref[j, 4 * i : 4 * i + 4, :] = recv_ref[i * gy_total + j, at : at + 4, :]


def fine_sweep(src_ref, dst_ref, f1x_ref, livex_ref):
    def row(y, carry):
        region = jnp.where(y < 16, 0, jnp.where(y < 18, 1, 2))
        live = livex_ref[region] > 0.0
        cur, new = fine_relax(src_ref, y, [f1x_ref[o, y] for o in range(8)])
        for o in range(8):
            dst_ref[o, y] = jnp.where(live, new[o], cur[o])
        return carry

    lax.fori_loop(0, YF, row, 0, unroll=UNROLL)


def middle_kernel(
    recv_ref, e0x_ref, k0x_ref, e1_ref, k1_ref,
    f1_ref, q_ref, brhs_ref, rxlo_ref, rxhi_ref, rylo_ref, ryhi_ref, eylo_ref, eyhi_ref,
    u3_ref, f1x_ref, livex_ref, k2_ref, e0_ref, exlo_ref, exhi_ref,
    w_ref, table_ref, row_ref, m2_ref, mg1_ref, e1p_ref, e0p_ref, corr_ref, ua_ref, ub_ref, v_ref,
):
    gather_coarse(recv_ref, 0, w_ref)
    gather_coarse(recv_ref, 4, k2_ref)
    mg2 = coarse_solve(w_ref[...], k2_ref[...])
    spread_coarse(mg2, table_ref, row_ref, m2_ref)
    up_levels(m2_ref, e1_ref, k1_ref, mg1_ref, e0x_ref, k0x_ref, corr_ref, e1p_ref, e0p_ref)

    row8 = lax.broadcasted_iota(jnp.int32, (8, LANES), 0)
    own_live = jnp.where(q_ref[0, 0] > 0.0, 1.0, 0.0).astype(F32)
    livex_ref[0] = jnp.concatenate([own_live, side_live(rxlo_ref, rxhi_ref, row8)], axis=0)
    ylo_here, yhi_here = inside("gy")
    livex_ref[1] = kept(yhi_here, jnp.concatenate([ryhi_ref[16], eyhi_ref[80]], axis=0))
    livex_ref[2] = kept(ylo_here, jnp.concatenate([rylo_ref[16], eylo_ref[80]], axis=0))

    def fill(y, carry):
        for o in range(8):
            f1x_ref[o, y, 0:16, :] = f1_ref[o, y]
            f1x_ref[o, y, 16:24, :] = side_tile(rxlo_ref, rxhi_ref, (o // 4) * 16 + y, o % 4)
        return carry

    lax.fori_loop(0, 16, fill, 0, unroll=UNROLL)
    for o in range(8):
        for j in range(2):
            f1x_ref[o, 16 + j, 0:16, :] = kept(yhi_here, ryhi_ref[o * 2 + j])
            f1x_ref[o, 16 + j, 16:24, :] = kept(yhi_here, eyhi_ref[64 + o * 2 + j])
            f1x_ref[o, 18 + j, 0:16, :] = kept(ylo_here, rylo_ref[o * 2 + j])
            f1x_ref[o, 18 + j, 16:24, :] = kept(ylo_here, eylo_ref[64 + o * 2 + j])

    def add(y, carry):
        c = corr_ref[y]
        for o in range(8):
            ua_ref[o, y] = f1x_ref[o, y] + c
        return carry

    lax.fori_loop(0, YF, add, 0, unroll=UNROLL)
    fine_sweep(ua_ref, ub_ref, f1x_ref, livex_ref)

    def base(y, carry):
        v_ref[y] = mean8([ub_ref[o, y] for o in range(8)])
        return carry

    lax.fori_loop(0, YF, base, 0, unroll=UNROLL)
    fine_sweep(ub_ref, u3_ref, f1x_ref, livex_ref)

    def left(y, carry):
        cur, new = fine_relax(u3_ref, y, [f1x_ref[o, y] for o in range(8)])
        fine_left = mean8([q_ref[o, y] * (new[o][0:16] - cur[o][0:16]) for o in range(8)])
        k0 = k0x_ref[y][0:16]
        v = v_ref[y]
        s = around(v, v_ref[jnp.where(y == 0, YF - 1, y - 1)], v_ref[y + 1], 1)
        base_left = brhs_ref[pl.ds(y, 16, stride=16), :] - k0 * (v * (2.0 / 3.0) - s * NINTH)[0:16]
        e0 = jnp.where(q_ref[0, y] > 0.0, fine_left, base_left) / k0
        e0_ref[y] = e0
        exlo_ref[y] = e0[0:8]
        exhi_ref[y] = e0[8:16]
        return carry

    lax.fori_loop(0, 16, left, 0, unroll=UNROLL)


def last_kernel(
    site_ref, count_ref, recv_ref, k2_ref, e0x_ref, k0x_ref, e1_ref, k1_ref, u3_ref, f1x_ref, livex_ref,
    fine_ref, base_ref,
    w_ref, table_ref, row_ref, m2_ref, mg1_ref, e1p_ref, e0p_ref, corr_ref, ua_ref, ub_ref, out_ref,
):
    gather_coarse(recv_ref, 0, w_ref)
    mg2 = coarse_solve(w_ref[...], k2_ref[...])
    spread_coarse(mg2, table_ref, row_ref, m2_ref)
    up_levels(m2_ref, e1_ref, k1_ref, mg1_ref, e0x_ref, k0x_ref, corr_ref, e1p_ref, e0p_ref)

    def add(y, carry):
        c = corr_ref[y]
        for o in range(8):
            ua_ref[o, y] = u3_ref[o, y] + c
        return carry

    lax.fori_loop(0, YF, add, 0, unroll=UNROLL)
    live = livex_ref[0] > 0.0

    def row(y, carry):
        cur, new = fine_relax(ua_ref, y, [f1x_ref[o, y] for o in range(8)])
        got = [jnp.where(live, new[o], cur[o])[0:16] for o in range(8)]
        for o in range(8):
            ub_ref[o, y] = got[o]
        base_ref[pl.ds(y, 16, stride=16), :] = mean8(got)
        return carry

    lax.fori_loop(0, 16, row, 0, unroll=UNROLL)

    lane = lax.broadcasted_iota(jnp.int32, (16, LANES), 1)
    for s in range(4):
        idx = site_ref[0, 0, s] * 16 + ((lane & 31) // 2)
        live_slot = s < count_ref[0, 0]
        for px in range(2):
            for t in range(8):
                out = jnp.zeros((16, LANES), F32)
                for g in range(8):
                    yy, pz = g // 2, g % 2
                    src = ub_ref[px * 4 + (yy % 2) * 2 + pz, 2 * t + yy // 2]
                    here = ((lane // 32) == yy) & ((lane & 1) == pz) & live_slot
                    out = jnp.where(here, lane_gather(src, idx), out)
                out_ref[s, t, pl.ds(px, 16, stride=2), :] = out
        for t in range(8):
            fine_ref[0, 0, s, :, t * LANES : (t + 1) * LANES] = out_ref[s, t]


def call(kernel, name, out_shapes, n_smem, n_vmem, scratch=()):
    vmem = pl.BlockSpec(memory_space=pltpu.VMEM)
    smem = pl.BlockSpec(memory_space=pltpu.SMEM)
    return pl.pallas_call(
        kernel,
        name=name,
        out_shape=[jax.ShapeDtypeStruct(s, F32) for s in out_shapes],
        in_specs=[smem] * n_smem + [vmem] * n_vmem,
        out_specs=[vmem] * len(out_shapes),
        scratch_shapes=[pltpu.VMEM(s, F32) for s in scratch],
        compiler_params=pltpu.CompilerParams(vmem_limit_bytes=VMEM_LIMIT),
    )


def step(value, axis, by):
    count = lax.axis_size(axis)
    return lax.ppermute(value, axis, [(i, (i + by) % count) for i in range(count)])


def from_sides(to_low, to_high, axis):
    return step(to_high, axis, 1), step(to_low, axis, -1)


def local(fine_rhs, fine_beta, base_rhs, base_beta, slot_site, ghost_list, box_count):
    gx_total, gy_total = lax.axis_size("gx"), lax.axis_size("gy")
    devices = gx_total * gy_total

    rhs = base_rhs.reshape(256, LANES)
    octets = (8, 16, 16, LANES)
    own = (16, 16, LANES)
    f1, q, k0, fxlo, fxhi, fylo, fyhi = call(
        prepare_kernel, "prepare",
        [octets, octets, own, (33, 8, LANES), (33, 8, LANES), (17, 16, LANES), (17, 16, LANES)], 2, 3,
        [(4, 8, 32, LANES), (4, 8, 32, LANES)],
    )(slot_site, box_count, fine_rhs, fine_beta, base_beta.reshape(256, LANES))
    rxlo, rxhi = from_sides(fxlo, fxhi, "gx")
    rylo, ryhi = from_sides(fylo, fyhi, "gy")
    e0, exlo, exhi = call(
        first_residual_kernel, "first_residual",
        [own, (32, 8, LANES), (32, 8, LANES)], 0, 8, [(8, YF, XF, LANES)],
    )(f1, q, k0, rhs, rxlo, rxhi, rylo, ryhi)
    sxlo, sxhi = from_sides(exlo, exhi, "gx")
    eylo, eyhi = call(
        pack_y_first_kernel, "pack_y_first", [(81, 8, LANES), (81, 8, LANES)], 0, 6
    )(e0, k0, sxlo, sxhi, rxlo, rxhi)
    sylo, syhi = from_sides(eylo, eyhi, "gy")
    wide = (32, 32, LANES)
    half = (16, 32, LANES)
    send, e0x, k0x, e1, k1 = call(
        down_first_kernel, "down_first", [(devices, 8, LANES), wide, wide, half, half], 0, 6, [(16, LANES)]
    )(e0, k0, sxlo, sxhi, sylo, syhi)
    recv = lax.all_to_all(send, ("gx", "gy"), 0, 0, tiled=True)

    fine_ext = (8, YF, XF, LANES)
    coarse = (gy_total, 4 * gx_total, LANES)
    coarse_scratch = [
        coarse, (gy_total + 2, gx_total + 2, 8, LANES), (32, LANES), (8, 32, LANES), half, half, wide,
        (YF, XF, LANES),
    ]
    u3, f1x, livex, k2, e0, exlo, exhi = call(
        middle_kernel, "middle",
        [fine_ext, fine_ext, (3, XF, LANES), coarse, own, (16, 8, LANES), (16, 8, LANES)],
        0, 14, coarse_scratch + [fine_ext, fine_ext, (YF, XF, LANES)],
    )(recv, e0x, k0x, e1, k1, f1, q, rhs, rxlo, rxhi, rylo, ryhi, sylo, syhi)
    sxlo, sxhi = from_sides(exlo, exhi, "gx")
    eylo, eyhi = call(
        pack_y_kernel, "pack_y", [(32, 8, LANES), (32, 8, LANES)], 0, 3
    )(e0, sxlo, sxhi)
    sylo, syhi = from_sides(eylo, eyhi, "gy")
    send, e0x, e1 = call(
        down_kernel, "down", [(devices, 4, LANES), wide, half], 0, 7, [(16, LANES)]
    )(e0, k0x, k1, sxlo, sxhi, sylo, syhi)
    recv = lax.all_to_all(send, ("gx", "gy"), 0, 0, tiled=True)
    fine, base = call(
        last_kernel, "last", [fine_rhs.shape, (256, LANES)], 2, 9,
        coarse_scratch + [fine_ext, octets, (4, 8, 32, LANES)],
    )(slot_site, box_count, recv, k2, e0x, k0x, e1, k1, u3, f1x, livex)
    return fine, base.reshape(base_rhs.shape)


def solution(mesh):
    return jax.shard_map(
        local,
        mesh=mesh,
        in_specs=(
            P("gx", "gy", None, None, None),
            P("gx", "gy", None, None, None),
            P("gx", "gy", None),
            P("gx", "gy", None),
            P("gx", "gy", None),
            P("gx", "gy", None, None),
            P("gx", "gy"),
        ),
        out_specs=(P("gx", "gy", None, None, None), P("gx", "gy", None)),
        check_vma=False,
    )
```

time: 895 us -> 95.3 us (0.11)
  the two profiles are of different devices: /device:TPU:28 before, /device:TPU:0 now
where the time goes in v1:
time: 95.3 us; the launch traced here: 95 us
  waiting for transfers between devices  24.2 us (25%)
  blocking collectives  23.7 us (25%)
  starting transfers between devices  20.9 us (22%)
  Pallas kernels  20.4 us (21%)
  local copies, waits for them, and re-layouts  4.55 us (5%)
  between operations  1.36 us (1%)
    ppermute x12, waiting for transfers between devices, step(): lax.ppermute(value, axis, [(i, (i + by) % count) for i in range(count)])  24.2 us
    all_to_all x2, blocking collectives, local(): recv = lax.all_to_all(send, ('gx', 'gy'), 0, 0, tiled=True)  23.7 us
    ppermute x12, starting transfers between devices, step(): lax.ppermute(value, axis, [(i, (i + by) % count) for i in range(count)])  20.9 us
    pallas_call x1, Pallas kernels, local(): call(middle_kernel, 'middle', [fine_ext, fine_ext, (3, XF, LANES), coarse...  6.17 us
    pallas_call x1, Pallas kernels, local(): call(last_kernel, 'last', [fine_rhs.shape, (256, LANES)], 2, 9, coarse_sc...  6.03 us
    unnamed x14, local copies, waits for them, and re-layouts  4.55 us
    pallas_call x1, Pallas kernels, local(): call(prepare_kernel, 'prepare', [octets, octets, own, (33, 8, LANES), (33...  4.45 us
  transfers between devices with their start and end apart: 12, of which 7 were waited for; matrix products, arithmetic and copies ran while one was open for 0% of the time, Pallas kernels for 0%

profile of v1, /device:TPU:0, one launch (start us, length us, event | category | flops | bytes accessed | tf_op | source)
XLA Modules:
  0.0 95.0 jit_solution(10131248920261865832)
XLA Ops:
  1.3 0.0 copy-start.2
  1.3 1.0 %copy-done.2 = f32[1,1,4,32,1024]{4,3,2,1,0:T(8,128)S(1)} copy-done((f32[1,1,4,32,1024]{4,3,2,1,0:T(8,128)S(1)}, f32[1,1,4,32,1024]{4,3,2,1,0:T(8,128)}, u32[]{:S(2)}) %copy-start.2) | copy-done | bytes 524312
  2.3 0.0 copy-start.3
  2.3 1.0 %copy-done.3 = f32[1,1,4,32,1024]{4,3,2,1,0:T(8,128)S(1)} copy-done((f32[1,1,4,32,1024]{4,3,2,1,0:T(8,128)S(1)}, f32[1,1,4,32,1024]{4,3,2,1,0:T(8,128)}, u32[]{:S(2)}) %copy-start.3) | copy-done | bytes 524312
  3.4 0.0 copy-start.4
  3.4 0.9 copy-done.4
  4.3 0.0 copy-start.5
  4.3 0.7 copy-done.5
  4.9 4.4 %prepare.1 = (f32[8,16,16,128]{3,2,1,0:T(8,128)S(1)}, f32[8,16,16,128]{3,2,1,0:T(8,128)S(1)}, f32[16,16,128]{2,1,0:T(8,128)S(1)}, f32[33,8,128]{2,1,0:T(8,128)S(...) custom-call(s32[1,1,4]{2,1,0:T(1,128)S(1)} %copy-done.5, ...), custom_call_target="tpu_custom_call" | custom-call | tf_op jit(solution)/shard_map/prepare/pallas_call | solution.py:613
  9.4 0.5 collective-permute-start.2
  9.9 2.9 %collective-permute-start.3 = (f32[17,16,128]{2,1,0:T(8,128)S(1)}, f32[17,16,128]{2,1,0:T(8,128)S(1)}, u32[]{:S(2)}, u32[]{:S(2)}) collective-permute-start(f32[17,16,128]{2,1,0:T(8,128)S(1)} %get-tuple-element.39), channel_id=1, source_target_pairs={{0,7},{1,0},{2,1},{3,2},{4,3},{5,4},{6,5},{7,6},{8,15},{9,8},{10,9... | collective-permute-start | bytes 417800 | tf_op jit(solution)/shard_map/ppermute | solution.py:599
  12.8 2.3 %collective-permute-start = (f32[33,8,128]{2,1,0:T(8,128)S(1)}, f32[33,8,128]{2,1,0:T(8,128)S(1)}, u32[]{:S(2)}, u32[]{:S(2)}) collective-permute-start(f32[33,8,128]{2,1,0:T(8,128)S(1)} %get-tuple-element.36), channel_id=1, source_target_pairs={{0,8},{8,16},{16,24},{24,0},{1,9},{9,17},{17,25},{25,1},{2,10},{10... | collective-permute-start | bytes 405512 | tf_op jit(solution)/shard_map/ppermute | solution.py:599
  15.1 2.0 %collective-permute-start.1 = (f32[33,8,128]{2,1,0:T(8,128)S(1)}, f32[33,8,128]{2,1,0:T(8,128)S(1)}, u32[]{:S(2)}, u32[]{:S(2)}) collective-permute-start(f32[33,8,128]{2,1,0:T(8,128)S(1)} %get-tuple-element.37), channel_id=1, source_target_pairs={{0,24},{8,0},{16,8},{24,16},{1,25},{9,1},{17,9},{25,17},{2,26},{10... | collective-permute-start | bytes 405512 | tf_op jit(solution)/shard_map/ppermute | solution.py:599
  17.1 4.2 %collective-permute-done.rxlo_ref.fxlo_ref = f32[33,8,128]{2,1,0:T(8,128)S(1)} collective-permute-done((f32[33,8,128]{2,1,0:T(8,128)S(1)}, f32[33,8,128]{2,1,0:T(8,128)S(1)}, u32[]{:S(2)}, u32[]{:S(2)}) %collective-permute-start) | collective-permute-done | bytes 135200 | tf_op jit(solution)/shard_map/ppermute | solution.py:599
  21.3 0.8 collective-permute-done.1.rxhi_ref.fxhi_ref
  22.2 0.0 collective-permute-done.2.rylo_ref
  22.2 0.0 collective-permute-done.3.ryhi_ref
  22.2 0.0 copy-start
  22.2 0.9 copy-done
  23.1 0.0 copy-start.1
  23.1 0.9 first_residual.1
  23.9 1.2 %collective-permute-start.4 = (f32[32,8,128]{2,1,0:T(8,128)S(1)}, f32[32,8,128]{2,1,0:T(8,128)S(1)}, u32[]{:S(2)}, u32[]{:S(2)}) collective-permute-start(f32[32,8,128]{2,1,0:T(8,128)S(1)} %get-tuple-element.41), channel_id=1, source_target_pairs={{0,8},{8,16},{16,24},{24,0},{1,9},{9,17},{17,25},{25,1},{2,10},{10... | collective-permute-start | bytes 393224 | tf_op jit(solution)/shard_map/ppermute | solution.py:599
  25.1 2.7 %collective-permute-start.5 = (f32[32,8,128]{2,1,0:T(8,128)S(1)}, f32[32,8,128]{2,1,0:T(8,128)S(1)}, u32[]{:S(2)}, u32[]{:S(2)}) collective-permute-start(f32[32,8,128]{2,1,0:T(8,128)S(1)} %get-tuple-element.42), channel_id=1, source_target_pairs={{0,24},{8,0},{16,8},{24,16},{1,25},{9,1},{17,9},{25,17},{2,26},{10... | collective-permute-start | bytes 393224 | tf_op jit(solution)/shard_map/ppermute | solution.py:599
  27.8 3.9 %collective-permute-done.4.exlo_ref = f32[32,8,128]{2,1,0:T(8,128)S(1)} collective-permute-done((f32[32,8,128]{2,1,0:T(8,128)S(1)}, f32[32,8,128]{2,1,0:T(8,128)S(1)}, u32[]{:S(2)}, u32[]{:S(2)}) %collective-permute-start.4) | collective-permute-done | bytes 131104 | tf_op jit(solution)/shard_map/ppermute | solution.py:599
  31.7 0.6 collective-permute-done.5.exhi_ref
  32.3 0.1 pack_y_first.1
  32.4 0.1 collective-permute-start.6
  32.5 2.6 %collective-permute-start.7 = (f32[81,8,128]{2,1,0:T(8,128)S(1)}, f32[81,8,128]{2,1,0:T(8,128)S(1)}, u32[]{:S(2)}, u32[]{:S(2)}) collective-permute-start(f32[81,8,128]{2,1,0:T(8,128)S(1)} %get-tuple-element.44), channel_id=1, source_target_pairs={{0,7},{1,0},{2,1},{3,2},{4,3},{5,4},{6,5},{7,6},{8,15},{9,8},{10,9... | collective-permute-start | bytes 995336 | tf_op jit(solution)/shard_map/ppermute | solution.py:599
  35.1 7.8 %collective-permute-done.6.eylo_ref = f32[81,8,128]{2,1,0:T(8,128)S(1)} collective-permute-done((f32[81,8,128]{2,1,0:T(8,128)S(1)}, f32[81,8,128]{2,1,0:T(8,128)S(1)}, u32[]{:S(2)}, u32[]{:S(2)}) %collective-permute-start.6) | collective-permute-done | bytes 331808 | tf_op jit(solution)/shard_map/ppermute | solution.py:599
  42.9 0.0 collective-permute-done.7.eyhi_ref
  42.9 1.5 %down_first.1 = (f32[32,8,128]{2,1,0:T(8,128)S(1)}, f32[32,32,128]{2,1,0:T(8,128)S(1)}, f32[32,32,128]{2,1,0:T(8,128)S(1)}, f32[16,32,128]{2,1,0:T(8,128)S(1)}, f32[16,32,128]{2,1,0:T(8,128)S(1)}) custom-call(f32[16,16,128]{2,1,0:T(8,128)S(1)} %get-tuple-element.40.e0_ref, f32[16,16,128]{2,1,0:T(8,128)S(1)} %get-tuple-element.35.k0_ref, ...), custom_call_target="tpu_custom_call" | custom-call | tf_op jit(solution)/shard_map/down_first/pallas_call | solution.py:631
  44.4 12.2 %all_to_all.10.recv_ref = f32[32,8,128]{2,1,0:T(8,128)S(1)} all-to-all(f32[32,8,128]{2,1,0:T(8,128)S(1)} %get-tuple-element.45), channel_id=1, replica_groups=mesh['gx'=4,'gy'=8] {'gx','gy'}, dimensions={0} | all-to-all | bytes 262144 | tf_op jit(solution)/shard_map/all_to_all | solution.py:634
  56.6 0.0 copy-done.1
  56.6 0.0 copy-start.6
  56.6 6.2 %middle.1 = (f32[8,20,24,128]{3,2,1,0:T(8,128)S(1)}, f32[8,20,24,128]{3,2,1,0:T(8,128)S(1)}, f32[3,24,128]{2,1,0:T(8,128)S(1)}, f32[8,16,128]{2,1,0:T(8,128)S(1)...) custom-call(f32[32,8,128]{2,1,0:T(8,128)S(1)} %all_to_all.10.recv_ref, ...), custom_call_target="tpu_custom_call" | custom-call | tf_op jit(solution)/shard_map/middle/pallas_call | solution.py:642
  62.8 0.7 collective-permute-start.8
  63.5 3.2 %collective-permute-start.9 = (f32[16,8,128]{2,1,0:T(8,128)S(1)}, f32[16,8,128]{2,1,0:T(8,128)S(1)}, u32[]{:S(2)}, u32[]{:S(2)}) collective-permute-start(f32[16,8,128]{2,1,0:T(8,128)S(1)} %get-tuple-element.52), channel_id=1, source_target_pairs={{0,24},{8,0},{16,8},{24,16},{1,25},{9,1},{17,9},{25,17},{2,26},{10... | collective-permute-start | bytes 196616 | tf_op jit(solution)/shard_map/ppermute | solution.py:599
  66.6 2.9 %collective-permute-done.8.exlo_ref = f32[16,8,128]{2,1,0:T(8,128)S(1)} collective-permute-done((f32[16,8,128]{2,1,0:T(8,128)S(1)}, f32[16,8,128]{2,1,0:T(8,128)S(1)}, u32[]{:S(2)}, u32[]{:S(2)}) %collective-permute-start.8) | collective-permute-done | bytes 65568 | tf_op jit(solution)/shard_map/ppermute | solution.py:599
  69.5 0.0 collective-permute-done.9.exhi_ref
  69.6 0.1 collective-permute-start.10
  69.6 2.6 %collective-permute-start.11 = (f32[32,8,128]{2,1,0:T(8,128)S(1)}, f32[32,8,128]{2,1,0:T(8,128)S(1)}, u32[]{:S(2)}, u32[]{:S(2)}) collective-permute-start(f32[32,8,128]{2,1,0:T(8,128)S(1)} %get-tuple-element.54), channel_id=1, source_target_pairs={{0,7},{1,0},{2,1},{3,2},{4,3},{5,4},{6,5},{7,6},{8,15},{9,8},{10,9... | collective-permute-start | bytes 393224 | tf_op jit(solution)/shard_map/ppermute | solution.py:599
  72.3 4.0 %collective-permute-done.10.eylo_ref = f32[32,8,128]{2,1,0:T(8,128)S(1)} collective-permute-done((f32[32,8,128]{2,1,0:T(8,128)S(1)}, f32[32,8,128]{2,1,0:T(8,128)S(1)}, u32[]{:S(2)}, u32[]{:S(2)}) %collective-permute-start.10) | collective-permute-done | bytes 131104 | tf_op jit(solution)/shard_map/ppermute | solution.py:599
  76.2 0.0 collective-permute-done.11.eyhi_ref
  76.2 1.2 %down.1 = (f32[32,4,128]{2,1,0:T(4,128)S(1)}, f32[32,32,128]{2,1,0:T(8,128)S(1)}, f32[16,32,128]{2,1,0:T(8,128)S(1)}) custom-call(f32[16,16,128]{2,1,0:T(8,128)S(1)} %get-tuple-element.50.e0_ref, f32[32,32,128]{2,1,0:T(8,128)S(1)} %get-tuple-element.47.k0x_ref, f32[16,32,128]{2,1,0:T(8,128)S(1)} %get-tuple-element.49.k1_ref, ...), custom_call_target="tpu_custom_call" | custom-call | tf_op jit(solution)/shard_map/down/pallas_call | solution.py:652
  77.5 11.5 %all_to_all.11.recv_ref = f32[32,4,128]{2,1,0:T(4,128)S(1)} all-to-all(f32[32,4,128]{2,1,0:T(4,128)S(1)} %get-tuple-element.55), channel_id=1, replica_groups=mesh['gx'=4,'gy'=8] {'gx','gy'}, dimensions={0} | all-to-all | bytes 131072 | tf_op jit(solution)/shard_map/all_to_all | solution.py:655
  89.0 0.0 copy-done.6
  89.0 6.0 %last.1 = (f32[1,1,4,32,1024]{4,3,2,1,0:T(8,128)}, f32[256,128]{1,0:T(8,128)}) custom-call(s32[1,1,4]{2,1,0:T(1,128)S(1)} %copy-done.6, s32[1,1]{1,0:T(1,128)S(6)} %copy.8.count_ref, f32[32,4,128]{2,1,0:T(4,128)S(1)} %all_to_all.11.recv_ref, f32[8,16,128]{2,1,0:T(8,128)S(1)} %get-tuple-element.56.k2_ref, f32[32,32,128]{2,1,0:T(8,128)S(1)} %get-tuple-element.57.e0x_ref, ...), custom_call_target="tpu_custom_call" | custom-call | tf_op jit(solution)/shard_map/last/pallas_call | solution.py:656
  (1 shorter events, 0.0 us)
Async XLA Ops:
  1.3 1.0 %copy-start.2 = (f32[1,1,4,32,1024]{4,3,2,1,0:T(8,128)S(1)}, f32[1,1,4,32,1024]{4,3,2,1,0:T(8,128)}, u32[]{:S(2)}) copy-start(f32[1,1,4,32,1024]{4,3,2,1,0:T(8,128)} %rhs_ref.1) | copy-start | bytes 1572868
  2.3 1.0 %copy-start.3 = (f32[1,1,4,32,1024]{4,3,2,1,0:T(8,128)S(1)}, f32[1,1,4,32,1024]{4,3,2,1,0:T(8,128)}, u32[]{:S(2)}) copy-start(f32[1,1,4,32,1024]{4,3,2,1,0:T(8,128)} %beta_ref.1) | copy-start | bytes 1572868
  3.4 0.9 copy-start.4
  4.3 0.7 copy-start.5
  9.4 12.8 %collective-permute-start.2 = (f32[17,16,128]{2,1,0:T(8,128)S(1)}, f32[17,16,128]{2,1,0:T(8,128)S(1)}, u32[]{:S(2)}, u32[]{:S(2)}) collective-permute-start(f32[17,16,128]{2,1,0:T(8,128)S(1)} %get-tuple-element.38), channel_id=1, source_target_pairs={{0,1},{1,2},{2,3},{3,4},{4,5},{5,6},{6,7},{7,0},{8,9},{9,10},{10,1... | collective-permute-start | bytes 417800 | tf_op jit(solution)/shard_map/ppermute | solution.py:599
  9.9 12.3 %collective-permute-start.3 = (f32[17,16,128]{2,1,0:T(8,128)S(1)}, f32[17,16,128]{2,1,0:T(8,128)S(1)}, u32[]{:S(2)}, u32[]{:S(2)}) collective-permute-start(f32[17,16,128]{2,1,0:T(8,128)S(1)} %get-tuple-element.39), channel_id=1, source_target_pairs={{0,7},{1,0},{2,1},{3,2},{4,3},{5,4},{6,5},{7,6},{8,15},{9,8},{10,9... | collective-permute-start | bytes 417800 | tf_op jit(solution)/shard_map/ppermute | solution.py:599
  12.8 8.5 %collective-permute-start = (f32[33,8,128]{2,1,0:T(8,128)S(1)}, f32[33,8,128]{2,1,0:T(8,128)S(1)}, u32[]{:S(2)}, u32[]{:S(2)}) collective-permute-start(f32[33,8,128]{2,1,0:T(8,128)S(1)} %get-tuple-element.36), channel_id=1, source_target_pairs={{0,8},{8,16},{16,24},{24,0},{1,9},{9,17},{17,25},{25,1},{2,10},{10... | collective-permute-start | bytes 405512 | tf_op jit(solution)/shard_map/ppermute | solution.py:599
  15.1 7.1 %collective-permute-start.1 = (f32[33,8,128]{2,1,0:T(8,128)S(1)}, f32[33,8,128]{2,1,0:T(8,128)S(1)}, u32[]{:S(2)}, u32[]{:S(2)}) collective-permute-start(f32[33,8,128]{2,1,0:T(8,128)S(1)} %get-tuple-element.37), channel_id=1, source_target_pairs={{0,24},{8,0},{16,8},{24,16},{1,25},{9,1},{17,9},{25,17},{2,26},{10... | collective-permute-start | bytes 405512 | tf_op jit(solution)/shard_map/ppermute | solution.py:599
  22.2 0.9 copy-start
  23.1 33.5 %copy-start.1 = (f32[16,16,128]{2,1,0:T(8,128)S(1)}, f32[16,16,128]{2,1,0:T(8,128)}, u32[]{:S(2)}) copy-start(f32[16,16,128]{2,1,0:T(8,128)} %param.9) | copy-start | bytes 393220
  23.9 7.8 %collective-permute-start.4 = (f32[32,8,128]{2,1,0:T(8,128)S(1)}, f32[32,8,128]{2,1,0:T(8,128)S(1)}, u32[]{:S(2)}, u32[]{:S(2)}) collective-permute-start(f32[32,8,128]{2,1,0:T(8,128)S(1)} %get-tuple-element.41), channel_id=1, source_target_pairs={{0,8},{8,16},{16,24},{24,0},{1,9},{9,17},{17,25},{25,1},{2,10},{10... | collective-permute-start | bytes 393224 | tf_op jit(solution)/shard_map/ppermute | solution.py:599
  25.1 7.2 %collective-permute-start.5 = (f32[32,8,128]{2,1,0:T(8,128)S(1)}, f32[32,8,128]{2,1,0:T(8,128)S(1)}, u32[]{:S(2)}, u32[]{:S(2)}) collective-permute-start(f32[32,8,128]{2,1,0:T(8,128)S(1)} %get-tuple-element.42), channel_id=1, source_target_pairs={{0,24},{8,0},{16,8},{24,16},{1,25},{9,1},{17,9},{25,17},{2,26},{10... | collective-permute-start | bytes 393224 | tf_op jit(solution)/shard_map/ppermute | solution.py:599
  32.4 10.5 %collective-permute-start.6 = (f32[81,8,128]{2,1,0:T(8,128)S(1)}, f32[81,8,128]{2,1,0:T(8,128)S(1)}, u32[]{:S(2)}, u32[]{:S(2)}) collective-permute-start(f32[81,8,128]{2,1,0:T(8,128)S(1)} %get-tuple-element.43), channel_id=1, source_target_pairs={{0,1},{1,2},{2,3},{3,4},{4,5},{5,6},{6,7},{7,0},{8,9},{9,10},{10,1... | collective-permute-start | bytes 995336 | tf_op jit(solution)/shard_map/ppermute | solution.py:599
  32.5 10.4 %collective-permute-start.7 = (f32[81,8,128]{2,1,0:T(8,128)S(1)}, f32[81,8,128]{2,1,0:T(8,128)S(1)}, u32[]{:S(2)}, u32[]{:S(2)}) collective-permute-start(f32[81,8,128]{2,1,0:T(8,128)S(1)} %get-tuple-element.44), channel_id=1, source_target_pairs={{0,7},{1,0},{2,1},{3,2},{4,3},{5,4},{6,5},{7,6},{8,15},{9,8},{10,9... | collective-permute-start | bytes 995336 | tf_op jit(solution)/shard_map/ppermute | solution.py:599
  56.6 32.4 %copy-start.6 = (s32[1,1,4]{2,1,0:T(1,128)S(1)}, s32[1,1,4]{2,1,0:T(1,128)}, u32[]{:S(2)}) copy-start(s32[1,1,4]{2,1,0:T(1,128)} %site_ref.3) | copy-start | bytes 52
  62.8 6.8 %collective-permute-start.8 = (f32[16,8,128]{2,1,0:T(8,128)S(1)}, f32[16,8,128]{2,1,0:T(8,128)S(1)}, u32[]{:S(2)}, u32[]{:S(2)}) collective-permute-start(f32[16,8,128]{2,1,0:T(8,128)S(1)} %get-tuple-element.51), channel_id=1, source_target_pairs={{0,8},{8,16},{16,24},{24,0},{1,9},{9,17},{17,25},{25,1},{2,10},{10... | collective-permute-start | bytes 196616 | tf_op jit(solution)/shard_map/ppermute | solution.py:599
  63.5 6.1 %collective-permute-start.9 = (f32[16,8,128]{2,1,0:T(8,128)S(1)}, f32[16,8,128]{2,1,0:T(8,128)S(1)}, u32[]{:S(2)}, u32[]{:S(2)}) collective-permute-start(f32[16,8,128]{2,1,0:T(8,128)S(1)} %get-tuple-element.52), channel_id=1, source_target_pairs={{0,24},{8,0},{16,8},{24,16},{1,25},{9,1},{17,9},{25,17},{2,26},{10... | collective-permute-start | bytes 196616 | tf_op jit(solution)/shard_map/ppermute | solution.py:599
  69.6 6.7 %collective-permute-start.10 = (f32[32,8,128]{2,1,0:T(8,128)S(1)}, f32[32,8,128]{2,1,0:T(8,128)S(1)}, u32[]{:S(2)}, u32[]{:S(2)}) collective-permute-start(f32[32,8,128]{2,1,0:T(8,128)S(1)} %get-tuple-element.53), channel_id=1, source_target_pairs={{0,1},{1,2},{2,3},{3,4},{4,5},{5,6},{6,7},{7,0},{8,9},{9,10},{10,1... | collective-permute-start | bytes 393224 | tf_op jit(solution)/shard_map/ppermute | solution.py:599
  69.6 6.6 %collective-permute-start.11 = (f32[32,8,128]{2,1,0:T(8,128)S(1)}, f32[32,8,128]{2,1,0:T(8,128)S(1)}, u32[]{:S(2)}, u32[]{:S(2)}) collective-permute-start(f32[32,8,128]{2,1,0:T(8,128)S(1)} %get-tuple-element.54), channel_id=1, source_target_pairs={{0,7},{1,0},{2,1},{3,2},{4,3},{5,4},{6,5},{7,6},{8,15},{9,8},{10,9... | collective-permute-start | bytes 393224 | tf_op jit(solution)/shard_map/ppermute | solution.py:599

commit v2 on v1

v2 whole, which is shorter than its diff:
```python
import functools

import jax
import jax.numpy as jnp
from jax import lax
from jax.experimental import pallas as pl
from jax.experimental.pallas import tpu as pltpu
from jax.sharding import PartitionSpec as P

CYCLES = 2
SWEEPS = 6
THIRD = 1.0 / 3.0
NINTH = 1.0 / 9.0
F32 = jnp.float32
LANES = 128
VMEM_LIMIT = 16 * 1024 * 1024
UNROLL = 4


def lanes_of(v):
    return lax.broadcasted_iota(jnp.int32, v.shape, v.ndim - 1)


def rows_of(v):
    return lax.broadcasted_iota(jnp.int32, v.shape, v.ndim - 2)


def z_low(v, n):
    return jnp.where(lanes_of(v) >= n, pltpu.roll(v, n, v.ndim - 1), 0.0)


def z_high(v, n):
    return jnp.where(lanes_of(v) < LANES - n, pltpu.roll(v, LANES - n, v.ndim - 1), 0.0)


def x_low(v, n):
    return pltpu.roll(v, n, v.ndim - 2)


def x_high(v, n):
    return pltpu.roll(v, v.shape[-2] - n, v.ndim - 2)


def pair_x(v, n):
    return v + jnp.where((rows_of(v) & n) == 0, x_high(v, n), x_low(v, n))


def pair_z(v, n):
    lane = lanes_of(v)
    return v + jnp.where(
        (lane & n) == 0, pltpu.roll(v, LANES - n, v.ndim - 1), pltpu.roll(v, n, v.ndim - 1)
    )


def lane_gather(v, idx):
    return jnp.take_along_axis(v, idx, axis=1)


def around(v, low_y, high_y, n):
    return (x_low(v, n) + x_high(v, n)) + (low_y + high_y) + (z_low(v, n) + z_high(v, n))


def relax(v, low_y, high_y, n):
    return v * THIRD + around(v, low_y, high_y, n) * NINTH


YF = 20
XF = 24


def fine_relax(ref, y, f1_rows):
    below, above = (y + YF - 1) % YF, (y + 1) % YF
    cur = [ref[o, y] for o in range(8)]
    out = []
    for o in range(8):
        ox, oy, oz = o ^ 4, o ^ 2, o ^ 1
        s = (cur[ox] + cur[oy]) + cur[oz]
        s = s + (x_low(cur[ox], 1) if o & 4 == 0 else x_high(cur[ox], 1))
        s = s + (ref[oy, below] if o & 2 == 0 else ref[oy, above])
        s = s + (z_low(cur[oz], 1) if o & 1 == 0 else z_high(cur[oz], 1))
        new = cur[o] * THIRD + s * NINTH
        out.append(new if f1_rows is None else new + f1_rows[o])
    return cur, out


def each(count, body):
    for n in range(count):
        body(n)


def inside(axis):
    at = lax.axis_index(axis)
    return at > 0, at < lax.axis_size(axis) - 1


def kept(here, v):
    return jnp.where(here, v, 0.0)


def mean8(rows):
    return (
        ((rows[0] + rows[1]) + (rows[2] + rows[3])) + ((rows[4] + rows[5]) + (rows[6] + rows[7]))
    ) * 0.125


def slot_map(site_ref, count_ref, shape):
    lane_site = lax.broadcasted_iota(jnp.int32, shape, 1) // 16
    out = jnp.zeros(shape, F32)
    for s in range(4):
        site = jnp.where(s < count_ref[0, 0], site_ref[0, 0, s], -1)
        out = jnp.where(lane_site == site, float(s + 1), out)
    return out


def transpose_blocks(v):
    block = lanes_of(v[0]) // 32
    out = []
    for j in range(4):
        row = v[j]
        for i in range(4):
            if i != j:
                row = jnp.where(block == i, pltpu.roll(v[i], 32 * (i - j) % LANES, 1), row)
        out.append(row)
    return out


def expand(v, slots, pz):
    lane = lanes_of(v)
    slot = slots.astype(jnp.int32) - 1
    idx = jnp.maximum(slot, 0) * 32 + (2 * (lane & 15) + pz)
    return jnp.where(slot >= 0, lane_gather(v, idx), 0.0)


def faces_kernel(
    site_ref, count_ref, rhs_hbm, beta_hbm,
    fxlo_ref, fxhi_ref, fylo_ref, fyhi_ref,
    rhs_ref, beta_ref, sem_ref,
):
    parts = (
        (slice(0, 8), slice(0, 1024)),
        (slice(24, 32), slice(0, 1024)),
        (slice(8, 24), slice(0, 128)),
        (slice(8, 24), slice(896, 1024)),
    )
    copies = []
    for n, (src, dst) in enumerate(((rhs_hbm, rhs_ref), (beta_hbm, beta_ref))):
        for m, (rows, cols) in enumerate(parts):
            copies.append(
                pltpu.make_async_copy(
                    src.at[0, 0, :, rows, cols], dst.at[:, rows, cols], sem_ref.at[n, m]
                )
            )
    for copy in copies:
        copy.start()
    slots = slot_map(site_ref, count_ref, (8, LANES))
    for ref in (fxlo_ref, fxhi_ref, fylo_ref, fyhi_ref):
        ref[16] = slots
    for copy in copies:
        copy.wait()
    for xt in range(4):
        for t in range(8) if xt in (0, 3) else (0, 7):
            rows, cols = slice(8 * xt, 8 * xt + 8), slice(t * LANES, (t + 1) * LANES)
            f = [rhs_ref[s, rows, cols] / (beta_ref[s, rows, cols] * 9.0) for s in range(4)]
            for yy, v in enumerate(transpose_blocks(f)):
                y16, at = 2 * t + yy // 2, (yy % 2) * 4
                if xt == 0:
                    fxlo_ref[y16, at : at + 4, :] = v[0:4]
                if xt == 3:
                    fxhi_ref[y16, at : at + 4, :] = v[4:8]
                if t == 0:
                    fylo_ref[yy * 4 + xt] = v
                if t == 7:
                    fyhi_ref[yy * 4 + xt] = v


def boxes_kernel(site_ref, count_ref, rhs_ref, beta_ref, bbeta_ref, f1_ref, q_ref, k0_ref, f_ref, c_ref):
    for y in range(16):
        k0_ref[y] = bbeta_ref[pl.ds(y, 16, stride=16), :] * 2.25
    for xt in range(4):
        for t in range(8):
            rows, cols = slice(8 * xt, 8 * xt + 8), slice(t * LANES, (t + 1) * LANES)
            q = [beta_ref[0, 0, s, rows, cols] * 9.0 for s in range(4)]
            f = [rhs_ref[0, 0, s, rows, cols] / q[s] for s in range(4)]
            for yy, v in enumerate(transpose_blocks(q)):
                c_ref[4 * t + yy, rows, :] = v
            for yy, v in enumerate(transpose_blocks(f)):
                f_ref[4 * t + yy, rows, :] = v
    slots = slot_map(site_ref, count_ref, (16, LANES))

    def row(y):
        for py in range(2):
            for px in range(2):
                f = f_ref[2 * y + py, pl.ds(px, 16, stride=2), :]
                c = c_ref[2 * y + py, pl.ds(px, 16, stride=2), :]
                for pz in range(2):
                    o = px * 4 + py * 2 + pz
                    f1_ref[o, y] = expand(f, slots, pz)
                    q_ref[o, y] = expand(c, slots, pz)

    each(16, row)


def side_rows(dst_ref, o, y, hi, lo):
    dst_ref[o, y, 16:18, :] = hi
    dst_ref[o, y, 18:22, :] = jnp.zeros((4, LANES), F32)
    dst_ref[o, y, 22:24, :] = lo


def spread(row, rows):
    return jnp.broadcast_to(row, (rows, LANES))


def extend_x(dst_ref, f1_ref, rxlo_ref, rxhi_ref, xs_ref):
    lo_here, hi_here = inside("gx")
    hi_slots = kept(hi_here, spread(rxhi_ref[16, 0:1, :], 8))
    lo_slots = kept(lo_here, spread(rxlo_ref[16, 0:1, :], 8))
    for y in range(16):
        for pz in range(2):
            xs_ref[y, pz] = expand(rxhi_ref[y], hi_slots, pz)
            xs_ref[y, 2 + pz] = expand(rxlo_ref[y], lo_slots, pz)
    for y in range(16):
        for o in range(8):
            px, py, pz = o // 4, (o // 2) % 2, o % 2
            dst_ref[o, y, 0:16, :] = f1_ref[o, y]
            side_rows(
                dst_ref, o, y,
                xs_ref[y, pz, pl.ds(py * 4 + px, 2, stride=2), :],
                xs_ref[y, 2 + pz, pl.ds(py * 4 + px, 2, stride=2), :],
            )
    return hi_slots, lo_slots


def extend_y(dst_ref, rylo_ref, ryhi_ref, ys_ref, layers):
    lo_here, hi_here = inside("gy")
    slots = []
    for n, (ref, here, first) in enumerate(((ryhi_ref, hi_here, 16), (rylo_ref, lo_here, 18))):
        own = kept(here, spread(ref[16, 0:1, :], 32))
        slots.append(own)
        for layer in range(layers) if n == 0 else range(4 - layers, 4):
            v = jnp.concatenate([ref[layer * 4 + xt] for xt in range(4)], axis=0)
            for pz in range(2):
                ys_ref[n, layer, pz] = expand(v, own, pz)
    for n, first in enumerate((16, 18)):
        for layer in range(layers) if n == 0 else range(4 - layers, 4):
            y, py = first + layer // 2, layer % 2
            for px in range(2):
                for pz in range(2):
                    o = px * 4 + py * 2 + pz
                    dst_ref[o, y, 0:16, :] = ys_ref[n, layer, pz, pl.ds(px, 16, stride=2), :]
                    dst_ref[o, y, 16:24, :] = jnp.zeros((8, LANES), F32)
    return slots


def first_kernel(
    f1_ref, q_ref, k0_ref, brhs_ref, rxlo_ref, rxhi_ref, rylo_ref, ryhi_ref,
    e0_ref, exlo_ref, exhi_ref, u_ref, xs_ref, ys_ref,
):
    extend_x(u_ref, f1_ref, rxlo_ref, rxhi_ref, xs_ref)
    extend_y(u_ref, rylo_ref, ryhi_ref, ys_ref, 1)

    def row(y):
        cur, new = fine_relax(u_ref, y, None)
        q = [q_ref[o, y] for o in range(8)]
        k0 = k0_ref[y]
        left = mean8([q[o] * new[o][0:16] for o in range(8)])
        e0 = jnp.where(q[0] > 0.0, left, brhs_ref[pl.ds(y, 16, stride=16), :]) / k0
        e0_ref[y] = e0
        exlo_ref[y] = e0[0:8]
        exhi_ref[y] = e0[8:16]
        exlo_ref[16 + y] = k0[0:8]
        exhi_ref[16 + y] = k0[8:16]

    each(16, row)
    lo_here, hi_here = inside("gy")
    for layer in range(4):
        exlo_ref[32 + layer, 0:4, :] = ryhi_ref[layer * 4, 0:4, :]
        exlo_ref[32 + layer, 4:8, :] = rylo_ref[layer * 4, 0:4, :]
        exhi_ref[32 + layer, 0:4, :] = ryhi_ref[layer * 4 + 3, 4:8, :]
        exhi_ref[32 + layer, 4:8, :] = rylo_ref[layer * 4 + 3, 4:8, :]
    for ref in (exlo_ref, exhi_ref):
        ref[36, 0:1, :] = kept(hi_here, ryhi_ref[16, 0:1, :])
        ref[36, 1:2, :] = kept(lo_here, rylo_ref[16, 0:1, :])
        ref[36, 2:8, :] = jnp.zeros((6, LANES), F32)


def extend_kernel(
    f1_ref, q_ref, rxlo_ref, rxhi_ref, rylo_ref, ryhi_ref, sxlo_ref, sxhi_ref,
    f1x_ref, livex_ref, xs_ref, ys_ref, cs_ref,
):
    xlo_here, xhi_here = inside("gx")
    row8 = lax.broadcasted_iota(jnp.int32, (8, LANES), 0)
    hi_slots, lo_slots = extend_x(f1x_ref, f1_ref, rxlo_ref, rxhi_ref, xs_ref)
    y_slots = extend_y(f1x_ref, rylo_ref, ryhi_ref, ys_ref, 4)
    own_live = jnp.where(q_ref[0, 0] > 0.0, 1.0, 0.0)
    side = jnp.where(row8 < 4, hi_slots, lo_slots)
    livex_ref[0] = jnp.concatenate([own_live, jnp.where(side > 0.0, 1.0, 0.0)], axis=0)
    for n, first in enumerate((16, 18)):
        hi = kept(xhi_here, spread(sxhi_ref[36, n : n + 1, :], 8))
        lo = kept(xlo_here, spread(sxlo_ref[36, n : n + 1, :], 8))
        side = jnp.where(row8 < 4, hi, lo)
        live = jnp.concatenate([y_slots[n][0:16], side], axis=0) > 0.0
        livex_ref[1 + n] = jnp.where(live, 1.0, 0.0)
        for layer in range(4):
            at = slice(4 * n, 4 * n + 4)
            v = jnp.concatenate([sxhi_ref[32 + layer, at, :], sxlo_ref[32 + layer, at, :]], axis=0)
            for pz in range(2):
                cs_ref[n, layer, pz] = expand(v, side, pz)
    for n, first in enumerate((16, 18)):
        for layer in range(4):
            y, py = first + layer // 2, layer % 2
            for px in range(2):
                for pz in range(2):
                    o = px * 4 + py * 2 + pz
                    f1x_ref[o, y, 16:18, :] = cs_ref[n, layer, pz, pl.ds(px, 2, stride=2), :]
                    f1x_ref[o, y, 22:24, :] = cs_ref[n, layer, pz, pl.ds(4 + px, 2, stride=2), :]


def pack_y_first_kernel(e0_ref, k0_ref, exlo_ref, exhi_ref, eylo_ref, eyhi_ref):
    lo_here, hi_here = inside("gx")

    def row(y):
        for j, src in ((0, e0_ref), (1, k0_ref)):
            for out, at in ((eylo_ref, y), (eyhi_ref, y + 8)):
                v = src[at]
                n = (j * 8 + y) * 4
                out[n] = v[0:8]
                out[n + 1] = v[8:16]
                out[n + 2] = kept(hi_here, exhi_ref[j * 16 + at])
                out[n + 3] = kept(lo_here, exlo_ref[j * 16 + at])

    each(8, row)


def pack_y_kernel(e0_ref, exlo_ref, exhi_ref, eylo_ref, eyhi_ref):
    lo_here, hi_here = inside("gx")

    def row(y):
        for out, at in ((eylo_ref, y), (eyhi_ref, y + 8)):
            v = e0_ref[at]
            n = y * 4
            out[n] = v[0:8]
            out[n + 1] = v[8:16]
            out[n + 2] = kept(hi_here, exhi_ref[at])
            out[n + 3] = kept(lo_here, exlo_ref[at])

    each(8, row)


def assemble_base(dst_ref, own_ref, exlo_ref, exhi_ref, eylo_ref, eyhi_ref, x_at, y_at):
    xlo_here, xhi_here = inside("gx")
    ylo_here, yhi_here = inside("gy")

    def own(y):
        dst_ref[y, 0:16, :] = own_ref[y]
        dst_ref[y, 16:24, :] = kept(xhi_here, exhi_ref[x_at + y])
        dst_ref[y, 24:32, :] = kept(xlo_here, exlo_ref[x_at + y])

    each(16, own)

    def side(y):
        for t in range(4):
            dst_ref[16 + y, 8 * t : 8 * t + 8, :] = kept(yhi_here, eyhi_ref[y_at + y * 4 + t])
            dst_ref[24 + y, 8 * t : 8 * t + 8, :] = kept(ylo_here, eylo_ref[y_at + y * 4 + t])

    each(8, side)


def down_level0(e_ref, k_ref, e1_ref, k1_ref, make_k1):
    def row(y1, carry):
        parts = []
        for j in range(2):
            y = 2 * y1 + j
            low = e_ref[(y + 31) % 32]
            high = e_ref[(y + 1) % 32]
            parts.append(k_ref[y] * relax(e_ref[y], low, high, 1))
        r1 = pair_z(pair_x(parts[0] + parts[1], 1), 1) * 0.125
        if make_k1:
            k1 = pair_z(pair_x(k_ref[2 * y1] + k_ref[2 * y1 + 1], 1), 1) * (0.125 * 0.25)
            k1_ref[y1] = k1
        else:
            k1 = k1_ref[y1]
        e1_ref[y1] = jnp.where(k1 > 0.0, r1 / jnp.where(k1 > 0.0, k1, 1.0), 0.0)
        return carry

    lax.fori_loop(0, 16, row, 0, unroll=UNROLL)


def pack_four(rows, pack_ref):
    lane = lanes_of(rows[0]) & 3
    v = jnp.where(
        lane < 2,
        jnp.where(lane == 0, rows[0], rows[1]),
        jnp.where(lane == 2, rows[2], rows[3]),
    )
    pack_ref[...] = v
    return pack_ref[pl.ds(0, 4, stride=4), :]


def down_level1(e1_ref, k1_ref, pack_ref):
    r2 = []
    for y2 in range(4):
        parts = []
        for j in range(2):
            y = 2 * y2 + j
            parts.append(
                k1_ref[y] * relax(e1_ref[y], e1_ref[(y + 15) % 16], e1_ref[(y + 1) % 16], 2)
            )
        r2.append((pair_z(pair_x(parts[0] + parts[1], 2), 2) * 0.125)[0:16])
    return pack_four(r2, pack_ref)


def down_first_kernel(
    live_ref, e0_ref, k0_ref, exlo_ref, exhi_ref, eylo_ref, eyhi_ref,
    send_ref, e0x_ref, k0x_ref, e1_ref, k1_ref, pack_ref,
):
    assemble_base(e0x_ref, e0_ref, exlo_ref, exhi_ref, eylo_ref, eyhi_ref, 0, 0)
    assemble_base(k0x_ref, k0_ref, exlo_ref, exhi_ref, eylo_ref, eyhi_ref, 16, 32)
    down_level0(e0x_ref, k0x_ref, e1_ref, k1_ref, True)
    r2 = down_level1(e1_ref, k1_ref, pack_ref)
    k2 = []
    for y2 in range(4):
        v = pair_z(pair_x(k1_ref[2 * y2] + k1_ref[2 * y2 + 1], 2), 2) * (0.125 * 0.25)
        k2.append(v[0:16])
    k2 = pack_four(k2, pack_ref)
    both = jnp.concatenate([r2, k2], axis=0)

    def put(d):
        send_ref[d] = both

    each(send_ref.shape[0], put)


def down_kernel(
    e0_ref, k0x_ref, k1_ref, exlo_ref, exhi_ref, eylo_ref, eyhi_ref,
    send_ref, e0x_ref, e1_ref, pack_ref,
):
    assemble_base(e0x_ref, e0_ref, exlo_ref, exhi_ref, eylo_ref, eyhi_ref, 0, 0)
    down_level0(e0x_ref, k0x_ref, e1_ref, k1_ref, False)
    r2 = down_level1(e1_ref, k1_ref, pack_ref)

    def put(d):
        send_ref[d] = r2

    each(send_ref.shape[0], put)


def coarse_shift_x(v, n):
    rows = v.shape[1]
    r = rows_of(v)
    low = jnp.where(r >= n, pltpu.roll(v, n, 1), 0.0)
    high = jnp.where(r < rows - n, pltpu.roll(v, rows - n, 1), 0.0)
    return low + high


def coarse_shift_y(v, n):
    zero = jnp.zeros_like(v[0:1])
    lane = lanes_of(v) & 3
    up, down = pltpu.roll(v, LANES - n, 2), pltpu.roll(v, n, 2)
    across_up = down if n == 2 else pltpu.roll(v, 4 - n, 2)
    across_down = up if n == 2 else pltpu.roll(v, LANES - 4 + n, 2)
    above = jnp.concatenate([across_up[1:], zero], axis=0)
    below = jnp.concatenate([zero, across_down[:-1]], axis=0)
    return jnp.where(lane < 4 - n, up, above) + jnp.where(lane >= n, down, below)


def coarse_relax(v, n):
    s = coarse_shift_x(v, n) + coarse_shift_y(v, n) + (z_low(v, 4 * n) + z_high(v, 4 * n))
    return v * THIRD + s * NINTH


def coarse_solve(r2, k2):
    e2 = r2 / k2
    left = k2 * coarse_relax(e2, 1)

    def pool(v):
        v = pair_x(v, 1)
        v = pair_z(v, 1)
        return pair_z(v, 4) * 0.125

    k3 = pool(k2) * 0.25
    first = pool(left) / k3
    e3 = first
    for _ in range(SWEEPS - 1):
        e3 = coarse_relax(e3, 2) + first
    mid = e2 + e3
    return coarse_relax(mid, 1) + e2


def spread_coarse(mg2, table_ref, row_ref, m2_ref):
    gy_total, rows = mg2.shape[0], mg2.shape[1]
    gx_total = rows // 4
    zero = jnp.zeros((8, LANES), F32)
    for j in range(gx_total + 2):
        table_ref[0, j] = zero
        table_ref[gy_total + 1, j] = zero
    for j in range(gy_total):
        table_ref[j + 1, 0] = zero
        table_ref[j + 1, gx_total + 1] = zero
        for i in range(gx_total):
            table_ref[j + 1, i + 1, 0:4, :] = mg2[j, 4 * i : 4 * i + 4, :]
    gx = lax.axis_index("gx") + 1
    gy = lax.axis_index("gy") + 1
    lane = lax.broadcasted_iota(jnp.int32, (32, LANES), 1)
    group = lane & ~3
    for dy, picks in ((0, ((0, 0), (1, 1), (2, 2), (3, 3))), (1, ((4, 0), (5, 1))), (-1, ((6, 2), (7, 3)))):
        own = table_ref[gy + dy, gx, 0:4, :]
        high = table_ref[gy + dy, gx + 1, 0:2, :]
        low = table_ref[gy + dy, gx - 1, 2:4, :]
        for r in range(4):
            row_ref[pl.ds(r, 4, stride=4), :] = own
            row_ref[pl.ds(16 + r, 2, stride=4), :] = high
            row_ref[pl.ds(24 + r, 2, stride=4), :] = low
        v = row_ref[...]
        for at, y in picks:
            m2_ref[at] = lane_gather(v, group + y)


def up_levels(m2_ref, e1_ref, k1_ref, mg1_ref, e0x_ref, k0x_ref, corr_ref, e1p_ref, e0p_ref):
    def mid1(y):
        e1p_ref[y] = jnp.where(k1_ref[y] > 0.0, e1_ref[y] + m2_ref[y // 2], 0.0)

    each(16, mid1)

    def post1(y):
        v = relax(e1p_ref[y], e1p_ref[(y + 15) % 16], e1p_ref[(y + 1) % 16], 2) + e1_ref[y]
        mg1_ref[y] = jnp.where(k1_ref[y] > 0.0, v, 0.0)

    each(16, post1)

    def mid0(y):
        e0p_ref[y] = e0x_ref[y] + mg1_ref[y // 2]

    each(32, mid0)

    def post0(i):
        y = i + 12 if i >= 18 else i
        v = relax(e0p_ref[y], e0p_ref[(y + 31) % 32], e0p_ref[(y + 1) % 32], 1) + e0x_ref[y]
        v = jnp.where(k0x_ref[y] > 0.0, v, 0.0)
        third = jnp.where(rows_of(v[16:24]) < 4, v[16:24], v[24:32])
        corr_ref[i] = jnp.concatenate([v[0:16], third], axis=0)

    each(YF, post0)


def gather_coarse(recv_ref, at, w_ref):
    gy_total, rows = w_ref.shape[0], w_ref.shape[1]
    for i in range(rows // 4):
        for j in range(gy_total):
            w_ref[j, 4 * i : 4 * i + 4, :] = recv_ref[i * gy_total + j, at : at + 4, :]


def fine_sweep(src_ref, dst_ref, f1x_ref, livex_ref):
    def row(y):
        region = 0 if y < 16 else 1 if y < 18 else 2
        live = livex_ref[region] > 0.0
        cur, new = fine_relax(src_ref, y, [f1x_ref[o, y] for o in range(8)])
        for o in range(8):
            dst_ref[o, y] = jnp.where(live, new[o], cur[o])

    each(YF, row)


def middle_kernel(
    recv_ref, e0x_ref, k0x_ref, e1_ref, k1_ref, f1x_ref, livex_ref, q_ref, brhs_ref,
    u3_ref, k2_ref, e0_ref, exlo_ref, exhi_ref,
    w_ref, table_ref, row_ref, m2_ref, mg1_ref, e1p_ref, e0p_ref, corr_ref, ua_ref, ub_ref, v_ref,
):
    gather_coarse(recv_ref, 0, w_ref)
    gather_coarse(recv_ref, 4, k2_ref)
    mg2 = coarse_solve(w_ref[...], k2_ref[...])
    spread_coarse(mg2, table_ref, row_ref, m2_ref)
    up_levels(m2_ref, e1_ref, k1_ref, mg1_ref, e0x_ref, k0x_ref, corr_ref, e1p_ref, e0p_ref)

    def add(y):
        c = corr_ref[y]
        for o in range(8):
            ua_ref[o, y] = f1x_ref[o, y] + c

    each(YF, add)
    fine_sweep(ua_ref, ub_ref, f1x_ref, livex_ref)

    def base(y):
        v_ref[y] = mean8([ub_ref[o, y] for o in range(8)])

    each(YF, base)
    fine_sweep(ub_ref, u3_ref, f1x_ref, livex_ref)

    def left(y):
        cur, new = fine_relax(u3_ref, y, [f1x_ref[o, y] for o in range(8)])
        fine_left = mean8([q_ref[o, y] * (new[o][0:16] - cur[o][0:16]) for o in range(8)])
        k0 = k0x_ref[y][0:16]
        v = v_ref[y]
        s = around(v, v_ref[(y + YF - 1) % YF], v_ref[y + 1], 1)
        base_left = brhs_ref[pl.ds(y, 16, stride=16), :] - k0 * (v * (2.0 / 3.0) - s * NINTH)[0:16]
        e0 = jnp.where(q_ref[0, y] > 0.0, fine_left, base_left) / k0
        e0_ref[y] = e0
        exlo_ref[y] = e0[0:8]
        exhi_ref[y] = e0[8:16]

    each(16, left)


def last_kernel(
    site_ref, count_ref, recv_ref, k2_ref, e0x_ref, k0x_ref, e1_ref, k1_ref, u3_ref, f1x_ref, livex_ref,
    fine_ref, base_ref,
    w_ref, table_ref, row_ref, m2_ref, mg1_ref, e1p_ref, e0p_ref, corr_ref, ua_ref, ub_ref, c_ref,
):
    gather_coarse(recv_ref, 0, w_ref)
    mg2 = coarse_solve(w_ref[...], k2_ref[...])
    spread_coarse(mg2, table_ref, row_ref, m2_ref)
    up_levels(m2_ref, e1_ref, k1_ref, mg1_ref, e0x_ref, k0x_ref, corr_ref, e1p_ref, e0p_ref)

    def add(y):
        c = corr_ref[y]
        for o in range(8):
            ua_ref[o, y] = u3_ref[o, y] + c

    each(YF, add)
    live = livex_ref[0] > 0.0

    def row(y):
        cur, new = fine_relax(ua_ref, y, [f1x_ref[o, y] for o in range(8)])
        got = [jnp.where(live, new[o], cur[o])[0:16] for o in range(8)]
        for o in range(8):
            ub_ref[o, y] = got[o]
        base_ref[pl.ds(y, 16, stride=16), :] = mean8(got)

    each(16, row)

    lane = lax.broadcasted_iota(jnp.int32, (16, LANES), 1)
    idx = jnp.zeros((16, LANES), jnp.int32)
    for s in range(4):
        idx = jnp.where((lane // 32) == s, site_ref[0, 0, s], idx)
    idx = idx * 16 + (lane & 31) // 2
    live_slot = (lane // 32) < count_ref[0, 0]
    odd = (lane & 1) == 1

    def pack(y):
        for py in range(2):
            for px in range(2):
                o = px * 4 + py * 2
                v = jnp.where(odd, lane_gather(ub_ref[o + 1, y], idx), lane_gather(ub_ref[o, y], idx))
                c_ref[2 * y + py, pl.ds(px, 16, stride=2), :] = jnp.where(live_slot, v, 0.0)

    each(16, pack)
    for xt in range(4):
        for t in range(8):
            rows, cols = slice(8 * xt, 8 * xt + 8), slice(t * LANES, (t + 1) * LANES)
            for s, v in enumerate(transpose_blocks([c_ref[4 * t + yy, rows, :] for yy in range(4)])):
                fine_ref[0, 0, s, rows, cols] = v


def call(kernel, name, out_shapes, n_smem, n_any, n_vmem, scratch=(), cost=None):
    vmem = pl.BlockSpec(memory_space=pltpu.VMEM)
    smem = pl.BlockSpec(memory_space=pltpu.SMEM)
    anywhere = pl.BlockSpec(memory_space=pl.ANY)
    return pl.pallas_call(
        kernel,
        name=name,
        out_shape=[jax.ShapeDtypeStruct(s, F32) for s in out_shapes],
        in_specs=[smem] * n_smem + [anywhere] * n_any + [vmem] * n_vmem,
        out_specs=[vmem] * len(out_shapes),
        scratch_shapes=[pltpu.VMEM(s, F32) if isinstance(s, tuple) else s for s in scratch],
        cost_estimate=cost,
        compiler_params=pltpu.CompilerParams(vmem_limit_bytes=VMEM_LIMIT),
    )


def step(value, axis, by):
    count = lax.axis_size(axis)
    return lax.ppermute(value, axis, [(i, (i + by) % count) for i in range(count)])


def from_sides(to_low, to_high, axis):
    return step(to_high, axis, 1), step(to_low, axis, -1)


def local(fine_rhs, fine_beta, base_rhs, base_beta, slot_site, ghost_list, box_count):
    gx_total, gy_total = lax.axis_size("gx"), lax.axis_size("gy")
    devices = gx_total * gy_total
    rhs = base_rhs.reshape(256, LANES)
    octets = (8, 16, 16, LANES)
    own = (16, 16, LANES)
    wide = (32, 32, LANES)
    half = (16, 32, LANES)
    fine_ext = (8, YF, XF, LANES)
    coarse = (gy_total, 4 * gx_total, LANES)
    raw = (4, 32, 1024)
    rows = (32, 32, LANES)
    x_side, y_side, corner = (16, 4, 8, LANES), (2, 4, 2, 32, LANES), (2, 4, 2, 8, LANES)

    def tiles(n):
        return (n, 8, LANES)

    def beside(us):
        return pl.CostEstimate(flops=int(us * 1e6), bytes_accessed=int(us * 3e6), transcendentals=0)

    fxlo, fxhi, fylo, fyhi = call(
        faces_kernel, "faces", [tiles(17)] * 4, 2, 2, 0, [raw, raw, pltpu.SemaphoreType.DMA((2, 4))],
    )(slot_site, box_count, fine_rhs, fine_beta)
    rxlo, rxhi = from_sides(fxlo, fxhi, "gx")
    rylo, ryhi = from_sides(fylo, fyhi, "gy")
    f1, q, k0 = call(
        boxes_kernel, "boxes", [octets, octets, own], 2, 0, 3, [rows, rows], beside(3)
    )(slot_site, box_count, fine_rhs, fine_beta, base_beta.reshape(256, LANES))
    e0, exlo, exhi = call(
        first_kernel, "first_residual", [own, tiles(37), tiles(37)], 0, 0, 8, [fine_ext, x_side, y_side]
    )(f1, q, k0, rhs, rxlo, rxhi, rylo, ryhi)
    sxlo, sxhi = from_sides(exlo, exhi, "gx")
    eylo, eyhi = call(pack_y_first_kernel, "pack_y_first", [tiles(64), tiles(64)], 0, 0, 4)(e0, k0, sxlo, sxhi)
    sylo, syhi = from_sides(eylo, eyhi, "gy")
    f1x, livex = call(
        extend_kernel, "extend", [fine_ext, (3, XF, LANES)], 0, 0, 8, [x_side, y_side, corner], beside(2)
    )(f1, q, rxlo, rxhi, rylo, ryhi, sxlo, sxhi)
    send, e0x, k0x, e1, k1 = call(
        down_first_kernel, "down_first", [(devices, 8, LANES), wide, wide, half, half], 0, 0, 7, [(16, LANES)]
    )(livex, e0, k0, sxlo, sxhi, sylo, syhi)
    recv = lax.all_to_all(send, ("gx", "gy"), 0, 0, tiled=True)

    up_scratch = [
        coarse, (gy_total + 2, gx_total + 2, 8, LANES), (32, LANES), (8, 32, LANES), half, half, wide,
        (YF, XF, LANES),
    ]
    u3, k2, e0, exlo, exhi = call(
        middle_kernel, "middle", [fine_ext, coarse, own, tiles(16), tiles(16)], 0, 0, 9,
        up_scratch + [fine_ext, fine_ext, (YF, XF, LANES)],
    )(recv, e0x, k0x, e1, k1, f1x, livex, q, rhs)
    sxlo, sxhi = from_sides(exlo, exhi, "gx")
    eylo, eyhi = call(pack_y_kernel, "pack_y", [tiles(32), tiles(32)], 0, 0, 3)(e0, sxlo, sxhi)
    sylo, syhi = from_sides(eylo, eyhi, "gy")
    send, e0x, e1 = call(
        down_kernel, "down", [(devices, 4, LANES), wide, half], 0, 0, 7, [(16, LANES)]
    )(e0, k0x, k1, sxlo, sxhi, sylo, syhi)
    recv = lax.all_to_all(send, ("gx", "gy"), 0, 0, tiled=True)
    fine, base = call(
        last_kernel, "last", [fine_rhs.shape, (256, LANES)], 2, 0, 9, up_scratch + [fine_ext, octets, rows]
    )(slot_site, box_count, recv, k2, e0x, k0x, e1, k1, u3, f1x, livex)
    return fine, base.reshape(base_rhs.shape)


def solution(mesh):
    return jax.shard_map(
        local,
        mesh=mesh,
        in_specs=(
            P("gx", "gy", None, None, None),
            P("gx", "gy", None, None, None),
            P("gx", "gy", None),
            P("gx", "gy", None),
            P("gx", "gy", None),
            P("gx", "gy", None, None),
            P("gx", "gy"),
        ),
        out_specs=(P("gx", "gy", None, None, None), P("gx", "gy", None)),
        check_vma=False,
    )
```

time: 95.3 us -> 83.8 us (0.88)
  waiting for transfers between devices: 24.2 us -> 16.7 us
  Pallas kernels: 20.4 us -> 16.2 us
    ppermute x12, waiting for transfers between devices: 24.2 us -> 16.7 us  [step(): lax.ppermute(value, axis, [(i, (i + by) % count) for i in range(count)])]
    pallas_call x7 -> x9, Pallas kernels: 18.8 us -> 14.7 us  [the longest x1 4.26 us: local(): call(middle_kernel, 'middle', [fine_ext, coarse, own, tiles(16), tiles(16...]
    unnamed x14 -> x12, local copies, waits for them, and re-layouts: 4.55 us -> 3.64 us
  transfers between devices with their start and end apart: 12 -> 12, of which waited for: 7 -> 5; matrix products, arithmetic and copies ran while one was open for 0% -> 0% of each run, Pallas kernels for 0% -> 3%
where the time goes in v2:
time: 83.8 us; the launch traced here: 83.5 us
  blocking collectives  24.6 us (29%)
  starting transfers between devices  20.9 us (25%)
  waiting for transfers between devices  16.7 us (20%)
  Pallas kernels  16.2 us (19%)
  local copies, waits for them, and re-layouts  3.64 us (4%)
  between operations  1.42 us (2%)
    all_to_all x2, blocking collectives, local(): recv = lax.all_to_all(send, ('gx', 'gy'), 0, 0, tiled=True)  24.6 us
    ppermute x12, starting transfers between devices, step(): lax.ppermute(value, axis, [(i, (i + by) % count) for i in range(count)])  20.9 us
    ppermute x12, waiting for transfers between devices, step(): lax.ppermute(value, axis, [(i, (i + by) % count) for i in range(count)])  16.7 us
    pallas_call x1, Pallas kernels, local(): call(middle_kernel, 'middle', [fine_ext, coarse, own, tiles(16), tiles(16...  4.26 us
    pallas_call x1, Pallas kernels, local(): call(last_kernel, 'last', [fine_rhs.shape, (256, LANES)], 2, 0, 9, up_scr...  4.21 us
    unnamed x12, local copies, waits for them, and re-layouts  3.64 us
    pallas_call x1, Pallas kernels, local(): call(boxes_kernel, 'boxes', [octets, octets, own], 2, 0, 3, [rows, rows],...  2.36 us
  transfers between devices with their start and end apart: 12, of which 5 were waited for; matrix products, arithmetic and copies ran while one was open for 0% of the time, Pallas kernels for 3%

profile of v2, /device:TPU:0, one launch (start us, length us, event | category | flops | bytes accessed | tf_op | source)
XLA Modules:
  0.0 83.5 jit_solution(13270682904710345235)
XLA Ops:
  1.3 0.0 copy-start
  1.3 1.0 %copy-done = f32[1,1,4,32,1024]{4,3,2,1,0:T(8,128)S(1)} copy-done((f32[1,1,4,32,1024]{4,3,2,1,0:T(8,128)S(1)}, f32[1,1,4,32,1024]{4,3,2,1,0:T(8,128)}, u32[]{:S(2)}) %copy-start) | copy-done | bytes 524312
  2.3 0.0 copy-start.1
  2.3 1.0 %copy-done.1 = f32[1,1,4,32,1024]{4,3,2,1,0:T(8,128)S(1)} copy-done((f32[1,1,4,32,1024]{4,3,2,1,0:T(8,128)S(1)}, f32[1,1,4,32,1024]{4,3,2,1,0:T(8,128)}, u32[]{:S(2)}) %copy-start.1) | copy-done | bytes 524312
  3.4 0.0 copy-start.4
  3.4 0.7 copy-done.4
  4.0 0.0 copy-start.2
  4.0 1.2 %faces.1 = (f32[17,8,128]{2,1,0:T(8,128)S(1)}, f32[17,8,128]{2,1,0:T(8,128)S(1)}, f32[17,8,128]{2,1,0:T(8,128)S(1)}, f32[17,8,128]{2,1,0:T(8,128)S(1)}) custom-call(s32[1,1,4]{2,1,0:T(1,128)S(1)} %copy-done.4, s32[1,1]{1,0:T(1,128)S(6)} %copy.8.count_ref, f32[1,1,4,32,1024]{4,3,2,1,0:T(8,128)S(1)} %copy-done, f32[1,1,4,32,1024]{4,3,2,1,0:T(8,128)S(1)} %copy-done.1), custom_call_target="tpu_custom_call" | custom-call | tf_op jit(solution)/shard_map/faces/pallas_call | solution.py:698
  5.2 3.1 %collective-permute-start = (f32[17,8,128]{2,1,0:T(8,128)S(1)}, f32[17,8,128]{2,1,0:T(8,128)S(1)}, u32[]{:S(2)}, u32[]{:S(2)}) collective-permute-start(f32[17,8,128]{2,1,0:T(8,128)S(1)} %get-tuple-element.35), channel_id=1, source_target_pairs={{0,8},{8,16},{16,24},{24,0},{1,9},{9,17},{17,25},{25,1},{2,10},{10... | collective-permute-start | bytes 208904 | tf_op jit(solution)/shard_map/ppermute | solution.py:671
  8.3 2.1 %collective-permute-start.1 = (f32[17,8,128]{2,1,0:T(8,128)S(1)}, f32[17,8,128]{2,1,0:T(8,128)S(1)}, u32[]{:S(2)}, u32[]{:S(2)}) collective-permute-start(f32[17,8,128]{2,1,0:T(8,128)S(1)} %get-tuple-element.36), channel_id=1, source_target_pairs={{0,24},{8,0},{16,8},{24,16},{1,25},{9,1},{17,9},{25,17},{2,26},{10... | collective-permute-start | bytes 208904 | tf_op jit(solution)/shard_map/ppermute | solution.py:671
  10.3 0.0 collective-permute-start.2
  10.4 2.6 %collective-permute-start.3 = (f32[17,8,128]{2,1,0:T(8,128)S(1)}, f32[17,8,128]{2,1,0:T(8,128)S(1)}, u32[]{:S(2)}, u32[]{:S(2)}) collective-permute-start(f32[17,8,128]{2,1,0:T(8,128)S(1)} %get-tuple-element.38), channel_id=1, source_target_pairs={{0,7},{1,0},{2,1},{3,2},{4,3},{5,4},{6,5},{7,6},{8,15},{9,8},{10,9... | collective-permute-start | bytes 208904 | tf_op jit(solution)/shard_map/ppermute | solution.py:671
  13.0 0.0 copy-start.3
  13.0 0.9 %copy-done.3 = f32[16,16,128]{2,1,0:T(8,128)S(1)} copy-done((f32[16,16,128]{2,1,0:T(8,128)S(1)}, f32[16,16,128]{2,1,0:T(8,128)}, u32[]{:S(2)}) %copy-start.3) | copy-done | bytes 131096
  13.9 2.4 %boxes.1 = (f32[8,16,16,128]{3,2,1,0:T(8,128)S(1)}, f32[8,16,16,128]{3,2,1,0:T(8,128)S(1)}, f32[16,16,128]{2,1,0:T(8,128)S(1)}) custom-call(s32[1,1,4]{2,1,0:T(1,128)S(1)} %copy-done.4, s32[1,1]{1,0:T(1,128)S(6)} %copy.8.count_ref, f32[1,1,4,32,1024]{4,3,2,1,0:T(8,128)S(1)} %copy-done, f32[1,1,4,32,1024]{4,3,2,1,0:T(8,128)S(1)} %copy-done.1, ...), custom_call_target="tpu_custom_call" | custom-call | flops 3000000 | bytes 9000000 | tf_op jit(solution)/shard_map/boxes/pallas_call | solution.py:703
  16.3 0.0 collective-permute-done.rxlo_ref
  16.3 0.0 collective-permute-done.1.rxhi_ref
  16.3 0.0 collective-permute-done.2.rylo_ref
  16.3 0.0 collective-permute-done.3.ryhi_ref
  16.3 0.0 copy-done.2
  16.3 0.9 %first_residual.1 = (f32[16,16,128]{2,1,0:T(8,128)S(1)}, f32[37,8,128]{2,1,0:T(8,128)S(1)}, f32[37,8,128]{2,1,0:T(8,128)S(1)}) custom-call(f32[8,16,16,128]{3,2,1,0:T(8,128)S(1)} %get-tuple-element.33.f1_ref, f32[8,16,16,128]{3,2,1,0:T(8,128)S(1)} %get-tuple-element.34.q_ref, f32[16,16,128]{2,1,0:T(8,128)S(1)} %get-tuple-element.39.k0_ref, ...), custom_call_target="tpu_custom_call" | custom-call | tf_op jit(solution)/shard_map/first_residual/pallas_call | solution.py:706
  17.3 0.1 collective-permute-start.4
  17.3 3.8 %collective-permute-start.5 = (f32[37,8,128]{2,1,0:T(8,128)S(1)}, f32[37,8,128]{2,1,0:T(8,128)S(1)}, u32[]{:S(2)}, u32[]{:S(2)}) collective-permute-start(f32[37,8,128]{2,1,0:T(8,128)S(1)} %get-tuple-element.41), channel_id=1, source_target_pairs={{0,24},{8,0},{16,8},{24,16},{1,25},{9,1},{17,9},{25,17},{2,26},{10... | collective-permute-start | bytes 454664 | tf_op jit(solution)/shard_map/ppermute | solution.py:671
  21.1 4.8 %collective-permute-done.4.sxlo_ref.exlo_ref = f32[37,8,128]{2,1,0:T(8,128)S(1)} collective-permute-done((f32[37,8,128]{2,1,0:T(8,128)S(1)}, f32[37,8,128]{2,1,0:T(8,128)S(1)}, u32[]{:S(2)}, u32[]{:S(2)}) %collective-permute-start.4) | collective-permute-done | bytes 151584 | tf_op jit(solution)/shard_map/ppermute | solution.py:671
  26.0 0.0 collective-permute-done.5.sxhi_ref.exhi_ref
  26.0 0.1 pack_y_first.1
  26.1 0.1 collective-permute-start.6
  26.1 2.6 %collective-permute-start.7 = (f32[64,8,128]{2,1,0:T(8,128)S(1)}, f32[64,8,128]{2,1,0:T(8,128)S(1)}, u32[]{:S(2)}, u32[]{:S(2)}) collective-permute-start(f32[64,8,128]{2,1,0:T(8,128)S(1)} %get-tuple-element.45), channel_id=1, source_target_pairs={{0,7},{1,0},{2,1},{3,2},{4,3},{5,4},{6,5},{7,6},{8,15},{9,8},{10,9... | collective-permute-start | bytes 786440 | tf_op jit(solution)/shard_map/ppermute | solution.py:671
  28.8 0.5 extend.1
  29.3 4.7 %collective-permute-done.6.eylo_ref = f32[64,8,128]{2,1,0:T(8,128)S(1)} collective-permute-done((f32[64,8,128]{2,1,0:T(8,128)S(1)}, f32[64,8,128]{2,1,0:T(8,128)S(1)}, u32[]{:S(2)}, u32[]{:S(2)}) %collective-permute-start.6) | collective-permute-done | bytes 262176 | tf_op jit(solution)/shard_map/ppermute | solution.py:671
  34.0 0.2 collective-permute-done.7.eyhi_ref
  34.2 1.5 %down_first.1 = (f32[32,8,128]{2,1,0:T(8,128)S(1)}, f32[32,32,128]{2,1,0:T(8,128)S(1)}, f32[32,32,128]{2,1,0:T(8,128)S(1)}, f32[16,32,128]{2,1,0:T(8,128)S(1)}, f32[16,32,128]{2,1,0:T(8,128)S(1)}) custom-call(f32[3,24,128]{2,1,0:T(8,128)S(1)} %get-tuple-element.42.live_ref.livex_ref, f32[16,16,128]{2,1,0:T(8,128)S(1)} %get-tuple-element.43.e0_ref, ...), custom_call_target="tpu_custom_call" | custom-call | tf_op jit(solution)/shard_map/down_first/pallas_call | solution.py:715
  35.7 13.1 %all_to_all.10.recv_ref = f32[32,8,128]{2,1,0:T(8,128)S(1)} all-to-all(f32[32,8,128]{2,1,0:T(8,128)S(1)} %get-tuple-element.46), channel_id=1, replica_groups=mesh['gx'=4,'gy'=8] {'gx','gy'}, dimensions={0} | all-to-all | bytes 262144 | tf_op jit(solution)/shard_map/all_to_all | solution.py:718
  48.8 0.0 copy-start.5
  48.8 4.3 %middle.1 = (f32[8,20,24,128]{3,2,1,0:T(8,128)S(1)}, f32[8,16,128]{2,1,0:T(8,128)S(1)}, f32[16,16,128]{2,1,0:T(8,128)S(1)}, f32[16,8,128]{2,1,0:T(8,128)S(1)}, f32[16,8,128]{2,1,0:T(8,128)S(1)}) custom-call(f32[32,8,128]{2,1,0:T(8,128)S(1)} %all_to_all.10.recv_ref, f32[32,32,128]{2,1,0:T(8,128)S(1)} %get-tuple-element.47.e0x_ref, ...), custom_call_target="tpu_custom_call" | custom-call | tf_op jit(solution)/shard_map/middle/pallas_call | solution.py:724
  53.1 0.7 collective-permute-start.8
  53.8 3.2 %collective-permute-start.9 = (f32[16,8,128]{2,1,0:T(8,128)S(1)}, f32[16,8,128]{2,1,0:T(8,128)S(1)}, u32[]{:S(2)}, u32[]{:S(2)}) collective-permute-start(f32[16,8,128]{2,1,0:T(8,128)S(1)} %get-tuple-element.54), channel_id=1, source_target_pairs={{0,24},{8,0},{16,8},{24,16},{1,25},{9,1},{17,9},{25,17},{2,26},{10... | collective-permute-start | bytes 196616 | tf_op jit(solution)/shard_map/ppermute | solution.py:671
  56.9 2.9 %collective-permute-done.8.exlo_ref = f32[16,8,128]{2,1,0:T(8,128)S(1)} collective-permute-done((f32[16,8,128]{2,1,0:T(8,128)S(1)}, f32[16,8,128]{2,1,0:T(8,128)S(1)}, u32[]{:S(2)}, u32[]{:S(2)}) %collective-permute-start.8) | collective-permute-done | bytes 65568 | tf_op jit(solution)/shard_map/ppermute | solution.py:671
  59.8 0.0 collective-permute-done.9.exhi_ref
  59.9 0.1 collective-permute-start.10
  59.9 2.6 %collective-permute-start.11 = (f32[32,8,128]{2,1,0:T(8,128)S(1)}, f32[32,8,128]{2,1,0:T(8,128)S(1)}, u32[]{:S(2)}, u32[]{:S(2)}) collective-permute-start(f32[32,8,128]{2,1,0:T(8,128)S(1)} %get-tuple-element.56), channel_id=1, source_target_pairs={{0,7},{1,0},{2,1},{3,2},{4,3},{5,4},{6,5},{7,6},{8,15},{9,8},{10,9... | collective-permute-start | bytes 393224 | tf_op jit(solution)/shard_map/ppermute | solution.py:671
  62.6 4.0 %collective-permute-done.10.eylo_ref = f32[32,8,128]{2,1,0:T(8,128)S(1)} collective-permute-done((f32[32,8,128]{2,1,0:T(8,128)S(1)}, f32[32,8,128]{2,1,0:T(8,128)S(1)}, u32[]{:S(2)}, u32[]{:S(2)}) %collective-permute-start.10) | collective-permute-done | bytes 131104 | tf_op jit(solution)/shard_map/ppermute | solution.py:671
  66.6 0.0 collective-permute-done.11.eyhi_ref
  66.6 1.2 %down.1 = (f32[32,4,128]{2,1,0:T(4,128)S(1)}, f32[32,32,128]{2,1,0:T(8,128)S(1)}, f32[16,32,128]{2,1,0:T(8,128)S(1)}) custom-call(f32[16,16,128]{2,1,0:T(8,128)S(1)} %get-tuple-element.52.e0_ref, f32[32,32,128]{2,1,0:T(8,128)S(1)} %get-tuple-element.48.k0x_ref, f32[16,32,128]{2,1,0:T(8,128)S(1)} %get-tuple-element.50.k1_ref, ...), custom_call_target="tpu_custom_call" | custom-call | tf_op jit(solution)/shard_map/down/pallas_call | solution.py:731
  67.8 11.5 %all_to_all.11.recv_ref = f32[32,4,128]{2,1,0:T(4,128)S(1)} all-to-all(f32[32,4,128]{2,1,0:T(4,128)S(1)} %get-tuple-element.57), channel_id=1, replica_groups=mesh['gx'=4,'gy'=8] {'gx','gy'}, dimensions={0} | all-to-all | bytes 131072 | tf_op jit(solution)/shard_map/all_to_all | solution.py:734
  79.3 0.0 copy-done.5
  79.3 4.2 %last.1 = (f32[1,1,4,32,1024]{4,3,2,1,0:T(8,128)}, f32[256,128]{1,0:T(8,128)}) custom-call(s32[1,1,4]{2,1,0:T(1,128)S(1)} %copy-done.5, s32[1,1]{1,0:T(1,128)S(6)} %copy.8.count_ref, f32[32,4,128]{2,1,0:T(4,128)S(1)} %all_to_all.11.recv_ref, f32[8,16,128]{2,1,0:T(8,128)S(1)} %get-tuple-element.58.k2_ref, f32[32,32,128]{2,1,0:T(8,128)S(1)} %get-tuple-element.59.e0x_ref, ...), custom_call_target="tpu_custom_call" | custom-call | tf_op jit(solution)/shard_map/last/pallas_call | solution.py:735
  (1 shorter events, 0.0 us)
Async XLA Ops:
  1.3 1.0 %copy-start = (f32[1,1,4,32,1024]{4,3,2,1,0:T(8,128)S(1)}, f32[1,1,4,32,1024]{4,3,2,1,0:T(8,128)}, u32[]{:S(2)}) copy-start(f32[1,1,4,32,1024]{4,3,2,1,0:T(8,128)} %rhs_hbm.1) | copy-start | bytes 1572868
  2.3 1.0 %copy-start.1 = (f32[1,1,4,32,1024]{4,3,2,1,0:T(8,128)S(1)}, f32[1,1,4,32,1024]{4,3,2,1,0:T(8,128)}, u32[]{:S(2)}) copy-start(f32[1,1,4,32,1024]{4,3,2,1,0:T(8,128)} %beta_hbm.1) | copy-start | bytes 1572868
  3.4 0.7 copy-start.4
  4.0 12.3 %copy-start.2 = (f32[16,16,128]{2,1,0:T(8,128)S(1)}, f32[16,16,128]{2,1,0:T(8,128)}, u32[]{:S(2)}) copy-start(f32[16,16,128]{2,1,0:T(8,128)} %param.9) | copy-start | bytes 393220
  5.2 11.1 %collective-permute-start = (f32[17,8,128]{2,1,0:T(8,128)S(1)}, f32[17,8,128]{2,1,0:T(8,128)S(1)}, u32[]{:S(2)}, u32[]{:S(2)}) collective-permute-start(f32[17,8,128]{2,1,0:T(8,128)S(1)} %get-tuple-element.35), channel_id=1, source_target_pairs={{0,8},{8,16},{16,24},{24,0},{1,9},{9,17},{17,25},{25,1},{2,10},{10... | collective-permute-start | bytes 208904 | tf_op jit(solution)/shard_map/ppermute | solution.py:671
  8.3 8.0 %collective-permute-start.1 = (f32[17,8,128]{2,1,0:T(8,128)S(1)}, f32[17,8,128]{2,1,0:T(8,128)S(1)}, u32[]{:S(2)}, u32[]{:S(2)}) collective-permute-start(f32[17,8,128]{2,1,0:T(8,128)S(1)} %get-tuple-element.36), channel_id=1, source_target_pairs={{0,24},{8,0},{16,8},{24,16},{1,25},{9,1},{17,9},{25,17},{2,26},{10... | collective-permute-start | bytes 208904 | tf_op jit(solution)/shard_map/ppermute | solution.py:671
  10.3 5.9 %collective-permute-start.2 = (f32[17,8,128]{2,1,0:T(8,128)S(1)}, f32[17,8,128]{2,1,0:T(8,128)S(1)}, u32[]{:S(2)}, u32[]{:S(2)}) collective-permute-start(f32[17,8,128]{2,1,0:T(8,128)S(1)} %get-tuple-element.37), channel_id=1, source_target_pairs={{0,1},{1,2},{2,3},{3,4},{4,5},{5,6},{6,7},{7,0},{8,9},{9,10},{10,1... | collective-permute-start | bytes 208904 | tf_op jit(solution)/shard_map/ppermute | solution.py:671
  10.4 5.9 %collective-permute-start.3 = (f32[17,8,128]{2,1,0:T(8,128)S(1)}, f32[17,8,128]{2,1,0:T(8,128)S(1)}, u32[]{:S(2)}, u32[]{:S(2)}) collective-permute-start(f32[17,8,128]{2,1,0:T(8,128)S(1)} %get-tuple-element.38), channel_id=1, source_target_pairs={{0,7},{1,0},{2,1},{3,2},{4,3},{5,4},{6,5},{7,6},{8,15},{9,8},{10,9... | collective-permute-start | bytes 208904 | tf_op jit(solution)/shard_map/ppermute | solution.py:671
  13.0 0.9 %copy-start.3 = (f32[16,16,128]{2,1,0:T(8,128)S(1)}, f32[16,16,128]{2,1,0:T(8,128)}, u32[]{:S(2)}) copy-start(f32[16,16,128]{2,1,0:T(8,128)} %param.10) | copy-start | bytes 393220
  17.3 8.7 %collective-permute-start.4 = (f32[37,8,128]{2,1,0:T(8,128)S(1)}, f32[37,8,128]{2,1,0:T(8,128)S(1)}, u32[]{:S(2)}, u32[]{:S(2)}) collective-permute-start(f32[37,8,128]{2,1,0:T(8,128)S(1)} %get-tuple-element.40), channel_id=1, source_target_pairs={{0,8},{8,16},{16,24},{24,0},{1,9},{9,17},{17,25},{25,1},{2,10},{10... | collective-permute-start | bytes 454664 | tf_op jit(solution)/shard_map/ppermute | solution.py:671
  17.3 8.7 %collective-permute-start.5 = (f32[37,8,128]{2,1,0:T(8,128)S(1)}, f32[37,8,128]{2,1,0:T(8,128)S(1)}, u32[]{:S(2)}, u32[]{:S(2)}) collective-permute-start(f32[37,8,128]{2,1,0:T(8,128)S(1)} %get-tuple-element.41), channel_id=1, source_target_pairs={{0,24},{8,0},{16,8},{24,16},{1,25},{9,1},{17,9},{25,17},{2,26},{10... | collective-permute-start | bytes 454664 | tf_op jit(solution)/shard_map/ppermute | solution.py:671
  26.1 7.9 %collective-permute-start.6 = (f32[64,8,128]{2,1,0:T(8,128)S(1)}, f32[64,8,128]{2,1,0:T(8,128)S(1)}, u32[]{:S(2)}, u32[]{:S(2)}) collective-permute-start(f32[64,8,128]{2,1,0:T(8,128)S(1)} %get-tuple-element.44), channel_id=1, source_target_pairs={{0,1},{1,2},{2,3},{3,4},{4,5},{5,6},{6,7},{7,0},{8,9},{9,10},{10,1... | collective-permute-start | bytes 786440 | tf_op jit(solution)/shard_map/ppermute | solution.py:671
  26.1 8.1 %collective-permute-start.7 = (f32[64,8,128]{2,1,0:T(8,128)S(1)}, f32[64,8,128]{2,1,0:T(8,128)S(1)}, u32[]{:S(2)}, u32[]{:S(2)}) collective-permute-start(f32[64,8,128]{2,1,0:T(8,128)S(1)} %get-tuple-element.45), channel_id=1, source_target_pairs={{0,7},{1,0},{2,1},{3,2},{4,3},{5,4},{6,5},{7,6},{8,15},{9,8},{10,9... | collective-permute-start | bytes 786440 | tf_op jit(solution)/shard_map/ppermute | solution.py:671
  48.8 30.5 %copy-start.5 = (s32[1,1,4]{2,1,0:T(1,128)S(1)}, s32[1,1,4]{2,1,0:T(1,128)}, u32[]{:S(2)}) copy-start(s32[1,1,4]{2,1,0:T(1,128)} %site_ref.5) | copy-start | bytes 52
  53.1 6.8 %collective-permute-start.8 = (f32[16,8,128]{2,1,0:T(8,128)S(1)}, f32[16,8,128]{2,1,0:T(8,128)S(1)}, u32[]{:S(2)}, u32[]{:S(2)}) collective-permute-start(f32[16,8,128]{2,1,0:T(8,128)S(1)} %get-tuple-element.53), channel_id=1, source_target_pairs={{0,8},{8,16},{16,24},{24,0},{1,9},{9,17},{17,25},{25,1},{2,10},{10... | collective-permute-start | bytes 196616 | tf_op jit(solution)/shard_map/ppermute | solution.py:671
  53.8 6.1 %collective-permute-start.9 = (f32[16,8,128]{2,1,0:T(8,128)S(1)}, f32[16,8,128]{2,1,0:T(8,128)S(1)}, u32[]{:S(2)}, u32[]{:S(2)}) collective-permute-start(f32[16,8,128]{2,1,0:T(8,128)S(1)} %get-tuple-element.54), channel_id=1, source_target_pairs={{0,24},{8,0},{16,8},{24,16},{1,25},{9,1},{17,9},{25,17},{2,26},{10... | collective-permute-start | bytes 196616 | tf_op jit(solution)/shard_map/ppermute | solution.py:671
  59.9 6.7 %collective-permute-start.10 = (f32[32,8,128]{2,1,0:T(8,128)S(1)}, f32[32,8,128]{2,1,0:T(8,128)S(1)}, u32[]{:S(2)}, u32[]{:S(2)}) collective-permute-start(f32[32,8,128]{2,1,0:T(8,128)S(1)} %get-tuple-element.55), channel_id=1, source_target_pairs={{0,1},{1,2},{2,3},{3,4},{4,5},{5,6},{6,7},{7,0},{8,9},{9,10},{10,1... | collective-permute-start | bytes 393224 | tf_op jit(solution)/shard_map/ppermute | solution.py:671
  59.9 6.6 %collective-permute-start.11 = (f32[32,8,128]{2,1,0:T(8,128)S(1)}, f32[32,8,128]{2,1,0:T(8,128)S(1)}, u32[]{:S(2)}, u32[]{:S(2)}) collective-permute-start(f32[32,8,128]{2,1,0:T(8,128)S(1)} %get-tuple-element.56), channel_id=1, source_target_pairs={{0,7},{1,0},{2,1},{3,2},{4,3},{5,4},{6,5},{7,6},{8,15},{9,8},{10,9... | collective-permute-start | bytes 393224 | tf_op jit(solution)/shard_map/ppermute | solution.py:671

commit v3 on v2

--- a/solution.py
+++ b/solution.py
@@ -15,6 +15,8 @@
 LANES = 128
 VMEM_LIMIT = 16 * 1024 * 1024
 UNROLL = 4
+ROWS_FIRST = 7
+ROWS_LAST = 5
 
 
 def lanes_of(v):
@@ -81,6 +83,18 @@
         new = cur[o] * THIRD + s * NINTH
         out.append(new if f1_rows is None else new + f1_rows[o])
     return cur, out
+
+
+def relax_copies(ref, y, total):
+    c = ref[y]
+    x = x_low(c, 1), x_high(c, 1)
+    z = z_low(c, 1), z_high(c, 1)
+    rows = ref[(y + total - 1) % total], ref[(y + 1) % total]
+    base = c * (2.0 / 3.0)
+    out = []
+    for o in range(8):
+        out.append(base + ((x[o // 4] + rows[(o // 2) % 2]) + z[o % 2]) * NINTH)
+    return c, out
 
 
 def each(count, body):
@@ -173,9 +187,7 @@
                     fyhi_ref[yy * 4 + xt] = v
 
 
-def boxes_kernel(site_ref, count_ref, rhs_ref, beta_ref, bbeta_ref, f1_ref, q_ref, k0_ref, f_ref, c_ref):
-    for y in range(16):
-        k0_ref[y] = bbeta_ref[pl.ds(y, 16, stride=16), :] * 2.25
+def boxes_kernel(site_ref, count_ref, rhs_ref, beta_ref, f1_ref, q_ref, f_ref, c_ref):
     for xt in range(4):
         for t in range(8):
             rows, cols = slice(8 * xt, 8 * xt + 8), slice(t * LANES, (t + 1) * LANES)
@@ -251,42 +263,62 @@
     return slots
 
 
+class Swapped:
+    def __init__(self, on_even, on_odd):
+        self.refs = on_even, on_odd
+
+    def __getitem__(self, at):
+        on_even, on_odd = self.refs
+        return jnp.where(lax.axis_index("gx") % 2 == 0, on_even[at], on_odd[at])
+
+
 def first_kernel(
-    f1_ref, q_ref, k0_ref, brhs_ref, rxlo_ref, rxhi_ref, rylo_ref, ryhi_ref,
-    e0_ref, exlo_ref, exhi_ref, u_ref, xs_ref, ys_ref,
+    f1_ref, q_ref, bbeta_ref, brhs_ref, rxlo_ref, rxhi_ref, rylo_ref, ryhi_ref,
+    e0_ref, k0_ref, ea_ref, eb_ref, u_ref, xs_ref, ys_ref,
 ):
+    even = lax.axis_index("gx") % 2 == 0
+
+    def put(at, lo, hi):
+        ea_ref[at] = jnp.where(even, hi, lo)
+        eb_ref[at] = jnp.where(even, lo, hi)
+
     extend_x(u_ref, f1_ref, rxlo_ref, rxhi_ref, xs_ref)
     extend_y(u_ref, rylo_ref, ryhi_ref, ys_ref, 1)
 
     def row(y):
         cur, new = fine_relax(u_ref, y, None)
         q = [q_ref[o, y] for o in range(8)]
-        k0 = k0_ref[y]
+        k0 = bbeta_ref[pl.ds(y, 16, stride=16), :] * 2.25
         left = mean8([q[o] * new[o][0:16] for o in range(8)])
         e0 = jnp.where(q[0] > 0.0, left, brhs_ref[pl.ds(y, 16, stride=16), :]) / k0
         e0_ref[y] = e0
-        exlo_ref[y] = e0[0:8]
-        exhi_ref[y] = e0[8:16]
-        exlo_ref[16 + y] = k0[0:8]
-        exhi_ref[16 + y] = k0[8:16]
+        k0_ref[y] = k0
+        put(y, e0[0:8], e0[8:16])
+        put(16 + y, k0[0:8], k0[8:16])
 
     each(16, row)
     lo_here, hi_here = inside("gy")
     for layer in range(4):
-        exlo_ref[32 + layer, 0:4, :] = ryhi_ref[layer * 4, 0:4, :]
-        exlo_ref[32 + layer, 4:8, :] = rylo_ref[layer * 4, 0:4, :]
-        exhi_ref[32 + layer, 0:4, :] = ryhi_ref[layer * 4 + 3, 4:8, :]
-        exhi_ref[32 + layer, 4:8, :] = rylo_ref[layer * 4 + 3, 4:8, :]
-    for ref in (exlo_ref, exhi_ref):
-        ref[36, 0:1, :] = kept(hi_here, ryhi_ref[16, 0:1, :])
-        ref[36, 1:2, :] = kept(lo_here, rylo_ref[16, 0:1, :])
-        ref[36, 2:8, :] = jnp.zeros((6, LANES), F32)
+        hi, lo = ryhi_ref[layer * 4], rylo_ref[layer * 4]
+        to_lo = jnp.concatenate([hi[0:4], lo[0:4]], axis=0)
+        hi, lo = ryhi_ref[layer * 4 + 3], rylo_ref[layer * 4 + 3]
+        put(32 + layer, to_lo, jnp.concatenate([hi[4:8], lo[4:8]], axis=0))
+    slots = jnp.concatenate(
+        [
+            kept(hi_here, ryhi_ref[16, 0:1, :]),
+            kept(lo_here, rylo_ref[16, 0:1, :]),
+            jnp.zeros((6, LANES), F32),
+        ],
+        axis=0,
+    )
+    put(36, slots, slots)
 
 
 def extend_kernel(
-    f1_ref, q_ref, rxlo_ref, rxhi_ref, rylo_ref, ryhi_ref, sxlo_ref, sxhi_ref,
-    f1x_ref, livex_ref, xs_ref, ys_ref, cs_ref,
+    f1_ref, q_ref, rxlo_ref, rxhi_ref, rylo_ref, ryhi_ref, sa_ref, sb_ref,
+    f1x_ref, livex_ref, w2x_ref, xs_ref, ys_ref, cs_ref,
 ):
+    sxlo_ref, sxhi_ref = Swapped(sb_ref, sa_ref), Swapped(sa_ref, sb_ref)
     xlo_here, xhi_here = inside("gx")
     row8 = lax.broadcasted_iota(jnp.int32, (8, LANES), 0)
     hi_slots, lo_slots = extend_x(f1x_ref, f1_ref, rxlo_ref, rxhi_ref, xs_ref)
@@ -295,14 +327,14 @@
     side = jnp.where(row8 < 4, hi_slots, lo_slots)
     livex_ref[0] = jnp.concatenate([own_live, jnp.where(side > 0.0, 1.0, 0.0)], axis=0)
     for n, first in enumerate((16, 18)):
-        hi = kept(xhi_here, spread(sxhi_ref[36, n : n + 1, :], 8))
-        lo = kept(xlo_here, spread(sxlo_ref[36, n : n + 1, :], 8))
+        hi = kept(xhi_here, spread(sxhi_ref[36][n : n + 1], 8))
+        lo = kept(xlo_here, spread(sxlo_ref[36][n : n + 1], 8))
         side = jnp.where(row8 < 4, hi, lo)
         live = jnp.concatenate([y_slots[n][0:16], side], axis=0) > 0.0
         livex_ref[1 + n] = jnp.where(live, 1.0, 0.0)
         for layer in range(4):
             at = slice(4 * n, 4 * n + 4)
-            v = jnp.concatenate([sxhi_ref[32 + layer, at, :], sxlo_ref[32 + layer, at, :]], axis=0)
+            v = jnp.concatenate([sxhi_ref[32 + layer][at], sxlo_ref[32 + layer][at]], axis=0)
             for pz in range(2):
                 cs_ref[n, layer, pz] = expand(v, side, pz)
     for n, first in enumerate((16, 18)):
@@ -314,55 +346,50 @@
                     f1x_ref[o, y, 16:18, :] = cs_ref[n, layer, pz, pl.ds(px, 2, stride=2), :]
                     f1x_ref[o, y, 22:24, :] = cs_ref[n, layer, pz, pl.ds(4 + px, 2, stride=2), :]
 
-
-def pack_y_first_kernel(e0_ref, k0_ref, exlo_ref, exhi_ref, eylo_ref, eyhi_ref):
+    def sweep(y):
+        cur, new = fine_relax(f1x_ref, y, None)
+        for o in range(8):
+            w2x_ref[o, y] = new[o] + cur[o]
+
+    each(YF, sweep)
+
+
+def pack_y(rows, sources, eylo_ref, eyhi_ref):
     lo_here, hi_here = inside("gx")
-
-    def row(y):
-        for j, src in ((0, e0_ref), (1, k0_ref)):
-            for out, at in ((eylo_ref, y), (eyhi_ref, y + 8)):
-                v = src[at]
-                n = (j * 8 + y) * 4
+    for j, (own_ref, exlo_ref, exhi_ref, x_at) in enumerate(sources):
+        for y in range(rows):
+            for out, at in ((eylo_ref, y), (eyhi_ref, 16 - rows + y)):
+                v = own_ref[at]
+                n = (j * rows + y) * 4
                 out[n] = v[0:8]
                 out[n + 1] = v[8:16]
-                out[n + 2] = kept(hi_here, exhi_ref[j * 16 + at])
-                out[n + 3] = kept(lo_here, exlo_ref[j * 16 + at])
-
-    each(8, row)
-
-
-def pack_y_kernel(e0_ref, exlo_ref, exhi_ref, eylo_ref, eyhi_ref):
-    lo_here, hi_here = inside("gx")
-
-    def row(y):
-        for out, at in ((eylo_ref, y), (eyhi_ref, y + 8)):
-            v = e0_ref[at]
-            n = y * 4
-            out[n] = v[0:8]
-            out[n + 1] = v[8:16]
-            out[n + 2] = kept(hi_here, exhi_ref[at])
-            out[n + 3] = kept(lo_here, exlo_ref[at])
-
-    each(8, row)
-
-
-def assemble_base(dst_ref, own_ref, exlo_ref, exhi_ref, eylo_ref, eyhi_ref, x_at, y_at):
+                out[n + 2] = kept(hi_here, exhi_ref[x_at + at])
+                out[n + 3] = kept(lo_here, exlo_ref[x_at + at])
+
+
+def pack_y_first_kernel(e0_ref, k0_ref, ea_ref, eb_ref, eylo_ref, eyhi_ref):
+    exlo_ref, exhi_ref = Swapped(eb_ref, ea_ref), Swapped(ea_ref, eb_ref)
+    sources = (e0_ref, exlo_ref, exhi_ref, 0), (k0_ref, exlo_ref, exhi_ref, 16)
+    pack_y(ROWS_FIRST, sources, eylo_ref, eyhi_ref)
+
+
+def pack_y_kernel(recv_ref, e0_ref, exlo_ref, exhi_ref, eylo_ref, eyhi_ref):
+    pack_y(ROWS_LAST, ((e0_ref, exlo_ref, exhi_ref, 0),), eylo_ref, eyhi_ref)
+
+
+def assemble_base(dst_ref, own_ref, exlo_ref, exhi_ref, eylo_ref, eyhi_ref, x_at, y_at, rows):
     xlo_here, xhi_here = inside("gx")
     ylo_here, yhi_here = inside("gy")
-
-    def own(y):
+    for y in range(16):
         dst_ref[y, 0:16, :] = own_ref[y]
         dst_ref[y, 16:24, :] = kept(xhi_here, exhi_ref[x_at + y])
         dst_ref[y, 24:32, :] = kept(xlo_here, exlo_ref[x_at + y])
-
-    each(16, own)
-
-    def side(y):
+    for y in range(rows):
         for t in range(4):
             dst_ref[16 + y, 8 * t : 8 * t + 8, :] = kept(yhi_here, eyhi_ref[y_at + y * 4 + t])
-            dst_ref[24 + y, 8 * t : 8 * t + 8, :] = kept(ylo_here, eylo_ref[y_at + y * 4 + t])
-
-    each(8, side)
+            dst_ref[32 - rows + y, 8 * t : 8 * t + 8, :] = kept(ylo_here, eylo_ref[y_at + y * 4 + t])
+    for y in range(16 + rows, 32 - rows):
+        dst_ref[y] = jnp.zeros((32, LANES), F32)
 
 
 def down_level0(e_ref, k_ref, e1_ref, k1_ref, make_k1):
@@ -410,11 +437,14 @@
 
 
 def down_first_kernel(
-    live_ref, e0_ref, k0_ref, exlo_ref, exhi_ref, eylo_ref, eyhi_ref,
+    live_ref, e0_ref, k0_ref, ea_ref, eb_ref, eylo_ref, eyhi_ref,
     send_ref, e0x_ref, k0x_ref, e1_ref, k1_ref, pack_ref,
 ):
-    assemble_base(e0x_ref, e0_ref, exlo_ref, exhi_ref, eylo_ref, eyhi_ref, 0, 0)
-    assemble_base(k0x_ref, k0_ref, exlo_ref, exhi_ref, eylo_ref, eyhi_ref, 16, 32)
+    exlo_ref, exhi_ref = Swapped(eb_ref, ea_ref), Swapped(ea_ref, eb_ref)
+    assemble_base(e0x_ref, e0_ref, exlo_ref, exhi_ref, eylo_ref, eyhi_ref, 0, 0, ROWS_FIRST)
+    assemble_base(
+        k0x_ref, k0_ref, exlo_ref, exhi_ref, eylo_ref, eyhi_ref, 16, 4 * ROWS_FIRST, ROWS_FIRST
+    )
     down_level0(e0x_ref, k0x_ref, e1_ref, k1_ref, True)
     r2 = down_level1(e1_ref, k1_ref, pack_ref)
     k2 = []
@@ -430,18 +460,53 @@
     each(send_ref.shape[0], put)
 
 
-def down_kernel(
-    e0_ref, k0x_ref, k1_ref, exlo_ref, exhi_ref, eylo_ref, eyhi_ref,
-    send_ref, e0x_ref, e1_ref, pack_ref,
-):
-    assemble_base(e0x_ref, e0_ref, exlo_ref, exhi_ref, eylo_ref, eyhi_ref, 0, 0)
-    down_level0(e0x_ref, k0x_ref, e1_ref, k1_ref, False)
-    r2 = down_level1(e1_ref, k1_ref, pack_ref)
-
-    def put(d):
-        send_ref[d] = r2
-
-    each(send_ref.shape[0], put)
+def narrow(v):
+    third = jnp.where(rows_of(v[16:24]) < 4, v[16:24], v[24:32])
+    return jnp.concatenate([v[0:16], third], axis=0)
+
+
+def share_kernel(e0_ref, k0x_ref, k1_ref, send_ref, ez_ref, e1z_ref, pack_ref):
+    for y in range(24):
+        if y < 16:
+            ez_ref[y, 0:16, :] = e0_ref[y]
+            ez_ref[y, 16:24, :] = jnp.zeros((8, LANES), F32)
+        else:
+            ez_ref[y] = jnp.zeros((24, LANES), F32)
+
+    def row(y1, carry):
+        parts = []
+        for j in range(2):
+            y = 2 * y1 + j
+            k = narrow(k0x_ref[jnp.where(y >= 20, y + 8, y)])
+            parts.append(k * relax(ez_ref[y], ez_ref[(y + 23) % 24], ez_ref[(y + 1) % 24], 1))
+        r1 = pair_z(pair_x(parts[0] + parts[1], 1), 1) * 0.125
+        k1 = narrow(k1_ref[jnp.where(y1 >= 10, y1 + 4, y1)])
+        e1z_ref[y1] = jnp.where(k1 > 0.0, r1 / jnp.where(k1 > 0.0, k1, 1.0), 0.0)
+        return carry
+
+    lax.fori_loop(0, 12, row, 0, unroll=UNROLL)
+    r2 = []
+    for y2 in range(6):
+        parts = []
+        for j in range(2):
+            y = 2 * y2 + j
+            k = narrow(k1_ref[y + 4 if y >= 10 else y])
+            parts.append(k * relax(e1z_ref[y], e1z_ref[(y + 11) % 12], e1z_ref[(y + 1) % 12], 2))
+        r2.append(pair_z(pair_x(parts[0] + parts[1], 2), 2) * 0.125)
+    lane = lanes_of(r2[0]) & 3
+    inner = jnp.where(
+        lane < 2, jnp.where(lane == 0, r2[0], r2[1]), jnp.where(lane == 2, r2[2], r2[3])
+    )
+    outer = jnp.where(lane == 0, r2[4], jnp.where(lane == 3, r2[5], 0.0))
+    pack_ref[0] = inner
+    pack_ref[1] = outer
+    inner = pack_ref[0, pl.ds(0, 6, stride=4), :]
+    outer = pack_ref[1, pl.ds(0, 6, stride=4), :]
+    tiles = [inner[0:4], outer[0:4], jnp.concatenate([inner[4:6], outer[4:6]], axis=0)]
+    count = len(tiles)
+
+    for n in range(send_ref.shape[0]):
+        send_ref[n] = tiles[n % count]
 
 
 def coarse_shift_x(v, n):
@@ -463,27 +528,33 @@
     return jnp.where(lane < 4 - n, up, above) + jnp.where(lane >= n, down, below)
 
 
-def coarse_relax(v, n):
-    s = coarse_shift_x(v, n) + coarse_shift_y(v, n) + (z_low(v, 4 * n) + z_high(v, 4 * n))
+def coarse_relax(v, rows, n):
+    s = coarse_shift_x(v, rows) + coarse_shift_y(v, n) + (z_low(v, 4 * n) + z_high(v, 4 * n))
     return v * THIRD + s * NINTH
 
 
-def coarse_solve(r2, k2):
+def coarse_solve(r2, k2, pairs_ref):
     e2 = r2 / k2
-    left = k2 * coarse_relax(e2, 1)
+    left = k2 * coarse_relax(e2, 1, 1)
+    gy_total, rows = r2.shape[0], r2.shape[1]
 
     def pool(v):
-        v = pair_x(v, 1)
-        v = pair_z(v, 1)
-        return pair_z(v, 4) * 0.125
+        v = pair_z(pair_z(v, 1), 4) * 0.125
+        pairs_ref[...] = v.reshape(gy_total * rows, LANES)
+        half = gy_total * rows // 2
+        v = pairs_ref[pl.ds(0, half, stride=2), :] + pairs_ref[pl.ds(1, half, stride=2), :]
+        return v.reshape(gy_total, rows // 2, LANES)
 
     k3 = pool(k2) * 0.25
     first = pool(left) / k3
     e3 = first
     for _ in range(SWEEPS - 1):
-        e3 = coarse_relax(e3, 2) + first
-    mid = e2 + e3
-    return coarse_relax(mid, 1) + e2
+        e3 = coarse_relax(e3, 1, 2) + first
+    flat = e3.reshape(gy_total * rows // 2, LANES)
+    for n in range(2):
+        pairs_ref[pl.ds(n, gy_total * rows // 2, stride=2), :] = flat
+    mid = e2 + pairs_ref[...].reshape(gy_total, rows, LANES)
+    return coarse_relax(mid, 1, 1) + e2
 
 
 def spread_coarse(mg2, table_ref, row_ref, m2_ref):
@@ -536,8 +607,7 @@
         y = i + 12 if i >= 18 else i
         v = relax(e0p_ref[y], e0p_ref[(y + 31) % 32], e0p_ref[(y + 1) % 32], 1) + e0x_ref[y]
         v = jnp.where(k0x_ref[y] > 0.0, v, 0.0)
-        third = jnp.where(rows_of(v[16:24]) < 4, v[16:24], v[24:32])
-        corr_ref[i] = jnp.concatenate([v[0:16], third], axis=0)
+        corr_ref[i] = narrow(v)
 
     each(YF, post0)
 
@@ -547,6 +617,29 @@
     for i in range(rows // 4):
         for j in range(gy_total):
             w_ref[j, 4 * i : 4 * i + 4, :] = recv_ref[i * gy_total + j, at : at + 4, :]
+
+
+def gather_shares(recv_ref, count, wa_ref, wb_ref):
+    gy_total, gx_total = wa_ref.shape[0], wa_ref.shape[1] // 4
+    for i in range(gx_total):
+        for j in range(gy_total):
+            n = (i * gy_total + j) * count
+            wa_ref[j, 4 * i : 4 * i + 4, :] = recv_ref[n]
+            wb_ref[j, 4 * i : 4 * i + 4, :] = recv_ref[n + 1]
+    for i in range(gx_total):
+        for j in range(gy_total):
+            n = (i * gy_total + j) * count + 2
+            for ref, at in ((wa_ref, 0), (wb_ref, 2)):
+                if i + 1 < gx_total:
+                    ref[j, 4 * i + 4 : 4 * i + 5, :] += recv_ref[n, at : at + 1, :]
+                if i > 0:
+                    ref[j, 4 * i - 1 : 4 * i, :] += recv_ref[n, at + 1 : at + 2, :]
+    wb = wb_ref[...]
+    lane = lanes_of(wb) & 3
+    zero = jnp.zeros_like(wb[0:1])
+    above = jnp.concatenate([wb[1:], zero], axis=0)
+    below = jnp.concatenate([zero, wb[:-1]], axis=0)
+    return wa_ref[...] + (jnp.where(lane == 0, below, 0.0) + jnp.where(lane == 3, above, 0.0))
 
 
 def fine_sweep(src_ref, dst_ref, f1x_ref, livex_ref):
@@ -561,33 +654,36 @@
 
 
 def middle_kernel(
-    recv_ref, e0x_ref, k0x_ref, e1_ref, k1_ref, f1x_ref, livex_ref, q_ref, brhs_ref,
-    u3_ref, k2_ref, e0_ref, exlo_ref, exhi_ref,
-    w_ref, table_ref, row_ref, m2_ref, mg1_ref, e1p_ref, e0p_ref, corr_ref, ua_ref, ub_ref, v_ref,
+    recv_ref, e0x_ref, k0x_ref, e1_ref, k1_ref, f1x_ref, w2x_ref, livex_ref, q_ref, brhs_ref,
+    w4_ref, k2_ref, e0_ref, exlo_ref, exhi_ref,
+    w_ref, pairs_ref, table_ref, row_ref, m2_ref, mg1_ref, e1p_ref, e0p_ref, corr_ref, ua_ref, ub_ref, v_ref,
 ):
     gather_coarse(recv_ref, 0, w_ref)
     gather_coarse(recv_ref, 4, k2_ref)
-    mg2 = coarse_solve(w_ref[...], k2_ref[...])
+    mg2 = coarse_solve(w_ref[...], k2_ref[...], pairs_ref)
     spread_coarse(mg2, table_ref, row_ref, m2_ref)
     up_levels(m2_ref, e1_ref, k1_ref, mg1_ref, e0x_ref, k0x_ref, corr_ref, e1p_ref, e0p_ref)
 
-    def add(y):
-        c = corr_ref[y]
+    def first_sweep(y):
+        live = livex_ref[0 if y < 16 else 1 if y < 18 else 2] > 0.0
+        c, new = relax_copies(corr_ref, y, YF)
+        u2 = [jnp.where(live, w2x_ref[o, y] + new[o], c) for o in range(8)]
         for o in range(8):
-            ua_ref[o, y] = f1x_ref[o, y] + c
-
-    each(YF, add)
-    fine_sweep(ua_ref, ub_ref, f1x_ref, livex_ref)
-
-    def base(y):
-        v_ref[y] = mean8([ub_ref[o, y] for o in range(8)])
-
-    each(YF, base)
-    fine_sweep(ub_ref, u3_ref, f1x_ref, livex_ref)
+            ub_ref[o, y] = u2[o]
+        v_ref[y] = mean8(u2)
+
+    each(YF, first_sweep)
+    fine_sweep(ub_ref, ua_ref, f1x_ref, livex_ref)
+    own_live = livex_ref[0, 0:16, :] > 0.0
 
     def left(y):
-        cur, new = fine_relax(u3_ref, y, [f1x_ref[o, y] for o in range(8)])
-        fine_left = mean8([q_ref[o, y] * (new[o][0:16] - cur[o][0:16]) for o in range(8)])
+        cur, new = fine_relax(ua_ref, y, None)
+        change = []
+        for o in range(8):
+            u3, u4 = cur[o][0:16], new[o][0:16] + f1x_ref[o, y, 0:16, :]
+            change.append(q_ref[o, y] * (u4 - u3))
+            w4_ref[o, y] = jnp.where(own_live, u4, u3)
+        fine_left = mean8(change)
         k0 = k0x_ref[y][0:16]
         v = v_ref[y]
         s = around(v, v_ref[(y + YF - 1) % YF], v_ref[y + 1], 1)
@@ -601,26 +697,23 @@
 
 
 def last_kernel(
-    site_ref, count_ref, recv_ref, k2_ref, e0x_ref, k0x_ref, e1_ref, k1_ref, u3_ref, f1x_ref, livex_ref,
+    site_ref, count_ref, recv_ref, k2_ref, e0_ref, exlo_ref, exhi_ref, eylo_ref, eyhi_ref, k0x_ref, k1_ref,
+    w4_ref, livex_ref,
     fine_ref, base_ref,
-    w_ref, table_ref, row_ref, m2_ref, mg1_ref, e1p_ref, e0p_ref, corr_ref, ua_ref, ub_ref, c_ref,
+    w_ref, pairs_ref, table_ref, row_ref, m2_ref, mg1_ref, e1p_ref, e0p_ref, corr_ref, ub_ref, c_ref,
+    wb_ref, e0x_ref, e1_ref,
 ):
-    gather_coarse(recv_ref, 0, w_ref)
-    mg2 = coarse_solve(w_ref[...], k2_ref[...])
+    mg2 = coarse_solve(gather_shares(recv_ref, 3, w_ref, wb_ref), k2_ref[...], pairs_ref)
     spread_coarse(mg2, table_ref, row_ref, m2_ref)
+    assemble_base(e0x_ref, e0_ref, exlo_ref, exhi_ref, eylo_ref, eyhi_ref, 0, 0, ROWS_LAST)
+    down_level0(e0x_ref, k0x_ref, e1_ref, k1_ref, False)
     up_levels(m2_ref, e1_ref, k1_ref, mg1_ref, e0x_ref, k0x_ref, corr_ref, e1p_ref, e0p_ref)
 
-    def add(y):
-        c = corr_ref[y]
-        for o in range(8):
-            ua_ref[o, y] = u3_ref[o, y] + c
-
-    each(YF, add)
-    live = livex_ref[0] > 0.0
+    live = livex_ref[0, 0:16, :] > 0.0
 
     def row(y):
-        cur, new = fine_relax(ua_ref, y, [f1x_ref[o, y] for o in range(8)])
-        got = [jnp.where(live, new[o], cur[o])[0:16] for o in range(8)]
+        c, new = relax_copies(corr_ref, y, YF)
+        got = [w4_ref[o, y] + jnp.where(live, new[o][0:16], c[0:16]) for o in range(8)]
         for o in range(8):
             ub_ref[o, y] = got[o]
         base_ref[pl.ds(y, 16, stride=16), :] = mean8(got)
@@ -671,6 +764,12 @@
     return lax.ppermute(value, axis, [(i, (i + by) % count) for i in range(count)])
 
 
+def swap_pairs(value, axis, first):
+    count = lax.axis_size(axis)
+    partner = [((i - first) ^ 1) + first for i in range(count)]
+    return lax.ppermute(value, axis, [(i, j if 0 <= j < count else i) for i, j in enumerate(partner)])
+
+
 def from_sides(to_low, to_high, axis):
     return step(to_high, axis, 1), step(to_low, axis, -1)
 
@@ -700,41 +799,45 @@
     )(slot_site, box_count, fine_rhs, fine_beta)
     rxlo, rxhi = from_sides(fxlo, fxhi, "gx")
     rylo, ryhi = from_sides(fylo, fyhi, "gy")
-    f1, q, k0 = call(
-        boxes_kernel, "boxes", [octets, octets, own], 2, 0, 3, [rows, rows], beside(3)
-    )(slot_site, box_count, fine_rhs, fine_beta, base_beta.reshape(256, LANES))
-    e0, exlo, exhi = call(
-        first_kernel, "first_residual", [own, tiles(37), tiles(37)], 0, 0, 8, [fine_ext, x_side, y_side]
-    )(f1, q, k0, rhs, rxlo, rxhi, rylo, ryhi)
-    sxlo, sxhi = from_sides(exlo, exhi, "gx")
-    eylo, eyhi = call(pack_y_first_kernel, "pack_y_first", [tiles(64), tiles(64)], 0, 0, 4)(e0, k0, sxlo, sxhi)
+    f1, q = call(
+        boxes_kernel, "boxes", [octets, octets], 2, 0, 2, [rows, rows], beside(3)
+    )(slot_site, box_count, fine_rhs, fine_beta)
+    e0, k0, ea, eb = call(
+        first_kernel, "first_residual", [own, own, tiles(37), tiles(37)], 0, 0, 8, [fine_ext, x_side, y_side]
+    )(f1, q, base_beta.reshape(256, LANES), rhs, rxlo, rxhi, rylo, ryhi)
+    sa, sb = swap_pairs(ea, "gx", 0), swap_pairs(eb, "gx", 1)
+    eylo, eyhi = call(
+        pack_y_first_kernel, "pack_y_first", [tiles(8 * ROWS_FIRST)] * 2, 0, 0, 4
+    )(e0, k0, sa, sb)
     sylo, syhi = from_sides(eylo, eyhi, "gy")
-    f1x, livex = call(
-        extend_kernel, "extend", [fine_ext, (3, XF, LANES)], 0, 0, 8, [x_side, y_side, corner], beside(2)
-    )(f1, q, rxlo, rxhi, rylo, ryhi, sxlo, sxhi)
+    f1x, livex, w2x = call(
+        extend_kernel, "extend", [fine_ext, (3, XF, LANES), fine_ext], 0, 0, 8, [x_side, y_side, corner], beside(2)
+    )(f1, q, rxlo, rxhi, rylo, ryhi, sa, sb)
     send, e0x, k0x, e1, k1 = call(
         down_first_kernel, "down_first", [(devices, 8, LANES), wide, wide, half, half], 0, 0, 7, [(16, LANES)]
-    )(livex, e0, k0, sxlo, sxhi, sylo, syhi)
+    )(livex, e0, k0, sa, sb, sylo, syhi)
     recv = lax.all_to_all(send, ("gx", "gy"), 0, 0, tiled=True)
 
     up_scratch = [
-        coarse, (gy_total + 2, gx_total + 2, 8, LANES), (32, LANES), (8, 32, LANES), half, half, wide,
+        coarse, (4 * devices, LANES), (gy_total + 2, gx_total + 2, 8, LANES), (32, LANES), (8, 32, LANES), half, half, wide,
         (YF, XF, LANES),
     ]
-    u3, k2, e0, exlo, exhi = call(
-        middle_kernel, "middle", [fine_ext, coarse, own, tiles(16), tiles(16)], 0, 0, 9,
+    w4, k2, e0, exlo, exhi = call(
+        middle_kernel, "middle", [octets, coarse, own, tiles(16), tiles(16)], 0, 0, 10,
         up_scratch + [fine_ext, fine_ext, (YF, XF, LANES)],
-    )(recv, e0x, k0x, e1, k1, f1x, livex, q, rhs)
+    )(recv, e0x, k0x, e1, k1, f1x, w2x, livex, q, rhs)
     sxlo, sxhi = from_sides(exlo, exhi, "gx")
-    eylo, eyhi = call(pack_y_kernel, "pack_y", [tiles(32), tiles(32)], 0, 0, 3)(e0, sxlo, sxhi)
+    send = call(
+        share_kernel, "share", [(devices * 3, 4, LANES)], 0, 0, 3,
+        [(24, 24, LANES), (12, 24, LANES), (2, 24, LANES)], beside(1),
+    )(e0, k0x, k1)[0]
+    recv = lax.all_to_all(send, ("gx", "gy"), 0, 0, tiled=True)
+    eylo, eyhi = call(pack_y_kernel, "pack_y", [tiles(4 * ROWS_LAST)] * 2, 0, 0, 4)(recv, e0, sxlo, sxhi)
     sylo, syhi = from_sides(eylo, eyhi, "gy")
-    send, e0x, e1 = call(
-        down_kernel, "down", [(devices, 4, LANES), wide, half], 0, 0, 7, [(16, LANES)]
-    )(e0, k0x, k1, sxlo, sxhi, sylo, syhi)
-    recv = lax.all_to_all(send, ("gx", "gy"), 0, 0, tiled=True)
     fine, base = call(
-        last_kernel, "last", [fine_rhs.shape, (256, LANES)], 2, 0, 9, up_scratch + [fine_ext, octets, rows]
-    )(slot_site, box_count, recv, k2, e0x, k0x, e1, k1, u3, f1x, livex)
+        last_kernel, "last", [fine_rhs.shape, (256, LANES)], 2, 0, 11,
+        up_scratch + [octets, rows, coarse, wide, half],
+    )(slot_site, box_count, recv, k2, e0, sxlo, sxhi, sylo, syhi, k0x, k1, w4, livex)
     return fine, base.reshape(base_rhs.shape)
 
 

time: 83.8 us -> 74 us (0.88)
  blocking collectives: 24.6 us -> 14.6 us
  Pallas kernels: 16.2 us -> 17.4 us
  local copies, waits for them, and re-layouts: 3.64 us -> 2.74 us
    all_to_all x2 -> x1, blocking collectives: 24.6 us -> 14.6 us  [local(): recv = lax.all_to_all(send, ('gx', 'gy'), 0, 0, tiled=True)]
    ppermute x12 -> x10, waiting for transfers between devices: 16.7 us -> 11 us  [step(): lax.ppermute(value, axis, [(i, (i + by) % count) for i in range(count)])]
    ppermute x0 -> x2, waiting for transfers between devices: none -> 5.6 us  [swap_pairs(): lax.ppermute(value, axis, [(i, j if 0 <= j < count else i) for i, j in en...]
    ppermute x12 -> x10, starting transfers between devices: 20.9 us -> 17.1 us  [step(): lax.ppermute(value, axis, [(i, (i + by) % count) for i in range(count)])]
    all_to_all x0 -> x1, starting transfers between devices: none -> 2.58 us  [local(): recv = lax.all_to_all(send, ('gx', 'gy'), 0, 0, tiled=True)]
    pallas_call x8, Pallas kernels: 13.6 us -> 14.8 us  [the longest x1 4.8 us: local(): call(last_kernel, 'last', [fine_rhs.shape, (256, LANES)], 2, 0, 11, up_sc...]
    unnamed x12, local copies, waits for them, and re-layouts: 3.64 us -> 2.74 us
  transfers between devices with their start and end apart: 12 -> 13, of which waited for: 5 -> 5; matrix products, arithmetic and copies ran while one was open for 0% -> 0% of each run, Pallas kernels for 3% -> 5%
where the time goes in v3:
time: 74 us; the launch traced here: 73.2 us
  starting transfers between devices  20.4 us (28%)
  Pallas kernels  17.4 us (24%)
  waiting for transfers between devices  16.7 us (23%)
  blocking collectives  14.6 us (20%)
  local copies, waits for them, and re-layouts  2.74 us (4%)
  between operations  1.43 us (2%)
    ppermute x10, starting transfers between devices, step(): lax.ppermute(value, axis, [(i, (i + by) % count) for i in range(count)])  17.1 us
    all_to_all x1, blocking collectives, local(): recv = lax.all_to_all(send, ('gx', 'gy'), 0, 0, tiled=True)  14.6 us
    ppermute x10, waiting for transfers between devices, step(): lax.ppermute(value, axis, [(i, (i + by) % count) for i in range(count)])  11 us
    ppermute x2, waiting for transfers between devices, swap_pairs(): lax.ppermute(value, axis, [(i, j if 0 <= j < count else i) for i, j in en...  5.6 us
    pallas_call x1, Pallas kernels, local(): call(last_kernel, 'last', [fine_rhs.shape, (256, LANES)], 2, 0, 11, up_sc...  4.8 us
    pallas_call x1, Pallas kernels, local(): call(middle_kernel, 'middle', [octets, coarse, own, tiles(16), tiles(16)]...  3.48 us
    unnamed x12, local copies, waits for them, and re-layouts  2.74 us
    all_to_all x1, starting transfers between devices, local(): recv = lax.all_to_all(send, ('gx', 'gy'), 0, 0, tiled=True)  2.58 us
  transfers between devices with their start and end apart: 13, of which 5 were waited for; matrix products, arithmetic and copies ran while one was open for 0% of the time, Pallas kernels for 5%

profile of v3, /device:TPU:0, one launch (start us, length us, event | category | flops | bytes accessed | tf_op | source)
XLA Modules:
  0.0 73.2 jit_solution(3104810514190319665)
XLA Ops:
  1.3 0.0 copy-start
  1.3 1.0 %copy-done = f32[1,1,4,32,1024]{4,3,2,1,0:T(8,128)S(1)} copy-done((f32[1,1,4,32,1024]{4,3,2,1,0:T(8,128)S(1)}, f32[1,1,4,32,1024]{4,3,2,1,0:T(8,128)}, u32[]{:S(2)}) %copy-start) | copy-done | bytes 524312
  2.3 0.0 copy-start.1
  2.3 1.0 %copy-done.1 = f32[1,1,4,32,1024]{4,3,2,1,0:T(8,128)S(1)} copy-done((f32[1,1,4,32,1024]{4,3,2,1,0:T(8,128)S(1)}, f32[1,1,4,32,1024]{4,3,2,1,0:T(8,128)}, u32[]{:S(2)}) %copy-start.1) | copy-done | bytes 524312
  3.4 0.0 copy-start.4
  3.4 0.7 copy-done.4
  4.0 0.0 copy-start.2
  4.0 0.0 copy-start.3
  4.0 1.2 %faces.1 = (f32[17,8,128]{2,1,0:T(8,128)S(1)}, f32[17,8,128]{2,1,0:T(8,128)S(1)}, f32[17,8,128]{2,1,0:T(8,128)S(1)}, f32[17,8,128]{2,1,0:T(8,128)S(1)}) custom-call(s32[1,1,4]{2,1,0:T(1,128)S(1)} %copy-done.4, s32[1,1]{1,0:T(1,128)S(6)} %copy.8.count_ref, f32[1,1,4,32,1024]{4,3,2,1,0:T(8,128)S(1)} %copy-done, f32[1,1,4,32,1024]{4,3,2,1,0:T(8,128)S(1)} %copy-done.1), custom_call_target="tpu_custom_call" | custom-call | tf_op jit(solution)/shard_map/faces/pallas_call | solution.py:797
  5.2 3.1 %collective-permute-start = (f32[17,8,128]{2,1,0:T(8,128)S(1)}, f32[17,8,128]{2,1,0:T(8,128)S(1)}, u32[]{:S(2)}, u32[]{:S(2)}) collective-permute-start(f32[17,8,128]{2,1,0:T(8,128)S(1)} %get-tuple-element.33), channel_id=1, source_target_pairs={{0,8},{8,16},{16,24},{24,0},{1,9},{9,17},{17,25},{25,1},{2,10},{10... | collective-permute-start | bytes 208904 | tf_op jit(solution)/shard_map/ppermute | solution.py:764
  8.3 2.1 %collective-permute-start.1 = (f32[17,8,128]{2,1,0:T(8,128)S(1)}, f32[17,8,128]{2,1,0:T(8,128)S(1)}, u32[]{:S(2)}, u32[]{:S(2)}) collective-permute-start(f32[17,8,128]{2,1,0:T(8,128)S(1)} %get-tuple-element.34), channel_id=1, source_target_pairs={{0,24},{8,0},{16,8},{24,16},{1,25},{9,1},{17,9},{25,17},{2,26},{10... | collective-permute-start | bytes 208904 | tf_op jit(solution)/shard_map/ppermute | solution.py:764
  10.4 0.0 collective-permute-start.2
  10.4 2.6 %collective-permute-start.3 = (f32[17,8,128]{2,1,0:T(8,128)S(1)}, f32[17,8,128]{2,1,0:T(8,128)S(1)}, u32[]{:S(2)}, u32[]{:S(2)}) collective-permute-start(f32[17,8,128]{2,1,0:T(8,128)S(1)} %get-tuple-element.36), channel_id=1, source_target_pairs={{0,7},{1,0},{2,1},{3,2},{4,3},{5,4},{6,5},{7,6},{8,15},{9,8},{10,9... | collective-permute-start | bytes 208904 | tf_op jit(solution)/shard_map/ppermute | solution.py:764
  13.0 2.3 %boxes.1 = (f32[8,16,16,128]{3,2,1,0:T(8,128)S(1)}, f32[8,16,16,128]{3,2,1,0:T(8,128)S(1)}) custom-call(s32[1,1,4]{2,1,0:T(1,128)S(1)} %copy-done.4, s32[1,1]{1,0:T(1,128)S(6)} %copy.8.count_ref, f32[1,1,4,32,1024]{4,3,2,1,0:T(8,128)S(1)} %copy-done, f32[1,1,4,32,1024]{4,3,2,1,0:T(8,128)S(1)} %copy-done.1), custom_call_target="tpu_custom_call" | custom-call | flops 3000000 | bytes 9000000 | tf_op jit(solution)/shard_map/boxes/pallas_call | solution.py:802
  15.4 0.0 collective-permute-done.rxlo_ref
  15.4 0.0 collective-permute-done.1.rxhi_ref
  15.4 0.0 collective-permute-done.2.rylo_ref
  15.4 0.0 collective-permute-done.3.ryhi_ref
  15.4 0.0 copy-done.2
  15.4 0.0 copy-done.3
  15.4 1.0 %first_residual.1 = (f32[16,16,128]{2,1,0:T(8,128)S(1)}, f32[16,16,128]{2,1,0:T(8,128)S(1)}, f32[37,8,128]{2,1,0:T(8,128)S(1)}, f32[37,8,128]{2,1,0:T(8,128)S(1)}) custom-call(f32[8,16,16,128]{3,2,1,0:T(8,128)S(1)} %get-tuple-element.31.f1_ref, f32[8,16,16,128]{3,2,1,0:T(8,128)S(1)} %get-tuple-element.32.q_ref, f32[256,128]{1,0:T(8,128)S(1)} %bitcast.5, ...), custom_call_target="tpu_custom_call" | custom-call | tf_op jit(solution)/shard_map/first_residual/pallas_call | solution.py:805
  16.4 0.1 collective-permute-start.4
  16.5 0.7 collective-permute-start.5
  17.2 5.6 %collective-permute-done.4.sa_ref.ea_ref = f32[37,8,128]{2,1,0:T(8,128)S(1)} collective-permute-done((f32[37,8,128]{2,1,0:T(8,128)S(1)}, f32[37,8,128]{2,1,0:T(8,128)S(1)}, u32[]{:S(2)}, u32[]{:S(2)}) %collective-permute-start.4) | collective-permute-done | bytes 151584 | tf_op jit(solution)/shard_map/ppermute | solution.py:770
  22.8 0.0 collective-permute-done.5.sb_ref.eb_ref
  22.8 0.1 collective-permute-start.6
  22.9 2.6 %collective-permute-start.7 = (f32[56,8,128]{2,1,0:T(8,128)S(1)}, f32[56,8,128]{2,1,0:T(8,128)S(1)}, u32[]{:S(2)}, u32[]{:S(2)}) collective-permute-start(f32[56,8,128]{2,1,0:T(8,128)S(1)} %get-tuple-element.43), channel_id=1, source_target_pairs={{0,7},{1,0},{2,1},{3,2},{4,3},{5,4},{6,5},{7,6},{8,15},{9,8},{10,9... | collective-permute-start | bytes 688136 | tf_op jit(solution)/shard_map/ppermute | solution.py:764
  25.5 1.5 %extend.1 = (f32[8,20,24,128]{3,2,1,0:T(8,128)S(1)}, f32[3,24,128]{2,1,0:T(8,128)S(1)}, f32[8,20,24,128]{3,2,1,0:T(8,128)S(1)}) custom-call(f32[8,16,16,128]{3,2,1,0:T(8,128)S(1)} %get-tuple-element.31.f1_ref, f32[8,16,16,128]{3,2,1,0:T(8,128)S(1)} %get-tuple-element.32.q_ref, f32[17,8,128]{2,1,0:T(8,128)S(1)} %collective-permute-done.rxlo_ref, ...), custom_call_target="tpu_custom_call" | custom-call | flops 2000000 | bytes 6000000 | tf_op jit(solution)/shard_map/extend/pallas_call | solution.py:813
  27.0 3.0 %collective-permute-done.6.eylo_ref = f32[56,8,128]{2,1,0:T(8,128)S(1)} collective-permute-done((f32[56,8,128]{2,1,0:T(8,128)S(1)}, f32[56,8,128]{2,1,0:T(8,128)S(1)}, u32[]{:S(2)}, u32[]{:S(2)}) %collective-permute-start.6) | collective-permute-done | bytes 229408 | tf_op jit(solution)/shard_map/ppermute | solution.py:764
  30.0 0.0 collective-permute-done.7.eyhi_ref
  30.0 1.5 %down_first.1 = (f32[32,8,128]{2,1,0:T(8,128)S(1)}, f32[32,32,128]{2,1,0:T(8,128)S(1)}, f32[32,32,128]{2,1,0:T(8,128)S(1)}, f32[16,32,128]{2,1,0:T(8,128)S(1)}, f32[16,32,128]{2,1,0:T(8,128)S(1)}) custom-call(f32[3,24,128]{2,1,0:T(8,128)S(1)} %get-tuple-element.39.live_ref.livex_ref, f32[16,16,128]{2,1,0:T(8,128)S(1)} %get-tuple-element.40.e0_ref, ...), custom_call_target="tpu_custom_call" | custom-call | tf_op jit(solution)/shard_map/down_first/pallas_call | solution.py:816
  31.5 14.6 %all_to_all.10.recv_ref = f32[32,8,128]{2,1,0:T(8,128)S(1)} all-to-all(f32[32,8,128]{2,1,0:T(8,128)S(1)} %get-tuple-element.44), channel_id=1, replica_groups=mesh['gx'=4,'gy'=8] {'gx','gy'}, dimensions={0} | all-to-all | bytes 262144 | tf_op jit(solution)/shard_map/all_to_all | solution.py:819
  46.1 3.5 %middle.1 = (f32[8,16,16,128]{3,2,1,0:T(8,128)S(1)}, f32[8,16,128]{2,1,0:T(8,128)S(1)}, f32[16,16,128]{2,1,0:T(8,128)S(1)}, f32[16,8,128]{2,1,0:T(8,128)S(1)}, f32[16,8,128]{2,1,0:T(8,128)S(1)}) custom-call(f32[32,8,128]{2,1,0:T(8,128)S(1)} %all_to_all.10.recv_ref, f32[32,32,128]{2,1,0:T(8,128)S(1)} %get-tuple-element.45.e0x_ref, ...), custom_call_target="tpu_custom_call" | custom-call | tf_op jit(solution)/shard_map/middle/pallas_call | solution.py:825
  49.6 0.0 copy-start.5
  49.6 1.6 %share.1 = f32[96,4,128]{2,1,0:T(4,128)} custom-call(f32[16,16,128]{2,1,0:T(8,128)S(1)} %get-tuple-element.51.e0_ref, f32[32,32,128]{2,1,0:T(8,128)S(1)} %get-tuple-element.46.k0x_ref, f32[16,32,128]{2,1,0:T(8,128)S(1)} %get-tuple-element.48.k1_ref), custom_call_target="tpu_custom_call" | custom-call | flops 1000000 | bytes 3000000 | tf_op jit(solution)/shard_map/share/pallas_call | solution.py:830
  51.2 2.6 %all-to-all-start.1 = ((f32[96,4,128]{2,1,0:T(4,128)}), f32[96,4,128]{2,1,0:T(4,128)S(1)}, u32[]{:S(2)}, u32[]{:S(2)}) async-start(f32[96,4,128]{2,1,0:T(4,128)} %share.1), calls=%async_computation.1 | async-start | bytes 393216 | tf_op jit(solution)/shard_map/all_to_all | solution.py:834
  53.8 1.7 %collective-permute-start.8 = (f32[16,8,128]{2,1,0:T(8,128)S(1)}, f32[16,8,128]{2,1,0:T(8,128)S(1)}, u32[]{:S(2)}, u32[]{:S(2)}) collective-permute-start(f32[16,8,128]{2,1,0:T(8,128)S(1)} %get-tuple-element.53), channel_id=1, source_target_pairs={{0,8},{8,16},{16,24},{24,0},{1,9},{9,17},{17,25},{25,1},{2,10},{10... | collective-permute-start | bytes 196616 | tf_op jit(solution)/shard_map/ppermute | solution.py:764
  55.5 2.1 %collective-permute-start.9 = (f32[16,8,128]{2,1,0:T(8,128)S(1)}, f32[16,8,128]{2,1,0:T(8,128)S(1)}, u32[]{:S(2)}, u32[]{:S(2)}) collective-permute-start(f32[16,8,128]{2,1,0:T(8,128)S(1)} %get-tuple-element.54), channel_id=1, source_target_pairs={{0,24},{8,0},{16,8},{24,16},{1,25},{9,1},{17,9},{25,17},{2,26},{10... | collective-permute-start | bytes 196616 | tf_op jit(solution)/shard_map/ppermute | solution.py:764
  57.6 5.9 %collective-permute-done.8.exlo_ref = f32[16,8,128]{2,1,0:T(8,128)S(1)} collective-permute-done((f32[16,8,128]{2,1,0:T(8,128)S(1)}, f32[16,8,128]{2,1,0:T(8,128)S(1)}, u32[]{:S(2)}, u32[]{:S(2)}) %collective-permute-start.8) | collective-permute-done | bytes 65568 | tf_op jit(solution)/shard_map/ppermute | solution.py:764
  63.5 0.0 collective-permute-done.9.exhi_ref
  63.5 0.1 all-to-all-done.1.recv_ref
  63.6 0.1 collective-permute-start.10
  63.7 2.6 %collective-permute-start.11 = (f32[20,8,128]{2,1,0:T(8,128)S(1)}, f32[20,8,128]{2,1,0:T(8,128)S(1)}, u32[]{:S(2)}, u32[]{:S(2)}) collective-permute-start(f32[20,8,128]{2,1,0:T(8,128)S(1)} %get-tuple-element.56), channel_id=1, source_target_pairs={{0,7},{1,0},{2,1},{3,2},{4,3},{5,4},{6,5},{7,6},{8,15},{9,8},{10,9... | collective-permute-start | bytes 245768 | tf_op jit(solution)/shard_map/ppermute | solution.py:764
  66.3 2.1 %collective-permute-done.10.eylo_ref = f32[20,8,128]{2,1,0:T(8,128)S(1)} collective-permute-done((f32[20,8,128]{2,1,0:T(8,128)S(1)}, f32[20,8,128]{2,1,0:T(8,128)S(1)}, u32[]{:S(2)}, u32[]{:S(2)}) %collective-permute-start.10) | collective-permute-done | bytes 81952 | tf_op jit(solution)/shard_map/ppermute | solution.py:764
  68.4 0.0 collective-permute-done.11.eyhi_ref
  68.4 0.0 copy-done.5
  68.4 4.8 %last.1 = (f32[1,1,4,32,1024]{4,3,2,1,0:T(8,128)}, f32[256,128]{1,0:T(8,128)}) custom-call(s32[1,1,4]{2,1,0:T(1,128)S(1)} %copy-done.5, s32[1,1]{1,0:T(1,128)S(6)} %copy.8.count_ref, f32[96,4,128]{2,1,0:T(4,128)S(1)} %all-to-all-done.1.recv_ref, f32[8,16,128]{2,1,0:T(8,128)S(1)} %get-tuple-element.52.k2_ref, f32[16,16,128]{2,1,0:T(8,128)S(1)} %get-tuple-element.51.e0_ref, ...), custom_call_target="tpu_custom_call" | custom-call | tf_op jit(solution)/shard_map/last/pallas_call | solution.py:837
  (2 shorter events, 0.1 us)
Async XLA Ops:
  1.3 1.0 %copy-start = (f32[1,1,4,32,1024]{4,3,2,1,0:T(8,128)S(1)}, f32[1,1,4,32,1024]{4,3,2,1,0:T(8,128)}, u32[]{:S(2)}) copy-start(f32[1,1,4,32,1024]{4,3,2,1,0:T(8,128)} %rhs_hbm.1) | copy-start | bytes 1572868
  2.3 1.0 %copy-start.1 = (f32[1,1,4,32,1024]{4,3,2,1,0:T(8,128)S(1)}, f32[1,1,4,32,1024]{4,3,2,1,0:T(8,128)}, u32[]{:S(2)}) copy-start(f32[1,1,4,32,1024]{4,3,2,1,0:T(8,128)} %beta_hbm.1) | copy-start | bytes 1572868
  3.4 0.7 copy-start.4
  4.0 11.4 %copy-start.2 = (f32[16,16,128]{2,1,0:T(8,128)S(1)}, f32[16,16,128]{2,1,0:T(8,128)}, u32[]{:S(2)}) copy-start(f32[16,16,128]{2,1,0:T(8,128)} %param.9) | copy-start | bytes 393220
  4.0 11.4 %copy-start.3 = (f32[16,16,128]{2,1,0:T(8,128)S(1)}, f32[16,16,128]{2,1,0:T(8,128)}, u32[]{:S(2)}) copy-start(f32[16,16,128]{2,1,0:T(8,128)} %param.10) | copy-start | bytes 393220
  5.2 10.2 %collective-permute-start = (f32[17,8,128]{2,1,0:T(8,128)S(1)}, f32[17,8,128]{2,1,0:T(8,128)S(1)}, u32[]{:S(2)}, u32[]{:S(2)}) collective-permute-start(f32[17,8,128]{2,1,0:T(8,128)S(1)} %get-tuple-element.33), channel_id=1, source_target_pairs={{0,8},{8,16},{16,24},{24,0},{1,9},{9,17},{17,25},{25,1},{2,10},{10... | collective-permute-start | bytes 208904 | tf_op jit(solution)/shard_map/ppermute | solution.py:764
  8.3 7.1 %collective-permute-start.1 = (f32[17,8,128]{2,1,0:T(8,128)S(1)}, f32[17,8,128]{2,1,0:T(8,128)S(1)}, u32[]{:S(2)}, u32[]{:S(2)}) collective-permute-start(f32[17,8,128]{2,1,0:T(8,128)S(1)} %get-tuple-element.34), channel_id=1, source_target_pairs={{0,24},{8,0},{16,8},{24,16},{1,25},{9,1},{17,9},{25,17},{2,26},{10... | collective-permute-start | bytes 208904 | tf_op jit(solution)/shard_map/ppermute | solution.py:764
  10.4 5.0 %collective-permute-start.2 = (f32[17,8,128]{2,1,0:T(8,128)S(1)}, f32[17,8,128]{2,1,0:T(8,128)S(1)}, u32[]{:S(2)}, u32[]{:S(2)}) collective-permute-start(f32[17,8,128]{2,1,0:T(8,128)S(1)} %get-tuple-element.35), channel_id=1, source_target_pairs={{0,1},{1,2},{2,3},{3,4},{4,5},{5,6},{6,7},{7,0},{8,9},{9,10},{10,1... | collective-permute-start | bytes 208904 | tf_op jit(solution)/shard_map/ppermute | solution.py:764
  10.4 5.0 %collective-permute-start.3 = (f32[17,8,128]{2,1,0:T(8,128)S(1)}, f32[17,8,128]{2,1,0:T(8,128)S(1)}, u32[]{:S(2)}, u32[]{:S(2)}) collective-permute-start(f32[17,8,128]{2,1,0:T(8,128)S(1)} %get-tuple-element.36), channel_id=1, source_target_pairs={{0,7},{1,0},{2,1},{3,2},{4,3},{5,4},{6,5},{7,6},{8,15},{9,8},{10,9... | collective-permute-start | bytes 208904 | tf_op jit(solution)/shard_map/ppermute | solution.py:764
  16.4 6.4 %collective-permute-start.4 = (f32[37,8,128]{2,1,0:T(8,128)S(1)}, f32[37,8,128]{2,1,0:T(8,128)S(1)}, u32[]{:S(2)}, u32[]{:S(2)}) collective-permute-start(f32[37,8,128]{2,1,0:T(8,128)S(1)} %get-tuple-element.37), channel_id=1, source_target_pairs={{0,8},{8,0},{16,24},{24,16},{1,9},{9,1},{17,25},{25,17},{2,10},{10... | collective-permute-start | bytes 454664 | tf_op jit(solution)/shard_map/ppermute | solution.py:770
  16.5 6.3 %collective-permute-start.5 = (f32[37,8,128]{2,1,0:T(8,128)S(1)}, f32[37,8,128]{2,1,0:T(8,128)S(1)}, u32[]{:S(2)}, u32[]{:S(2)}) collective-permute-start(f32[37,8,128]{2,1,0:T(8,128)S(1)} %get-tuple-element.38), channel_id=1, source_target_pairs={{0,0},{8,16},{16,8},{24,24},{1,1},{9,17},{17,9},{25,25},{2,2},{10,... | collective-permute-start | bytes 454664 | tf_op jit(solution)/shard_map/ppermute | solution.py:770
  22.8 7.2 %collective-permute-start.6 = (f32[56,8,128]{2,1,0:T(8,128)S(1)}, f32[56,8,128]{2,1,0:T(8,128)S(1)}, u32[]{:S(2)}, u32[]{:S(2)}) collective-permute-start(f32[56,8,128]{2,1,0:T(8,128)S(1)} %get-tuple-element.42), channel_id=1, source_target_pairs={{0,1},{1,2},{2,3},{3,4},{4,5},{5,6},{6,7},{7,0},{8,9},{9,10},{10,1... | collective-permute-start | bytes 688136 | tf_op jit(solution)/shard_map/ppermute | solution.py:764
  22.9 7.2 %collective-permute-start.7 = (f32[56,8,128]{2,1,0:T(8,128)S(1)}, f32[56,8,128]{2,1,0:T(8,128)S(1)}, u32[]{:S(2)}, u32[]{:S(2)}) collective-permute-start(f32[56,8,128]{2,1,0:T(8,128)S(1)} %get-tuple-element.43), channel_id=1, source_target_pairs={{0,7},{1,0},{2,1},{3,2},{4,3},{5,4},{6,5},{7,6},{8,15},{9,8},{10,9... | collective-permute-start | bytes 688136 | tf_op jit(solution)/shard_map/ppermute | solution.py:764
  49.6 18.9 %copy-start.5 = (s32[1,1,4]{2,1,0:T(1,128)S(1)}, s32[1,1,4]{2,1,0:T(1,128)}, u32[]{:S(2)}) copy-start(s32[1,1,4]{2,1,0:T(1,128)} %site_ref.5) | copy-start | bytes 52
  51.2 12.4 %all-to-all-start.1 = ((f32[96,4,128]{2,1,0:T(4,128)}), f32[96,4,128]{2,1,0:T(4,128)S(1)}, u32[]{:S(2)}, u32[]{:S(2)}) async-start(f32[96,4,128]{2,1,0:T(4,128)} %share.1), calls=%async_computation.1 | async-start | bytes 393216 | tf_op jit(solution)/shard_map/all_to_all | solution.py:834
  53.8 9.8 %collective-permute-start.8 = (f32[16,8,128]{2,1,0:T(8,128)S(1)}, f32[16,8,128]{2,1,0:T(8,128)S(1)}, u32[]{:S(2)}, u32[]{:S(2)}) collective-permute-start(f32[16,8,128]{2,1,0:T(8,128)S(1)} %get-tuple-element.53), channel_id=1, source_target_pairs={{0,8},{8,16},{16,24},{24,0},{1,9},{9,17},{17,25},{25,1},{2,10},{10... | collective-permute-start | bytes 196616 | tf_op jit(solution)/shard_map/ppermute | solution.py:764
  55.5 8.0 %collective-permute-start.9 = (f32[16,8,128]{2,1,0:T(8,128)S(1)}, f32[16,8,128]{2,1,0:T(8,128)S(1)}, u32[]{:S(2)}, u32[]{:S(2)}) collective-permute-start(f32[16,8,128]{2,1,0:T(8,128)S(1)} %get-tuple-element.54), channel_id=1, source_target_pairs={{0,24},{8,0},{16,8},{24,16},{1,25},{9,1},{17,9},{25,17},{2,26},{10... | collective-permute-start | bytes 196616 | tf_op jit(solution)/shard_map/ppermute | solution.py:764
  63.6 4.8 %collective-permute-start.10 = (f32[20,8,128]{2,1,0:T(8,128)S(1)}, f32[20,8,128]{2,1,0:T(8,128)S(1)}, u32[]{:S(2)}, u32[]{:S(2)}) collective-permute-start(f32[20,8,128]{2,1,0:T(8,128)S(1)} %get-tuple-element.55), channel_id=1, source_target_pairs={{0,1},{1,2},{2,3},{3,4},{4,5},{5,6},{6,7},{7,0},{8,9},{9,10},{10,1... | collective-permute-start | bytes 245768 | tf_op jit(solution)/shard_map/ppermute | solution.py:764
  63.7 4.7 %collective-permute-start.11 = (f32[20,8,128]{2,1,0:T(8,128)S(1)}, f32[20,8,128]{2,1,0:T(8,128)S(1)}, u32[]{:S(2)}, u32[]{:S(2)}) collective-permute-start(f32[20,8,128]{2,1,0:T(8,128)S(1)} %get-tuple-element.56), channel_id=1, source_target_pairs={{0,7},{1,0},{2,1},{3,2},{4,3},{5,4},{6,5},{7,6},{8,15},{9,8},{10,9... | collective-permute-start | bytes 245768 | tf_op jit(solution)/shard_map/ppermute | solution.py:764

commit v4 on v3

--- a/solution.py
+++ b/solution.py
@@ -16,6 +16,7 @@
 VMEM_LIMIT = 16 * 1024 * 1024
 UNROLL = 4
 ROWS_FIRST = 7
+ROWS_DIAGONAL = 6
 ROWS_LAST = 5
 
 
@@ -117,13 +118,17 @@
     ) * 0.125
 
 
-def slot_map(site_ref, count_ref, shape):
-    lane_site = lax.broadcasted_iota(jnp.int32, shape, 1) // 16
-    out = jnp.zeros(shape, F32)
+def tables_kernel(site_ref, count_ref, tables_ref):
+    lane = lax.broadcasted_iota(jnp.int32, (8, LANES), 1)
+    slots = jnp.zeros((8, LANES), jnp.int32)
+    lanes = jnp.zeros((8, LANES), jnp.int32)
     for s in range(4):
         site = jnp.where(s < count_ref[0, 0], site_ref[0, 0, s], -1)
-        out = jnp.where(lane_site == site, float(s + 1), out)
-    return out
+        slots = jnp.where(lane // 16 == site, s + 1, slots)
+        at = jnp.where(site >= 0, 1 + site * 16 + (lane & 31) // 2, 0)
+        lanes = jnp.where(lane // 32 == s, at, lanes)
+    tables_ref[0:8, :] = slots.astype(F32)
+    tables_ref[8:16, :] = lanes.astype(F32)
 
 
 def transpose_blocks(v):
@@ -146,35 +151,20 @@
 
 
 def faces_kernel(
-    site_ref, count_ref, rhs_hbm, beta_hbm,
-    fxlo_ref, fxhi_ref, fylo_ref, fyhi_ref,
-    rhs_ref, beta_ref, sem_ref,
+    tables_ref, rhs_ref, beta_ref,
+    fxlo_ref, fxhi_ref, fylo_ref, fyhi_ref, raw_f_ref, raw_q_ref,
 ):
-    parts = (
-        (slice(0, 8), slice(0, 1024)),
-        (slice(24, 32), slice(0, 1024)),
-        (slice(8, 24), slice(0, 128)),
-        (slice(8, 24), slice(896, 1024)),
-    )
-    copies = []
-    for n, (src, dst) in enumerate(((rhs_hbm, rhs_ref), (beta_hbm, beta_ref))):
-        for m, (rows, cols) in enumerate(parts):
-            copies.append(
-                pltpu.make_async_copy(
-                    src.at[0, 0, :, rows, cols], dst.at[:, rows, cols], sem_ref.at[n, m]
-                )
-            )
-    for copy in copies:
-        copy.start()
-    slots = slot_map(site_ref, count_ref, (8, LANES))
+    for s in range(4):
+        q = beta_ref[0, 0, s] * 9.0
+        raw_q_ref[s] = q
+        raw_f_ref[s] = rhs_ref[0, 0, s] / q
+    slots = tables_ref[0:8, :]
     for ref in (fxlo_ref, fxhi_ref, fylo_ref, fyhi_ref):
         ref[16] = slots
-    for copy in copies:
-        copy.wait()
     for xt in range(4):
         for t in range(8) if xt in (0, 3) else (0, 7):
             rows, cols = slice(8 * xt, 8 * xt + 8), slice(t * LANES, (t + 1) * LANES)
-            f = [rhs_ref[s, rows, cols] / (beta_ref[s, rows, cols] * 9.0) for s in range(4)]
+            f = [raw_f_ref[s, rows, cols] for s in range(4)]
             for yy, v in enumerate(transpose_blocks(f)):
                 y16, at = 2 * t + yy // 2, (yy % 2) * 4
                 if xt == 0:
@@ -187,17 +177,17 @@
                     fyhi_ref[yy * 4 + xt] = v
 
 
-def boxes_kernel(site_ref, count_ref, rhs_ref, beta_ref, f1_ref, q_ref, f_ref, c_ref):
+def boxes_kernel(tables_ref, raw_f_ref, raw_q_ref, f1_ref, q_ref, f_ref, c_ref):
     for xt in range(4):
         for t in range(8):
             rows, cols = slice(8 * xt, 8 * xt + 8), slice(t * LANES, (t + 1) * LANES)
-            q = [beta_ref[0, 0, s, rows, cols] * 9.0 for s in range(4)]
-            f = [rhs_ref[0, 0, s, rows, cols] / q[s] for s in range(4)]
+            q = [raw_q_ref[s, rows, cols] for s in range(4)]
+            f = [raw_f_ref[s, rows, cols] for s in range(4)]
             for yy, v in enumerate(transpose_blocks(q)):
                 c_ref[4 * t + yy, rows, :] = v
             for yy, v in enumerate(transpose_blocks(f)):
                 f_ref[4 * t + yy, rows, :] = v
-    slots = slot_map(site_ref, count_ref, (16, LANES))
+    slots = spread(tables_ref[0:1, :], 16)
 
     def row(y):
         for py in range(2):
@@ -354,27 +344,28 @@
     each(YF, sweep)
 
 
-def pack_y(rows, sources, eylo_ref, eyhi_ref):
+def pack_y(sources, eylo_ref, eyhi_ref):
     lo_here, hi_here = inside("gx")
-    for j, (own_ref, exlo_ref, exhi_ref, x_at) in enumerate(sources):
+    n = 0
+    for own_ref, exlo_ref, exhi_ref, x_at, rows in sources:
         for y in range(rows):
             for out, at in ((eylo_ref, y), (eyhi_ref, 16 - rows + y)):
                 v = own_ref[at]
-                n = (j * rows + y) * 4
                 out[n] = v[0:8]
                 out[n + 1] = v[8:16]
                 out[n + 2] = kept(hi_here, exhi_ref[x_at + at])
                 out[n + 3] = kept(lo_here, exlo_ref[x_at + at])
+            n += 4
 
 
 def pack_y_first_kernel(e0_ref, k0_ref, ea_ref, eb_ref, eylo_ref, eyhi_ref):
     exlo_ref, exhi_ref = Swapped(eb_ref, ea_ref), Swapped(ea_ref, eb_ref)
-    sources = (e0_ref, exlo_ref, exhi_ref, 0), (k0_ref, exlo_ref, exhi_ref, 16)
-    pack_y(ROWS_FIRST, sources, eylo_ref, eyhi_ref)
+    sources = (e0_ref, exlo_ref, exhi_ref, 0, ROWS_FIRST), (k0_ref, exlo_ref, exhi_ref, 16, ROWS_DIAGONAL)
+    pack_y(sources, eylo_ref, eyhi_ref)
 
 
 def pack_y_kernel(recv_ref, e0_ref, exlo_ref, exhi_ref, eylo_ref, eyhi_ref):
-    pack_y(ROWS_LAST, ((e0_ref, exlo_ref, exhi_ref, 0),), eylo_ref, eyhi_ref)
+    pack_y(((e0_ref, exlo_ref, exhi_ref, 0, ROWS_LAST),), eylo_ref, eyhi_ref)
 
 
 def assemble_base(dst_ref, own_ref, exlo_ref, exhi_ref, eylo_ref, eyhi_ref, x_at, y_at, rows):
@@ -392,8 +383,15 @@
         dst_ref[y] = jnp.zeros((32, LANES), F32)
 
 
-def down_level0(e_ref, k_ref, e1_ref, k1_ref, make_k1):
-    def row(y1, carry):
+def ringed(count, total, ring):
+    return list(range(count + ring)) + list(range(total - ring, total))
+
+
+def down_level0(e_ref, k_ref, e1_ref, k1_ref, make_k1, ring):
+    rows = 8 + 2 * ring
+
+    def row(n, carry):
+        y1 = n if rows == 16 else jnp.where(n < 8 + ring, n, n + 16 - rows)
         parts = []
         for j in range(2):
             y = 2 * y1 + j
@@ -409,7 +407,7 @@
         e1_ref[y1] = jnp.where(k1 > 0.0, r1 / jnp.where(k1 > 0.0, k1, 1.0), 0.0)
         return carry
 
-    lax.fori_loop(0, 16, row, 0, unroll=UNROLL)
+    lax.fori_loop(0, rows, row, 0, unroll=UNROLL)
 
 
 def pack_four(rows, pack_ref):
@@ -443,9 +441,9 @@
     exlo_ref, exhi_ref = Swapped(eb_ref, ea_ref), Swapped(ea_ref, eb_ref)
     assemble_base(e0x_ref, e0_ref, exlo_ref, exhi_ref, eylo_ref, eyhi_ref, 0, 0, ROWS_FIRST)
     assemble_base(
-        k0x_ref, k0_ref, exlo_ref, exhi_ref, eylo_ref, eyhi_ref, 16, 4 * ROWS_FIRST, ROWS_FIRST
+        k0x_ref, k0_ref, exlo_ref, exhi_ref, eylo_ref, eyhi_ref, 16, 4 * ROWS_FIRST, ROWS_DIAGONAL
     )
-    down_level0(e0x_ref, k0x_ref, e1_ref, k1_ref, True)
+    down_level0(e0x_ref, k0x_ref, e1_ref, k1_ref, True, 4)
     r2 = down_level1(e1_ref, k1_ref, pack_ref)
     k2 = []
     for y2 in range(4):
@@ -473,18 +471,21 @@
         else:
             ez_ref[y] = jnp.zeros((24, LANES), F32)
 
-    def row(y1, carry):
+    def row(y1):
         parts = []
         for j in range(2):
             y = 2 * y1 + j
-            k = narrow(k0x_ref[jnp.where(y >= 20, y + 8, y)])
+            k = narrow(k0x_ref[y + 8 if y >= 20 else y])
             parts.append(k * relax(ez_ref[y], ez_ref[(y + 23) % 24], ez_ref[(y + 1) % 24], 1))
         r1 = pair_z(pair_x(parts[0] + parts[1], 1), 1) * 0.125
-        k1 = narrow(k1_ref[jnp.where(y1 >= 10, y1 + 4, y1)])
+        k1 = narrow(k1_ref[y1 + 4 if y1 >= 10 else y1])
         e1z_ref[y1] = jnp.where(k1 > 0.0, r1 / jnp.where(k1 > 0.0, k1, 1.0), 0.0)
-        return carry
-
-    lax.fori_loop(0, 12, row, 0, unroll=UNROLL)
+
+    for y1 in range(12):
+        if y1 in (9, 10):
+            e1z_ref[y1] = jnp.zeros((24, LANES), F32)
+        else:
+            row(y1)
     r2 = []
     for y2 in range(6):
         parts = []
@@ -500,11 +501,16 @@
     outer = jnp.where(lane == 0, r2[4], jnp.where(lane == 3, r2[5], 0.0))
     pack_ref[0] = inner
     pack_ref[1] = outer
+    pack_ref[2] = jnp.where(
+        lane == 1, pltpu.roll(outer, 1, 1), jnp.where(lane == 2, pltpu.roll(outer, LANES - 1, 1), 0.0)
+    )
     inner = pack_ref[0, pl.ds(0, 6, stride=4), :]
     outer = pack_ref[1, pl.ds(0, 6, stride=4), :]
-    tiles = [inner[0:4], outer[0:4], jnp.concatenate([inner[4:6], outer[4:6]], axis=0)]
+    corner = pack_ref[2, pl.ds(0, 6, stride=4), :]
+    outer_lo = jnp.concatenate([outer[0:1] + corner[5:6], outer[1:2]], axis=0)
+    outer_hi = jnp.concatenate([outer[2:3], outer[3:4] + corner[4:5]], axis=0)
+    tiles = [inner[0:2], inner[2:4], outer_lo, outer_hi, inner[4:6]]
     count = len(tiles)
-
     for n in range(send_ref.shape[0]):
         send_ref[n] = tiles[n % count]
 
@@ -586,22 +592,25 @@
             m2_ref[at] = lane_gather(v, group + y)
 
 
-def up_levels(m2_ref, e1_ref, k1_ref, mg1_ref, e0x_ref, k0x_ref, corr_ref, e1p_ref, e0p_ref):
+def up_levels(m2_ref, e1_ref, k1_ref, mg1_ref, e0x_ref, k0x_ref, corr_ref, e1p_ref, e0p_ref, ring):
     def mid1(y):
         e1p_ref[y] = jnp.where(k1_ref[y] > 0.0, e1_ref[y] + m2_ref[y // 2], 0.0)
 
-    each(16, mid1)
+    for y in ringed(8, 16, ring):
+        mid1(y)
 
     def post1(y):
         v = relax(e1p_ref[y], e1p_ref[(y + 15) % 16], e1p_ref[(y + 1) % 16], 2) + e1_ref[y]
         mg1_ref[y] = jnp.where(k1_ref[y] > 0.0, v, 0.0)
 
-    each(16, post1)
+    for y in ringed(8, 16, ring - 1):
+        post1(y)
 
     def mid0(y):
         e0p_ref[y] = e0x_ref[y] + mg1_ref[y // 2]
 
-    each(32, mid0)
+    for y in ringed(16, 32, ring):
+        mid0(y)
 
     def post0(i):
         y = i + 12 if i >= 18 else i
@@ -609,7 +618,8 @@
         v = jnp.where(k0x_ref[y] > 0.0, v, 0.0)
         corr_ref[i] = narrow(v)
 
-    each(YF, post0)
+    for y in ringed(16, YF, ring - 1):
+        post0(y)
 
 
 def gather_coarse(recv_ref, at, w_ref):
@@ -619,30 +629,38 @@
             w_ref[j, 4 * i : 4 * i + 4, :] = recv_ref[i * gy_total + j, at : at + 4, :]
 
 
-def gather_shares(recv_ref, count, wa_ref, wb_ref):
+def gather_shares(recv_ref, wa_ref, wb_ref):
     gy_total, gx_total = wa_ref.shape[0], wa_ref.shape[1] // 4
     for i in range(gx_total):
         for j in range(gy_total):
-            n = (i * gy_total + j) * count
-            wa_ref[j, 4 * i : 4 * i + 4, :] = recv_ref[n]
-            wb_ref[j, 4 * i : 4 * i + 4, :] = recv_ref[n + 1]
+            n = (i * gy_total + j) * 5
+            for half in range(2):
+                at = slice(4 * i + 2 * half, 4 * i + 2 * half + 2)
+                wa_ref[j, at, :] = recv_ref[n + half]
+                wb_ref[j, at, :] = recv_ref[n + 2 + half]
     for i in range(gx_total):
         for j in range(gy_total):
-            n = (i * gy_total + j) * count + 2
-            for ref, at in ((wa_ref, 0), (wb_ref, 2)):
-                if i + 1 < gx_total:
-                    ref[j, 4 * i + 4 : 4 * i + 5, :] += recv_ref[n, at : at + 1, :]
-                if i > 0:
-                    ref[j, 4 * i - 1 : 4 * i, :] += recv_ref[n, at + 1 : at + 2, :]
+            n = (i * gy_total + j) * 5 + 4
+            if i + 1 < gx_total:
+                wa_ref[j, 4 * i + 4 : 4 * i + 5, :] += recv_ref[n, 0:1, :]
+            if i > 0:
+                wa_ref[j, 4 * i - 1 : 4 * i, :] += recv_ref[n, 1:2, :]
     wb = wb_ref[...]
-    lane = lanes_of(wb) & 3
+    lane, row = lanes_of(wb) & 3, rows_of(wb) & 3
+    corner = jnp.where(
+        lane == 0, pltpu.roll(wb, LANES - 1, 2), jnp.where(lane == 3, pltpu.roll(wb, 1, 2), 0.0)
+    )
+    corner = jnp.where(row == 3, x_high(jnp.where(row == 0, corner, 0.0), 1), 0.0) + jnp.where(
+        row == 0, x_low(jnp.where(row == 3, corner, 0.0), 1), 0.0
+    )
+    wb = wb + corner
     zero = jnp.zeros_like(wb[0:1])
     above = jnp.concatenate([wb[1:], zero], axis=0)
     below = jnp.concatenate([zero, wb[:-1]], axis=0)
     return wa_ref[...] + (jnp.where(lane == 0, below, 0.0) + jnp.where(lane == 3, above, 0.0))
 
 
-def fine_sweep(src_ref, dst_ref, f1x_ref, livex_ref):
+def fine_sweep(src_ref, dst_ref, f1x_ref, livex_ref, ring):
     def row(y):
         region = 0 if y < 16 else 1 if y < 18 else 2
         live = livex_ref[region] > 0.0
@@ -650,7 +668,8 @@
         for o in range(8):
             dst_ref[o, y] = jnp.where(live, new[o], cur[o])
 
-    each(YF, row)
+    for y in ringed(16, YF, ring):
+        row(y)
 
 
 def middle_kernel(
@@ -662,7 +681,7 @@
     gather_coarse(recv_ref, 4, k2_ref)
     mg2 = coarse_solve(w_ref[...], k2_ref[...], pairs_ref)
     spread_coarse(mg2, table_ref, row_ref, m2_ref)
-    up_levels(m2_ref, e1_ref, k1_ref, mg1_ref, e0x_ref, k0x_ref, corr_ref, e1p_ref, e0p_ref)
+    up_levels(m2_ref, e1_ref, k1_ref, mg1_ref, e0x_ref, k0x_ref, corr_ref, e1p_ref, e0p_ref, 3)
 
     def first_sweep(y):
         live = livex_ref[0 if y < 16 else 1 if y < 18 else 2] > 0.0
@@ -673,7 +692,7 @@
         v_ref[y] = mean8(u2)
 
     each(YF, first_sweep)
-    fine_sweep(ub_ref, ua_ref, f1x_ref, livex_ref)
+    fine_sweep(ub_ref, ua_ref, f1x_ref, livex_ref, 1)
     own_live = livex_ref[0, 0:16, :] > 0.0
 
     def left(y):
@@ -696,46 +715,62 @@
     each(16, left)
 
 
+def coarse_kernel(recv_ref, k2_ref, m2_ref, w_ref, wb_ref, pairs_ref, table_ref, row_ref):
+    mg2 = coarse_solve(gather_shares(recv_ref, w_ref, wb_ref), k2_ref[...], pairs_ref)
+    spread_coarse(mg2, table_ref, row_ref, m2_ref)
+
+
+def box_rows(tables_ref, rows):
+    v = spread(tables_ref[8:9, :], rows)
+    return jnp.maximum(v.astype(jnp.int32) - 1, 0), v > 0.0, (lanes_of(v) & 1) == 1
+
+
+def settle_kernel(tables_ref, w4_ref, c4_ref, m4_ref):
+    idx, live_slot, odd = box_rows(tables_ref, 16)
+    for y in range(16):
+        rows = [w4_ref[o, y] for o in range(8)]
+        m4_ref[y] = mean8(rows)
+        for px in range(2):
+            for py in range(2):
+                o = px * 4 + py * 2
+                v = jnp.where(odd, lane_gather(rows[o + 1], idx), lane_gather(rows[o], idx))
+                c4_ref[2 * y + py, px] = jnp.where(live_slot, v, 0.0)
+
+
 def last_kernel(
-    site_ref, count_ref, recv_ref, k2_ref, e0_ref, exlo_ref, exhi_ref, eylo_ref, eyhi_ref, k0x_ref, k1_ref,
-    w4_ref, livex_ref,
+    tables_ref, m2_ref, e0_ref, exlo_ref, exhi_ref, eylo_ref, eyhi_ref, k0x_ref, k1_ref,
+    c4_ref, m4_ref, livex_ref,
     fine_ref, base_ref,
-    w_ref, pairs_ref, table_ref, row_ref, m2_ref, mg1_ref, e1p_ref, e0p_ref, corr_ref, ub_ref, c_ref,
-    wb_ref, e0x_ref, e1_ref,
+    mg1_ref, e1p_ref, e0p_ref, corr_ref, e0x_ref, e1_ref, g_ref, c_ref,
 ):
-    mg2 = coarse_solve(gather_shares(recv_ref, 3, w_ref, wb_ref), k2_ref[...], pairs_ref)
-    spread_coarse(mg2, table_ref, row_ref, m2_ref)
     assemble_base(e0x_ref, e0_ref, exlo_ref, exhi_ref, eylo_ref, eyhi_ref, 0, 0, ROWS_LAST)
-    down_level0(e0x_ref, k0x_ref, e1_ref, k1_ref, False)
-    up_levels(m2_ref, e1_ref, k1_ref, mg1_ref, e0x_ref, k0x_ref, corr_ref, e1p_ref, e0p_ref)
-
+    down_level0(e0x_ref, k0x_ref, e1_ref, k1_ref, False, 2)
+    up_levels(m2_ref, e1_ref, k1_ref, mg1_ref, e0x_ref, k0x_ref, corr_ref, e1p_ref, e0p_ref, 2)
+    idx = box_rows(tables_ref, 24)[0]
+    idx16, live_slot, odd = box_rows(tables_ref, 16)
     live = livex_ref[0, 0:16, :] > 0.0
+    for y in list(range(17)) + [YF - 1]:
+        g_ref[y] = lane_gather(corr_ref[y], idx)
 
     def row(y):
-        c, new = relax_copies(corr_ref, y, YF)
-        got = [w4_ref[o, y] + jnp.where(live, new[o][0:16], c[0:16]) for o in range(8)]
-        for o in range(8):
-            ub_ref[o, y] = got[o]
-        base_ref[pl.ds(y, 16, stride=16), :] = mean8(got)
+        below, above = (y + YF - 1) % YF, y + 1
+        c = corr_ref[y]
+        sides = (x_low(c, 1) + x_high(c, 1)) + (corr_ref[below] + corr_ref[above])
+        zlo, zhi = z_low(c, 1), z_high(c, 1)
+        mean = c * (2.0 / 3.0) + (sides + (zlo + zhi)) * (1.0 / 18.0)
+        base_ref[pl.ds(y, 16, stride=16), :] = m4_ref[y] + jnp.where(live, mean[0:16], c[0:16])
+        g = g_ref[y]
+        gx = x_low(g, 1)[0:16], x_high(g, 1)[0:16]
+        gy = g_ref[below, 0:16, :], g_ref[above, 0:16, :]
+        gz = jnp.where(odd, lane_gather(zhi[0:16], idx16), lane_gather(zlo[0:16], idx16))
+        base = g[0:16] * (2.0 / 3.0) + gz * NINTH
+        for px in range(2):
+            for py in range(2):
+                v = base + (gx[px] + gy[py]) * NINTH
+                v = c4_ref[2 * y + py, px] + jnp.where(live_slot, v, 0.0)
+                c_ref[2 * y + py, pl.ds(px, 16, stride=2), :] = v
 
     each(16, row)
-
-    lane = lax.broadcasted_iota(jnp.int32, (16, LANES), 1)
-    idx = jnp.zeros((16, LANES), jnp.int32)
-    for s in range(4):
-        idx = jnp.where((lane // 32) == s, site_ref[0, 0, s], idx)
-    idx = idx * 16 + (lane & 31) // 2
-    live_slot = (lane // 32) < count_ref[0, 0]
-    odd = (lane & 1) == 1
-
-    def pack(y):
-        for py in range(2):
-            for px in range(2):
-                o = px * 4 + py * 2
-                v = jnp.where(odd, lane_gather(ub_ref[o + 1, y], idx), lane_gather(ub_ref[o, y], idx))
-                c_ref[2 * y + py, pl.ds(px, 16, stride=2), :] = jnp.where(live_slot, v, 0.0)
-
-    each(16, pack)
     for xt in range(4):
         for t in range(8):
             rows, cols = slice(8 * xt, 8 * xt + 8), slice(t * LANES, (t + 1) * LANES)
@@ -794,20 +829,21 @@
     def beside(us):
         return pl.CostEstimate(flops=int(us * 1e6), bytes_accessed=int(us * 3e6), transcendentals=0)
 
-    fxlo, fxhi, fylo, fyhi = call(
-        faces_kernel, "faces", [tiles(17)] * 4, 2, 2, 0, [raw, raw, pltpu.SemaphoreType.DMA((2, 4))],
-    )(slot_site, box_count, fine_rhs, fine_beta)
+    tables = call(tables_kernel, "tables", [(16, LANES)], 2, 0, 0)(slot_site, box_count)[0]
+    fxlo, fxhi, fylo, fyhi, raw_f, raw_q = call(
+        faces_kernel, "faces", [tiles(17)] * 4 + [raw, raw], 0, 0, 3
+    )(tables, fine_rhs, fine_beta)
     rxlo, rxhi = from_sides(fxlo, fxhi, "gx")
     rylo, ryhi = from_sides(fylo, fyhi, "gy")
     f1, q = call(
-        boxes_kernel, "boxes", [octets, octets], 2, 0, 2, [rows, rows], beside(3)
-    )(slot_site, box_count, fine_rhs, fine_beta)
+        boxes_kernel, "boxes", [octets, octets], 0, 0, 3, [rows, rows], beside(3)
+    )(tables, raw_f, raw_q)
     e0, k0, ea, eb = call(
         first_kernel, "first_residual", [own, own, tiles(37), tiles(37)], 0, 0, 8, [fine_ext, x_side, y_side]
     )(f1, q, base_beta.reshape(256, LANES), rhs, rxlo, rxhi, rylo, ryhi)
     sa, sb = swap_pairs(ea, "gx", 0), swap_pairs(eb, "gx", 1)
     eylo, eyhi = call(
-        pack_y_first_kernel, "pack_y_first", [tiles(8 * ROWS_FIRST)] * 2, 0, 0, 4
+        pack_y_first_kernel, "pack_y_first", [tiles(4 * (ROWS_FIRST + ROWS_DIAGONAL))] * 2, 0, 0, 4
     )(e0, k0, sa, sb)
     sylo, syhi = from_sides(eylo, eyhi, "gy")
     f1x, livex, w2x = call(
@@ -828,16 +864,22 @@
     )(recv, e0x, k0x, e1, k1, f1x, w2x, livex, q, rhs)
     sxlo, sxhi = from_sides(exlo, exhi, "gx")
     send = call(
-        share_kernel, "share", [(devices * 3, 4, LANES)], 0, 0, 3,
-        [(24, 24, LANES), (12, 24, LANES), (2, 24, LANES)], beside(1),
+        share_kernel, "share", [(devices * 5, 2, LANES)], 0, 0, 3,
+        [(24, 24, LANES), (12, 24, LANES), (3, 24, LANES)], beside(1),
     )(e0, k0x, k1)[0]
     recv = lax.all_to_all(send, ("gx", "gy"), 0, 0, tiled=True)
+    c4, m4 = call(
+        settle_kernel, "settle", [(32, 2, 16, LANES), own], 0, 0, 2, (), beside(2)
+    )(tables, w4)
     eylo, eyhi = call(pack_y_kernel, "pack_y", [tiles(4 * ROWS_LAST)] * 2, 0, 0, 4)(recv, e0, sxlo, sxhi)
     sylo, syhi = from_sides(eylo, eyhi, "gy")
+    m2 = call(
+        coarse_kernel, "coarse", [(8, 32, LANES)], 0, 0, 2, [coarse, coarse] + up_scratch[1:4], beside(2)
+    )(recv, k2)[0]
     fine, base = call(
-        last_kernel, "last", [fine_rhs.shape, (256, LANES)], 2, 0, 11,
-        up_scratch + [octets, rows, coarse, wide, half],
-    )(slot_site, box_count, recv, k2, e0, sxlo, sxhi, sylo, syhi, k0x, k1, w4, livex)
+        last_kernel, "last", [fine_rhs.shape, (256, LANES)], 0, 0, 12,
+        [half, half, wide, (YF, XF, LANES), wide, half, (YF, XF, LANES), rows],
+    )(tables, m2, e0, sxlo, sxhi, sylo, syhi, k0x, k1, c4, m4, livex)
     return fine, base.reshape(base_rhs.shape)
 
 

time: 74 us -> 71.2 us (0.962)
  waiting for transfers between devices: 16.7 us -> 15.3 us
    ppermute x10, waiting for transfers between devices: 11 us -> 9.27 us  [step(): lax.ppermute(value, axis, [(i, (i + by) % count) for i in range(count)])]
    pallas_call x5 -> x8, Pallas kernels: 9.92 us -> 9.25 us  [the longest x1 3.53 us: local(): call(last_kernel, 'last', [fine_rhs.shape, (256, LANES)], 0, 0, 12, [half...]
    unnamed x12 -> x10, local copies, waits for them, and re-layouts: 2.74 us -> 2.73 us
  transfers between devices with their start and end apart: 13 -> 13, of which waited for: 5 -> 5; matrix products, arithmetic and copies ran while one was open for 0% -> 0% of each run, Pallas kernels for 5% -> 7%
where the time goes in v4:
time: 71.2 us; the launch traced here: 70.6 us
  starting transfers between devices  20.4 us (29%)
  Pallas kernels  16.7 us (23%)
  waiting for transfers between devices  15.3 us (21%)
  blocking collectives  13.9 us (20%)
  local copies, waits for them, and re-layouts  2.73 us (4%)
  between operations  1.46 us (2%)
    ppermute x10, starting transfers between devices, step(): lax.ppermute(value, axis, [(i, (i + by) % count) for i in range(count)])  17.1 us
    all_to_all x1, blocking collectives, local(): recv = lax.all_to_all(send, ('gx', 'gy'), 0, 0, tiled=True)  13.9 us
    ppermute x10, waiting for transfers between devices, step(): lax.ppermute(value, axis, [(i, (i + by) % count) for i in range(count)])  9.27 us
    ppermute x2, waiting for transfers between devices, swap_pairs(): lax.ppermute(value, axis, [(i, j if 0 <= j < count else i) for i, j in en...  6 us
    pallas_call x1, Pallas kernels, local(): call(last_kernel, 'last', [fine_rhs.shape, (256, LANES)], 0, 0, 12, [half...  3.53 us
    pallas_call x1, Pallas kernels, local(): call(middle_kernel, 'middle', [octets, coarse, own, tiles(16), tiles(16)]...  3.49 us
    unnamed x10, local copies, waits for them, and re-layouts  2.73 us
    all_to_all x1, starting transfers between devices, local(): recv = lax.all_to_all(send, ('gx', 'gy'), 0, 0, tiled=True)  2.58 us
  transfers between devices with their start and end apart: 13, of which 5 were waited for; matrix products, arithmetic and copies ran while one was open for 0% of the time, Pallas kernels for 7%

profile of v4, /device:TPU:0, one launch (start us, length us, event | category | flops | bytes accessed | tf_op | source)
XLA Modules:
  0.0 70.6 jit_solution(11635324815144015201)
XLA Ops:
  0.6 0.0 copy-start
  1.3 0.0 copy-start.4
  1.3 0.6 copy-done.4
  2.0 0.6 tables.1.tables_ref
  2.5 0.0 copy-start.1
  2.6 1.0 %copy-done.1 = f32[1,1,4,32,1024]{4,3,2,1,0:T(8,128)S(1)} copy-done((f32[1,1,4,32,1024]{4,3,2,1,0:T(8,128)S(1)}, f32[1,1,4,32,1024]{4,3,2,1,0:T(8,128)}, u32[]{:S(2)}) %copy-start.1) | copy-done | bytes 524312
  3.6 0.0 copy-start.2
  3.6 1.0 %copy-done.2 = f32[1,1,4,32,1024]{4,3,2,1,0:T(8,128)S(1)} copy-done((f32[1,1,4,32,1024]{4,3,2,1,0:T(8,128)S(1)}, f32[1,1,4,32,1024]{4,3,2,1,0:T(8,128)}, u32[]{:S(2)}) %copy-start.2) | copy-done | bytes 524312
  4.6 0.0 copy-start.3
  4.6 0.3 faces.1
  5.0 3.1 %collective-permute-start = (f32[17,8,128]{2,1,0:T(8,128)S(1)}, f32[17,8,128]{2,1,0:T(8,128)S(1)}, u32[]{:S(2)}, u32[]{:S(2)}) collective-permute-start(f32[17,8,128]{2,1,0:T(8,128)S(1)} %get-tuple-element.39), channel_id=1, source_target_pairs={{0,8},{8,16},{16,24},{24,0},{1,9},{9,17},{17,25},{25,1},{2,10},{10... | collective-permute-start | bytes 208904 | tf_op jit(solution)/shard_map/ppermute | solution.py:799
  8.0 2.1 %collective-permute-start.1 = (f32[17,8,128]{2,1,0:T(8,128)S(1)}, f32[17,8,128]{2,1,0:T(8,128)S(1)}, u32[]{:S(2)}, u32[]{:S(2)}) collective-permute-start(f32[17,8,128]{2,1,0:T(8,128)S(1)} %get-tuple-element.40), channel_id=1, source_target_pairs={{0,24},{8,0},{16,8},{24,16},{1,25},{9,1},{17,9},{25,17},{2,26},{10... | collective-permute-start | bytes 208904 | tf_op jit(solution)/shard_map/ppermute | solution.py:799
  10.1 0.0 collective-permute-start.2
  10.1 2.6 %collective-permute-start.3 = (f32[17,8,128]{2,1,0:T(8,128)S(1)}, f32[17,8,128]{2,1,0:T(8,128)S(1)}, u32[]{:S(2)}, u32[]{:S(2)}) collective-permute-start(f32[17,8,128]{2,1,0:T(8,128)S(1)} %get-tuple-element.42), channel_id=1, source_target_pairs={{0,7},{1,0},{2,1},{3,2},{4,3},{5,4},{6,5},{7,6},{8,15},{9,8},{10,9... | collective-permute-start | bytes 208904 | tf_op jit(solution)/shard_map/ppermute | solution.py:799
  12.8 1.8 %boxes.1 = (f32[8,16,16,128]{3,2,1,0:T(8,128)S(1)}, f32[8,16,16,128]{3,2,1,0:T(8,128)S(1)}) custom-call(f32[16,128]{1,0:T(8,128)S(1)} %tables.1.tables_ref, f32[4,32,1024]{2,1,0:T(8,128)S(1)} %get-tuple-element.35.raw_f_ref, f32[4,32,1024]{2,1,0:T(8,128)S(1)} %get-tuple-element.36.raw_q_ref), custom_call_target="tpu_custom_call" | custom-call | flops 3000000 | bytes 9000000 | tf_op jit(solution)/shard_map/boxes/pallas_call | solution.py:838
  14.6 0.0 collective-permute-done.rxlo_ref
  14.6 0.0 collective-permute-done.1.rxhi_ref
  14.6 0.2 collective-permute-done.2.rylo_ref
  14.8 0.0 collective-permute-done.3.ryhi_ref
  14.8 0.0 copy-done
  14.8 0.0 copy-done.3
  14.8 1.0 %first_residual.1 = (f32[16,16,128]{2,1,0:T(8,128)S(1)}, f32[16,16,128]{2,1,0:T(8,128)S(1)}, f32[37,8,128]{2,1,0:T(8,128)S(1)}, f32[37,8,128]{2,1,0:T(8,128)S(1)}) custom-call(f32[8,16,16,128]{3,2,1,0:T(8,128)S(1)} %get-tuple-element.37.f1_ref, f32[8,16,16,128]{3,2,1,0:T(8,128)S(1)} %get-tuple-element.38.q_ref, f32[256,128]{1,0:T(8,128)S(1)} %bitcast.5, ...), custom_call_target="tpu_custom_call" | custom-call | tf_op jit(solution)/shard_map/first_residual/pallas_call | solution.py:841
  15.8 0.1 collective-permute-start.4
  15.8 0.7 collective-permute-start.5
  16.5 6.0 %collective-permute-done.4.sa_ref.ea_ref = f32[37,8,128]{2,1,0:T(8,128)S(1)} collective-permute-done((f32[37,8,128]{2,1,0:T(8,128)S(1)}, f32[37,8,128]{2,1,0:T(8,128)S(1)}, u32[]{:S(2)}, u32[]{:S(2)}) %collective-permute-start.4) | collective-permute-done | bytes 151584 | tf_op jit(solution)/shard_map/ppermute | solution.py:805
  22.5 0.0 collective-permute-done.5.sb_ref.eb_ref
  22.6 0.1 collective-permute-start.6
  22.6 2.6 %collective-permute-start.7 = (f32[52,8,128]{2,1,0:T(8,128)S(1)}, f32[52,8,128]{2,1,0:T(8,128)S(1)}, u32[]{:S(2)}, u32[]{:S(2)}) collective-permute-start(f32[52,8,128]{2,1,0:T(8,128)S(1)} %get-tuple-element.49), channel_id=1, source_target_pairs={{0,7},{1,0},{2,1},{3,2},{4,3},{5,4},{6,5},{7,6},{8,15},{9,8},{10,9... | collective-permute-start | bytes 638984 | tf_op jit(solution)/shard_map/ppermute | solution.py:799
  25.3 1.5 %extend.1 = (f32[8,20,24,128]{3,2,1,0:T(8,128)S(1)}, f32[3,24,128]{2,1,0:T(8,128)S(1)}, f32[8,20,24,128]{3,2,1,0:T(8,128)S(1)}) custom-call(f32[8,16,16,128]{3,2,1,0:T(8,128)S(1)} %get-tuple-element.37.f1_ref, f32[8,16,16,128]{3,2,1,0:T(8,128)S(1)} %get-tuple-element.38.q_ref, f32[17,8,128]{2,1,0:T(8,128)S(1)} %collective-permute-done.rxlo_ref, ...), custom_call_target="tpu_custom_call" | custom-call | flops 2000000 | bytes 6000000 | tf_op jit(solution)/shard_map/extend/pallas_call | solution.py:849
  26.8 3.3 %collective-permute-done.6.eylo_ref = f32[52,8,128]{2,1,0:T(8,128)S(1)} collective-permute-done((f32[52,8,128]{2,1,0:T(8,128)S(1)}, f32[52,8,128]{2,1,0:T(8,128)S(1)}, u32[]{:S(2)}, u32[]{:S(2)}) %collective-permute-start.6) | collective-permute-done | bytes 213024 | tf_op jit(solution)/shard_map/ppermute | solution.py:799
  30.1 0.0 collective-permute-done.7.eyhi_ref
  30.1 1.5 %down_first.1 = (f32[32,8,128]{2,1,0:T(8,128)S(1)}, f32[32,32,128]{2,1,0:T(8,128)S(1)}, f32[32,32,128]{2,1,0:T(8,128)S(1)}, f32[16,32,128]{2,1,0:T(8,128)S(1)}, f32[16,32,128]{2,1,0:T(8,128)S(1)}) custom-call(f32[3,24,128]{2,1,0:T(8,128)S(1)} %get-tuple-element.45.live_ref.livex_ref, f32[16,16,128]{2,1,0:T(8,128)S(1)} %get-tuple-element.46.e0_ref, ...), custom_call_target="tpu_custom_call" | custom-call | tf_op jit(solution)/shard_map/down_first/pallas_call | solution.py:852
  31.6 13.9 %all_to_all.10.recv_ref = f32[32,8,128]{2,1,0:T(8,128)S(1)} all-to-all(f32[32,8,128]{2,1,0:T(8,128)S(1)} %get-tuple-element.50), channel_id=1, replica_groups=mesh['gx'=4,'gy'=8] {'gx','gy'}, dimensions={0} | all-to-all | bytes 262144 | tf_op jit(solution)/shard_map/all_to_all | solution.py:855
  45.5 3.5 %middle.1 = (f32[8,16,16,128]{3,2,1,0:T(8,128)S(1)}, f32[8,16,128]{2,1,0:T(8,128)S(1)}, f32[16,16,128]{2,1,0:T(8,128)S(1)}, f32[16,8,128]{2,1,0:T(8,128)S(1)}, f32[16,8,128]{2,1,0:T(8,128)S(1)}) custom-call(f32[32,8,128]{2,1,0:T(8,128)S(1)} %all_to_all.10.recv_ref, f32[32,32,128]{2,1,0:T(8,128)S(1)} %get-tuple-element.51.e0x_ref, ...), custom_call_target="tpu_custom_call" | custom-call | tf_op jit(solution)/shard_map/middle/pallas_call | solution.py:861
  49.0 1.3 %share.1 = f32[160,2,128]{2,1,0:T(2,128)} custom-call(f32[16,16,128]{2,1,0:T(8,128)S(1)} %get-tuple-element.57.e0_ref, f32[32,32,128]{2,1,0:T(8,128)S(1)} %get-tuple-element.52.k0x_ref, f32[16,32,128]{2,1,0:T(8,128)S(1)} %get-tuple-element.54.k1_ref), custom_call_target="tpu_custom_call" | custom-call | flops 1000000 | bytes 3000000 | tf_op jit(solution)/shard_map/share/pallas_call | solution.py:866
  50.4 2.6 %all-to-all-start.1 = ((f32[160,2,128]{2,1,0:T(2,128)}), f32[160,2,128]{2,1,0:T(2,128)S(1)}, u32[]{:S(2)}, u32[]{:S(2)}) async-start(f32[160,2,128]{2,1,0:T(2,128)} %share.1), calls=%async_computation.1 | async-start | bytes 327680 | tf_op jit(solution)/shard_map/all_to_all | solution.py:870
  52.9 1.7 %collective-permute-start.8 = (f32[16,8,128]{2,1,0:T(8,128)S(1)}, f32[16,8,128]{2,1,0:T(8,128)S(1)}, u32[]{:S(2)}, u32[]{:S(2)}) collective-permute-start(f32[16,8,128]{2,1,0:T(8,128)S(1)} %get-tuple-element.59), channel_id=1, source_target_pairs={{0,8},{8,16},{16,24},{24,0},{1,9},{9,17},{17,25},{25,1},{2,10},{10... | collective-permute-start | bytes 196616 | tf_op jit(solution)/shard_map/ppermute | solution.py:799
  54.7 2.1 %collective-permute-start.9 = (f32[16,8,128]{2,1,0:T(8,128)S(1)}, f32[16,8,128]{2,1,0:T(8,128)S(1)}, u32[]{:S(2)}, u32[]{:S(2)}) collective-permute-start(f32[16,8,128]{2,1,0:T(8,128)S(1)} %get-tuple-element.60), channel_id=1, source_target_pairs={{0,24},{8,0},{16,8},{24,16},{1,25},{9,1},{17,9},{25,17},{2,26},{10... | collective-permute-start | bytes 196616 | tf_op jit(solution)/shard_map/ppermute | solution.py:799
  56.8 5.3 %collective-permute-done.8.exlo_ref = f32[16,8,128]{2,1,0:T(8,128)S(1)} collective-permute-done((f32[16,8,128]{2,1,0:T(8,128)S(1)}, f32[16,8,128]{2,1,0:T(8,128)S(1)}, u32[]{:S(2)}, u32[]{:S(2)}) %collective-permute-start.8) | collective-permute-done | bytes 65568 | tf_op jit(solution)/shard_map/ppermute | solution.py:799
  62.2 0.0 collective-permute-done.9.exhi_ref
  62.2 0.0 all-to-all-done.1.recv_ref
  62.2 0.2 collective-permute-start.10
  62.4 2.5 %collective-permute-start.11 = (f32[20,8,128]{2,1,0:T(8,128)S(1)}, f32[20,8,128]{2,1,0:T(8,128)S(1)}, u32[]{:S(2)}, u32[]{:S(2)}) collective-permute-start(f32[20,8,128]{2,1,0:T(8,128)S(1)} %get-tuple-element.62), channel_id=1, source_target_pairs={{0,7},{1,0},{2,1},{3,2},{4,3},{5,4},{6,5},{7,6},{8,15},{9,8},{10,9... | collective-permute-start | bytes 245768 | tf_op jit(solution)/shard_map/ppermute | solution.py:799
  64.9 0.3 settle.1
  65.2 1.3 %coarse.1.m2_ref = f32[8,32,128]{2,1,0:T(8,128)S(1)} custom-call(f32[160,2,128]{2,1,0:T(2,128)S(1)} %all-to-all-done.1.recv_ref, f32[8,16,128]{2,1,0:T(8,128)S(1)} %get-tuple-element.58.k2_ref), custom_call_target="tpu_custom_call" | custom-call | flops 2000000 | bytes 6000000 | tf_op jit(solution)/shard_map/coarse/pallas_call | solution.py:876
  66.6 0.4 collective-permute-done.10.eylo_ref
  67.0 0.0 collective-permute-done.11.eyhi_ref
  67.0 3.5 %last.1 = (f32[1,1,4,32,1024]{4,3,2,1,0:T(8,128)}, f32[256,128]{1,0:T(8,128)}) custom-call(f32[16,128]{1,0:T(8,128)S(1)} %tables.1.tables_ref, f32[8,32,128]{2,1,0:T(8,128)S(1)} %coarse.1.m2_ref, f32[16,16,128]{2,1,0:T(8,128)S(1)} %get-tuple-element.57.e0_ref, f32[16,8,128]{2,1,0:T(8,128)S(1)} %collective-permute-done.8.exlo_ref, ...), custom_call_target="tpu_custom_call" | custom-call | tf_op jit(solution)/shard_map/last/pallas_call | solution.py:879
  (2 shorter events, 0.1 us)
Async XLA Ops:
  0.6 14.1 %copy-start = (f32[16,16,128]{2,1,0:T(8,128)S(1)}, f32[16,16,128]{2,1,0:T(8,128)}, u32[]{:S(2)}) copy-start(f32[16,16,128]{2,1,0:T(8,128)} %param.9) | copy-start | bytes 393220
  1.3 0.7 copy-start.4
  2.5 1.0 %copy-start.1 = (f32[1,1,4,32,1024]{4,3,2,1,0:T(8,128)S(1)}, f32[1,1,4,32,1024]{4,3,2,1,0:T(8,128)}, u32[]{:S(2)}) copy-start(f32[1,1,4,32,1024]{4,3,2,1,0:T(8,128)} %rhs_ref.1) | copy-start | bytes 1572868
  3.6 1.0 %copy-start.2 = (f32[1,1,4,32,1024]{4,3,2,1,0:T(8,128)S(1)}, f32[1,1,4,32,1024]{4,3,2,1,0:T(8,128)}, u32[]{:S(2)}) copy-start(f32[1,1,4,32,1024]{4,3,2,1,0:T(8,128)} %beta_ref.1) | copy-start | bytes 1572868
  4.6 10.1 %copy-start.3 = (f32[16,16,128]{2,1,0:T(8,128)S(1)}, f32[16,16,128]{2,1,0:T(8,128)}, u32[]{:S(2)}) copy-start(f32[16,16,128]{2,1,0:T(8,128)} %param.10) | copy-start | bytes 393220
  5.0 9.6 %collective-permute-start = (f32[17,8,128]{2,1,0:T(8,128)S(1)}, f32[17,8,128]{2,1,0:T(8,128)S(1)}, u32[]{:S(2)}, u32[]{:S(2)}) collective-permute-start(f32[17,8,128]{2,1,0:T(8,128)S(1)} %get-tuple-element.39), channel_id=1, source_target_pairs={{0,8},{8,16},{16,24},{24,0},{1,9},{9,17},{17,25},{25,1},{2,10},{10... | collective-permute-start | bytes 208904 | tf_op jit(solution)/shard_map/ppermute | solution.py:799
  8.0 6.6 %collective-permute-start.1 = (f32[17,8,128]{2,1,0:T(8,128)S(1)}, f32[17,8,128]{2,1,0:T(8,128)S(1)}, u32[]{:S(2)}, u32[]{:S(2)}) collective-permute-start(f32[17,8,128]{2,1,0:T(8,128)S(1)} %get-tuple-element.40), channel_id=1, source_target_pairs={{0,24},{8,0},{16,8},{24,16},{1,25},{9,1},{17,9},{25,17},{2,26},{10... | collective-permute-start | bytes 208904 | tf_op jit(solution)/shard_map/ppermute | solution.py:799
  10.1 4.6 %collective-permute-start.2 = (f32[17,8,128]{2,1,0:T(8,128)S(1)}, f32[17,8,128]{2,1,0:T(8,128)S(1)}, u32[]{:S(2)}, u32[]{:S(2)}) collective-permute-start(f32[17,8,128]{2,1,0:T(8,128)S(1)} %get-tuple-element.41), channel_id=1, source_target_pairs={{0,1},{1,2},{2,3},{3,4},{4,5},{5,6},{6,7},{7,0},{8,9},{9,10},{10,1... | collective-permute-start | bytes 208904 | tf_op jit(solution)/shard_map/ppermute | solution.py:799
  10.1 4.6 %collective-permute-start.3 = (f32[17,8,128]{2,1,0:T(8,128)S(1)}, f32[17,8,128]{2,1,0:T(8,128)S(1)}, u32[]{:S(2)}, u32[]{:S(2)}) collective-permute-start(f32[17,8,128]{2,1,0:T(8,128)S(1)} %get-tuple-element.42), channel_id=1, source_target_pairs={{0,7},{1,0},{2,1},{3,2},{4,3},{5,4},{6,5},{7,6},{8,15},{9,8},{10,9... | collective-permute-start | bytes 208904 | tf_op jit(solution)/shard_map/ppermute | solution.py:799
  15.8 6.8 %collective-permute-start.4 = (f32[37,8,128]{2,1,0:T(8,128)S(1)}, f32[37,8,128]{2,1,0:T(8,128)S(1)}, u32[]{:S(2)}, u32[]{:S(2)}) collective-permute-start(f32[37,8,128]{2,1,0:T(8,128)S(1)} %get-tuple-element.43), channel_id=1, source_target_pairs={{0,8},{8,0},{16,24},{24,16},{1,9},{9,1},{17,25},{25,17},{2,10},{10... | collective-permute-start | bytes 454664 | tf_op jit(solution)/shard_map/ppermute | solution.py:805
  15.8 6.7 %collective-permute-start.5 = (f32[37,8,128]{2,1,0:T(8,128)S(1)}, f32[37,8,128]{2,1,0:T(8,128)S(1)}, u32[]{:S(2)}, u32[]{:S(2)}) collective-permute-start(f32[37,8,128]{2,1,0:T(8,128)S(1)} %get-tuple-element.44), channel_id=1, source_target_pairs={{0,0},{8,16},{16,8},{24,24},{1,1},{9,17},{17,9},{25,25},{2,2},{10,... | collective-permute-start | bytes 454664 | tf_op jit(solution)/shard_map/ppermute | solution.py:805
  22.6 7.6 %collective-permute-start.6 = (f32[52,8,128]{2,1,0:T(8,128)S(1)}, f32[52,8,128]{2,1,0:T(8,128)S(1)}, u32[]{:S(2)}, u32[]{:S(2)}) collective-permute-start(f32[52,8,128]{2,1,0:T(8,128)S(1)} %get-tuple-element.48), channel_id=1, source_target_pairs={{0,1},{1,2},{2,3},{3,4},{4,5},{5,6},{6,7},{7,0},{8,9},{9,10},{10,1... | collective-permute-start | bytes 638984 | tf_op jit(solution)/shard_map/ppermute | solution.py:799
  22.6 7.5 %collective-permute-start.7 = (f32[52,8,128]{2,1,0:T(8,128)S(1)}, f32[52,8,128]{2,1,0:T(8,128)S(1)}, u32[]{:S(2)}, u32[]{:S(2)}) collective-permute-start(f32[52,8,128]{2,1,0:T(8,128)S(1)} %get-tuple-element.49), channel_id=1, source_target_pairs={{0,7},{1,0},{2,1},{3,2},{4,3},{5,4},{6,5},{7,6},{8,15},{9,8},{10,9... | collective-permute-start | bytes 638984 | tf_op jit(solution)/shard_map/ppermute | solution.py:799
  50.4 11.8 %all-to-all-start.1 = ((f32[160,2,128]{2,1,0:T(2,128)}), f32[160,2,128]{2,1,0:T(2,128)S(1)}, u32[]{:S(2)}, u32[]{:S(2)}) async-start(f32[160,2,128]{2,1,0:T(2,128)} %share.1), calls=%async_computation.1 | async-start | bytes 327680 | tf_op jit(solution)/shard_map/all_to_all | solution.py:870
  52.9 9.2 %collective-permute-start.8 = (f32[16,8,128]{2,1,0:T(8,128)S(1)}, f32[16,8,128]{2,1,0:T(8,128)S(1)}, u32[]{:S(2)}, u32[]{:S(2)}) collective-permute-start(f32[16,8,128]{2,1,0:T(8,128)S(1)} %get-tuple-element.59), channel_id=1, source_target_pairs={{0,8},{8,16},{16,24},{24,0},{1,9},{9,17},{17,25},{25,1},{2,10},{10... | collective-permute-start | bytes 196616 | tf_op jit(solution)/shard_map/ppermute | solution.py:799
  54.7 7.5 %collective-permute-start.9 = (f32[16,8,128]{2,1,0:T(8,128)S(1)}, f32[16,8,128]{2,1,0:T(8,128)S(1)}, u32[]{:S(2)}, u32[]{:S(2)}) collective-permute-start(f32[16,8,128]{2,1,0:T(8,128)S(1)} %get-tuple-element.60), channel_id=1, source_target_pairs={{0,24},{8,0},{16,8},{24,16},{1,25},{9,1},{17,9},{25,17},{2,26},{10... | collective-permute-start | bytes 196616 | tf_op jit(solution)/shard_map/ppermute | solution.py:799
  62.2 4.8 %collective-permute-start.10 = (f32[20,8,128]{2,1,0:T(8,128)S(1)}, f32[20,8,128]{2,1,0:T(8,128)S(1)}, u32[]{:S(2)}, u32[]{:S(2)}) collective-permute-start(f32[20,8,128]{2,1,0:T(8,128)S(1)} %get-tuple-element.61), channel_id=1, source_target_pairs={{0,1},{1,2},{2,3},{3,4},{4,5},{5,6},{6,7},{7,0},{8,9},{9,10},{10,1... | collective-permute-start | bytes 245768 | tf_op jit(solution)/shard_map/ppermute | solution.py:799
  62.4 4.6 %collective-permute-start.11 = (f32[20,8,128]{2,1,0:T(8,128)S(1)}, f32[20,8,128]{2,1,0:T(8,128)S(1)}, u32[]{:S(2)}, u32[]{:S(2)}) collective-permute-start(f32[20,8,128]{2,1,0:T(8,128)S(1)} %get-tuple-element.62), channel_id=1, source_target_pairs={{0,7},{1,0},{2,1},{3,2},{4,3},{5,4},{6,5},{7,6},{8,15},{9,8},{10,9... | collective-permute-start | bytes 245768 | tf_op jit(solution)/shard_map/ppermute | solution.py:799

commit v5 on v4

--- a/solution.py
+++ b/solution.py
@@ -344,41 +344,64 @@
     each(YF, sweep)
 
 
+def whole_corner(away, near):
+    return away <= near
+
+
 def pack_y(sources, eylo_ref, eyhi_ref):
     lo_here, hi_here = inside("gx")
+    row8 = lax.broadcasted_iota(jnp.int32, (8, LANES), 0)
     n = 0
-    for own_ref, exlo_ref, exhi_ref, x_at, rows in sources:
-        for y in range(rows):
-            for out, at in ((eylo_ref, y), (eyhi_ref, 16 - rows + y)):
+    for own_ref, exlo_ref, exhi_ref, x_at, rows, near in sources:
+        for away in range(1, rows + 1):
+            for out, at in ((eylo_ref, away - 1), (eyhi_ref, 16 - away)):
                 v = own_ref[at]
                 out[n] = v[0:8]
                 out[n + 1] = v[8:16]
-                out[n + 2] = kept(hi_here, exhi_ref[x_at + at])
-                out[n + 3] = kept(lo_here, exlo_ref[x_at + at])
-            n += 4
+                hi, lo = kept(hi_here, exhi_ref[x_at + at]), kept(lo_here, exlo_ref[x_at + at])
+                if whole_corner(away, near):
+                    out[n + 2] = hi
+                    out[n + 3] = lo
+                else:
+                    out[n + 2] = jnp.where(row8 < 4, hi, lo)
+            n += 4 if whole_corner(away, near) else 3
+
+
+def packed_tiles(rows, near):
+    return sum(4 if whole_corner(away, near) else 3 for away in range(1, rows + 1))
 
 
 def pack_y_first_kernel(e0_ref, k0_ref, ea_ref, eb_ref, eylo_ref, eyhi_ref):
     exlo_ref, exhi_ref = Swapped(eb_ref, ea_ref), Swapped(ea_ref, eb_ref)
-    sources = (e0_ref, exlo_ref, exhi_ref, 0, ROWS_FIRST), (k0_ref, exlo_ref, exhi_ref, 16, ROWS_DIAGONAL)
+    sources = (e0_ref, exlo_ref, exhi_ref, 0, ROWS_FIRST, 2), (k0_ref, exlo_ref, exhi_ref, 16, ROWS_DIAGONAL, 0)
     pack_y(sources, eylo_ref, eyhi_ref)
 
 
 def pack_y_kernel(recv_ref, e0_ref, exlo_ref, exhi_ref, eylo_ref, eyhi_ref):
-    pack_y(((e0_ref, exlo_ref, exhi_ref, 0, ROWS_LAST),), eylo_ref, eyhi_ref)
-
-
-def assemble_base(dst_ref, own_ref, exlo_ref, exhi_ref, eylo_ref, eyhi_ref, x_at, y_at, rows):
+    pack_y(((e0_ref, exlo_ref, exhi_ref, 0, ROWS_LAST, 2),), eylo_ref, eyhi_ref)
+
+
+def assemble_base(dst_ref, own_ref, exlo_ref, exhi_ref, eylo_ref, eyhi_ref, x_at, y_at, rows, near):
     xlo_here, xhi_here = inside("gx")
     ylo_here, yhi_here = inside("gy")
     for y in range(16):
         dst_ref[y, 0:16, :] = own_ref[y]
         dst_ref[y, 16:24, :] = kept(xhi_here, exhi_ref[x_at + y])
         dst_ref[y, 24:32, :] = kept(xlo_here, exlo_ref[x_at + y])
-    for y in range(rows):
-        for t in range(4):
-            dst_ref[16 + y, 8 * t : 8 * t + 8, :] = kept(yhi_here, eyhi_ref[y_at + y * 4 + t])
-            dst_ref[32 - rows + y, 8 * t : 8 * t + 8, :] = kept(ylo_here, eylo_ref[y_at + y * 4 + t])
+    row8 = lax.broadcasted_iota(jnp.int32, (8, LANES), 0)
+    n = y_at
+    for away in range(1, rows + 1):
+        for ref, here, at in ((eyhi_ref, yhi_here, 15 + away), (eylo_ref, ylo_here, 32 - away)):
+            dst_ref[at, 0:8, :] = kept(here, ref[n])
+            dst_ref[at, 8:16, :] = kept(here, ref[n + 1])
+            side = kept(here, ref[n + 2])
+            if whole_corner(away, near):
+                dst_ref[at, 16:24, :] = side
+                dst_ref[at, 24:32, :] = kept(here, ref[n + 3])
+            else:
+                dst_ref[at, 16:24, :] = jnp.where(row8 < 4, side, 0.0)
+                dst_ref[at, 24:32, :] = jnp.where(row8 < 4, 0.0, side)
+        n += 4 if whole_corner(away, near) else 3
     for y in range(16 + rows, 32 - rows):
         dst_ref[y] = jnp.zeros((32, LANES), F32)
 
@@ -439,9 +462,10 @@
     send_ref, e0x_ref, k0x_ref, e1_ref, k1_ref, pack_ref,
 ):
     exlo_ref, exhi_ref = Swapped(eb_ref, ea_ref), Swapped(ea_ref, eb_ref)
-    assemble_base(e0x_ref, e0_ref, exlo_ref, exhi_ref, eylo_ref, eyhi_ref, 0, 0, ROWS_FIRST)
+    assemble_base(e0x_ref, e0_ref, exlo_ref, exhi_ref, eylo_ref, eyhi_ref, 0, 0, ROWS_FIRST, 2)
     assemble_base(
-        k0x_ref, k0_ref, exlo_ref, exhi_ref, eylo_ref, eyhi_ref, 16, 4 * ROWS_FIRST, ROWS_DIAGONAL
+        k0x_ref, k0_ref, exlo_ref, exhi_ref, eylo_ref, eyhi_ref, 16, packed_tiles(ROWS_FIRST, 2),
+        ROWS_DIAGONAL, 0,
     )
     down_level0(e0x_ref, k0x_ref, e1_ref, k1_ref, True, 4)
     r2 = down_level1(e1_ref, k1_ref, pack_ref)
@@ -743,7 +767,7 @@
     fine_ref, base_ref,
     mg1_ref, e1p_ref, e0p_ref, corr_ref, e0x_ref, e1_ref, g_ref, c_ref,
 ):
-    assemble_base(e0x_ref, e0_ref, exlo_ref, exhi_ref, eylo_ref, eyhi_ref, 0, 0, ROWS_LAST)
+    assemble_base(e0x_ref, e0_ref, exlo_ref, exhi_ref, eylo_ref, eyhi_ref, 0, 0, ROWS_LAST, 2)
     down_level0(e0x_ref, k0x_ref, e1_ref, k1_ref, False, 2)
     up_levels(m2_ref, e1_ref, k1_ref, mg1_ref, e0x_ref, k0x_ref, corr_ref, e1p_ref, e0p_ref, 2)
     idx = box_rows(tables_ref, 24)[0]
@@ -843,7 +867,7 @@
     )(f1, q, base_beta.reshape(256, LANES), rhs, rxlo, rxhi, rylo, ryhi)
     sa, sb = swap_pairs(ea, "gx", 0), swap_pairs(eb, "gx", 1)
     eylo, eyhi = call(
-        pack_y_first_kernel, "pack_y_first", [tiles(4 * (ROWS_FIRST + ROWS_DIAGONAL))] * 2, 0, 0, 4
+        pack_y_first_kernel, "pack_y_first", [tiles(packed_tiles(ROWS_FIRST, 2) + packed_tiles(ROWS_DIAGONAL, 0))] * 2, 0, 0, 4
     )(e0, k0, sa, sb)
     sylo, syhi = from_sides(eylo, eyhi, "gy")
     f1x, livex, w2x = call(
@@ -871,7 +895,7 @@
     c4, m4 = call(
         settle_kernel, "settle", [(32, 2, 16, LANES), own], 0, 0, 2, (), beside(2)
     )(tables, w4)
-    eylo, eyhi = call(pack_y_kernel, "pack_y", [tiles(4 * ROWS_LAST)] * 2, 0, 0, 4)(recv, e0, sxlo, sxhi)
+    eylo, eyhi = call(pack_y_kernel, "pack_y", [tiles(packed_tiles(ROWS_LAST, 2))] * 2, 0, 0, 4)(recv, e0, sxlo, sxhi)
     sylo, syhi = from_sides(eylo, eyhi, "gy")
     m2 = call(
         coarse_kernel, "coarse", [(8, 32, LANES)], 0, 0, 2, [coarse, coarse] + up_scratch[1:4], beside(2)

time: 71.2 us -> 70.1 us (0.985)
  waiting for transfers between devices: 15.3 us -> 14.2 us
    ppermute x10, waiting for transfers between devices: 9.27 us -> 8.17 us  [step(): lax.ppermute(value, axis, [(i, (i + by) % count) for i in range(count)])]
where the time goes in v5:
time: 70.1 us; the launch traced here: 69.4 us
  starting transfers between devices  20.4 us (29%)
  Pallas kernels  16.7 us (24%)
  waiting for transfers between devices  14.2 us (20%)
  blocking collectives  13.9 us (20%)
  local copies, waits for them, and re-layouts  2.73 us (4%)
  between operations  1.46 us (2%)
    ppermute x10, starting transfers between devices, step(): lax.ppermute(value, axis, [(i, (i + by) % count) for i in range(count)])  17.1 us
    all_to_all x1, blocking collectives, local(): recv = lax.all_to_all(send, ('gx', 'gy'), 0, 0, tiled=True)  13.9 us
    ppermute x10, waiting for transfers between devices, step(): lax.ppermute(value, axis, [(i, (i + by) % count) for i in range(count)])  8.17 us
    ppermute x2, waiting for transfers between devices, swap_pairs(): lax.ppermute(value, axis, [(i, j if 0 <= j < count else i) for i, j in en...  6 us
    pallas_call x1, Pallas kernels, local(): call(last_kernel, 'last', [fine_rhs.shape, (256, LANES)], 0, 0, 12, [half...  3.53 us
    pallas_call x1, Pallas kernels, local(): call(middle_kernel, 'middle', [octets, coarse, own, tiles(16), tiles(16)]...  3.49 us
    unnamed x10, local copies, waits for them, and re-layouts  2.73 us
    all_to_all x1, starting transfers between devices, local(): recv = lax.all_to_all(send, ('gx', 'gy'), 0, 0, tiled=True)  2.58 us
  transfers between devices with their start and end apart: 13, of which 5 were waited for; matrix products, arithmetic and copies ran while one was open for 0% of the time, Pallas kernels for 7%

profile of v5, /device:TPU:0, one launch (start us, length us, event | category | flops | bytes accessed | tf_op | source)
XLA Modules:
  0.0 69.4 jit_solution(3366961379951402366)
XLA Ops:
  0.6 0.0 copy-start
  1.3 0.0 copy-start.4
  1.3 0.6 copy-done.4
  2.0 0.6 tables.1.tables_ref
  2.5 0.0 copy-start.1
  2.6 1.0 %copy-done.1 = f32[1,1,4,32,1024]{4,3,2,1,0:T(8,128)S(1)} copy-done((f32[1,1,4,32,1024]{4,3,2,1,0:T(8,128)S(1)}, f32[1,1,4,32,1024]{4,3,2,1,0:T(8,128)}, u32[]{:S(2)}) %copy-start.1) | copy-done | bytes 524312
  3.6 0.0 copy-start.2
  3.6 1.0 %copy-done.2 = f32[1,1,4,32,1024]{4,3,2,1,0:T(8,128)S(1)} copy-done((f32[1,1,4,32,1024]{4,3,2,1,0:T(8,128)S(1)}, f32[1,1,4,32,1024]{4,3,2,1,0:T(8,128)}, u32[]{:S(2)}) %copy-start.2) | copy-done | bytes 524312
  4.6 0.0 copy-start.3
  4.6 0.3 faces.1
  5.0 3.1 %collective-permute-start = (f32[17,8,128]{2,1,0:T(8,128)S(1)}, f32[17,8,128]{2,1,0:T(8,128)S(1)}, u32[]{:S(2)}, u32[]{:S(2)}) collective-permute-start(f32[17,8,128]{2,1,0:T(8,128)S(1)} %get-tuple-element.39), channel_id=1, source_target_pairs={{0,8},{8,16},{16,24},{24,0},{1,9},{9,17},{17,25},{25,1},{2,10},{10... | collective-permute-start | bytes 208904 | tf_op jit(solution)/shard_map/ppermute | solution.py:823
  8.0 2.1 %collective-permute-start.1 = (f32[17,8,128]{2,1,0:T(8,128)S(1)}, f32[17,8,128]{2,1,0:T(8,128)S(1)}, u32[]{:S(2)}, u32[]{:S(2)}) collective-permute-start(f32[17,8,128]{2,1,0:T(8,128)S(1)} %get-tuple-element.40), channel_id=1, source_target_pairs={{0,24},{8,0},{16,8},{24,16},{1,25},{9,1},{17,9},{25,17},{2,26},{10... | collective-permute-start | bytes 208904 | tf_op jit(solution)/shard_map/ppermute | solution.py:823
  10.1 0.0 collective-permute-start.2
  10.1 2.6 %collective-permute-start.3 = (f32[17,8,128]{2,1,0:T(8,128)S(1)}, f32[17,8,128]{2,1,0:T(8,128)S(1)}, u32[]{:S(2)}, u32[]{:S(2)}) collective-permute-start(f32[17,8,128]{2,1,0:T(8,128)S(1)} %get-tuple-element.42), channel_id=1, source_target_pairs={{0,7},{1,0},{2,1},{3,2},{4,3},{5,4},{6,5},{7,6},{8,15},{9,8},{10,9... | collective-permute-start | bytes 208904 | tf_op jit(solution)/shard_map/ppermute | solution.py:823
  12.8 1.8 %boxes.1 = (f32[8,16,16,128]{3,2,1,0:T(8,128)S(1)}, f32[8,16,16,128]{3,2,1,0:T(8,128)S(1)}) custom-call(f32[16,128]{1,0:T(8,128)S(1)} %tables.1.tables_ref, f32[4,32,1024]{2,1,0:T(8,128)S(1)} %get-tuple-element.35.raw_f_ref, f32[4,32,1024]{2,1,0:T(8,128)S(1)} %get-tuple-element.36.raw_q_ref), custom_call_target="tpu_custom_call" | custom-call | flops 3000000 | bytes 9000000 | tf_op jit(solution)/shard_map/boxes/pallas_call | solution.py:862
  14.6 0.0 collective-permute-done.rxlo_ref
  14.6 0.0 collective-permute-done.1.rxhi_ref
  14.6 0.2 collective-permute-done.2.rylo_ref
  14.8 0.0 collective-permute-done.3.ryhi_ref
  14.8 0.0 copy-done
  14.8 0.0 copy-done.3
  14.8 1.0 %first_residual.1 = (f32[16,16,128]{2,1,0:T(8,128)S(1)}, f32[16,16,128]{2,1,0:T(8,128)S(1)}, f32[37,8,128]{2,1,0:T(8,128)S(1)}, f32[37,8,128]{2,1,0:T(8,128)S(1)}) custom-call(f32[8,16,16,128]{3,2,1,0:T(8,128)S(1)} %get-tuple-element.37.f1_ref, f32[8,16,16,128]{3,2,1,0:T(8,128)S(1)} %get-tuple-element.38.q_ref, f32[256,128]{1,0:T(8,128)S(1)} %bitcast.5, ...), custom_call_target="tpu_custom_call" | custom-call | tf_op jit(solution)/shard_map/first_residual/pallas_call | solution.py:865
  15.8 0.1 collective-permute-start.4
  15.8 0.7 collective-permute-start.5
  16.5 6.0 %collective-permute-done.4.sa_ref.ea_ref = f32[37,8,128]{2,1,0:T(8,128)S(1)} collective-permute-done((f32[37,8,128]{2,1,0:T(8,128)S(1)}, f32[37,8,128]{2,1,0:T(8,128)S(1)}, u32[]{:S(2)}, u32[]{:S(2)}) %collective-permute-start.4) | collective-permute-done | bytes 151584 | tf_op jit(solution)/shard_map/ppermute | solution.py:829
  22.5 0.0 collective-permute-done.5.sb_ref.eb_ref
  22.6 0.1 collective-permute-start.6
  22.6 2.6 %collective-permute-start.7 = (f32[41,8,128]{2,1,0:T(8,128)S(1)}, f32[41,8,128]{2,1,0:T(8,128)S(1)}, u32[]{:S(2)}, u32[]{:S(2)}) collective-permute-start(f32[41,8,128]{2,1,0:T(8,128)S(1)} %get-tuple-element.49), channel_id=1, source_target_pairs={{0,7},{1,0},{2,1},{3,2},{4,3},{5,4},{6,5},{7,6},{8,15},{9,8},{10,9... | collective-permute-start | bytes 503816 | tf_op jit(solution)/shard_map/ppermute | solution.py:823
  25.3 1.5 %extend.1 = (f32[8,20,24,128]{3,2,1,0:T(8,128)S(1)}, f32[3,24,128]{2,1,0:T(8,128)S(1)}, f32[8,20,24,128]{3,2,1,0:T(8,128)S(1)}) custom-call(f32[8,16,16,128]{3,2,1,0:T(8,128)S(1)} %get-tuple-element.37.f1_ref, f32[8,16,16,128]{3,2,1,0:T(8,128)S(1)} %get-tuple-element.38.q_ref, f32[17,8,128]{2,1,0:T(8,128)S(1)} %collective-permute-done.rxlo_ref, ...), custom_call_target="tpu_custom_call" | custom-call | flops 2000000 | bytes 6000000 | tf_op jit(solution)/shard_map/extend/pallas_call | solution.py:873
  26.8 2.4 %collective-permute-done.6.eylo_ref = f32[41,8,128]{2,1,0:T(8,128)S(1)} collective-permute-done((f32[41,8,128]{2,1,0:T(8,128)S(1)}, f32[41,8,128]{2,1,0:T(8,128)S(1)}, u32[]{:S(2)}, u32[]{:S(2)}) %collective-permute-start.6) | collective-permute-done | bytes 167968 | tf_op jit(solution)/shard_map/ppermute | solution.py:823
  29.2 0.0 collective-permute-done.7.eyhi_ref
  29.2 1.5 %down_first.1 = (f32[32,8,128]{2,1,0:T(8,128)S(1)}, f32[32,32,128]{2,1,0:T(8,128)S(1)}, f32[32,32,128]{2,1,0:T(8,128)S(1)}, f32[16,32,128]{2,1,0:T(8,128)S(1)}, f32[16,32,128]{2,1,0:T(8,128)S(1)}) custom-call(f32[3,24,128]{2,1,0:T(8,128)S(1)} %get-tuple-element.45.live_ref.livex_ref, f32[16,16,128]{2,1,0:T(8,128)S(1)} %get-tuple-element.46.e0_ref, ...), custom_call_target="tpu_custom_call" | custom-call | tf_op jit(solution)/shard_map/down_first/pallas_call | solution.py:876
  30.6 13.9 %all_to_all.10.recv_ref = f32[32,8,128]{2,1,0:T(8,128)S(1)} all-to-all(f32[32,8,128]{2,1,0:T(8,128)S(1)} %get-tuple-element.50), channel_id=1, replica_groups=mesh['gx'=4,'gy'=8] {'gx','gy'}, dimensions={0} | all-to-all | bytes 262144 | tf_op jit(solution)/shard_map/all_to_all | solution.py:879
  44.6 3.5 %middle.1 = (f32[8,16,16,128]{3,2,1,0:T(8,128)S(1)}, f32[8,16,128]{2,1,0:T(8,128)S(1)}, f32[16,16,128]{2,1,0:T(8,128)S(1)}, f32[16,8,128]{2,1,0:T(8,128)S(1)}, f32[16,8,128]{2,1,0:T(8,128)S(1)}) custom-call(f32[32,8,128]{2,1,0:T(8,128)S(1)} %all_to_all.10.recv_ref, f32[32,32,128]{2,1,0:T(8,128)S(1)} %get-tuple-element.51.e0x_ref, ...), custom_call_target="tpu_custom_call" | custom-call | tf_op jit(solution)/shard_map/middle/pallas_call | solution.py:885
  48.1 1.3 %share.1 = f32[160,2,128]{2,1,0:T(2,128)} custom-call(f32[16,16,128]{2,1,0:T(8,128)S(1)} %get-tuple-element.57.e0_ref, f32[32,32,128]{2,1,0:T(8,128)S(1)} %get-tuple-element.52.k0x_ref, f32[16,32,128]{2,1,0:T(8,128)S(1)} %get-tuple-element.54.k1_ref), custom_call_target="tpu_custom_call" | custom-call | flops 1000000 | bytes 3000000 | tf_op jit(solution)/shard_map/share/pallas_call | solution.py:890
  49.4 2.6 %all-to-all-start.1 = ((f32[160,2,128]{2,1,0:T(2,128)}), f32[160,2,128]{2,1,0:T(2,128)S(1)}, u32[]{:S(2)}, u32[]{:S(2)}) async-start(f32[160,2,128]{2,1,0:T(2,128)} %share.1), calls=%async_computation.1 | async-start | bytes 327680 | tf_op jit(solution)/shard_map/all_to_all | solution.py:894
  52.0 1.7 %collective-permute-start.8 = (f32[16,8,128]{2,1,0:T(8,128)S(1)}, f32[16,8,128]{2,1,0:T(8,128)S(1)}, u32[]{:S(2)}, u32[]{:S(2)}) collective-permute-start(f32[16,8,128]{2,1,0:T(8,128)S(1)} %get-tuple-element.59), channel_id=1, source_target_pairs={{0,8},{8,16},{16,24},{24,0},{1,9},{9,17},{17,25},{25,1},{2,10},{10... | collective-permute-start | bytes 196616 | tf_op jit(solution)/shard_map/ppermute | solution.py:823
  53.7 2.1 %collective-permute-start.9 = (f32[16,8,128]{2,1,0:T(8,128)S(1)}, f32[16,8,128]{2,1,0:T(8,128)S(1)}, u32[]{:S(2)}, u32[]{:S(2)}) collective-permute-start(f32[16,8,128]{2,1,0:T(8,128)S(1)} %get-tuple-element.60), channel_id=1, source_target_pairs={{0,24},{8,0},{16,8},{24,16},{1,25},{9,1},{17,9},{25,17},{2,26},{10... | collective-permute-start | bytes 196616 | tf_op jit(solution)/shard_map/ppermute | solution.py:823
  55.8 5.3 %collective-permute-done.8.exlo_ref = f32[16,8,128]{2,1,0:T(8,128)S(1)} collective-permute-done((f32[16,8,128]{2,1,0:T(8,128)S(1)}, f32[16,8,128]{2,1,0:T(8,128)S(1)}, u32[]{:S(2)}, u32[]{:S(2)}) %collective-permute-start.8) | collective-permute-done | bytes 65568 | tf_op jit(solution)/shard_map/ppermute | solution.py:823
  61.2 0.0 collective-permute-done.9.exhi_ref
  61.2 0.0 all-to-all-done.1.recv_ref
  61.2 0.2 collective-permute-start.10
  61.4 2.5 %collective-permute-start.11 = (f32[17,8,128]{2,1,0:T(8,128)S(1)}, f32[17,8,128]{2,1,0:T(8,128)S(1)}, u32[]{:S(2)}, u32[]{:S(2)}) collective-permute-start(f32[17,8,128]{2,1,0:T(8,128)S(1)} %get-tuple-element.62), channel_id=1, source_target_pairs={{0,7},{1,0},{2,1},{3,2},{4,3},{5,4},{6,5},{7,6},{8,15},{9,8},{10,9... | collective-permute-start | bytes 208904 | tf_op jit(solution)/shard_map/ppermute | solution.py:823
  63.9 0.3 settle.1
  64.3 1.3 %coarse.1.m2_ref = f32[8,32,128]{2,1,0:T(8,128)S(1)} custom-call(f32[160,2,128]{2,1,0:T(2,128)S(1)} %all-to-all-done.1.recv_ref, f32[8,16,128]{2,1,0:T(8,128)S(1)} %get-tuple-element.58.k2_ref), custom_call_target="tpu_custom_call" | custom-call | flops 2000000 | bytes 6000000 | tf_op jit(solution)/shard_map/coarse/pallas_call | solution.py:900
  65.6 0.3 collective-permute-done.10.eylo_ref
  65.9 0.0 collective-permute-done.11.eyhi_ref
  65.9 3.5 %last.1 = (f32[1,1,4,32,1024]{4,3,2,1,0:T(8,128)}, f32[256,128]{1,0:T(8,128)}) custom-call(f32[16,128]{1,0:T(8,128)S(1)} %tables.1.tables_ref, f32[8,32,128]{2,1,0:T(8,128)S(1)} %coarse.1.m2_ref, f32[16,16,128]{2,1,0:T(8,128)S(1)} %get-tuple-element.57.e0_ref, f32[16,8,128]{2,1,0:T(8,128)S(1)} %collective-permute-done.8.exlo_ref, ...), custom_call_target="tpu_custom_call" | custom-call | tf_op jit(solution)/shard_map/last/pallas_call | solution.py:903
  (2 shorter events, 0.1 us)
Async XLA Ops:
  0.6 14.1 %copy-start = (f32[16,16,128]{2,1,0:T(8,128)S(1)}, f32[16,16,128]{2,1,0:T(8,128)}, u32[]{:S(2)}) copy-start(f32[16,16,128]{2,1,0:T(8,128)} %param.9) | copy-start | bytes 393220
  1.3 0.7 copy-start.4
  2.5 1.0 %copy-start.1 = (f32[1,1,4,32,1024]{4,3,2,1,0:T(8,128)S(1)}, f32[1,1,4,32,1024]{4,3,2,1,0:T(8,128)}, u32[]{:S(2)}) copy-start(f32[1,1,4,32,1024]{4,3,2,1,0:T(8,128)} %rhs_ref.1) | copy-start | bytes 1572868
  3.6 1.0 %copy-start.2 = (f32[1,1,4,32,1024]{4,3,2,1,0:T(8,128)S(1)}, f32[1,1,4,32,1024]{4,3,2,1,0:T(8,128)}, u32[]{:S(2)}) copy-start(f32[1,1,4,32,1024]{4,3,2,1,0:T(8,128)} %beta_ref.1) | copy-start | bytes 1572868
  4.6 10.1 %copy-start.3 = (f32[16,16,128]{2,1,0:T(8,128)S(1)}, f32[16,16,128]{2,1,0:T(8,128)}, u32[]{:S(2)}) copy-start(f32[16,16,128]{2,1,0:T(8,128)} %param.10) | copy-start | bytes 393220
  5.0 9.6 %collective-permute-start = (f32[17,8,128]{2,1,0:T(8,128)S(1)}, f32[17,8,128]{2,1,0:T(8,128)S(1)}, u32[]{:S(2)}, u32[]{:S(2)}) collective-permute-start(f32[17,8,128]{2,1,0:T(8,128)S(1)} %get-tuple-element.39), channel_id=1, source_target_pairs={{0,8},{8,16},{16,24},{24,0},{1,9},{9,17},{17,25},{25,1},{2,10},{10... | collective-permute-start | bytes 208904 | tf_op jit(solution)/shard_map/ppermute | solution.py:823
  8.0 6.6 %collective-permute-start.1 = (f32[17,8,128]{2,1,0:T(8,128)S(1)}, f32[17,8,128]{2,1,0:T(8,128)S(1)}, u32[]{:S(2)}, u32[]{:S(2)}) collective-permute-start(f32[17,8,128]{2,1,0:T(8,128)S(1)} %get-tuple-element.40), channel_id=1, source_target_pairs={{0,24},{8,0},{16,8},{24,16},{1,25},{9,1},{17,9},{25,17},{2,26},{10... | collective-permute-start | bytes 208904 | tf_op jit(solution)/shard_map/ppermute | solution.py:823
  10.1 4.6 %collective-permute-start.2 = (f32[17,8,128]{2,1,0:T(8,128)S(1)}, f32[17,8,128]{2,1,0:T(8,128)S(1)}, u32[]{:S(2)}, u32[]{:S(2)}) collective-permute-start(f32[17,8,128]{2,1,0:T(8,128)S(1)} %get-tuple-element.41), channel_id=1, source_target_pairs={{0,1},{1,2},{2,3},{3,4},{4,5},{5,6},{6,7},{7,0},{8,9},{9,10},{10,1... | collective-permute-start | bytes 208904 | tf_op jit(solution)/shard_map/ppermute | solution.py:823
  10.1 4.6 %collective-permute-start.3 = (f32[17,8,128]{2,1,0:T(8,128)S(1)}, f32[17,8,128]{2,1,0:T(8,128)S(1)}, u32[]{:S(2)}, u32[]{:S(2)}) collective-permute-start(f32[17,8,128]{2,1,0:T(8,128)S(1)} %get-tuple-element.42), channel_id=1, source_target_pairs={{0,7},{1,0},{2,1},{3,2},{4,3},{5,4},{6,5},{7,6},{8,15},{9,8},{10,9... | collective-permute-start | bytes 208904 | tf_op jit(solution)/shard_map/ppermute | solution.py:823
  15.8 6.8 %collective-permute-start.4 = (f32[37,8,128]{2,1,0:T(8,128)S(1)}, f32[37,8,128]{2,1,0:T(8,128)S(1)}, u32[]{:S(2)}, u32[]{:S(2)}) collective-permute-start(f32[37,8,128]{2,1,0:T(8,128)S(1)} %get-tuple-element.43), channel_id=1, source_target_pairs={{0,8},{8,0},{16,24},{24,16},{1,9},{9,1},{17,25},{25,17},{2,10},{10... | collective-permute-start | bytes 454664 | tf_op jit(solution)/shard_map/ppermute | solution.py:829
  15.8 6.7 %collective-permute-start.5 = (f32[37,8,128]{2,1,0:T(8,128)S(1)}, f32[37,8,128]{2,1,0:T(8,128)S(1)}, u32[]{:S(2)}, u32[]{:S(2)}) collective-permute-start(f32[37,8,128]{2,1,0:T(8,128)S(1)} %get-tuple-element.44), channel_id=1, source_target_pairs={{0,0},{8,16},{16,8},{24,24},{1,1},{9,17},{17,9},{25,25},{2,2},{10,... | collective-permute-start | bytes 454664 | tf_op jit(solution)/shard_map/ppermute | solution.py:829
  22.6 6.6 %collective-permute-start.6 = (f32[41,8,128]{2,1,0:T(8,128)S(1)}, f32[41,8,128]{2,1,0:T(8,128)S(1)}, u32[]{:S(2)}, u32[]{:S(2)}) collective-permute-start(f32[41,8,128]{2,1,0:T(8,128)S(1)} %get-tuple-element.48), channel_id=1, source_target_pairs={{0,1},{1,2},{2,3},{3,4},{4,5},{5,6},{6,7},{7,0},{8,9},{9,10},{10,1... | collective-permute-start | bytes 503816 | tf_op jit(solution)/shard_map/ppermute | solution.py:823
  22.6 6.5 %collective-permute-start.7 = (f32[41,8,128]{2,1,0:T(8,128)S(1)}, f32[41,8,128]{2,1,0:T(8,128)S(1)}, u32[]{:S(2)}, u32[]{:S(2)}) collective-permute-start(f32[41,8,128]{2,1,0:T(8,128)S(1)} %get-tuple-element.49), channel_id=1, source_target_pairs={{0,7},{1,0},{2,1},{3,2},{4,3},{5,4},{6,5},{7,6},{8,15},{9,8},{10,9... | collective-permute-start | bytes 503816 | tf_op jit(solution)/shard_map/ppermute | solution.py:823
  49.4 11.8 %all-to-all-start.1 = ((f32[160,2,128]{2,1,0:T(2,128)}), f32[160,2,128]{2,1,0:T(2,128)S(1)}, u32[]{:S(2)}, u32[]{:S(2)}) async-start(f32[160,2,128]{2,1,0:T(2,128)} %share.1), calls=%async_computation.1 | async-start | bytes 327680 | tf_op jit(solution)/shard_map/all_to_all | solution.py:894
  52.0 9.2 %collective-permute-start.8 = (f32[16,8,128]{2,1,0:T(8,128)S(1)}, f32[16,8,128]{2,1,0:T(8,128)S(1)}, u32[]{:S(2)}, u32[]{:S(2)}) collective-permute-start(f32[16,8,128]{2,1,0:T(8,128)S(1)} %get-tuple-element.59), channel_id=1, source_target_pairs={{0,8},{8,16},{16,24},{24,0},{1,9},{9,17},{17,25},{25,1},{2,10},{10... | collective-permute-start | bytes 196616 | tf_op jit(solution)/shard_map/ppermute | solution.py:823
  53.7 7.5 %collective-permute-start.9 = (f32[16,8,128]{2,1,0:T(8,128)S(1)}, f32[16,8,128]{2,1,0:T(8,128)S(1)}, u32[]{:S(2)}, u32[]{:S(2)}) collective-permute-start(f32[16,8,128]{2,1,0:T(8,128)S(1)} %get-tuple-element.60), channel_id=1, source_target_pairs={{0,24},{8,0},{16,8},{24,16},{1,25},{9,1},{17,9},{25,17},{2,26},{10... | collective-permute-start | bytes 196616 | tf_op jit(solution)/shard_map/ppermute | solution.py:823
  61.2 4.7 %collective-permute-start.10 = (f32[17,8,128]{2,1,0:T(8,128)S(1)}, f32[17,8,128]{2,1,0:T(8,128)S(1)}, u32[]{:S(2)}, u32[]{:S(2)}) collective-permute-start(f32[17,8,128]{2,1,0:T(8,128)S(1)} %get-tuple-element.61), channel_id=1, source_target_pairs={{0,1},{1,2},{2,3},{3,4},{4,5},{5,6},{6,7},{7,0},{8,9},{9,10},{10,1... | collective-permute-start | bytes 208904 | tf_op jit(solution)/shard_map/ppermute | solution.py:823
  61.4 4.5 %collective-permute-start.11 = (f32[17,8,128]{2,1,0:T(8,128)S(1)}, f32[17,8,128]{2,1,0:T(8,128)S(1)}, u32[]{:S(2)}, u32[]{:S(2)}) collective-permute-start(f32[17,8,128]{2,1,0:T(8,128)S(1)} %get-tuple-element.62), channel_id=1, source_target_pairs={{0,7},{1,0},{2,1},{3,2},{4,3},{5,4},{6,5},{7,6},{8,15},{9,8},{10,9... | collective-permute-start | bytes 208904 | tf_op jit(solution)/shard_map/ppermute | solution.py:823

commit v6 on v5

--- a/solution.py
+++ b/solution.py
@@ -410,6 +410,40 @@
     return list(range(count + ring)) + list(range(total - ring, total))
 
 
+def pooled(left):
+    return pair_z(pair_x(left, 1), 1) * 0.125
+
+
+def over(r1, k1):
+    return jnp.where(k1 > 0.0, r1 / jnp.where(k1 > 0.0, k1, 1.0), 0.0)
+
+
+def inner_kernel(
+    e0_ref, k0_ref, ea_ref, eb_ref,
+    e1i_ref, k1i_ref, k2_ref,
+    ex_ref, kx_ref, pack_ref,
+):
+    exlo_ref, exhi_ref = Swapped(eb_ref, ea_ref), Swapped(ea_ref, eb_ref)
+    lo_here, hi_here = inside("gx")
+    for dst, own, at in ((ex_ref, e0_ref, 0), (kx_ref, k0_ref, 16)):
+        for y in range(16):
+            dst[y, 0:16, :] = own[y]
+            dst[y, 16:24, :] = kept(hi_here, exhi_ref[at + y])
+            dst[y, 24:32, :] = kept(lo_here, exlo_ref[at + y])
+    for y1 in range(8):
+        k1i_ref[y1] = pooled(kx_ref[2 * y1] + kx_ref[2 * y1 + 1]) * 0.25
+    for y1 in range(1, 7):
+        parts = []
+        for y in (2 * y1, 2 * y1 + 1):
+            parts.append(kx_ref[y] * relax(ex_ref[y], ex_ref[y - 1], ex_ref[y + 1], 1))
+        e1i_ref[y1] = over(pooled(parts[0] + parts[1]), k1i_ref[y1])
+    k2 = []
+    for y2 in range(4):
+        v = pair_z(pair_x(k1i_ref[2 * y2] + k1i_ref[2 * y2 + 1], 2), 2) * (0.125 * 0.25)
+        k2.append(v[0:16])
+    k2_ref[...] = pack_four(k2, pack_ref)
+
+
 def down_level0(e_ref, k_ref, e1_ref, k1_ref, make_k1, ring):
     rows = 8 + 2 * ring
 
@@ -458,7 +492,7 @@
 
 
 def down_first_kernel(
-    live_ref, e0_ref, k0_ref, ea_ref, eb_ref, eylo_ref, eyhi_ref,
+    live_ref, e0_ref, k0_ref, ea_ref, eb_ref, eylo_ref, eyhi_ref, e1i_ref, k1i_ref, k2_ref,
     send_ref, e0x_ref, k0x_ref, e1_ref, k1_ref, pack_ref,
 ):
     exlo_ref, exhi_ref = Swapped(eb_ref, ea_ref), Swapped(ea_ref, eb_ref)
@@ -467,14 +501,26 @@
         k0x_ref, k0_ref, exlo_ref, exhi_ref, eylo_ref, eyhi_ref, 16, packed_tiles(ROWS_FIRST, 2),
         ROWS_DIAGONAL, 0,
     )
-    down_level0(e0x_ref, k0x_ref, e1_ref, k1_ref, True, 4)
-    r2 = down_level1(e1_ref, k1_ref, pack_ref)
-    k2 = []
-    for y2 in range(4):
-        v = pair_z(pair_x(k1_ref[2 * y2] + k1_ref[2 * y2 + 1], 2), 2) * (0.125 * 0.25)
-        k2.append(v[0:16])
-    k2 = pack_four(k2, pack_ref)
-    both = jnp.concatenate([r2, k2], axis=0)
+    for y1 in range(8):
+        k1_ref[y1] = k1i_ref[y1]
+    for y1 in range(1, 7):
+        e1_ref[y1] = e1i_ref[y1]
+    for y1 in range(8, 16):
+        k1_ref[y1] = pooled(k0x_ref[2 * y1] + k0x_ref[2 * y1 + 1]) * 0.25
+
+    def row(n, carry):
+        y1 = jnp.where(n == 0, 0, jnp.where(n < 5, n + 6, n + 8))
+        parts = []
+        for j in range(2):
+            y = 2 * y1 + j
+            parts.append(k0x_ref[y] * relax(e0x_ref[y], e0x_ref[(y + 31) % 32], e0x_ref[(y + 1) % 32], 1))
+        e1_ref[y1] = over(pooled(parts[0] + parts[1]), k1_ref[y1])
+        return carry
+
+    lax.fori_loop(0, 8, row, 0, unroll=UNROLL)
+    for y1 in (11, 12):
+        e1_ref[y1] = jnp.zeros((32, LANES), F32)
+    both = jnp.concatenate([down_level1(e1_ref, k1_ref, pack_ref), k2_ref[...]], axis=0)
 
     def put(d):
         send_ref[d] = both
@@ -873,9 +919,13 @@
     f1x, livex, w2x = call(
         extend_kernel, "extend", [fine_ext, (3, XF, LANES), fine_ext], 0, 0, 8, [x_side, y_side, corner], beside(2)
     )(f1, q, rxlo, rxhi, rylo, ryhi, sa, sb)
+    e1i, k1i, k2i = call(
+        inner_kernel, "inner", [(8, 32, LANES), (8, 32, LANES), (4, LANES)], 0, 0, 4,
+        [(16, 32, LANES), (16, 32, LANES), (16, LANES)], beside(2),
+    )(e0, k0, sa, sb)
     send, e0x, k0x, e1, k1 = call(
-        down_first_kernel, "down_first", [(devices, 8, LANES), wide, wide, half, half], 0, 0, 7, [(16, LANES)]
-    )(livex, e0, k0, sa, sb, sylo, syhi)
+        down_first_kernel, "down_first", [(devices, 8, LANES), wide, wide, half, half], 0, 0, 10, [(16, LANES)]
+    )(livex, e0, k0, sa, sb, sylo, syhi, e1i, k1i, k2i)
     recv = lax.all_to_all(send, ("gx", "gy"), 0, 0, tiled=True)
 
     up_scratch = [

time: 70.1 us -> 69.5 us (level)
  transfers between devices with their start and end apart: 13 -> 13, of which waited for: 5 -> 5; matrix products, arithmetic and copies ran while one was open for 0% -> 0% of each run, Pallas kernels for 7% -> 8%
where the time goes in v6:
time: 69.5 us; the launch traced here: 68.8 us
  starting transfers between devices  20.4 us (29%)
  Pallas kernels  16.7 us (24%)
  blocking collectives  13.9 us (20%)
  waiting for transfers between devices  13.6 us (20%)
  local copies, waits for them, and re-layouts  2.73 us (4%)
  between operations  1.47 us (2%)
    ppermute x10, starting transfers between devices, step(): lax.ppermute(value, axis, [(i, (i + by) % count) for i in range(count)])  17.1 us
    all_to_all x1, blocking collectives, local(): recv = lax.all_to_all(send, ('gx', 'gy'), 0, 0, tiled=True)  13.9 us
    ppermute x10, waiting for transfers between devices, step(): lax.ppermute(value, axis, [(i, (i + by) % count) for i in range(count)])  7.59 us
    ppermute x2, waiting for transfers between devices, swap_pairs(): lax.ppermute(value, axis, [(i, j if 0 <= j < count else i) for i, j in en...  6.01 us
    pallas_call x1, Pallas kernels, local(): call(last_kernel, 'last', [fine_rhs.shape, (256, LANES)], 0, 0, 12, [half...  3.53 us
    pallas_call x1, Pallas kernels, local(): call(middle_kernel, 'middle', [octets, coarse, own, tiles(16), tiles(16)]...  3.49 us
    unnamed x10, local copies, waits for them, and re-layouts  2.73 us
    all_to_all x1, starting transfers between devices, local(): recv = lax.all_to_all(send, ('gx', 'gy'), 0, 0, tiled=True)  2.58 us
  transfers between devices with their start and end apart: 13, of which 5 were waited for; matrix products, arithmetic and copies ran while one was open for 0% of the time, Pallas kernels for 8%

profile of v6, /device:TPU:0, one launch (start us, length us, event | category | flops | bytes accessed | tf_op | source)
XLA Modules:
  0.0 68.8 jit_solution(3735017561957450687)
XLA Ops:
  0.6 0.0 copy-start
  1.3 0.0 copy-start.4
  1.3 0.6 copy-done.4
  2.0 0.6 tables.1.tables_ref
  2.5 0.0 copy-start.1
  2.6 1.0 %copy-done.1 = f32[1,1,4,32,1024]{4,3,2,1,0:T(8,128)S(1)} copy-done((f32[1,1,4,32,1024]{4,3,2,1,0:T(8,128)S(1)}, f32[1,1,4,32,1024]{4,3,2,1,0:T(8,128)}, u32[]{:S(2)}) %copy-start.1) | copy-done | bytes 524312
  3.6 0.0 copy-start.2
  3.6 1.0 %copy-done.2 = f32[1,1,4,32,1024]{4,3,2,1,0:T(8,128)S(1)} copy-done((f32[1,1,4,32,1024]{4,3,2,1,0:T(8,128)S(1)}, f32[1,1,4,32,1024]{4,3,2,1,0:T(8,128)}, u32[]{:S(2)}) %copy-start.2) | copy-done | bytes 524312
  4.6 0.3 faces.1
  5.0 3.1 %collective-permute-start = (f32[17,8,128]{2,1,0:T(8,128)S(1)}, f32[17,8,128]{2,1,0:T(8,128)S(1)}, u32[]{:S(2)}, u32[]{:S(2)}) collective-permute-start(f32[17,8,128]{2,1,0:T(8,128)S(1)} %get-tuple-element.42), channel_id=1, source_target_pairs={{0,8},{8,16},{16,24},{24,0},{1,9},{9,17},{17,25},{25,1},{2,10},{10... | collective-permute-start | bytes 208904 | tf_op jit(solution)/shard_map/ppermute | solution.py:869
  8.0 2.1 %collective-permute-start.1 = (f32[17,8,128]{2,1,0:T(8,128)S(1)}, f32[17,8,128]{2,1,0:T(8,128)S(1)}, u32[]{:S(2)}, u32[]{:S(2)}) collective-permute-start(f32[17,8,128]{2,1,0:T(8,128)S(1)} %get-tuple-element.43), channel_id=1, source_target_pairs={{0,24},{8,0},{16,8},{24,16},{1,25},{9,1},{17,9},{25,17},{2,26},{10... | collective-permute-start | bytes 208904 | tf_op jit(solution)/shard_map/ppermute | solution.py:869
  10.1 0.0 collective-permute-start.2
  10.1 2.6 %collective-permute-start.3 = (f32[17,8,128]{2,1,0:T(8,128)S(1)}, f32[17,8,128]{2,1,0:T(8,128)S(1)}, u32[]{:S(2)}, u32[]{:S(2)}) collective-permute-start(f32[17,8,128]{2,1,0:T(8,128)S(1)} %get-tuple-element.45), channel_id=1, source_target_pairs={{0,7},{1,0},{2,1},{3,2},{4,3},{5,4},{6,5},{7,6},{8,15},{9,8},{10,9... | collective-permute-start | bytes 208904 | tf_op jit(solution)/shard_map/ppermute | solution.py:869
  12.8 1.8 %boxes.1 = (f32[8,16,16,128]{3,2,1,0:T(8,128)S(1)}, f32[8,16,16,128]{3,2,1,0:T(8,128)S(1)}) custom-call(f32[16,128]{1,0:T(8,128)S(1)} %tables.1.tables_ref, f32[4,32,1024]{2,1,0:T(8,128)S(1)} %get-tuple-element.38.raw_f_ref, f32[4,32,1024]{2,1,0:T(8,128)S(1)} %get-tuple-element.39.raw_q_ref), custom_call_target="tpu_custom_call" | custom-call | flops 3000000 | bytes 9000000 | tf_op jit(solution)/shard_map/boxes/pallas_call | solution.py:908
  14.6 0.0 collective-permute-done.rxlo_ref
  14.6 0.0 collective-permute-done.1.rxhi_ref
  14.6 0.2 collective-permute-done.2.rylo_ref
  14.8 0.0 collective-permute-done.3.ryhi_ref
  14.8 0.0 copy-done
  14.8 0.0 copy-done.3
  14.8 1.0 %first_residual.1 = (f32[16,16,128]{2,1,0:T(8,128)S(1)}, f32[16,16,128]{2,1,0:T(8,128)S(1)}, f32[37,8,128]{2,1,0:T(8,128)S(1)}, f32[37,8,128]{2,1,0:T(8,128)S(1)}) custom-call(f32[8,16,16,128]{3,2,1,0:T(8,128)S(1)} %get-tuple-element.40.f1_ref, f32[8,16,16,128]{3,2,1,0:T(8,128)S(1)} %get-tuple-element.41.q_ref, f32[256,128]{1,0:T(8,128)S(1)} %bitcast.5, ...), custom_call_target="tpu_custom_call" | custom-call | tf_op jit(solution)/shard_map/first_residual/pallas_call | solution.py:911
  15.8 0.1 collective-permute-start.4
  15.8 0.7 collective-permute-start.5
  16.5 6.0 %collective-permute-done.4.sa_ref.ea_ref = f32[37,8,128]{2,1,0:T(8,128)S(1)} collective-permute-done((f32[37,8,128]{2,1,0:T(8,128)S(1)}, f32[37,8,128]{2,1,0:T(8,128)S(1)}, u32[]{:S(2)}, u32[]{:S(2)}) %collective-permute-start.4) | collective-permute-done | bytes 151584 | tf_op jit(solution)/shard_map/ppermute | solution.py:875
  22.5 0.0 collective-permute-done.5.sb_ref.eb_ref
  22.6 0.1 collective-permute-start.6
  22.6 2.6 %collective-permute-start.7 = (f32[41,8,128]{2,1,0:T(8,128)S(1)}, f32[41,8,128]{2,1,0:T(8,128)S(1)}, u32[]{:S(2)}, u32[]{:S(2)}) collective-permute-start(f32[41,8,128]{2,1,0:T(8,128)S(1)} %get-tuple-element.52), channel_id=1, source_target_pairs={{0,7},{1,0},{2,1},{3,2},{4,3},{5,4},{6,5},{7,6},{8,15},{9,8},{10,9... | collective-permute-start | bytes 503816 | tf_op jit(solution)/shard_map/ppermute | solution.py:869
  25.3 0.6 inner.1
  25.8 1.5 %extend.1 = (f32[8,20,24,128]{3,2,1,0:T(8,128)S(1)}, f32[3,24,128]{2,1,0:T(8,128)S(1)}, f32[8,20,24,128]{3,2,1,0:T(8,128)S(1)}) custom-call(f32[8,16,16,128]{3,2,1,0:T(8,128)S(1)} %get-tuple-element.40.f1_ref, f32[8,16,16,128]{3,2,1,0:T(8,128)S(1)} %get-tuple-element.41.q_ref, f32[17,8,128]{2,1,0:T(8,128)S(1)} %collective-permute-done.rxlo_ref, ...), custom_call_target="tpu_custom_call" | custom-call | flops 2000000 | bytes 6000000 | tf_op jit(solution)/shard_map/extend/pallas_call | solution.py:919
  27.4 1.8 %collective-permute-done.6.eylo_ref = f32[41,8,128]{2,1,0:T(8,128)S(1)} collective-permute-done((f32[41,8,128]{2,1,0:T(8,128)S(1)}, f32[41,8,128]{2,1,0:T(8,128)S(1)}, u32[]{:S(2)}, u32[]{:S(2)}) %collective-permute-start.6) | collective-permute-done | bytes 167968 | tf_op jit(solution)/shard_map/ppermute | solution.py:869
  29.2 0.0 collective-permute-done.7.eyhi_ref
  29.2 0.9 %down_first.1 = (f32[32,8,128]{2,1,0:T(8,128)S(1)}, f32[32,32,128]{2,1,0:T(8,128)S(1)}, f32[32,32,128]{2,1,0:T(8,128)S(1)}, f32[16,32,128]{2,1,0:T(8,128)S(1)}, f32[16,32,128]{2,1,0:T(8,128)S(1)}) custom-call(f32[3,24,128]{2,1,0:T(8,128)S(1)} %get-tuple-element.48.live_ref.livex_ref, f32[16,16,128]{2,1,0:T(8,128)S(1)} %get-tuple-element.49.e0_ref, ...), custom_call_target="tpu_custom_call" | custom-call | tf_op jit(solution)/shard_map/down_first/pallas_call | solution.py:926
  30.0 13.9 %all_to_all.10.recv_ref = f32[32,8,128]{2,1,0:T(8,128)S(1)} all-to-all(f32[32,8,128]{2,1,0:T(8,128)S(1)} %get-tuple-element.56), channel_id=1, replica_groups=mesh['gx'=4,'gy'=8] {'gx','gy'}, dimensions={0} | all-to-all | bytes 262144 | tf_op jit(solution)/shard_map/all_to_all | solution.py:929
  44.0 3.5 %middle.1 = (f32[8,16,16,128]{3,2,1,0:T(8,128)S(1)}, f32[8,16,128]{2,1,0:T(8,128)S(1)}, f32[16,16,128]{2,1,0:T(8,128)S(1)}, f32[16,8,128]{2,1,0:T(8,128)S(1)}, f32[16,8,128]{2,1,0:T(8,128)S(1)}) custom-call(f32[32,8,128]{2,1,0:T(8,128)S(1)} %all_to_all.10.recv_ref, f32[32,32,128]{2,1,0:T(8,128)S(1)} %get-tuple-element.57.e0x_ref, ...), custom_call_target="tpu_custom_call" | custom-call | tf_op jit(solution)/shard_map/middle/pallas_call | solution.py:935
  47.5 1.3 %share.1 = f32[160,2,128]{2,1,0:T(2,128)} custom-call(f32[16,16,128]{2,1,0:T(8,128)S(1)} %get-tuple-element.63.e0_ref, f32[32,32,128]{2,1,0:T(8,128)S(1)} %get-tuple-element.58.k0x_ref, f32[16,32,128]{2,1,0:T(8,128)S(1)} %get-tuple-element.60.k1_ref), custom_call_target="tpu_custom_call" | custom-call | flops 1000000 | bytes 3000000 | tf_op jit(solution)/shard_map/share/pallas_call | solution.py:940
  48.8 2.6 %all-to-all-start.1 = ((f32[160,2,128]{2,1,0:T(2,128)}), f32[160,2,128]{2,1,0:T(2,128)S(1)}, u32[]{:S(2)}, u32[]{:S(2)}) async-start(f32[160,2,128]{2,1,0:T(2,128)} %share.1), calls=%async_computation.1 | async-start | bytes 327680 | tf_op jit(solution)/shard_map/all_to_all | solution.py:944
  51.4 1.7 %collective-permute-start.8 = (f32[16,8,128]{2,1,0:T(8,128)S(1)}, f32[16,8,128]{2,1,0:T(8,128)S(1)}, u32[]{:S(2)}, u32[]{:S(2)}) collective-permute-start(f32[16,8,128]{2,1,0:T(8,128)S(1)} %get-tuple-element.65), channel_id=1, source_target_pairs={{0,8},{8,16},{16,24},{24,0},{1,9},{9,17},{17,25},{25,1},{2,10},{10... | collective-permute-start | bytes 196616 | tf_op jit(solution)/shard_map/ppermute | solution.py:869
  53.1 2.1 %collective-permute-start.9 = (f32[16,8,128]{2,1,0:T(8,128)S(1)}, f32[16,8,128]{2,1,0:T(8,128)S(1)}, u32[]{:S(2)}, u32[]{:S(2)}) collective-permute-start(f32[16,8,128]{2,1,0:T(8,128)S(1)} %get-tuple-element.66), channel_id=1, source_target_pairs={{0,24},{8,0},{16,8},{24,16},{1,25},{9,1},{17,9},{25,17},{2,26},{10... | collective-permute-start | bytes 196616 | tf_op jit(solution)/shard_map/ppermute | solution.py:869
  55.2 5.3 %collective-permute-done.8.exlo_ref = f32[16,8,128]{2,1,0:T(8,128)S(1)} collective-permute-done((f32[16,8,128]{2,1,0:T(8,128)S(1)}, f32[16,8,128]{2,1,0:T(8,128)S(1)}, u32[]{:S(2)}, u32[]{:S(2)}) %collective-permute-start.8) | collective-permute-done | bytes 65568 | tf_op jit(solution)/shard_map/ppermute | solution.py:869
  60.6 0.0 collective-permute-done.9.exhi_ref
  60.6 0.0 all-to-all-done.1.recv_ref
  60.6 0.2 collective-permute-start.10
  60.8 2.5 %collective-permute-start.11 = (f32[17,8,128]{2,1,0:T(8,128)S(1)}, f32[17,8,128]{2,1,0:T(8,128)S(1)}, u32[]{:S(2)}, u32[]{:S(2)}) collective-permute-start(f32[17,8,128]{2,1,0:T(8,128)S(1)} %get-tuple-element.68), channel_id=1, source_target_pairs={{0,7},{1,0},{2,1},{3,2},{4,3},{5,4},{6,5},{7,6},{8,15},{9,8},{10,9... | collective-permute-start | bytes 208904 | tf_op jit(solution)/shard_map/ppermute | solution.py:869
  63.3 0.3 settle.1
  63.7 1.3 %coarse.1.m2_ref = f32[8,32,128]{2,1,0:T(8,128)S(1)} custom-call(f32[160,2,128]{2,1,0:T(2,128)S(1)} %all-to-all-done.1.recv_ref, f32[8,16,128]{2,1,0:T(8,128)S(1)} %get-tuple-element.64.k2_ref), custom_call_target="tpu_custom_call" | custom-call | flops 2000000 | bytes 6000000 | tf_op jit(solution)/shard_map/coarse/pallas_call | solution.py:950
  65.0 0.3 collective-permute-done.10.eylo_ref
  65.3 0.0 collective-permute-done.11.eyhi_ref
  65.3 3.5 %last.1 = (f32[1,1,4,32,1024]{4,3,2,1,0:T(8,128)}, f32[256,128]{1,0:T(8,128)}) custom-call(f32[16,128]{1,0:T(8,128)S(1)} %tables.1.tables_ref, f32[8,32,128]{2,1,0:T(8,128)S(1)} %coarse.1.m2_ref, f32[16,16,128]{2,1,0:T(8,128)S(1)} %get-tuple-element.63.e0_ref, f32[16,8,128]{2,1,0:T(8,128)S(1)} %collective-permute-done.8.exlo_ref, ...), custom_call_target="tpu_custom_call" | custom-call | tf_op jit(solution)/shard_map/last/pallas_call | solution.py:953
  (3 shorter events, 0.1 us)
Async XLA Ops:
  0.6 14.1 %copy-start = (f32[16,16,128]{2,1,0:T(8,128)S(1)}, f32[16,16,128]{2,1,0:T(8,128)}, u32[]{:S(2)}) copy-start(f32[16,16,128]{2,1,0:T(8,128)} %param.9) | copy-start | bytes 393220
  1.3 0.7 copy-start.4
  2.5 1.0 %copy-start.1 = (f32[1,1,4,32,1024]{4,3,2,1,0:T(8,128)S(1)}, f32[1,1,4,32,1024]{4,3,2,1,0:T(8,128)}, u32[]{:S(2)}) copy-start(f32[1,1,4,32,1024]{4,3,2,1,0:T(8,128)} %rhs_ref.1) | copy-start | bytes 1572868
  3.6 1.0 %copy-start.2 = (f32[1,1,4,32,1024]{4,3,2,1,0:T(8,128)S(1)}, f32[1,1,4,32,1024]{4,3,2,1,0:T(8,128)}, u32[]{:S(2)}) copy-start(f32[1,1,4,32,1024]{4,3,2,1,0:T(8,128)} %beta_ref.1) | copy-start | bytes 1572868
  4.6 10.1 %copy-start.3 = (f32[16,16,128]{2,1,0:T(8,128)S(1)}, f32[16,16,128]{2,1,0:T(8,128)}, u32[]{:S(2)}) copy-start(f32[16,16,128]{2,1,0:T(8,128)} %param.10) | copy-start | bytes 393220
  5.0 9.6 %collective-permute-start = (f32[17,8,128]{2,1,0:T(8,128)S(1)}, f32[17,8,128]{2,1,0:T(8,128)S(1)}, u32[]{:S(2)}, u32[]{:S(2)}) collective-permute-start(f32[17,8,128]{2,1,0:T(8,128)S(1)} %get-tuple-element.42), channel_id=1, source_target_pairs={{0,8},{8,16},{16,24},{24,0},{1,9},{9,17},{17,25},{25,1},{2,10},{10... | collective-permute-start | bytes 208904 | tf_op jit(solution)/shard_map/ppermute | solution.py:869
  8.0 6.6 %collective-permute-start.1 = (f32[17,8,128]{2,1,0:T(8,128)S(1)}, f32[17,8,128]{2,1,0:T(8,128)S(1)}, u32[]{:S(2)}, u32[]{:S(2)}) collective-permute-start(f32[17,8,128]{2,1,0:T(8,128)S(1)} %get-tuple-element.43), channel_id=1, source_target_pairs={{0,24},{8,0},{16,8},{24,16},{1,25},{9,1},{17,9},{25,17},{2,26},{10... | collective-permute-start | bytes 208904 | tf_op jit(solution)/shard_map/ppermute | solution.py:869
  10.1 4.6 %collective-permute-start.2 = (f32[17,8,128]{2,1,0:T(8,128)S(1)}, f32[17,8,128]{2,1,0:T(8,128)S(1)}, u32[]{:S(2)}, u32[]{:S(2)}) collective-permute-start(f32[17,8,128]{2,1,0:T(8,128)S(1)} %get-tuple-element.44), channel_id=1, source_target_pairs={{0,1},{1,2},{2,3},{3,4},{4,5},{5,6},{6,7},{7,0},{8,9},{9,10},{10,1... | collective-permute-start | bytes 208904 | tf_op jit(solution)/shard_map/ppermute | solution.py:869
  10.1 4.6 %collective-permute-start.3 = (f32[17,8,128]{2,1,0:T(8,128)S(1)}, f32[17,8,128]{2,1,0:T(8,128)S(1)}, u32[]{:S(2)}, u32[]{:S(2)}) collective-permute-start(f32[17,8,128]{2,1,0:T(8,128)S(1)} %get-tuple-element.45), channel_id=1, source_target_pairs={{0,7},{1,0},{2,1},{3,2},{4,3},{5,4},{6,5},{7,6},{8,15},{9,8},{10,9... | collective-permute-start | bytes 208904 | tf_op jit(solution)/shard_map/ppermute | solution.py:869
  15.8 6.8 %collective-permute-start.4 = (f32[37,8,128]{2,1,0:T(8,128)S(1)}, f32[37,8,128]{2,1,0:T(8,128)S(1)}, u32[]{:S(2)}, u32[]{:S(2)}) collective-permute-start(f32[37,8,128]{2,1,0:T(8,128)S(1)} %get-tuple-element.46), channel_id=1, source_target_pairs={{0,8},{8,0},{16,24},{24,16},{1,9},{9,1},{17,25},{25,17},{2,10},{10... | collective-permute-start | bytes 454664 | tf_op jit(solution)/shard_map/ppermute | solution.py:875
  15.8 6.7 %collective-permute-start.5 = (f32[37,8,128]{2,1,0:T(8,128)S(1)}, f32[37,8,128]{2,1,0:T(8,128)S(1)}, u32[]{:S(2)}, u32[]{:S(2)}) collective-permute-start(f32[37,8,128]{2,1,0:T(8,128)S(1)} %get-tuple-element.47), channel_id=1, source_target_pairs={{0,0},{8,16},{16,8},{24,24},{1,1},{9,17},{17,9},{25,25},{2,2},{10,... | collective-permute-start | bytes 454664 | tf_op jit(solution)/shard_map/ppermute | solution.py:875
  22.6 6.6 %collective-permute-start.6 = (f32[41,8,128]{2,1,0:T(8,128)S(1)}, f32[41,8,128]{2,1,0:T(8,128)S(1)}, u32[]{:S(2)}, u32[]{:S(2)}) collective-permute-start(f32[41,8,128]{2,1,0:T(8,128)S(1)} %get-tuple-element.51), channel_id=1, source_target_pairs={{0,1},{1,2},{2,3},{3,4},{4,5},{5,6},{6,7},{7,0},{8,9},{9,10},{10,1... | collective-permute-start | bytes 503816 | tf_op jit(solution)/shard_map/ppermute | solution.py:869
  22.6 6.5 %collective-permute-start.7 = (f32[41,8,128]{2,1,0:T(8,128)S(1)}, f32[41,8,128]{2,1,0:T(8,128)S(1)}, u32[]{:S(2)}, u32[]{:S(2)}) collective-permute-start(f32[41,8,128]{2,1,0:T(8,128)S(1)} %get-tuple-element.52), channel_id=1, source_target_pairs={{0,7},{1,0},{2,1},{3,2},{4,3},{5,4},{6,5},{7,6},{8,15},{9,8},{10,9... | collective-permute-start | bytes 503816 | tf_op jit(solution)/shard_map/ppermute | solution.py:869
  48.8 11.8 %all-to-all-start.1 = ((f32[160,2,128]{2,1,0:T(2,128)}), f32[160,2,128]{2,1,0:T(2,128)S(1)}, u32[]{:S(2)}, u32[]{:S(2)}) async-start(f32[160,2,128]{2,1,0:T(2,128)} %share.1), calls=%async_computation.1 | async-start | bytes 327680 | tf_op jit(solution)/shard_map/all_to_all | solution.py:944
  51.4 9.2 %collective-permute-start.8 = (f32[16,8,128]{2,1,0:T(8,128)S(1)}, f32[16,8,128]{2,1,0:T(8,128)S(1)}, u32[]{:S(2)}, u32[]{:S(2)}) collective-permute-start(f32[16,8,128]{2,1,0:T(8,128)S(1)} %get-tuple-element.65), channel_id=1, source_target_pairs={{0,8},{8,16},{16,24},{24,0},{1,9},{9,17},{17,25},{25,1},{2,10},{10... | collective-permute-start | bytes 196616 | tf_op jit(solution)/shard_map/ppermute | solution.py:869
  53.1 7.5 %collective-permute-start.9 = (f32[16,8,128]{2,1,0:T(8,128)S(1)}, f32[16,8,128]{2,1,0:T(8,128)S(1)}, u32[]{:S(2)}, u32[]{:S(2)}) collective-permute-start(f32[16,8,128]{2,1,0:T(8,128)S(1)} %get-tuple-element.66), channel_id=1, source_target_pairs={{0,24},{8,0},{16,8},{24,16},{1,25},{9,1},{17,9},{25,17},{2,26},{10... | collective-permute-start | bytes 196616 | tf_op jit(solution)/shard_map/ppermute | solution.py:869
  60.6 4.7 %collective-permute-start.10 = (f32[17,8,128]{2,1,0:T(8,128)S(1)}, f32[17,8,128]{2,1,0:T(8,128)S(1)}, u32[]{:S(2)}, u32[]{:S(2)}) collective-permute-start(f32[17,8,128]{2,1,0:T(8,128)S(1)} %get-tuple-element.67), channel_id=1, source_target_pairs={{0,1},{1,2},{2,3},{3,4},{4,5},{5,6},{6,7},{7,0},{8,9},{9,10},{10,1... | collective-permute-start | bytes 208904 | tf_op jit(solution)/shard_map/ppermute | solution.py:869
  60.8 4.5 %collective-permute-start.11 = (f32[17,8,128]{2,1,0:T(8,128)S(1)}, f32[17,8,128]{2,1,0:T(8,128)S(1)}, u32[]{:S(2)}, u32[]{:S(2)}) collective-permute-start(f32[17,8,128]{2,1,0:T(8,128)S(1)} %get-tuple-element.68), channel_id=1, source_target_pairs={{0,7},{1,0},{2,1},{3,2},{4,3},{5,4},{6,5},{7,6},{8,15},{9,8},{10,9... | collective-permute-start | bytes 208904 | tf_op jit(solution)/shard_map/ppermute | solution.py:869

commit v7 on v6

--- a/solution.py
+++ b/solution.py
@@ -377,7 +377,7 @@
     pack_y(sources, eylo_ref, eyhi_ref)
 
 
-def pack_y_kernel(recv_ref, e0_ref, exlo_ref, exhi_ref, eylo_ref, eyhi_ref):
+def pack_y_kernel(recv_ref, m4_ref, e0_ref, exlo_ref, exhi_ref, eylo_ref, eyhi_ref):
     pack_y(((e0_ref, exlo_ref, exhi_ref, 0, ROWS_LAST, 2),), eylo_ref, eyhi_ref)
 
 
@@ -444,27 +444,25 @@
     k2_ref[...] = pack_four(k2, pack_ref)
 
 
-def down_level0(e_ref, k_ref, e1_ref, k1_ref, make_k1, ring):
-    rows = 8 + 2 * ring
-
-    def row(n, carry):
-        y1 = n if rows == 16 else jnp.where(n < 8 + ring, n, n + 16 - rows)
+def inner_last_kernel(e0_ref, k0x_ref, k1_ref, exlo_ref, exhi_ref, e1i_ref, ex_ref):
+    lo_here, hi_here = inside("gx")
+    for y in range(16):
+        ex_ref[y, 0:16, :] = e0_ref[y]
+        ex_ref[y, 16:24, :] = kept(hi_here, exhi_ref[y])
+        ex_ref[y, 24:32, :] = kept(lo_here, exlo_ref[y])
+    for y1 in range(1, 7):
         parts = []
-        for j in range(2):
-            y = 2 * y1 + j
-            low = e_ref[(y + 31) % 32]
-            high = e_ref[(y + 1) % 32]
-            parts.append(k_ref[y] * relax(e_ref[y], low, high, 1))
-        r1 = pair_z(pair_x(parts[0] + parts[1], 1), 1) * 0.125
-        if make_k1:
-            k1 = pair_z(pair_x(k_ref[2 * y1] + k_ref[2 * y1 + 1], 1), 1) * (0.125 * 0.25)
-            k1_ref[y1] = k1
-        else:
-            k1 = k1_ref[y1]
-        e1_ref[y1] = jnp.where(k1 > 0.0, r1 / jnp.where(k1 > 0.0, k1, 1.0), 0.0)
-        return carry
-
-    lax.fori_loop(0, rows, row, 0, unroll=UNROLL)
+        for y in (2 * y1, 2 * y1 + 1):
+            parts.append(k0x_ref[y] * relax(ex_ref[y], ex_ref[y - 1], ex_ref[y + 1], 1))
+        e1i_ref[y1] = over(pooled(parts[0] + parts[1]), k1_ref[y1])
+
+
+def down_level0(e_ref, k_ref, e1_ref, k1_ref):
+    for y1 in (0, 7, 8, 9, 14, 15):
+        parts = []
+        for y in (2 * y1, 2 * y1 + 1):
+            parts.append(k_ref[y] * relax(e_ref[y], e_ref[(y + 31) % 32], e_ref[(y + 1) % 32], 1))
+        e1_ref[y1] = over(pooled(parts[0] + parts[1]), k1_ref[y1])
 
 
 def pack_four(rows, pack_ref):
@@ -809,12 +807,14 @@
 
 def last_kernel(
     tables_ref, m2_ref, e0_ref, exlo_ref, exhi_ref, eylo_ref, eyhi_ref, k0x_ref, k1_ref,
-    c4_ref, m4_ref, livex_ref,
+    c4_ref, m4_ref, livex_ref, e1i_ref,
     fine_ref, base_ref,
     mg1_ref, e1p_ref, e0p_ref, corr_ref, e0x_ref, e1_ref, g_ref, c_ref,
 ):
     assemble_base(e0x_ref, e0_ref, exlo_ref, exhi_ref, eylo_ref, eyhi_ref, 0, 0, ROWS_LAST, 2)
-    down_level0(e0x_ref, k0x_ref, e1_ref, k1_ref, False, 2)
+    for y1 in range(1, 7):
+        e1_ref[y1] = e1i_ref[y1]
+    down_level0(e0x_ref, k0x_ref, e1_ref, k1_ref)
     up_levels(m2_ref, e1_ref, k1_ref, mg1_ref, e0x_ref, k0x_ref, corr_ref, e1p_ref, e0p_ref, 2)
     idx = box_rows(tables_ref, 24)[0]
     idx16, live_slot, odd = box_rows(tables_ref, 16)
@@ -945,15 +945,18 @@
     c4, m4 = call(
         settle_kernel, "settle", [(32, 2, 16, LANES), own], 0, 0, 2, (), beside(2)
     )(tables, w4)
-    eylo, eyhi = call(pack_y_kernel, "pack_y", [tiles(packed_tiles(ROWS_LAST, 2))] * 2, 0, 0, 4)(recv, e0, sxlo, sxhi)
+    eylo, eyhi = call(pack_y_kernel, "pack_y", [tiles(packed_tiles(ROWS_LAST, 2))] * 2, 0, 0, 5)(recv, m4, e0, sxlo, sxhi)
     sylo, syhi = from_sides(eylo, eyhi, "gy")
     m2 = call(
         coarse_kernel, "coarse", [(8, 32, LANES)], 0, 0, 2, [coarse, coarse] + up_scratch[1:4], beside(2)
     )(recv, k2)[0]
+    e1i = call(
+        inner_last_kernel, "inner_last", [(8, 32, LANES)], 0, 0, 5, [(16, 32, LANES)], beside(2)
+    )(e0, k0x, k1, sxlo, sxhi)[0]
     fine, base = call(
-        last_kernel, "last", [fine_rhs.shape, (256, LANES)], 0, 0, 12,
+        last_kernel, "last", [fine_rhs.shape, (256, LANES)], 0, 0, 13,
         [half, half, wide, (YF, XF, LANES), wide, half, (YF, XF, LANES), rows],
-    )(tables, m2, e0, sxlo, sxhi, sylo, syhi, k0x, k1, c4, m4, livex)
+    )(tables, m2, e0, sxlo, sxhi, sylo, syhi, k0x, k1, c4, m4, livex, e1i)
     return fine, base.reshape(base_rhs.shape)
 
 

time: 69.5 us -> 69.1 us (level)
    pallas_call x1 -> x2, Pallas kernels: 3.53 us -> 3.49 us  [the longest x1 3.17 us: local(): call(last_kernel, 'last', [fine_rhs.shape, (256, LANES)], 0, 0, 13, [half...]
  transfers between devices with their start and end apart: 13 -> 13, of which waited for: 5 -> 5; matrix products, arithmetic and copies ran while one was open for 0% -> 0% of each run, Pallas kernels for 8% -> 9%
where the time goes in v7:
time: 69.1 us; the launch traced here: 68.5 us
  starting transfers between devices  20.4 us (30%)
  Pallas kernels  16.7 us (24%)
  blocking collectives  13.9 us (20%)
  waiting for transfers between devices  13.3 us (19%)
  local copies, waits for them, and re-layouts  2.73 us (4%)
  between operations  1.48 us (2%)
    ppermute x10, starting transfers between devices, step(): lax.ppermute(value, axis, [(i, (i + by) % count) for i in range(count)])  17.1 us
    all_to_all x1, blocking collectives, local(): recv = lax.all_to_all(send, ('gx', 'gy'), 0, 0, tiled=True)  13.9 us
    ppermute x10, waiting for transfers between devices, step(): lax.ppermute(value, axis, [(i, (i + by) % count) for i in range(count)])  7.27 us
    ppermute x2, waiting for transfers between devices, swap_pairs(): lax.ppermute(value, axis, [(i, j if 0 <= j < count else i) for i, j in en...  6.01 us
    pallas_call x1, Pallas kernels, local(): call(middle_kernel, 'middle', [octets, coarse, own, tiles(16), tiles(16)]...  3.49 us
    pallas_call x1, Pallas kernels, local(): call(last_kernel, 'last', [fine_rhs.shape, (256, LANES)], 0, 0, 13, [half...  3.17 us
    unnamed x10, local copies, waits for them, and re-layouts  2.73 us
    all_to_all x1, starting transfers between devices, local(): recv = lax.all_to_all(send, ('gx', 'gy'), 0, 0, tiled=True)  2.58 us
  transfers between devices with their start and end apart: 13, of which 5 were waited for; matrix products, arithmetic and copies ran while one was open for 0% of the time, Pallas kernels for 9%

profile of v7, /device:TPU:0, one launch (start us, length us, event | category | flops | bytes accessed | tf_op | source)
XLA Modules:
  0.0 68.5 jit_solution(14531486148336565736)
XLA Ops:
  0.6 0.0 copy-start
  1.3 0.0 copy-start.4
  1.3 0.6 copy-done.4
  2.0 0.6 tables.1.tables_ref
  2.5 0.0 copy-start.1
  2.6 1.0 %copy-done.1 = f32[1,1,4,32,1024]{4,3,2,1,0:T(8,128)S(1)} copy-done((f32[1,1,4,32,1024]{4,3,2,1,0:T(8,128)S(1)}, f32[1,1,4,32,1024]{4,3,2,1,0:T(8,128)}, u32[]{:S(2)}) %copy-start.1) | copy-done | bytes 524312
  3.6 1.0 %copy-done.2 = f32[1,1,4,32,1024]{4,3,2,1,0:T(8,128)S(1)} copy-done((f32[1,1,4,32,1024]{4,3,2,1,0:T(8,128)S(1)}, f32[1,1,4,32,1024]{4,3,2,1,0:T(8,128)}, u32[]{:S(2)}) %copy-start.2) | copy-done | bytes 524312
  4.6 0.3 faces.1
  5.0 3.1 %collective-permute-start = (f32[17,8,128]{2,1,0:T(8,128)S(1)}, f32[17,8,128]{2,1,0:T(8,128)S(1)}, u32[]{:S(2)}, u32[]{:S(2)}) collective-permute-start(f32[17,8,128]{2,1,0:T(8,128)S(1)} %get-tuple-element.42), channel_id=1, source_target_pairs={{0,8},{8,16},{16,24},{24,0},{1,9},{9,17},{17,25},{25,1},{2,10},{10... | collective-permute-start | bytes 208904 | tf_op jit(solution)/shard_map/ppermute | solution.py:869
  8.0 2.1 %collective-permute-start.1 = (f32[17,8,128]{2,1,0:T(8,128)S(1)}, f32[17,8,128]{2,1,0:T(8,128)S(1)}, u32[]{:S(2)}, u32[]{:S(2)}) collective-permute-start(f32[17,8,128]{2,1,0:T(8,128)S(1)} %get-tuple-element.43), channel_id=1, source_target_pairs={{0,24},{8,0},{16,8},{24,16},{1,25},{9,1},{17,9},{25,17},{2,26},{10... | collective-permute-start | bytes 208904 | tf_op jit(solution)/shard_map/ppermute | solution.py:869
  10.1 0.0 collective-permute-start.2
  10.1 2.6 %collective-permute-start.3 = (f32[17,8,128]{2,1,0:T(8,128)S(1)}, f32[17,8,128]{2,1,0:T(8,128)S(1)}, u32[]{:S(2)}, u32[]{:S(2)}) collective-permute-start(f32[17,8,128]{2,1,0:T(8,128)S(1)} %get-tuple-element.45), channel_id=1, source_target_pairs={{0,7},{1,0},{2,1},{3,2},{4,3},{5,4},{6,5},{7,6},{8,15},{9,8},{10,9... | collective-permute-start | bytes 208904 | tf_op jit(solution)/shard_map/ppermute | solution.py:869
  12.8 1.8 %boxes.1 = (f32[8,16,16,128]{3,2,1,0:T(8,128)S(1)}, f32[8,16,16,128]{3,2,1,0:T(8,128)S(1)}) custom-call(f32[16,128]{1,0:T(8,128)S(1)} %tables.1.tables_ref, f32[4,32,1024]{2,1,0:T(8,128)S(1)} %get-tuple-element.38.raw_f_ref, f32[4,32,1024]{2,1,0:T(8,128)S(1)} %get-tuple-element.39.raw_q_ref), custom_call_target="tpu_custom_call" | custom-call | flops 3000000 | bytes 9000000 | tf_op jit(solution)/shard_map/boxes/pallas_call | solution.py:908
  14.6 0.0 collective-permute-done.rxlo_ref
  14.6 0.0 collective-permute-done.1.rxhi_ref
  14.6 0.2 collective-permute-done.2.rylo_ref
  14.8 0.0 collective-permute-done.3.ryhi_ref
  14.8 0.0 copy-done
  14.8 0.0 copy-done.3
  14.8 1.0 %first_residual.1 = (f32[16,16,128]{2,1,0:T(8,128)S(1)}, f32[16,16,128]{2,1,0:T(8,128)S(1)}, f32[37,8,128]{2,1,0:T(8,128)S(1)}, f32[37,8,128]{2,1,0:T(8,128)S(1)}) custom-call(f32[8,16,16,128]{3,2,1,0:T(8,128)S(1)} %get-tuple-element.40.f1_ref, f32[8,16,16,128]{3,2,1,0:T(8,128)S(1)} %get-tuple-element.41.q_ref, f32[256,128]{1,0:T(8,128)S(1)} %bitcast.5, ...), custom_call_target="tpu_custom_call" | custom-call | tf_op jit(solution)/shard_map/first_residual/pallas_call | solution.py:911
  15.8 0.1 collective-permute-start.4
  15.8 0.7 collective-permute-start.5
  16.5 6.0 %collective-permute-done.4.sa_ref.ea_ref = f32[37,8,128]{2,1,0:T(8,128)S(1)} collective-permute-done((f32[37,8,128]{2,1,0:T(8,128)S(1)}, f32[37,8,128]{2,1,0:T(8,128)S(1)}, u32[]{:S(2)}, u32[]{:S(2)}) %collective-permute-start.4) | collective-permute-done | bytes 151584 | tf_op jit(solution)/shard_map/ppermute | solution.py:875
  22.5 0.0 collective-permute-done.5.sb_ref.eb_ref
  22.6 0.1 collective-permute-start.6
  22.6 2.6 %collective-permute-start.7 = (f32[41,8,128]{2,1,0:T(8,128)S(1)}, f32[41,8,128]{2,1,0:T(8,128)S(1)}, u32[]{:S(2)}, u32[]{:S(2)}) collective-permute-start(f32[41,8,128]{2,1,0:T(8,128)S(1)} %get-tuple-element.52), channel_id=1, source_target_pairs={{0,7},{1,0},{2,1},{3,2},{4,3},{5,4},{6,5},{7,6},{8,15},{9,8},{10,9... | collective-permute-start | bytes 503816 | tf_op jit(solution)/shard_map/ppermute | solution.py:869
  25.3 0.6 inner.1
  25.8 1.5 %extend.1 = (f32[8,20,24,128]{3,2,1,0:T(8,128)S(1)}, f32[3,24,128]{2,1,0:T(8,128)S(1)}, f32[8,20,24,128]{3,2,1,0:T(8,128)S(1)}) custom-call(f32[8,16,16,128]{3,2,1,0:T(8,128)S(1)} %get-tuple-element.40.f1_ref, f32[8,16,16,128]{3,2,1,0:T(8,128)S(1)} %get-tuple-element.41.q_ref, f32[17,8,128]{2,1,0:T(8,128)S(1)} %collective-permute-done.rxlo_ref, ...), custom_call_target="tpu_custom_call" | custom-call | flops 2000000 | bytes 6000000 | tf_op jit(solution)/shard_map/extend/pallas_call | solution.py:919
  27.4 1.8 %collective-permute-done.6.eylo_ref = f32[41,8,128]{2,1,0:T(8,128)S(1)} collective-permute-done((f32[41,8,128]{2,1,0:T(8,128)S(1)}, f32[41,8,128]{2,1,0:T(8,128)S(1)}, u32[]{:S(2)}, u32[]{:S(2)}) %collective-permute-start.6) | collective-permute-done | bytes 167968 | tf_op jit(solution)/shard_map/ppermute | solution.py:869
  29.2 0.0 collective-permute-done.7.eyhi_ref
  29.2 0.9 %down_first.1 = (f32[32,8,128]{2,1,0:T(8,128)S(1)}, f32[32,32,128]{2,1,0:T(8,128)S(1)}, f32[32,32,128]{2,1,0:T(8,128)S(1)}, f32[16,32,128]{2,1,0:T(8,128)S(1)}, f32[16,32,128]{2,1,0:T(8,128)S(1)}) custom-call(f32[3,24,128]{2,1,0:T(8,128)S(1)} %get-tuple-element.48.live_ref.livex_ref, f32[16,16,128]{2,1,0:T(8,128)S(1)} %get-tuple-element.49.e0_ref, ...), custom_call_target="tpu_custom_call" | custom-call | tf_op jit(solution)/shard_map/down_first/pallas_call | solution.py:926
  30.0 13.9 %all_to_all.10.recv_ref = f32[32,8,128]{2,1,0:T(8,128)S(1)} all-to-all(f32[32,8,128]{2,1,0:T(8,128)S(1)} %get-tuple-element.56), channel_id=1, replica_groups=mesh['gx'=4,'gy'=8] {'gx','gy'}, dimensions={0} | all-to-all | bytes 262144 | tf_op jit(solution)/shard_map/all_to_all | solution.py:929
  44.0 3.5 %middle.1 = (f32[8,16,16,128]{3,2,1,0:T(8,128)S(1)}, f32[8,16,128]{2,1,0:T(8,128)S(1)}, f32[16,16,128]{2,1,0:T(8,128)S(1)}, f32[16,8,128]{2,1,0:T(8,128)S(1)}, f32[16,8,128]{2,1,0:T(8,128)S(1)}) custom-call(f32[32,8,128]{2,1,0:T(8,128)S(1)} %all_to_all.10.recv_ref, f32[32,32,128]{2,1,0:T(8,128)S(1)} %get-tuple-element.57.e0x_ref, ...), custom_call_target="tpu_custom_call" | custom-call | tf_op jit(solution)/shard_map/middle/pallas_call | solution.py:935
  47.5 1.3 %share.1 = f32[160,2,128]{2,1,0:T(2,128)} custom-call(f32[16,16,128]{2,1,0:T(8,128)S(1)} %get-tuple-element.63.e0_ref, f32[32,32,128]{2,1,0:T(8,128)S(1)} %get-tuple-element.58.k0x_ref, f32[16,32,128]{2,1,0:T(8,128)S(1)} %get-tuple-element.60.k1_ref), custom_call_target="tpu_custom_call" | custom-call | flops 1000000 | bytes 3000000 | tf_op jit(solution)/shard_map/share/pallas_call | solution.py:940
  48.8 2.6 %all-to-all-start.1 = ((f32[160,2,128]{2,1,0:T(2,128)}), f32[160,2,128]{2,1,0:T(2,128)S(1)}, u32[]{:S(2)}, u32[]{:S(2)}) async-start(f32[160,2,128]{2,1,0:T(2,128)} %share.1), calls=%async_computation.1 | async-start | bytes 327680 | tf_op jit(solution)/shard_map/all_to_all | solution.py:944
  51.4 1.7 %collective-permute-start.8 = (f32[16,8,128]{2,1,0:T(8,128)S(1)}, f32[16,8,128]{2,1,0:T(8,128)S(1)}, u32[]{:S(2)}, u32[]{:S(2)}) collective-permute-start(f32[16,8,128]{2,1,0:T(8,128)S(1)} %get-tuple-element.65), channel_id=1, source_target_pairs={{0,8},{8,16},{16,24},{24,0},{1,9},{9,17},{17,25},{25,1},{2,10},{10... | collective-permute-start | bytes 196616 | tf_op jit(solution)/shard_map/ppermute | solution.py:869
  53.1 2.1 %collective-permute-start.9 = (f32[16,8,128]{2,1,0:T(8,128)S(1)}, f32[16,8,128]{2,1,0:T(8,128)S(1)}, u32[]{:S(2)}, u32[]{:S(2)}) collective-permute-start(f32[16,8,128]{2,1,0:T(8,128)S(1)} %get-tuple-element.66), channel_id=1, source_target_pairs={{0,24},{8,0},{16,8},{24,16},{1,25},{9,1},{17,9},{25,17},{2,26},{10... | collective-permute-start | bytes 196616 | tf_op jit(solution)/shard_map/ppermute | solution.py:869
  55.2 0.3 settle.1
  55.6 5.0 %collective-permute-done.8.exlo_ref = f32[16,8,128]{2,1,0:T(8,128)S(1)} collective-permute-done((f32[16,8,128]{2,1,0:T(8,128)S(1)}, f32[16,8,128]{2,1,0:T(8,128)S(1)}, u32[]{:S(2)}, u32[]{:S(2)}) %collective-permute-start.8) | collective-permute-done | bytes 65568 | tf_op jit(solution)/shard_map/ppermute | solution.py:869
  60.6 0.0 collective-permute-done.9.exhi_ref
  60.6 0.0 all-to-all-done.1.recv_ref
  60.6 0.2 collective-permute-start.10
  60.8 2.5 %collective-permute-start.11 = (f32[17,8,128]{2,1,0:T(8,128)S(1)}, f32[17,8,128]{2,1,0:T(8,128)S(1)}, u32[]{:S(2)}, u32[]{:S(2)}) collective-permute-start(f32[17,8,128]{2,1,0:T(8,128)S(1)} %get-tuple-element.70), channel_id=1, source_target_pairs={{0,7},{1,0},{2,1},{3,2},{4,3},{5,4},{6,5},{7,6},{8,15},{9,8},{10,9... | collective-permute-start | bytes 208904 | tf_op jit(solution)/shard_map/ppermute | solution.py:869
  63.3 0.3 inner_last.1.e1i_ref
  63.6 1.3 %coarse.1.m2_ref = f32[8,32,128]{2,1,0:T(8,128)S(1)} custom-call(f32[160,2,128]{2,1,0:T(2,128)S(1)} %all-to-all-done.1.recv_ref, f32[8,16,128]{2,1,0:T(8,128)S(1)} %get-tuple-element.64.k2_ref), custom_call_target="tpu_custom_call" | custom-call | flops 2000000 | bytes 6000000 | tf_op jit(solution)/shard_map/coarse/pallas_call | solution.py:950
  65.0 0.3 collective-permute-done.10.eylo_ref
  65.3 0.0 collective-permute-done.11.eyhi_ref
  65.3 3.2 %last.1 = (f32[1,1,4,32,1024]{4,3,2,1,0:T(8,128)}, f32[256,128]{1,0:T(8,128)}) custom-call(f32[16,128]{1,0:T(8,128)S(1)} %tables.1.tables_ref, f32[8,32,128]{2,1,0:T(8,128)S(1)} %coarse.1.m2_ref, f32[16,16,128]{2,1,0:T(8,128)S(1)} %get-tuple-element.63.e0_ref, f32[16,8,128]{2,1,0:T(8,128)S(1)} %collective-permute-done.8.exlo_ref, ...), custom_call_target="tpu_custom_call" | custom-call | tf_op jit(solution)/shard_map/last/pallas_call | solution.py:956
  (4 shorter events, 0.1 us)
Async XLA Ops:
  0.6 14.1 %copy-start = (f32[16,16,128]{2,1,0:T(8,128)S(1)}, f32[16,16,128]{2,1,0:T(8,128)}, u32[]{:S(2)}) copy-start(f32[16,16,128]{2,1,0:T(8,128)} %param.9) | copy-start | bytes 393220
  1.3 0.7 copy-start.4
  2.5 1.0 %copy-start.1 = (f32[1,1,4,32,1024]{4,3,2,1,0:T(8,128)S(1)}, f32[1,1,4,32,1024]{4,3,2,1,0:T(8,128)}, u32[]{:S(2)}) copy-start(f32[1,1,4,32,1024]{4,3,2,1,0:T(8,128)} %rhs_ref.1) | copy-start | bytes 1572868
  3.6 1.0 %copy-start.2 = (f32[1,1,4,32,1024]{4,3,2,1,0:T(8,128)S(1)}, f32[1,1,4,32,1024]{4,3,2,1,0:T(8,128)}, u32[]{:S(2)}) copy-start(f32[1,1,4,32,1024]{4,3,2,1,0:T(8,128)} %beta_ref.1) | copy-start | bytes 1572868
  4.6 10.1 %copy-start.3 = (f32[16,16,128]{2,1,0:T(8,128)S(1)}, f32[16,16,128]{2,1,0:T(8,128)}, u32[]{:S(2)}) copy-start(f32[16,16,128]{2,1,0:T(8,128)} %param.10) | copy-start | bytes 393220
  5.0 9.6 %collective-permute-start = (f32[17,8,128]{2,1,0:T(8,128)S(1)}, f32[17,8,128]{2,1,0:T(8,128)S(1)}, u32[]{:S(2)}, u32[]{:S(2)}) collective-permute-start(f32[17,8,128]{2,1,0:T(8,128)S(1)} %get-tuple-element.42), channel_id=1, source_target_pairs={{0,8},{8,16},{16,24},{24,0},{1,9},{9,17},{17,25},{25,1},{2,10},{10... | collective-permute-start | bytes 208904 | tf_op jit(solution)/shard_map/ppermute | solution.py:869
  8.0 6.6 %collective-permute-start.1 = (f32[17,8,128]{2,1,0:T(8,128)S(1)}, f32[17,8,128]{2,1,0:T(8,128)S(1)}, u32[]{:S(2)}, u32[]{:S(2)}) collective-permute-start(f32[17,8,128]{2,1,0:T(8,128)S(1)} %get-tuple-element.43), channel_id=1, source_target_pairs={{0,24},{8,0},{16,8},{24,16},{1,25},{9,1},{17,9},{25,17},{2,26},{10... | collective-permute-start | bytes 208904 | tf_op jit(solution)/shard_map/ppermute | solution.py:869
  10.1 4.6 %collective-permute-start.2 = (f32[17,8,128]{2,1,0:T(8,128)S(1)}, f32[17,8,128]{2,1,0:T(8,128)S(1)}, u32[]{:S(2)}, u32[]{:S(2)}) collective-permute-start(f32[17,8,128]{2,1,0:T(8,128)S(1)} %get-tuple-element.44), channel_id=1, source_target_pairs={{0,1},{1,2},{2,3},{3,4},{4,5},{5,6},{6,7},{7,0},{8,9},{9,10},{10,1... | collective-permute-start | bytes 208904 | tf_op jit(solution)/shard_map/ppermute | solution.py:869
  10.1 4.6 %collective-permute-start.3 = (f32[17,8,128]{2,1,0:T(8,128)S(1)}, f32[17,8,128]{2,1,0:T(8,128)S(1)}, u32[]{:S(2)}, u32[]{:S(2)}) collective-permute-start(f32[17,8,128]{2,1,0:T(8,128)S(1)} %get-tuple-element.45), channel_id=1, source_target_pairs={{0,7},{1,0},{2,1},{3,2},{4,3},{5,4},{6,5},{7,6},{8,15},{9,8},{10,9... | collective-permute-start | bytes 208904 | tf_op jit(solution)/shard_map/ppermute | solution.py:869
  15.8 6.8 %collective-permute-start.4 = (f32[37,8,128]{2,1,0:T(8,128)S(1)}, f32[37,8,128]{2,1,0:T(8,128)S(1)}, u32[]{:S(2)}, u32[]{:S(2)}) collective-permute-start(f32[37,8,128]{2,1,0:T(8,128)S(1)} %get-tuple-element.46), channel_id=1, source_target_pairs={{0,8},{8,0},{16,24},{24,16},{1,9},{9,1},{17,25},{25,17},{2,10},{10... | collective-permute-start | bytes 454664 | tf_op jit(solution)/shard_map/ppermute | solution.py:875
  15.8 6.7 %collective-permute-start.5 = (f32[37,8,128]{2,1,0:T(8,128)S(1)}, f32[37,8,128]{2,1,0:T(8,128)S(1)}, u32[]{:S(2)}, u32[]{:S(2)}) collective-permute-start(f32[37,8,128]{2,1,0:T(8,128)S(1)} %get-tuple-element.47), channel_id=1, source_target_pairs={{0,0},{8,16},{16,8},{24,24},{1,1},{9,17},{17,9},{25,25},{2,2},{10,... | collective-permute-start | bytes 454664 | tf_op jit(solution)/shard_map/ppermute | solution.py:875
  22.6 6.6 %collective-permute-start.6 = (f32[41,8,128]{2,1,0:T(8,128)S(1)}, f32[41,8,128]{2,1,0:T(8,128)S(1)}, u32[]{:S(2)}, u32[]{:S(2)}) collective-permute-start(f32[41,8,128]{2,1,0:T(8,128)S(1)} %get-tuple-element.51), channel_id=1, source_target_pairs={{0,1},{1,2},{2,3},{3,4},{4,5},{5,6},{6,7},{7,0},{8,9},{9,10},{10,1... | collective-permute-start | bytes 503816 | tf_op jit(solution)/shard_map/ppermute | solution.py:869
  22.6 6.5 %collective-permute-start.7 = (f32[41,8,128]{2,1,0:T(8,128)S(1)}, f32[41,8,128]{2,1,0:T(8,128)S(1)}, u32[]{:S(2)}, u32[]{:S(2)}) collective-permute-start(f32[41,8,128]{2,1,0:T(8,128)S(1)} %get-tuple-element.52), channel_id=1, source_target_pairs={{0,7},{1,0},{2,1},{3,2},{4,3},{5,4},{6,5},{7,6},{8,15},{9,8},{10,9... | collective-permute-start | bytes 503816 | tf_op jit(solution)/shard_map/ppermute | solution.py:869
  48.8 11.8 %all-to-all-start.1 = ((f32[160,2,128]{2,1,0:T(2,128)}), f32[160,2,128]{2,1,0:T(2,128)S(1)}, u32[]{:S(2)}, u32[]{:S(2)}) async-start(f32[160,2,128]{2,1,0:T(2,128)} %share.1), calls=%async_computation.1 | async-start | bytes 327680 | tf_op jit(solution)/shard_map/all_to_all | solution.py:944
  51.4 9.2 %collective-permute-start.8 = (f32[16,8,128]{2,1,0:T(8,128)S(1)}, f32[16,8,128]{2,1,0:T(8,128)S(1)}, u32[]{:S(2)}, u32[]{:S(2)}) collective-permute-start(f32[16,8,128]{2,1,0:T(8,128)S(1)} %get-tuple-element.65), channel_id=1, source_target_pairs={{0,8},{8,16},{16,24},{24,0},{1,9},{9,17},{17,25},{25,1},{2,10},{10... | collective-permute-start | bytes 196616 | tf_op jit(solution)/shard_map/ppermute | solution.py:869
  53.1 7.5 %collective-permute-start.9 = (f32[16,8,128]{2,1,0:T(8,128)S(1)}, f32[16,8,128]{2,1,0:T(8,128)S(1)}, u32[]{:S(2)}, u32[]{:S(2)}) collective-permute-start(f32[16,8,128]{2,1,0:T(8,128)S(1)} %get-tuple-element.66), channel_id=1, source_target_pairs={{0,24},{8,0},{16,8},{24,16},{1,25},{9,1},{17,9},{25,17},{2,26},{10... | collective-permute-start | bytes 196616 | tf_op jit(solution)/shard_map/ppermute | solution.py:869
  60.6 4.7 %collective-permute-start.10 = (f32[17,8,128]{2,1,0:T(8,128)S(1)}, f32[17,8,128]{2,1,0:T(8,128)S(1)}, u32[]{:S(2)}, u32[]{:S(2)}) collective-permute-start(f32[17,8,128]{2,1,0:T(8,128)S(1)} %get-tuple-element.69), channel_id=1, source_target_pairs={{0,1},{1,2},{2,3},{3,4},{4,5},{5,6},{6,7},{7,0},{8,9},{9,10},{10,1... | collective-permute-start | bytes 208904 | tf_op jit(solution)/shard_map/ppermute | solution.py:869
  60.8 4.5 %collective-permute-start.11 = (f32[17,8,128]{2,1,0:T(8,128)S(1)}, f32[17,8,128]{2,1,0:T(8,128)S(1)}, u32[]{:S(2)}, u32[]{:S(2)}) collective-permute-start(f32[17,8,128]{2,1,0:T(8,128)S(1)} %get-tuple-element.70), channel_id=1, source_target_pairs={{0,7},{1,0},{2,1},{3,2},{4,3},{5,4},{6,5},{7,6},{8,15},{9,8},{10,9... | collective-permute-start | bytes 208904 | tf_op jit(solution)/shard_map/ppermute | solution.py:869

commit v8 on v7

--- a/solution.py
+++ b/solution.py
@@ -159,8 +159,10 @@
         raw_q_ref[s] = q
         raw_f_ref[s] = rhs_ref[0, 0, s] / q
     slots = tables_ref[0:8, :]
-    for ref in (fxlo_ref, fxhi_ref, fylo_ref, fyhi_ref):
+    for ref in (fxlo_ref, fxhi_ref):
         ref[16] = slots
+    for ref in (fylo_ref, fyhi_ref):
+        ref[12] = slots
     for xt in range(4):
         for t in range(8) if xt in (0, 3) else (0, 7):
             rows, cols = slice(8 * xt, 8 * xt + 8), slice(t * LANES, (t + 1) * LANES)
@@ -171,10 +173,10 @@
                     fxlo_ref[y16, at : at + 4, :] = v[0:4]
                 if xt == 3:
                     fxhi_ref[y16, at : at + 4, :] = v[4:8]
-                if t == 0:
+                if t == 0 and yy < 3:
                     fylo_ref[yy * 4 + xt] = v
-                if t == 7:
-                    fyhi_ref[yy * 4 + xt] = v
+                if t == 7 and yy > 0:
+                    fyhi_ref[(yy - 1) * 4 + xt] = v
 
 
 def boxes_kernel(tables_ref, raw_f_ref, raw_q_ref, f1_ref, q_ref, f_ref, c_ref):
@@ -236,10 +238,11 @@
     lo_here, hi_here = inside("gy")
     slots = []
     for n, (ref, here, first) in enumerate(((ryhi_ref, hi_here, 16), (rylo_ref, lo_here, 18))):
-        own = kept(here, spread(ref[16, 0:1, :], 32))
+        own = kept(here, spread(ref[12, 0:1, :], 32))
         slots.append(own)
         for layer in range(layers) if n == 0 else range(4 - layers, 4):
-            v = jnp.concatenate([ref[layer * 4 + xt] for xt in range(4)], axis=0)
+            at = (layer - n) * 4
+            v = jnp.concatenate([ref[at + xt] for xt in range(4)], axis=0)
             for pz in range(2):
                 ys_ref[n, layer, pz] = expand(v, own, pz)
     for n, first in enumerate((16, 18)):
@@ -288,20 +291,20 @@
 
     each(16, row)
     lo_here, hi_here = inside("gy")
-    for layer in range(4):
+    for layer in range(3):
         hi, lo = ryhi_ref[layer * 4], rylo_ref[layer * 4]
         to_lo = jnp.concatenate([hi[0:4], lo[0:4]], axis=0)
         hi, lo = ryhi_ref[layer * 4 + 3], rylo_ref[layer * 4 + 3]
         put(32 + layer, to_lo, jnp.concatenate([hi[4:8], lo[4:8]], axis=0))
     slots = jnp.concatenate(
         [
-            kept(hi_here, ryhi_ref[16, 0:1, :]),
-            kept(lo_here, rylo_ref[16, 0:1, :]),
+            kept(hi_here, ryhi_ref[12, 0:1, :]),
+            kept(lo_here, rylo_ref[12, 0:1, :]),
             jnp.zeros((6, LANES), F32),
         ],
         axis=0,
     )
-    put(36, slots, slots)
+    put(35, slots, slots)
 
 
 def extend_kernel(
@@ -312,29 +315,33 @@
     xlo_here, xhi_here = inside("gx")
     row8 = lax.broadcasted_iota(jnp.int32, (8, LANES), 0)
     hi_slots, lo_slots = extend_x(f1x_ref, f1_ref, rxlo_ref, rxhi_ref, xs_ref)
-    y_slots = extend_y(f1x_ref, rylo_ref, ryhi_ref, ys_ref, 4)
+    y_slots = extend_y(f1x_ref, rylo_ref, ryhi_ref, ys_ref, 3)
     own_live = jnp.where(q_ref[0, 0] > 0.0, 1.0, 0.0)
     side = jnp.where(row8 < 4, hi_slots, lo_slots)
     livex_ref[0] = jnp.concatenate([own_live, jnp.where(side > 0.0, 1.0, 0.0)], axis=0)
     for n, first in enumerate((16, 18)):
-        hi = kept(xhi_here, spread(sxhi_ref[36][n : n + 1], 8))
-        lo = kept(xlo_here, spread(sxlo_ref[36][n : n + 1], 8))
+        hi = kept(xhi_here, spread(sxhi_ref[35][n : n + 1], 8))
+        lo = kept(xlo_here, spread(sxlo_ref[35][n : n + 1], 8))
         side = jnp.where(row8 < 4, hi, lo)
         live = jnp.concatenate([y_slots[n][0:16], side], axis=0) > 0.0
         livex_ref[1 + n] = jnp.where(live, 1.0, 0.0)
-        for layer in range(4):
+        for layer in range(n, n + 3):
             at = slice(4 * n, 4 * n + 4)
-            v = jnp.concatenate([sxhi_ref[32 + layer][at], sxlo_ref[32 + layer][at]], axis=0)
+            v = jnp.concatenate([sxhi_ref[32 + layer - n][at], sxlo_ref[32 + layer - n][at]], axis=0)
             for pz in range(2):
                 cs_ref[n, layer, pz] = expand(v, side, pz)
     for n, first in enumerate((16, 18)):
-        for layer in range(4):
+        for layer in range(n, n + 3):
             y, py = first + layer // 2, layer % 2
             for px in range(2):
                 for pz in range(2):
                     o = px * 4 + py * 2 + pz
                     f1x_ref[o, y, 16:18, :] = cs_ref[n, layer, pz, pl.ds(px, 2, stride=2), :]
                     f1x_ref[o, y, 22:24, :] = cs_ref[n, layer, pz, pl.ds(4 + px, 2, stride=2), :]
+    for y, py in ((17, 1), (18, 0)):
+        for px in range(2):
+            for pz in range(2):
+                f1x_ref[px * 4 + py * 2 + pz, y] = jnp.zeros((XF, LANES), F32)
 
     def sweep(y):
         cur, new = fine_relax(f1x_ref, y, None)
@@ -901,7 +908,7 @@
 
     tables = call(tables_kernel, "tables", [(16, LANES)], 2, 0, 0)(slot_site, box_count)[0]
     fxlo, fxhi, fylo, fyhi, raw_f, raw_q = call(
-        faces_kernel, "faces", [tiles(17)] * 4 + [raw, raw], 0, 0, 3
+        faces_kernel, "faces", [tiles(17)] * 2 + [tiles(13)] * 2 + [raw, raw], 0, 0, 3
     )(tables, fine_rhs, fine_beta)
     rxlo, rxhi = from_sides(fxlo, fxhi, "gx")
     rylo, ryhi = from_sides(fylo, fyhi, "gy")
@@ -909,7 +916,7 @@
         boxes_kernel, "boxes", [octets, octets], 0, 0, 3, [rows, rows], beside(3)
     )(tables, raw_f, raw_q)
     e0, k0, ea, eb = call(
-        first_kernel, "first_residual", [own, own, tiles(37), tiles(37)], 0, 0, 8, [fine_ext, x_side, y_side]
+        first_kernel, "first_residual", [own, own, tiles(36), tiles(36)], 0, 0, 8, [fine_ext, x_side, y_side]
     )(f1, q, base_beta.reshape(256, LANES), rhs, rxlo, rxhi, rylo, ryhi)
     sa, sb = swap_pairs(ea, "gx", 0), swap_pairs(eb, "gx", 1)
     eylo, eyhi = call(

time: 69.1 us -> 68.6 us (level)
  transfers between devices with their start and end apart: 13 -> 13, of which waited for: 5 -> 4; matrix products, arithmetic and copies ran while one was open for 0% -> 0% of each run, Pallas kernels for 9% -> 9%
where the time goes in v8:
time: 68.6 us; the launch traced here: 67.9 us
  starting transfers between devices  20.4 us (30%)
  Pallas kernels  16.6 us (24%)
  blocking collectives  13.6 us (20%)
  waiting for transfers between devices  13.1 us (19%)
  local copies, waits for them, and re-layouts  2.73 us (4%)
  between operations  1.51 us (2%)
    ppermute x10, starting transfers between devices, step(): lax.ppermute(value, axis, [(i, (i + by) % count) for i in range(count)])  17.1 us
    all_to_all x1, blocking collectives, local(): recv = lax.all_to_all(send, ('gx', 'gy'), 0, 0, tiled=True)  13.6 us
    ppermute x10, waiting for transfers between devices, step(): lax.ppermute(value, axis, [(i, (i + by) % count) for i in range(count)])  7.24 us
    ppermute x2, waiting for transfers between devices, swap_pairs(): lax.ppermute(value, axis, [(i, j if 0 <= j < count else i) for i, j in en...  5.89 us
    pallas_call x1, Pallas kernels, local(): call(middle_kernel, 'middle', [octets, coarse, own, tiles(16), tiles(16)]...  3.47 us
    pallas_call x1, Pallas kernels, local(): call(last_kernel, 'last', [fine_rhs.shape, (256, LANES)], 0, 0, 13, [half...  3.17 us
    unnamed x10, local copies, waits for them, and re-layouts  2.73 us
    all_to_all x1, starting transfers between devices, local(): recv = lax.all_to_all(send, ('gx', 'gy'), 0, 0, tiled=True)  2.58 us
  transfers between devices with their start and end apart: 13, of which 4 were waited for; matrix products, arithmetic and copies ran while one was open for 0% of the time, Pallas kernels for 9%

profile of v8, /device:TPU:0, one launch (start us, length us, event | category | flops | bytes accessed | tf_op | source)
XLA Modules:
  0.0 67.9 jit_solution(14117487385412531342)
XLA Ops:
  0.6 0.0 copy-start
  1.3 0.0 copy-start.4
  1.3 0.6 copy-done.4
  2.0 0.6 tables.1.tables_ref
  2.5 0.0 copy-start.1
  2.6 1.0 %copy-done.1 = f32[1,1,4,32,1024]{4,3,2,1,0:T(8,128)S(1)} copy-done((f32[1,1,4,32,1024]{4,3,2,1,0:T(8,128)S(1)}, f32[1,1,4,32,1024]{4,3,2,1,0:T(8,128)}, u32[]{:S(2)}) %copy-start.1) | copy-done | bytes 524312
  3.6 1.0 %copy-done.2 = f32[1,1,4,32,1024]{4,3,2,1,0:T(8,128)S(1)} copy-done((f32[1,1,4,32,1024]{4,3,2,1,0:T(8,128)S(1)}, f32[1,1,4,32,1024]{4,3,2,1,0:T(8,128)}, u32[]{:S(2)}) %copy-start.2) | copy-done | bytes 524312
  4.6 0.3 faces.1
  4.9 3.1 %collective-permute-start = (f32[17,8,128]{2,1,0:T(8,128)S(1)}, f32[17,8,128]{2,1,0:T(8,128)S(1)}, u32[]{:S(2)}, u32[]{:S(2)}) collective-permute-start(f32[17,8,128]{2,1,0:T(8,128)S(1)} %get-tuple-element.42), channel_id=1, source_target_pairs={{0,8},{8,16},{16,24},{24,0},{1,9},{9,17},{17,25},{25,1},{2,10},{10... | collective-permute-start | bytes 208904 | tf_op jit(solution)/shard_map/ppermute | solution.py:876
  8.0 2.1 %collective-permute-start.1 = (f32[17,8,128]{2,1,0:T(8,128)S(1)}, f32[17,8,128]{2,1,0:T(8,128)S(1)}, u32[]{:S(2)}, u32[]{:S(2)}) collective-permute-start(f32[17,8,128]{2,1,0:T(8,128)S(1)} %get-tuple-element.43), channel_id=1, source_target_pairs={{0,24},{8,0},{16,8},{24,16},{1,25},{9,1},{17,9},{25,17},{2,26},{10... | collective-permute-start | bytes 208904 | tf_op jit(solution)/shard_map/ppermute | solution.py:876
  10.1 0.0 collective-permute-start.2
  10.1 2.6 %collective-permute-start.3 = (f32[13,8,128]{2,1,0:T(8,128)S(1)}, f32[13,8,128]{2,1,0:T(8,128)S(1)}, u32[]{:S(2)}, u32[]{:S(2)}) collective-permute-start(f32[13,8,128]{2,1,0:T(8,128)S(1)} %get-tuple-element.45), channel_id=1, source_target_pairs={{0,7},{1,0},{2,1},{3,2},{4,3},{5,4},{6,5},{7,6},{8,15},{9,8},{10,9... | collective-permute-start | bytes 159752 | tf_op jit(solution)/shard_map/ppermute | solution.py:876
  12.8 1.8 %boxes.1 = (f32[8,16,16,128]{3,2,1,0:T(8,128)S(1)}, f32[8,16,16,128]{3,2,1,0:T(8,128)S(1)}) custom-call(f32[16,128]{1,0:T(8,128)S(1)} %tables.1.tables_ref, f32[4,32,1024]{2,1,0:T(8,128)S(1)} %get-tuple-element.38.raw_f_ref, f32[4,32,1024]{2,1,0:T(8,128)S(1)} %get-tuple-element.39.raw_q_ref), custom_call_target="tpu_custom_call" | custom-call | flops 3000000 | bytes 9000000 | tf_op jit(solution)/shard_map/boxes/pallas_call | solution.py:915
  14.6 0.0 collective-permute-done.2.rylo_ref
  14.6 0.0 collective-permute-done.3.ryhi_ref
  14.6 0.0 collective-permute-done.rxlo_ref
  14.6 0.0 collective-permute-done.1.rxhi_ref
  14.6 0.0 copy-done
  14.6 0.0 copy-done.3
  14.6 1.0 %first_residual.1 = (f32[16,16,128]{2,1,0:T(8,128)S(1)}, f32[16,16,128]{2,1,0:T(8,128)S(1)}, f32[36,8,128]{2,1,0:T(8,128)S(1)}, f32[36,8,128]{2,1,0:T(8,128)S(1)}) custom-call(f32[8,16,16,128]{3,2,1,0:T(8,128)S(1)} %get-tuple-element.40.f1_ref, f32[8,16,16,128]{3,2,1,0:T(8,128)S(1)} %get-tuple-element.41.q_ref, f32[256,128]{1,0:T(8,128)S(1)} %bitcast.5, ...), custom_call_target="tpu_custom_call" | custom-call | tf_op jit(solution)/shard_map/first_residual/pallas_call | solution.py:918
  15.6 0.1 collective-permute-start.4
  15.7 0.7 collective-permute-start.5
  16.4 5.9 %collective-permute-done.4.sa_ref.ea_ref = f32[36,8,128]{2,1,0:T(8,128)S(1)} collective-permute-done((f32[36,8,128]{2,1,0:T(8,128)S(1)}, f32[36,8,128]{2,1,0:T(8,128)S(1)}, u32[]{:S(2)}, u32[]{:S(2)}) %collective-permute-start.4) | collective-permute-done | bytes 147488 | tf_op jit(solution)/shard_map/ppermute | solution.py:882
  22.3 0.0 collective-permute-done.5.sb_ref.eb_ref
  22.3 0.1 collective-permute-start.6
  22.4 2.6 %collective-permute-start.7 = (f32[41,8,128]{2,1,0:T(8,128)S(1)}, f32[41,8,128]{2,1,0:T(8,128)S(1)}, u32[]{:S(2)}, u32[]{:S(2)}) collective-permute-start(f32[41,8,128]{2,1,0:T(8,128)S(1)} %get-tuple-element.52), channel_id=1, source_target_pairs={{0,7},{1,0},{2,1},{3,2},{4,3},{5,4},{6,5},{7,6},{8,15},{9,8},{10,9... | collective-permute-start | bytes 503816 | tf_op jit(solution)/shard_map/ppermute | solution.py:876
  25.0 0.6 inner.1
  25.6 1.4 %extend.1 = (f32[8,20,24,128]{3,2,1,0:T(8,128)S(1)}, f32[3,24,128]{2,1,0:T(8,128)S(1)}, f32[8,20,24,128]{3,2,1,0:T(8,128)S(1)}) custom-call(f32[8,16,16,128]{3,2,1,0:T(8,128)S(1)} %get-tuple-element.40.f1_ref, f32[8,16,16,128]{3,2,1,0:T(8,128)S(1)} %get-tuple-element.41.q_ref, f32[17,8,128]{2,1,0:T(8,128)S(1)} %collective-permute-done.rxlo_ref, ...), custom_call_target="tpu_custom_call" | custom-call | flops 2000000 | bytes 6000000 | tf_op jit(solution)/shard_map/extend/pallas_call | solution.py:926
  27.1 1.9 %collective-permute-done.6.eylo_ref = f32[41,8,128]{2,1,0:T(8,128)S(1)} collective-permute-done((f32[41,8,128]{2,1,0:T(8,128)S(1)}, f32[41,8,128]{2,1,0:T(8,128)S(1)}, u32[]{:S(2)}, u32[]{:S(2)}) %collective-permute-start.6) | collective-permute-done | bytes 167968 | tf_op jit(solution)/shard_map/ppermute | solution.py:876
  29.0 0.0 collective-permute-done.7.eyhi_ref
  29.0 0.9 %down_first.1 = (f32[32,8,128]{2,1,0:T(8,128)S(1)}, f32[32,32,128]{2,1,0:T(8,128)S(1)}, f32[32,32,128]{2,1,0:T(8,128)S(1)}, f32[16,32,128]{2,1,0:T(8,128)S(1)}, f32[16,32,128]{2,1,0:T(8,128)S(1)}) custom-call(f32[3,24,128]{2,1,0:T(8,128)S(1)} %get-tuple-element.48.live_ref.livex_ref, f32[16,16,128]{2,1,0:T(8,128)S(1)} %get-tuple-element.49.e0_ref, ...), custom_call_target="tpu_custom_call" | custom-call | tf_op jit(solution)/shard_map/down_first/pallas_call | solution.py:933
  29.8 13.6 %all_to_all.10.recv_ref = f32[32,8,128]{2,1,0:T(8,128)S(1)} all-to-all(f32[32,8,128]{2,1,0:T(8,128)S(1)} %get-tuple-element.56), channel_id=1, replica_groups=mesh['gx'=4,'gy'=8] {'gx','gy'}, dimensions={0} | all-to-all | bytes 262144 | tf_op jit(solution)/shard_map/all_to_all | solution.py:936
  43.4 3.5 %middle.1 = (f32[8,16,16,128]{3,2,1,0:T(8,128)S(1)}, f32[8,16,128]{2,1,0:T(8,128)S(1)}, f32[16,16,128]{2,1,0:T(8,128)S(1)}, f32[16,8,128]{2,1,0:T(8,128)S(1)}, f32[16,8,128]{2,1,0:T(8,128)S(1)}) custom-call(f32[32,8,128]{2,1,0:T(8,128)S(1)} %all_to_all.10.recv_ref, f32[32,32,128]{2,1,0:T(8,128)S(1)} %get-tuple-element.57.e0x_ref, ...), custom_call_target="tpu_custom_call" | custom-call | tf_op jit(solution)/shard_map/middle/pallas_call | solution.py:942
  46.9 1.3 %share.1 = f32[160,2,128]{2,1,0:T(2,128)} custom-call(f32[16,16,128]{2,1,0:T(8,128)S(1)} %get-tuple-element.63.e0_ref, f32[32,32,128]{2,1,0:T(8,128)S(1)} %get-tuple-element.58.k0x_ref, f32[16,32,128]{2,1,0:T(8,128)S(1)} %get-tuple-element.60.k1_ref), custom_call_target="tpu_custom_call" | custom-call | flops 1000000 | bytes 3000000 | tf_op jit(solution)/shard_map/share/pallas_call | solution.py:947
  48.2 2.6 %all-to-all-start.1 = ((f32[160,2,128]{2,1,0:T(2,128)}), f32[160,2,128]{2,1,0:T(2,128)S(1)}, u32[]{:S(2)}, u32[]{:S(2)}) async-start(f32[160,2,128]{2,1,0:T(2,128)} %share.1), calls=%async_computation.1 | async-start | bytes 327680 | tf_op jit(solution)/shard_map/all_to_all | solution.py:951
  50.8 1.7 %collective-permute-start.8 = (f32[16,8,128]{2,1,0:T(8,128)S(1)}, f32[16,8,128]{2,1,0:T(8,128)S(1)}, u32[]{:S(2)}, u32[]{:S(2)}) collective-permute-start(f32[16,8,128]{2,1,0:T(8,128)S(1)} %get-tuple-element.65), channel_id=1, source_target_pairs={{0,8},{8,16},{16,24},{24,0},{1,9},{9,17},{17,25},{25,1},{2,10},{10... | collective-permute-start | bytes 196616 | tf_op jit(solution)/shard_map/ppermute | solution.py:876
  52.5 2.1 %collective-permute-start.9 = (f32[16,8,128]{2,1,0:T(8,128)S(1)}, f32[16,8,128]{2,1,0:T(8,128)S(1)}, u32[]{:S(2)}, u32[]{:S(2)}) collective-permute-start(f32[16,8,128]{2,1,0:T(8,128)S(1)} %get-tuple-element.66), channel_id=1, source_target_pairs={{0,24},{8,0},{16,8},{24,16},{1,25},{9,1},{17,9},{25,17},{2,26},{10... | collective-permute-start | bytes 196616 | tf_op jit(solution)/shard_map/ppermute | solution.py:876
  54.7 0.3 settle.1
  55.0 5.0 %collective-permute-done.8.exlo_ref = f32[16,8,128]{2,1,0:T(8,128)S(1)} collective-permute-done((f32[16,8,128]{2,1,0:T(8,128)S(1)}, f32[16,8,128]{2,1,0:T(8,128)S(1)}, u32[]{:S(2)}, u32[]{:S(2)}) %collective-permute-start.8) | collective-permute-done | bytes 65568 | tf_op jit(solution)/shard_map/ppermute | solution.py:876
  60.0 0.0 collective-permute-done.9.exhi_ref
  60.0 0.0 all-to-all-done.1.recv_ref
  60.1 0.2 collective-permute-start.10
  60.3 2.5 %collective-permute-start.11 = (f32[17,8,128]{2,1,0:T(8,128)S(1)}, f32[17,8,128]{2,1,0:T(8,128)S(1)}, u32[]{:S(2)}, u32[]{:S(2)}) collective-permute-start(f32[17,8,128]{2,1,0:T(8,128)S(1)} %get-tuple-element.70), channel_id=1, source_target_pairs={{0,7},{1,0},{2,1},{3,2},{4,3},{5,4},{6,5},{7,6},{8,15},{9,8},{10,9... | collective-permute-start | bytes 208904 | tf_op jit(solution)/shard_map/ppermute | solution.py:876
  62.8 0.3 inner_last.1.e1i_ref
  63.1 1.3 %coarse.1.m2_ref = f32[8,32,128]{2,1,0:T(8,128)S(1)} custom-call(f32[160,2,128]{2,1,0:T(2,128)S(1)} %all-to-all-done.1.recv_ref, f32[8,16,128]{2,1,0:T(8,128)S(1)} %get-tuple-element.64.k2_ref), custom_call_target="tpu_custom_call" | custom-call | flops 2000000 | bytes 6000000 | tf_op jit(solution)/shard_map/coarse/pallas_call | solution.py:957
  64.4 0.3 collective-permute-done.10.eylo_ref
  64.8 0.0 collective-permute-done.11.eyhi_ref
  64.8 3.2 %last.1 = (f32[1,1,4,32,1024]{4,3,2,1,0:T(8,128)}, f32[256,128]{1,0:T(8,128)}) custom-call(f32[16,128]{1,0:T(8,128)S(1)} %tables.1.tables_ref, f32[8,32,128]{2,1,0:T(8,128)S(1)} %coarse.1.m2_ref, f32[16,16,128]{2,1,0:T(8,128)S(1)} %get-tuple-element.63.e0_ref, f32[16,8,128]{2,1,0:T(8,128)S(1)} %collective-permute-done.8.exlo_ref, ...), custom_call_target="tpu_custom_call" | custom-call | tf_op jit(solution)/shard_map/last/pallas_call | solution.py:963
  (4 shorter events, 0.1 us)
Async XLA Ops:
  0.6 14.0 %copy-start = (f32[16,16,128]{2,1,0:T(8,128)S(1)}, f32[16,16,128]{2,1,0:T(8,128)}, u32[]{:S(2)}) copy-start(f32[16,16,128]{2,1,0:T(8,128)} %param.9) | copy-start | bytes 393220
  1.3 0.7 copy-start.4
  2.5 1.0 %copy-start.1 = (f32[1,1,4,32,1024]{4,3,2,1,0:T(8,128)S(1)}, f32[1,1,4,32,1024]{4,3,2,1,0:T(8,128)}, u32[]{:S(2)}) copy-start(f32[1,1,4,32,1024]{4,3,2,1,0:T(8,128)} %rhs_ref.1) | copy-start | bytes 1572868
  3.6 1.0 %copy-start.2 = (f32[1,1,4,32,1024]{4,3,2,1,0:T(8,128)S(1)}, f32[1,1,4,32,1024]{4,3,2,1,0:T(8,128)}, u32[]{:S(2)}) copy-start(f32[1,1,4,32,1024]{4,3,2,1,0:T(8,128)} %beta_ref.1) | copy-start | bytes 1572868
  4.6 10.0 %copy-start.3 = (f32[16,16,128]{2,1,0:T(8,128)S(1)}, f32[16,16,128]{2,1,0:T(8,128)}, u32[]{:S(2)}) copy-start(f32[16,16,128]{2,1,0:T(8,128)} %param.10) | copy-start | bytes 393220
  4.9 9.7 %collective-permute-start = (f32[17,8,128]{2,1,0:T(8,128)S(1)}, f32[17,8,128]{2,1,0:T(8,128)S(1)}, u32[]{:S(2)}, u32[]{:S(2)}) collective-permute-start(f32[17,8,128]{2,1,0:T(8,128)S(1)} %get-tuple-element.42), channel_id=1, source_target_pairs={{0,8},{8,16},{16,24},{24,0},{1,9},{9,17},{17,25},{25,1},{2,10},{10... | collective-permute-start | bytes 208904 | tf_op jit(solution)/shard_map/ppermute | solution.py:876
  8.0 6.6 %collective-permute-start.1 = (f32[17,8,128]{2,1,0:T(8,128)S(1)}, f32[17,8,128]{2,1,0:T(8,128)S(1)}, u32[]{:S(2)}, u32[]{:S(2)}) collective-permute-start(f32[17,8,128]{2,1,0:T(8,128)S(1)} %get-tuple-element.43), channel_id=1, source_target_pairs={{0,24},{8,0},{16,8},{24,16},{1,25},{9,1},{17,9},{25,17},{2,26},{10... | collective-permute-start | bytes 208904 | tf_op jit(solution)/shard_map/ppermute | solution.py:876
  10.1 4.5 %collective-permute-start.2 = (f32[13,8,128]{2,1,0:T(8,128)S(1)}, f32[13,8,128]{2,1,0:T(8,128)S(1)}, u32[]{:S(2)}, u32[]{:S(2)}) collective-permute-start(f32[13,8,128]{2,1,0:T(8,128)S(1)} %get-tuple-element.44), channel_id=1, source_target_pairs={{0,1},{1,2},{2,3},{3,4},{4,5},{5,6},{6,7},{7,0},{8,9},{9,10},{10,1... | collective-permute-start | bytes 159752 | tf_op jit(solution)/shard_map/ppermute | solution.py:876
  10.1 4.5 %collective-permute-start.3 = (f32[13,8,128]{2,1,0:T(8,128)S(1)}, f32[13,8,128]{2,1,0:T(8,128)S(1)}, u32[]{:S(2)}, u32[]{:S(2)}) collective-permute-start(f32[13,8,128]{2,1,0:T(8,128)S(1)} %get-tuple-element.45), channel_id=1, source_target_pairs={{0,7},{1,0},{2,1},{3,2},{4,3},{5,4},{6,5},{7,6},{8,15},{9,8},{10,9... | collective-permute-start | bytes 159752 | tf_op jit(solution)/shard_map/ppermute | solution.py:876
  15.6 6.6 %collective-permute-start.4 = (f32[36,8,128]{2,1,0:T(8,128)S(1)}, f32[36,8,128]{2,1,0:T(8,128)S(1)}, u32[]{:S(2)}, u32[]{:S(2)}) collective-permute-start(f32[36,8,128]{2,1,0:T(8,128)S(1)} %get-tuple-element.46), channel_id=1, source_target_pairs={{0,8},{8,0},{16,24},{24,16},{1,9},{9,1},{17,25},{25,17},{2,10},{10... | collective-permute-start | bytes 442376 | tf_op jit(solution)/shard_map/ppermute | solution.py:882
  15.7 6.6 %collective-permute-start.5 = (f32[36,8,128]{2,1,0:T(8,128)S(1)}, f32[36,8,128]{2,1,0:T(8,128)S(1)}, u32[]{:S(2)}, u32[]{:S(2)}) collective-permute-start(f32[36,8,128]{2,1,0:T(8,128)S(1)} %get-tuple-element.47), channel_id=1, source_target_pairs={{0,0},{8,16},{16,8},{24,24},{1,1},{9,17},{17,9},{25,25},{2,2},{10,... | collective-permute-start | bytes 442376 | tf_op jit(solution)/shard_map/ppermute | solution.py:882
  22.3 6.6 %collective-permute-start.6 = (f32[41,8,128]{2,1,0:T(8,128)S(1)}, f32[41,8,128]{2,1,0:T(8,128)S(1)}, u32[]{:S(2)}, u32[]{:S(2)}) collective-permute-start(f32[41,8,128]{2,1,0:T(8,128)S(1)} %get-tuple-element.51), channel_id=1, source_target_pairs={{0,1},{1,2},{2,3},{3,4},{4,5},{5,6},{6,7},{7,0},{8,9},{9,10},{10,1... | collective-permute-start | bytes 503816 | tf_op jit(solution)/shard_map/ppermute | solution.py:876
  22.4 6.6 %collective-permute-start.7 = (f32[41,8,128]{2,1,0:T(8,128)S(1)}, f32[41,8,128]{2,1,0:T(8,128)S(1)}, u32[]{:S(2)}, u32[]{:S(2)}) collective-permute-start(f32[41,8,128]{2,1,0:T(8,128)S(1)} %get-tuple-element.52), channel_id=1, source_target_pairs={{0,7},{1,0},{2,1},{3,2},{4,3},{5,4},{6,5},{7,6},{8,15},{9,8},{10,9... | collective-permute-start | bytes 503816 | tf_op jit(solution)/shard_map/ppermute | solution.py:876
  48.2 11.8 %all-to-all-start.1 = ((f32[160,2,128]{2,1,0:T(2,128)}), f32[160,2,128]{2,1,0:T(2,128)S(1)}, u32[]{:S(2)}, u32[]{:S(2)}) async-start(f32[160,2,128]{2,1,0:T(2,128)} %share.1), calls=%async_computation.1 | async-start | bytes 327680 | tf_op jit(solution)/shard_map/all_to_all | solution.py:951
  50.8 9.2 %collective-permute-start.8 = (f32[16,8,128]{2,1,0:T(8,128)S(1)}, f32[16,8,128]{2,1,0:T(8,128)S(1)}, u32[]{:S(2)}, u32[]{:S(2)}) collective-permute-start(f32[16,8,128]{2,1,0:T(8,128)S(1)} %get-tuple-element.65), channel_id=1, source_target_pairs={{0,8},{8,16},{16,24},{24,0},{1,9},{9,17},{17,25},{25,1},{2,10},{10... | collective-permute-start | bytes 196616 | tf_op jit(solution)/shard_map/ppermute | solution.py:876
  52.5 7.5 %collective-permute-start.9 = (f32[16,8,128]{2,1,0:T(8,128)S(1)}, f32[16,8,128]{2,1,0:T(8,128)S(1)}, u32[]{:S(2)}, u32[]{:S(2)}) collective-permute-start(f32[16,8,128]{2,1,0:T(8,128)S(1)} %get-tuple-element.66), channel_id=1, source_target_pairs={{0,24},{8,0},{16,8},{24,16},{1,25},{9,1},{17,9},{25,17},{2,26},{10... | collective-permute-start | bytes 196616 | tf_op jit(solution)/shard_map/ppermute | solution.py:876
  60.1 4.7 %collective-permute-start.10 = (f32[17,8,128]{2,1,0:T(8,128)S(1)}, f32[17,8,128]{2,1,0:T(8,128)S(1)}, u32[]{:S(2)}, u32[]{:S(2)}) collective-permute-start(f32[17,8,128]{2,1,0:T(8,128)S(1)} %get-tuple-element.69), channel_id=1, source_target_pairs={{0,1},{1,2},{2,3},{3,4},{4,5},{5,6},{6,7},{7,0},{8,9},{9,10},{10,1... | collective-permute-start | bytes 208904 | tf_op jit(solution)/shard_map/ppermute | solution.py:876
  60.3 4.5 %collective-permute-start.11 = (f32[17,8,128]{2,1,0:T(8,128)S(1)}, f32[17,8,128]{2,1,0:T(8,128)S(1)}, u32[]{:S(2)}, u32[]{:S(2)}) collective-permute-start(f32[17,8,128]{2,1,0:T(8,128)S(1)} %get-tuple-element.70), channel_id=1, source_target_pairs={{0,7},{1,0},{2,1},{3,2},{4,3},{5,4},{6,5},{7,6},{8,15},{9,8},{10,9... | collective-permute-start | bytes 208904 | tf_op jit(solution)/shard_map/ppermute | solution.py:876

commit v9 on v8

--- a/solution.py
+++ b/solution.py
@@ -815,8 +815,8 @@
 def last_kernel(
     tables_ref, m2_ref, e0_ref, exlo_ref, exhi_ref, eylo_ref, eyhi_ref, k0x_ref, k1_ref,
     c4_ref, m4_ref, livex_ref, e1i_ref,
-    fine_ref, base_ref,
-    mg1_ref, e1p_ref, e0p_ref, corr_ref, e0x_ref, e1_ref, g_ref, c_ref,
+    fine_hbm, base_hbm,
+    mg1_ref, e1p_ref, e0p_ref, corr_ref, e0x_ref, e1_ref, g_ref, c_ref, fine_ref, base_ref, sem_ref,
 ):
     assemble_base(e0x_ref, e0_ref, exlo_ref, exhi_ref, eylo_ref, eyhi_ref, 0, 0, ROWS_LAST, 2)
     for y1 in range(1, 7):
@@ -848,14 +848,26 @@
                 c_ref[2 * y + py, pl.ds(px, 16, stride=2), :] = v
 
     each(16, row)
-    for xt in range(4):
-        for t in range(8):
-            rows, cols = slice(8 * xt, 8 * xt + 8), slice(t * LANES, (t + 1) * LANES)
-            for s, v in enumerate(transpose_blocks([c_ref[4 * t + yy, rows, :] for yy in range(4)])):
-                fine_ref[0, 0, s, rows, cols] = v
-
-
-def call(kernel, name, out_shapes, n_smem, n_any, n_vmem, scratch=(), cost=None):
+    copies = [pltpu.make_async_copy(base_ref, base_hbm, sem_ref.at[4])]
+    copies[0].start()
+    block = lax.broadcasted_iota(jnp.int32, (8, LANES), 1) // 32
+    for s in range(4):
+        for xt in range(4):
+            rows = slice(8 * xt, 8 * xt + 8)
+            for t in range(8):
+                v = c_ref[4 * t + s, rows, :]
+                for yy in range(4):
+                    if yy != s:
+                        moved = pltpu.roll(c_ref[4 * t + yy, rows, :], 32 * (yy - s) % LANES, 1)
+                        v = jnp.where(block == yy, moved, v)
+                fine_ref[s, rows, t * LANES : (t + 1) * LANES] = v
+        copies.append(pltpu.make_async_copy(fine_ref.at[s], fine_hbm.at[0, 0, s], sem_ref.at[s]))
+        copies[-1].start()
+    for copy in copies:
+        copy.wait()
+
+
+def call(kernel, name, out_shapes, n_smem, n_any, n_vmem, scratch=(), cost=None, n_any_out=0):
     vmem = pl.BlockSpec(memory_space=pltpu.VMEM)
     smem = pl.BlockSpec(memory_space=pltpu.SMEM)
     anywhere = pl.BlockSpec(memory_space=pl.ANY)
@@ -864,7 +876,7 @@
         name=name,
         out_shape=[jax.ShapeDtypeStruct(s, F32) for s in out_shapes],
         in_specs=[smem] * n_smem + [anywhere] * n_any + [vmem] * n_vmem,
-        out_specs=[vmem] * len(out_shapes),
+        out_specs=[anywhere] * n_any_out + [vmem] * (len(out_shapes) - n_any_out),
         scratch_shapes=[pltpu.VMEM(s, F32) if isinstance(s, tuple) else s for s in scratch],
         cost_estimate=cost,
         compiler_params=pltpu.CompilerParams(vmem_limit_bytes=VMEM_LIMIT),
@@ -962,7 +974,8 @@
     )(e0, k0x, k1, sxlo, sxhi)[0]
     fine, base = call(
         last_kernel, "last", [fine_rhs.shape, (256, LANES)], 0, 0, 13,
-        [half, half, wide, (YF, XF, LANES), wide, half, (YF, XF, LANES), rows],
+        [half, half, wide, (YF, XF, LANES), wide, half, (YF, XF, LANES), rows, raw,
+         (256, LANES), pltpu.SemaphoreType.DMA((5,))], n_any_out=2,
     )(tables, m2, e0, sxlo, sxhi, sylo, syhi, k0x, k1, c4, m4, livex, e1i)
     return fine, base.reshape(base_rhs.shape)
 

time: 68.6 us -> 68.5 us (level)
  no operation moved by 1% of the time
where the time goes in v9:
time: 68.5 us; the launch traced here: 67.9 us
  starting transfers between devices  20.4 us (30%)
  Pallas kernels  16.5 us (24%)
  blocking collectives  13.6 us (20%)
  waiting for transfers between devices  13.1 us (19%)
  local copies, waits for them, and re-layouts  2.73 us (4%)
  between operations  1.51 us (2%)
    ppermute x10, starting transfers between devices, step(): lax.ppermute(value, axis, [(i, (i + by) % count) for i in range(count)])  17.1 us
    all_to_all x1, blocking collectives, local(): recv = lax.all_to_all(send, ('gx', 'gy'), 0, 0, tiled=True)  13.6 us
    ppermute x10, waiting for transfers between devices, step(): lax.ppermute(value, axis, [(i, (i + by) % count) for i in range(count)])  7.24 us
    ppermute x2, waiting for transfers between devices, swap_pairs(): lax.ppermute(value, axis, [(i, j if 0 <= j < count else i) for i, j in en...  5.89 us
    pallas_call x1, Pallas kernels, local(): call(middle_kernel, 'middle', [octets, coarse, own, tiles(16), tiles(16)]...  3.47 us
    pallas_call x1, Pallas kernels, local(): call(last_kernel, 'last', [fine_rhs.shape, (256, LANES)], 0, 0, 13, [half...  3.13 us
    unnamed x10, local copies, waits for them, and re-layouts  2.73 us
    all_to_all x1, starting transfers between devices, local(): recv = lax.all_to_all(send, ('gx', 'gy'), 0, 0, tiled=True)  2.58 us
  transfers between devices with their start and end apart: 13, of which 4 were waited for; matrix products, arithmetic and copies ran while one was open for 0% of the time, Pallas kernels for 9%

profile of v9, /device:TPU:0, one launch (start us, length us, event | category | flops | bytes accessed | tf_op | source)
XLA Modules:
  0.0 67.9 jit_solution(1824790940105547129)
XLA Ops:
  0.6 0.0 copy-start
  1.3 0.0 copy-start.4
  1.3 0.6 copy-done.4
  2.0 0.6 tables.1.tables_ref
  2.5 0.0 copy-start.1
  2.6 1.0 %copy-done.1 = f32[1,1,4,32,1024]{4,3,2,1,0:T(8,128)S(1)} copy-done((f32[1,1,4,32,1024]{4,3,2,1,0:T(8,128)S(1)}, f32[1,1,4,32,1024]{4,3,2,1,0:T(8,128)}, u32[]{:S(2)}) %copy-start.1) | copy-done | bytes 524312
  3.6 1.0 %copy-done.2 = f32[1,1,4,32,1024]{4,3,2,1,0:T(8,128)S(1)} copy-done((f32[1,1,4,32,1024]{4,3,2,1,0:T(8,128)S(1)}, f32[1,1,4,32,1024]{4,3,2,1,0:T(8,128)}, u32[]{:S(2)}) %copy-start.2) | copy-done | bytes 524312
  4.6 0.3 faces.1
  4.9 3.1 %collective-permute-start = (f32[17,8,128]{2,1,0:T(8,128)S(1)}, f32[17,8,128]{2,1,0:T(8,128)S(1)}, u32[]{:S(2)}, u32[]{:S(2)}) collective-permute-start(f32[17,8,128]{2,1,0:T(8,128)S(1)} %get-tuple-element.42), channel_id=1, source_target_pairs={{0,8},{8,16},{16,24},{24,0},{1,9},{9,17},{17,25},{25,1},{2,10},{10... | collective-permute-start | bytes 208904 | tf_op jit(solution)/shard_map/ppermute | solution.py:888
  8.0 2.1 %collective-permute-start.1 = (f32[17,8,128]{2,1,0:T(8,128)S(1)}, f32[17,8,128]{2,1,0:T(8,128)S(1)}, u32[]{:S(2)}, u32[]{:S(2)}) collective-permute-start(f32[17,8,128]{2,1,0:T(8,128)S(1)} %get-tuple-element.43), channel_id=1, source_target_pairs={{0,24},{8,0},{16,8},{24,16},{1,25},{9,1},{17,9},{25,17},{2,26},{10... | collective-permute-start | bytes 208904 | tf_op jit(solution)/shard_map/ppermute | solution.py:888
  10.1 0.0 collective-permute-start.2
  10.1 2.6 %collective-permute-start.3 = (f32[13,8,128]{2,1,0:T(8,128)S(1)}, f32[13,8,128]{2,1,0:T(8,128)S(1)}, u32[]{:S(2)}, u32[]{:S(2)}) collective-permute-start(f32[13,8,128]{2,1,0:T(8,128)S(1)} %get-tuple-element.45), channel_id=1, source_target_pairs={{0,7},{1,0},{2,1},{3,2},{4,3},{5,4},{6,5},{7,6},{8,15},{9,8},{10,9... | collective-permute-start | bytes 159752 | tf_op jit(solution)/shard_map/ppermute | solution.py:888
  12.8 1.8 %boxes.1 = (f32[8,16,16,128]{3,2,1,0:T(8,128)S(1)}, f32[8,16,16,128]{3,2,1,0:T(8,128)S(1)}) custom-call(f32[16,128]{1,0:T(8,128)S(1)} %tables.1.tables_ref, f32[4,32,1024]{2,1,0:T(8,128)S(1)} %get-tuple-element.38.raw_f_ref, f32[4,32,1024]{2,1,0:T(8,128)S(1)} %get-tuple-element.39.raw_q_ref), custom_call_target="tpu_custom_call" | custom-call | flops 3000000 | bytes 9000000 | tf_op jit(solution)/shard_map/boxes/pallas_call | solution.py:927
  14.6 0.0 collective-permute-done.2.rylo_ref
  14.6 0.0 collective-permute-done.3.ryhi_ref
  14.6 0.0 collective-permute-done.rxlo_ref
  14.6 0.0 collective-permute-done.1.rxhi_ref
  14.6 0.0 copy-done
  14.6 0.0 copy-done.3
  14.6 1.0 %first_residual.1 = (f32[16,16,128]{2,1,0:T(8,128)S(1)}, f32[16,16,128]{2,1,0:T(8,128)S(1)}, f32[36,8,128]{2,1,0:T(8,128)S(1)}, f32[36,8,128]{2,1,0:T(8,128)S(1)}) custom-call(f32[8,16,16,128]{3,2,1,0:T(8,128)S(1)} %get-tuple-element.40.f1_ref, f32[8,16,16,128]{3,2,1,0:T(8,128)S(1)} %get-tuple-element.41.q_ref, f32[256,128]{1,0:T(8,128)S(1)} %bitcast.5, ...), custom_call_target="tpu_custom_call" | custom-call | tf_op jit(solution)/shard_map/first_residual/pallas_call | solution.py:930
  15.6 0.1 collective-permute-start.4
  15.7 0.7 collective-permute-start.5
  16.4 5.9 %collective-permute-done.4.sa_ref.ea_ref = f32[36,8,128]{2,1,0:T(8,128)S(1)} collective-permute-done((f32[36,8,128]{2,1,0:T(8,128)S(1)}, f32[36,8,128]{2,1,0:T(8,128)S(1)}, u32[]{:S(2)}, u32[]{:S(2)}) %collective-permute-start.4) | collective-permute-done | bytes 147488 | tf_op jit(solution)/shard_map/ppermute | solution.py:894
  22.3 0.0 collective-permute-done.5.sb_ref.eb_ref
  22.3 0.1 collective-permute-start.6
  22.4 2.6 %collective-permute-start.7 = (f32[41,8,128]{2,1,0:T(8,128)S(1)}, f32[41,8,128]{2,1,0:T(8,128)S(1)}, u32[]{:S(2)}, u32[]{:S(2)}) collective-permute-start(f32[41,8,128]{2,1,0:T(8,128)S(1)} %get-tuple-element.52), channel_id=1, source_target_pairs={{0,7},{1,0},{2,1},{3,2},{4,3},{5,4},{6,5},{7,6},{8,15},{9,8},{10,9... | collective-permute-start | bytes 503816 | tf_op jit(solution)/shard_map/ppermute | solution.py:888
  25.0 0.6 inner.1
  25.6 1.4 %extend.1 = (f32[8,20,24,128]{3,2,1,0:T(8,128)S(1)}, f32[3,24,128]{2,1,0:T(8,128)S(1)}, f32[8,20,24,128]{3,2,1,0:T(8,128)S(1)}) custom-call(f32[8,16,16,128]{3,2,1,0:T(8,128)S(1)} %get-tuple-element.40.f1_ref, f32[8,16,16,128]{3,2,1,0:T(8,128)S(1)} %get-tuple-element.41.q_ref, f32[17,8,128]{2,1,0:T(8,128)S(1)} %collective-permute-done.rxlo_ref, ...), custom_call_target="tpu_custom_call" | custom-call | flops 2000000 | bytes 6000000 | tf_op jit(solution)/shard_map/extend/pallas_call | solution.py:938
  27.1 1.9 %collective-permute-done.6.eylo_ref = f32[41,8,128]{2,1,0:T(8,128)S(1)} collective-permute-done((f32[41,8,128]{2,1,0:T(8,128)S(1)}, f32[41,8,128]{2,1,0:T(8,128)S(1)}, u32[]{:S(2)}, u32[]{:S(2)}) %collective-permute-start.6) | collective-permute-done | bytes 167968 | tf_op jit(solution)/shard_map/ppermute | solution.py:888
  29.0 0.0 collective-permute-done.7.eyhi_ref
  29.0 0.9 %down_first.1 = (f32[32,8,128]{2,1,0:T(8,128)S(1)}, f32[32,32,128]{2,1,0:T(8,128)S(1)}, f32[32,32,128]{2,1,0:T(8,128)S(1)}, f32[16,32,128]{2,1,0:T(8,128)S(1)}, f32[16,32,128]{2,1,0:T(8,128)S(1)}) custom-call(f32[3,24,128]{2,1,0:T(8,128)S(1)} %get-tuple-element.48.live_ref.livex_ref, f32[16,16,128]{2,1,0:T(8,128)S(1)} %get-tuple-element.49.e0_ref, ...), custom_call_target="tpu_custom_call" | custom-call | tf_op jit(solution)/shard_map/down_first/pallas_call | solution.py:945
  29.8 13.6 %all_to_all.10.recv_ref = f32[32,8,128]{2,1,0:T(8,128)S(1)} all-to-all(f32[32,8,128]{2,1,0:T(8,128)S(1)} %get-tuple-element.56), channel_id=1, replica_groups=mesh['gx'=4,'gy'=8] {'gx','gy'}, dimensions={0} | all-to-all | bytes 262144 | tf_op jit(solution)/shard_map/all_to_all | solution.py:948
  43.4 3.5 %middle.1 = (f32[8,16,16,128]{3,2,1,0:T(8,128)S(1)}, f32[8,16,128]{2,1,0:T(8,128)S(1)}, f32[16,16,128]{2,1,0:T(8,128)S(1)}, f32[16,8,128]{2,1,0:T(8,128)S(1)}, f32[16,8,128]{2,1,0:T(8,128)S(1)}) custom-call(f32[32,8,128]{2,1,0:T(8,128)S(1)} %all_to_all.10.recv_ref, f32[32,32,128]{2,1,0:T(8,128)S(1)} %get-tuple-element.57.e0x_ref, ...), custom_call_target="tpu_custom_call" | custom-call | tf_op jit(solution)/shard_map/middle/pallas_call | solution.py:954
  46.9 1.3 %share.1 = f32[160,2,128]{2,1,0:T(2,128)} custom-call(f32[16,16,128]{2,1,0:T(8,128)S(1)} %get-tuple-element.63.e0_ref, f32[32,32,128]{2,1,0:T(8,128)S(1)} %get-tuple-element.58.k0x_ref, f32[16,32,128]{2,1,0:T(8,128)S(1)} %get-tuple-element.60.k1_ref), custom_call_target="tpu_custom_call" | custom-call | flops 1000000 | bytes 3000000 | tf_op jit(solution)/shard_map/share/pallas_call | solution.py:959
  48.2 2.6 %all-to-all-start.1 = ((f32[160,2,128]{2,1,0:T(2,128)}), f32[160,2,128]{2,1,0:T(2,128)S(1)}, u32[]{:S(2)}, u32[]{:S(2)}) async-start(f32[160,2,128]{2,1,0:T(2,128)} %share.1), calls=%async_computation.1 | async-start | bytes 327680 | tf_op jit(solution)/shard_map/all_to_all | solution.py:963
  50.8 1.7 %collective-permute-start.8 = (f32[16,8,128]{2,1,0:T(8,128)S(1)}, f32[16,8,128]{2,1,0:T(8,128)S(1)}, u32[]{:S(2)}, u32[]{:S(2)}) collective-permute-start(f32[16,8,128]{2,1,0:T(8,128)S(1)} %get-tuple-element.65), channel_id=1, source_target_pairs={{0,8},{8,16},{16,24},{24,0},{1,9},{9,17},{17,25},{25,1},{2,10},{10... | collective-permute-start | bytes 196616 | tf_op jit(solution)/shard_map/ppermute | solution.py:888
  52.5 2.1 %collective-permute-start.9 = (f32[16,8,128]{2,1,0:T(8,128)S(1)}, f32[16,8,128]{2,1,0:T(8,128)S(1)}, u32[]{:S(2)}, u32[]{:S(2)}) collective-permute-start(f32[16,8,128]{2,1,0:T(8,128)S(1)} %get-tuple-element.66), channel_id=1, source_target_pairs={{0,24},{8,0},{16,8},{24,16},{1,25},{9,1},{17,9},{25,17},{2,26},{10... | collective-permute-start | bytes 196616 | tf_op jit(solution)/shard_map/ppermute | solution.py:888
  54.7 0.3 settle.1
  55.0 5.0 %collective-permute-done.8.exlo_ref = f32[16,8,128]{2,1,0:T(8,128)S(1)} collective-permute-done((f32[16,8,128]{2,1,0:T(8,128)S(1)}, f32[16,8,128]{2,1,0:T(8,128)S(1)}, u32[]{:S(2)}, u32[]{:S(2)}) %collective-permute-start.8) | collective-permute-done | bytes 65568 | tf_op jit(solution)/shard_map/ppermute | solution.py:888
  60.0 0.0 collective-permute-done.9.exhi_ref
  60.0 0.0 all-to-all-done.1.recv_ref
  60.1 0.2 collective-permute-start.10
  60.3 2.5 %collective-permute-start.11 = (f32[17,8,128]{2,1,0:T(8,128)S(1)}, f32[17,8,128]{2,1,0:T(8,128)S(1)}, u32[]{:S(2)}, u32[]{:S(2)}) collective-permute-start(f32[17,8,128]{2,1,0:T(8,128)S(1)} %get-tuple-element.70), channel_id=1, source_target_pairs={{0,7},{1,0},{2,1},{3,2},{4,3},{5,4},{6,5},{7,6},{8,15},{9,8},{10,9... | collective-permute-start | bytes 208904 | tf_op jit(solution)/shard_map/ppermute | solution.py:888
  62.8 0.3 inner_last.1.e1i_ref
  63.1 1.3 %coarse.1.m2_ref = f32[8,32,128]{2,1,0:T(8,128)S(1)} custom-call(f32[160,2,128]{2,1,0:T(2,128)S(1)} %all-to-all-done.1.recv_ref, f32[8,16,128]{2,1,0:T(8,128)S(1)} %get-tuple-element.64.k2_ref), custom_call_target="tpu_custom_call" | custom-call | flops 2000000 | bytes 6000000 | tf_op jit(solution)/shard_map/coarse/pallas_call | solution.py:969
  64.4 0.3 collective-permute-done.10.eylo_ref
  64.8 0.0 collective-permute-done.11.eyhi_ref
  64.8 3.1 %last.1 = (f32[1,1,4,32,1024]{4,3,2,1,0:T(8,128)}, f32[256,128]{1,0:T(8,128)}) custom-call(f32[16,128]{1,0:T(8,128)S(1)} %tables.1.tables_ref, f32[8,32,128]{2,1,0:T(8,128)S(1)} %coarse.1.m2_ref, f32[16,16,128]{2,1,0:T(8,128)S(1)} %get-tuple-element.63.e0_ref, f32[16,8,128]{2,1,0:T(8,128)S(1)} %collective-permute-done.8.exlo_ref, ...), custom_call_target="tpu_custom_call" | custom-call | tf_op jit(solution)/shard_map/last/pallas_call | solution.py:975
  (4 shorter events, 0.1 us)
Async XLA Ops:
  0.6 14.0 %copy-start = (f32[16,16,128]{2,1,0:T(8,128)S(1)}, f32[16,16,128]{2,1,0:T(8,128)}, u32[]{:S(2)}) copy-start(f32[16,16,128]{2,1,0:T(8,128)} %param.9) | copy-start | bytes 393220
  1.3 0.7 copy-start.4
  2.5 1.0 %copy-start.1 = (f32[1,1,4,32,1024]{4,3,2,1,0:T(8,128)S(1)}, f32[1,1,4,32,1024]{4,3,2,1,0:T(8,128)}, u32[]{:S(2)}) copy-start(f32[1,1,4,32,1024]{4,3,2,1,0:T(8,128)} %rhs_ref.1) | copy-start | bytes 1572868
  3.6 1.0 %copy-start.2 = (f32[1,1,4,32,1024]{4,3,2,1,0:T(8,128)S(1)}, f32[1,1,4,32,1024]{4,3,2,1,0:T(8,128)}, u32[]{:S(2)}) copy-start(f32[1,1,4,32,1024]{4,3,2,1,0:T(8,128)} %beta_ref.1) | copy-start | bytes 1572868
  4.6 10.0 %copy-start.3 = (f32[16,16,128]{2,1,0:T(8,128)S(1)}, f32[16,16,128]{2,1,0:T(8,128)}, u32[]{:S(2)}) copy-start(f32[16,16,128]{2,1,0:T(8,128)} %param.10) | copy-start | bytes 393220
  4.9 9.7 %collective-permute-start = (f32[17,8,128]{2,1,0:T(8,128)S(1)}, f32[17,8,128]{2,1,0:T(8,128)S(1)}, u32[]{:S(2)}, u32[]{:S(2)}) collective-permute-start(f32[17,8,128]{2,1,0:T(8,128)S(1)} %get-tuple-element.42), channel_id=1, source_target_pairs={{0,8},{8,16},{16,24},{24,0},{1,9},{9,17},{17,25},{25,1},{2,10},{10... | collective-permute-start | bytes 208904 | tf_op jit(solution)/shard_map/ppermute | solution.py:888
  8.0 6.6 %collective-permute-start.1 = (f32[17,8,128]{2,1,0:T(8,128)S(1)}, f32[17,8,128]{2,1,0:T(8,128)S(1)}, u32[]{:S(2)}, u32[]{:S(2)}) collective-permute-start(f32[17,8,128]{2,1,0:T(8,128)S(1)} %get-tuple-element.43), channel_id=1, source_target_pairs={{0,24},{8,0},{16,8},{24,16},{1,25},{9,1},{17,9},{25,17},{2,26},{10... | collective-permute-start | bytes 208904 | tf_op jit(solution)/shard_map/ppermute | solution.py:888
  10.1 4.5 %collective-permute-start.2 = (f32[13,8,128]{2,1,0:T(8,128)S(1)}, f32[13,8,128]{2,1,0:T(8,128)S(1)}, u32[]{:S(2)}, u32[]{:S(2)}) collective-permute-start(f32[13,8,128]{2,1,0:T(8,128)S(1)} %get-tuple-element.44), channel_id=1, source_target_pairs={{0,1},{1,2},{2,3},{3,4},{4,5},{5,6},{6,7},{7,0},{8,9},{9,10},{10,1... | collective-permute-start | bytes 159752 | tf_op jit(solution)/shard_map/ppermute | solution.py:888
  10.1 4.5 %collective-permute-start.3 = (f32[13,8,128]{2,1,0:T(8,128)S(1)}, f32[13,8,128]{2,1,0:T(8,128)S(1)}, u32[]{:S(2)}, u32[]{:S(2)}) collective-permute-start(f32[13,8,128]{2,1,0:T(8,128)S(1)} %get-tuple-element.45), channel_id=1, source_target_pairs={{0,7},{1,0},{2,1},{3,2},{4,3},{5,4},{6,5},{7,6},{8,15},{9,8},{10,9... | collective-permute-start | bytes 159752 | tf_op jit(solution)/shard_map/ppermute | solution.py:888
  15.6 6.6 %collective-permute-start.4 = (f32[36,8,128]{2,1,0:T(8,128)S(1)}, f32[36,8,128]{2,1,0:T(8,128)S(1)}, u32[]{:S(2)}, u32[]{:S(2)}) collective-permute-start(f32[36,8,128]{2,1,0:T(8,128)S(1)} %get-tuple-element.46), channel_id=1, source_target_pairs={{0,8},{8,0},{16,24},{24,16},{1,9},{9,1},{17,25},{25,17},{2,10},{10... | collective-permute-start | bytes 442376 | tf_op jit(solution)/shard_map/ppermute | solution.py:894
  15.7 6.6 %collective-permute-start.5 = (f32[36,8,128]{2,1,0:T(8,128)S(1)}, f32[36,8,128]{2,1,0:T(8,128)S(1)}, u32[]{:S(2)}, u32[]{:S(2)}) collective-permute-start(f32[36,8,128]{2,1,0:T(8,128)S(1)} %get-tuple-element.47), channel_id=1, source_target_pairs={{0,0},{8,16},{16,8},{24,24},{1,1},{9,17},{17,9},{25,25},{2,2},{10,... | collective-permute-start | bytes 442376 | tf_op jit(solution)/shard_map/ppermute | solution.py:894
  22.3 6.6 %collective-permute-start.6 = (f32[41,8,128]{2,1,0:T(8,128)S(1)}, f32[41,8,128]{2,1,0:T(8,128)S(1)}, u32[]{:S(2)}, u32[]{:S(2)}) collective-permute-start(f32[41,8,128]{2,1,0:T(8,128)S(1)} %get-tuple-element.51), channel_id=1, source_target_pairs={{0,1},{1,2},{2,3},{3,4},{4,5},{5,6},{6,7},{7,0},{8,9},{9,10},{10,1... | collective-permute-start | bytes 503816 | tf_op jit(solution)/shard_map/ppermute | solution.py:888
  22.4 6.6 %collective-permute-start.7 = (f32[41,8,128]{2,1,0:T(8,128)S(1)}, f32[41,8,128]{2,1,0:T(8,128)S(1)}, u32[]{:S(2)}, u32[]{:S(2)}) collective-permute-start(f32[41,8,128]{2,1,0:T(8,128)S(1)} %get-tuple-element.52), channel_id=1, source_target_pairs={{0,7},{1,0},{2,1},{3,2},{4,3},{5,4},{6,5},{7,6},{8,15},{9,8},{10,9... | collective-permute-start | bytes 503816 | tf_op jit(solution)/shard_map/ppermute | solution.py:888
  48.2 11.8 %all-to-all-start.1 = ((f32[160,2,128]{2,1,0:T(2,128)}), f32[160,2,128]{2,1,0:T(2,128)S(1)}, u32[]{:S(2)}, u32[]{:S(2)}) async-start(f32[160,2,128]{2,1,0:T(2,128)} %share.1), calls=%async_computation.1 | async-start | bytes 327680 | tf_op jit(solution)/shard_map/all_to_all | solution.py:963
  50.8 9.2 %collective-permute-start.8 = (f32[16,8,128]{2,1,0:T(8,128)S(1)}, f32[16,8,128]{2,1,0:T(8,128)S(1)}, u32[]{:S(2)}, u32[]{:S(2)}) collective-permute-start(f32[16,8,128]{2,1,0:T(8,128)S(1)} %get-tuple-element.65), channel_id=1, source_target_pairs={{0,8},{8,16},{16,24},{24,0},{1,9},{9,17},{17,25},{25,1},{2,10},{10... | collective-permute-start | bytes 196616 | tf_op jit(solution)/shard_map/ppermute | solution.py:888
  52.5 7.5 %collective-permute-start.9 = (f32[16,8,128]{2,1,0:T(8,128)S(1)}, f32[16,8,128]{2,1,0:T(8,128)S(1)}, u32[]{:S(2)}, u32[]{:S(2)}) collective-permute-start(f32[16,8,128]{2,1,0:T(8,128)S(1)} %get-tuple-element.66), channel_id=1, source_target_pairs={{0,24},{8,0},{16,8},{24,16},{1,25},{9,1},{17,9},{25,17},{2,26},{10... | collective-permute-start | bytes 196616 | tf_op jit(solution)/shard_map/ppermute | solution.py:888
  60.1 4.7 %collective-permute-start.10 = (f32[17,8,128]{2,1,0:T(8,128)S(1)}, f32[17,8,128]{2,1,0:T(8,128)S(1)}, u32[]{:S(2)}, u32[]{:S(2)}) collective-permute-start(f32[17,8,128]{2,1,0:T(8,128)S(1)} %get-tuple-element.69), channel_id=1, source_target_pairs={{0,1},{1,2},{2,3},{3,4},{4,5},{5,6},{6,7},{7,0},{8,9},{9,10},{10,1... | collective-permute-start | bytes 208904 | tf_op jit(solution)/shard_map/ppermute | solution.py:888
  60.3 4.5 %collective-permute-start.11 = (f32[17,8,128]{2,1,0:T(8,128)S(1)}, f32[17,8,128]{2,1,0:T(8,128)S(1)}, u32[]{:S(2)}, u32[]{:S(2)}) collective-permute-start(f32[17,8,128]{2,1,0:T(8,128)S(1)} %get-tuple-element.70), channel_id=1, source_target_pairs={{0,7},{1,0},{2,1},{3,2},{4,3},{5,4},{6,5},{7,6},{8,15},{9,8},{10,9... | collective-permute-start | bytes 208904 | tf_op jit(solution)/shard_map/ppermute | solution.py:888
